TPU v7x, 256 devices: a whole 4x4x8 slice. The times are simulated.
256 devices in a mesh: scen: 4 (over x_hi, core), tm: 64 (over z, x_lo, y).
Axes of the slice: x: 4 (x_hi: 2, x_lo: 2; x = x_hi * 2 + x_lo), y: 4, z: 8, core: 2. Of those that a mesh axis runs over, the one named last changes fastest.
Arguments:
- weights: float32 [512, 8, 128, 128], P('tm'), may hold values from 0.0002 to 0.04
- pattern: int32 [512, 8], P('tm'), may hold values 0 or 1
- shift_reg: float32 [512, 128], P('tm'), may hold values from 0.2 to 2
- rhs: float32 [512, 256, 128], P('tm', 'scen'), parts along dimension 1, may hold values from -24 to 24
Outputs:
- solution: float32 [512, 256, 128], P('tm', 'scen'), parts along dimension 1
- residual: float32 [512, 256, 128], P('tm', 'scen'), parts along dimension 1
There are 4 independent parts, one for each index of `scen`. A program takes and returns all parts, laid end to end along the dimension named above; an argument that names none is the same for every part. Nothing has to cross between parts.
All inputs are finite; a program needn't handle non-finite values. No bound on the sum of `pattern` on one device may be relied on, other than what follows from the above.
Results may differ from a plain program's by a relative error of at most 0.0003.
Values sent between devices are 32-bit elements; how exact they have to be, the bound alone decides.
No kernel may reach another device: no remote copies, remote signals or barrier semaphores. Data moves between devices by JAX's collectives and lax.ppermute only.
A program may use at most 64 MiB of HBM per device.

v0:
```python
import jax
import jax.numpy as jnp
from jax import lax
from jax.sharding import PartitionSpec as P

ITERS = 3


def shifted(value, axis, steps):
    count = lax.axis_size(axis)
    pairs = [(source, (source + steps) % count) for source in range(count)]
    return lax.ppermute(value, axis, pairs)


def with_halo(cells, sides, width):
    for axis, dim in sides:
        count = lax.axis_size(axis)
        head = lax.slice_in_dim(cells, 0, width, axis=dim)
        tail = lax.slice_in_dim(cells, cells.shape[dim] - width, cells.shape[dim], axis=dim)
        cells = jnp.concatenate(
            [
                lax.ppermute(tail, axis, [(i, (i + 1) % count) for i in range(count)]),
                cells,
                lax.ppermute(head, axis, [((i + 1) % count, i) for i in range(count)]),
            ],
            axis=dim,
        )
    return cells


def inner(first, second):
    return jnp.sum(first * second, axis=(0, 2))


def forward_terms(extended, masked, start, count):
    total = jnp.zeros((count, extended.shape[1], extended.shape[2]), jnp.float32)
    for k in range(masked.shape[1]):
        lo = start + k + 1
        total = total + jnp.einsum(
            "trj,tij->tri", extended[lo : lo + count], masked[:, k], precision=lax.Precision.HIGHEST
        )
    return total


def precond_sum(residual, precond):
    return lax.psum(inner(residual, precond), "tm")


def shards(weights, pattern, shift_reg, rhs):
    count = weights.shape[0]
    width = weights.shape[1]
    masked = weights * pattern.astype(jnp.float32)[:, :, None, None]
    rowsum = jnp.sum(masked, axis=(1, 3))
    colsum = jnp.sum(masked, axis=2)
    earlier = shifted(masked, "tm", 1)
    wide = jnp.concatenate([earlier, masked], axis=0)
    colwide = jnp.concatenate([jnp.sum(earlier, axis=2), colsum], axis=0)
    inflow = jnp.zeros_like(rowsum)
    for k in range(width):
        lo = width - k - 1
        inflow = inflow + colwide[lo : lo + count, k]
    diag = rowsum + inflow + shift_reg
    scaled = diag[:, None, :]
    solution = jnp.zeros_like(rhs)
    residual = rhs
    precond = residual / scaled
    direction = precond
    norm_now = precond_sum(residual, precond)
    for step in range(ITERS):
        extended = with_halo(direction, (("tm", 0),), width)
        total = forward_terms(extended, masked, width, count)
        for coupled_k in range(width):
            coupled_lo = width - coupled_k - 1
            total = total + jnp.einsum(
                "tri,tij->trj",
                extended[coupled_lo : coupled_lo + count],
                wide[coupled_lo : coupled_lo + count, coupled_k],
                precision=lax.Precision.HIGHEST,
            )
        image = scaled * direction - total
        alpha = norm_now / lax.psum(inner(direction, image), "tm")
        solution = solution + alpha[None, :, None] * direction
        residual = residual - alpha[None, :, None] * image
        precond = residual / scaled
        norm_next = precond_sum(residual, precond)
        direction = precond + (norm_next / norm_now)[None, :, None] * direction
        norm_now = norm_next
    return (solution, residual)


def solution(mesh):
    return jax.shard_map(
        shards,
        mesh=mesh,
        in_specs=(P("tm", None, None, None), P("tm", None), P("tm", None), P("tm", "scen", None)),
        out_specs=(P("tm", "scen", None), P("tm", "scen", None)),
        check_vma=False,
    )
```

profile of v0, /device:TPU:4, one launch (start us, length us, event | category | flops | bytes accessed | tf_op | source)
XLA Modules:
  0.0 964.1 jit_solution(18409577244962974037)
XLA Ops:
  1.4 2.9 fusion.95
  4.3 1.9 copy-done
  7.8 98.0 %collective-permute-done = f32[8,8,128,128]{3,2,0,1:T(8,128)} collective-permute-done((f32[8,8,128,128]{3,2,0,1:T(8,128)S(1)}, f32[8,8,128,128]{3,2,0,1:T(8,128)}, u32[]{:S(2)}, u32[]{:S(2)}) %collective-permute-start) | collective-permute-done | bytes 4194336 | tf_op jit(solution)/shard_map/ppermute | solution.py:12
  105.8 2.6 reduce_sum.82
  108.5 1.8 collective-permute-start.1
  111.1 2.4 maximum_bitcast_fusion.5
  113.5 2.6 collective-permute-done.1
  129.7 2.1 multiply_reduce_fusion.4
  131.8 158.0 %all-reduce = (f32[64]{0:T(128)S(1)}, f32[64]{0:T(128)S(1)}) all-reduce(f32[64]{0:T(128)S(1)} %get-tuple-element.5, f32[64]{0:T(128)S(1)} %get-tuple-element.4), channel_id=1, replica_groups=mesh['scen'=4,'tm'=64] {'tm'}, use_global_device_ids=true, to_apply=%region_4.0 | all-reduce | flops 128 | bytes 1024 | tf_op jit(solution)/shard_map/psum | solution.py:46
  289.8 1.9 multiply_reduce_fusion.3
  291.7 152.5 %psum.44 = f32[64]{0:T(128)S(1)} all-reduce(f32[64]{0:T(128)S(1)} %get-tuple-element.10), channel_id=1, replica_groups=mesh['scen'=4,'tm'=64] {'tm'}, use_global_device_ids=true, to_apply=%region_8.0 | all-reduce | flops 64 | bytes 512 | tf_op jit(solution)/shard_map/psum | solution.py:46
  445.3 2.1 collective-permute-start.4
  447.4 4.4 collective-permute-start.3
  451.8 4.3 collective-permute-done.4
  470.8 2.0 multiply_reduce_fusion.2
  472.8 152.3 %psum.45 = f32[64]{0:T(128)S(1)} all-reduce(f32[64]{0:T(128)S(1)} %get-tuple-element.23), channel_id=1, replica_groups=mesh['scen'=4,'tm'=64] {'tm'}, use_global_device_ids=true, to_apply=%region_10.0 | all-reduce | flops 64 | bytes 512 | tf_op jit(solution)/shard_map/psum | solution.py:81
  626.4 154.5 %psum.46 = f32[64]{0:T(128)S(1)} all-reduce(f32[64]{0:T(128)S(1)} %get-tuple-element.8), channel_id=1, replica_groups=mesh['scen'=4,'tm'=64] {'tm'}, use_global_device_ids=true, to_apply=%region_12.0 | all-reduce | flops 64 | bytes 512 | tf_op jit(solution)/shard_map/psum | solution.py:46
  781.0 6.4 collective-permute-start.5
  787.4 4.2 collective-permute-done.6
  793.3 1.8 fusion.78
  798.0 1.6 fusion.67
  807.5 2.1 multiply_reduce_fusion
  809.6 152.3 %psum.47 = f32[64]{0:T(128)S(1)} all-reduce(f32[64]{0:T(128)S(1)} %get-tuple-element.25), channel_id=1, replica_groups=mesh['scen'=4,'tm'=64] {'tm'}, use_global_device_ids=true, to_apply=%region_14.0 | all-reduce | flops 64 | bytes 512 | tf_op jit(solution)/shard_map/psum | solution.py:81
  962.0 1.9 multiply_subtract_fusion
  (82 shorter events, 46.3 us)
Async XLA Ops:
  4.3 1.9 copy-start
  4.3 104.2 %copy-start.10 = (f32[8,128]{1,0:T(8,128)S(1)}, f32[8,128]{1,0:T(8,128)}, u32[]{:S(2)}) copy-start(f32[8,128]{1,0:T(8,128)} %param.6) | copy-start | bytes 12292
  4.3 104.2 %copy-start.6 = (f32[8,64,128]{2,1,0:T(8,128)S(1)}, f32[8,64,128]{2,1,0:T(8,128)}, u32[]{:S(2)}) copy-start(f32[8,64,128]{2,1,0:T(8,128)} %param.7) | copy-start | bytes 786436
  6.2 99.6 %collective-permute-start = (f32[8,8,128,128]{3,2,0,1:T(8,128)S(1)}, f32[8,8,128,128]{3,2,0,1:T(8,128)}, u32[]{:S(2)}, u32[]{:S(2)}) collective-permute-start(f32[8,8,128,128]{3,2,0,1:T(8,128)S(1)} %get-tuple-element.12), channel_id=1, source_target_pairs={{0,1},{1,2},{2,3},{3,4},{4,5},{5,6},{6,7},{7,8},{8,9},{9,10},{10,1... | collective-permute-start | bytes 12582920 | tf_op jit(solution)/shard_map/ppermute | solution.py:12
  108.5 7.6 copy-start.1
  108.5 7.6 collective-permute-start.1
  110.4 13.5 %collective-permute-start.2 = (f32[8,64,128]{2,1,0:T(8,128)S(1)}, f32[8,64,128]{2,1,0:T(8,128)S(1)}, u32[]{:S(2)}, u32[]{:S(2)}) collective-permute-start(f32[8,64,128]{2,1,0:T(8,128)S(1)} %broadcast_divide_fusion), channel_id=1, source_target_pairs={{0,1},{1,2},{2,3},{3,4},{4,5},{5,6},{6,7},{7,8},{8,9},{9,10},{10,1... | collective-permute-start | bytes 786440 | tf_op jit(solution)/shard_map/ppermute | solution.py:22
  113.5 15.0 %copy-start.5 = (f32[8,128,128]{2,1,0:T(8,128)}, f32[8,128,128]{2,1,0:T(8,128)S(1)}, u32[]{:S(2)}) copy-start(f32[8,128,128]{2,1,0:T(8,128)S(1)} %get-tuple-element.18) | copy-start | bytes 1572868
  113.5 344.2 %copy-start.4 = (f32[8,128,128]{2,1,0:T(8,128)}, f32[8,128,128]{2,1,0:T(8,128)S(1)}, u32[]{:S(2)}) copy-start(f32[8,128,128]{2,1,0:T(8,128)S(1)} %get-tuple-element.17) | copy-start | bytes 1572868
  126.1 3.6 copy-start.7
  445.3 10.8 %collective-permute-start.4 = (f32[8,64,128]{2,1,0:T(8,128)S(1)}, f32[8,64,128]{2,1,0:T(8,128)S(1)}, u32[]{:S(2)}, u32[]{:S(2)}) collective-permute-start(f32[8,64,128]{2,1,0:T(8,128)S(1)} %multiply_add_fusion.2), channel_id=1, source_target_pairs={{0,1},{1,2},{2,3},{3,4},{4,5},{5,6},{6,7},{7,8},{8,9},{9,10},{10,1... | collective-permute-start | bytes 786440 | tf_op jit(solution)/shard_map/ppermute | solution.py:22
  447.4 15.5 %collective-permute-start.3 = (f32[8,64,128]{2,1,0:T(8,128)S(1)}, f32[8,64,128]{2,1,0:T(8,128)S(1)}, u32[]{:S(2)}, u32[]{:S(2)}) collective-permute-start(f32[8,64,128]{2,1,0:T(8,128)S(1)} %multiply_add_fusion.2), channel_id=1, source_target_pairs={{1,0},{2,1},{3,2},{4,3},{5,4},{6,5},{7,6},{8,7},{9,8},{10,9},{11,1... | collective-permute-start | bytes 786440 | tf_op jit(solution)/shard_map/ppermute | solution.py:24
  457.7 5.2 copy-start.2
  468.5 156.7 %copy-start.9 = (f32[8,64,128]{2,1,0:T(8,128)S(1)}, f32[8,64,128]{2,1,0:T(8,128)}, u32[]{:S(2)}) copy-start(f32[8,64,128]{2,1,0:T(8,128)} %get-tuple-element.11) | copy-start | bytes 786436
  780.9 10.7 %collective-permute-start.6 = (f32[8,64,128]{2,1,0:T(8,128)S(1)}, f32[8,64,128]{2,1,0:T(8,128)S(1)}, u32[]{:S(2)}, u32[]{:S(2)}) collective-permute-start(f32[8,64,128]{2,1,0:T(8,128)S(1)} %multiply_add_fusion.1), channel_id=1, source_target_pairs={{0,1},{1,2},{2,3},{3,4},{4,5},{5,6},{6,7},{7,8},{8,9},{9,10},{10,1... | collective-permute-start | bytes 786440 | tf_op jit(solution)/shard_map/ppermute | solution.py:22
  781.0 18.6 %collective-permute-start.5 = (f32[8,64,128]{2,1,0:T(8,128)S(1)}, f32[8,64,128]{2,1,0:T(8,128)S(1)}, u32[]{:S(2)}, u32[]{:S(2)}) collective-permute-start(f32[8,64,128]{2,1,0:T(8,128)S(1)} %multiply_add_fusion.1), channel_id=1, source_target_pairs={{1,0},{2,1},{3,2},{4,3},{5,4},{6,5},{7,6},{8,7},{9,8},{10,9},{11,1... | collective-permute-start | bytes 786440 | tf_op jit(solution)/shard_map/ppermute | solution.py:24
  793.3 6.4 copy-start.3
  805.3 156.7 %copy-start.8 = (f32[8,64,128]{2,1,0:T(8,128)S(1)}, f32[8,64,128]{2,1,0:T(8,128)}, u32[]{:S(2)}) copy-start(f32[8,64,128]{2,1,0:T(8,128)} %param.7) | copy-start | bytes 786436
where the time goes:
time: 968 us; the launch traced here: 964 us
  blocking collectives  770 us (80%)
  waiting for transfers between devices  109 us (11%)
  matrix products  50.2 us (5%)
  starting transfers between devices  17.1 us (2%)
  other arithmetic  14.9 us (2%)
    psum x3, blocking collectives, precond_sum(): return lax.psum(inner(residual, precond), 'tm')  465 us
    psum x2, blocking collectives, shards(): alpha = norm_now / lax.psum(inner(direction, image), 'tm')  305 us
    ppermute x1, waiting for transfers between devices, shifted(): return lax.ppermute(value, axis, pairs)  98 us
    dot_general x24, matrix products, forward_terms(): jnp.einsum('trj,tij->tri', extended[lo:lo + count], masked[:, k], precisi...  29.6 us
    dot_general x24, matrix products, shards(): jnp.einsum('tri,tij->trj', extended[coupled_lo:coupled_lo + count], wide[...  20.6 us
  transfers between devices with their start and end apart: 7, of which 4 were waited for; matrix products, arithmetic and copies ran while one was open for 3% of the time, Pallas kernels for 0%

commit v1 on v0

v1 whole, which is shorter than its diff:
```python
import functools

import jax
import jax.numpy as jnp
from jax import lax
from jax.experimental import pallas as pl
from jax.experimental.pallas import tpu as pltpu
from jax.sharding import PartitionSpec as P

F32 = jnp.float32
BF16 = jnp.bfloat16
MIB = 1024 * 1024
N = 128
T = 8
R = 64
VMEM = pl.BlockSpec(memory_space=pltpu.VMEM)
SMEM = pl.BlockSpec(memory_space=pltpu.SMEM)

BAND = (T // 2, 2 * N, (T + 1) * N)


def call(body, outs, specs=None, scratch=(), limit=16, flops=0, moved=0):
    return pl.pallas_call(
        body,
        out_shape=outs,
        in_specs=specs,
        out_specs=jax.tree.map(lambda _: VMEM, outs),
        scratch_shapes=list(scratch),
        compiler_params=pltpu.CompilerParams(vmem_limit_bytes=limit * MIB),
        cost_estimate=pl.CostEstimate(flops=flops, bytes_accessed=moved, transcendentals=0),
    )


def shape(*dims, dtype=F32):
    return jax.ShapeDtypeStruct(dims, dtype)


def dot(a, b):
    return lax.dot_general(a, b, (((1,), (0,)), ((), ())), preferred_element_type=F32)


def dot_t(a, b):
    return lax.dot_general(a, b, (((1,), (1,)), ((), ())), preferred_element_type=F32)


def two_sum(a, b):
    s = a + b
    t = s - a
    return s, (a - (s - t)) + (b - t)


def dd_add(a, b):
    s, e = two_sum(a[0], b[0])
    return s, e + (a[1] + b[1])


def halves(a):
    t = a * 4097.0
    h = t - (t - a)
    return h, a - h


def two_prod(a, b):
    p = a * b
    ah, al = halves(a)
    bh, bl = halves(b)
    return p, ((ah * bh - p) + ah * bl + al * bh) + al * bl


def sums_kernel(pattern, weights, reg, high, low, own, ahead, buf, cols, sems):
    def copy(t):
        return pltpu.make_async_copy(weights.at[t], buf.at[t], sems.at[t])

    for t in range(T):
        copy(t).start()
    cols[...] = jnp.zeros_like(cols)
    zero = jnp.zeros((N, N), BF16)
    for a in range(T // 2):
        for piece in (high, low):
            piece[a, N : 2 * N, 0:N] = zero
            piece[a, 0:N, T * N : (T + 1) * N] = zero

    def step(a, carry):
        for half in range(2):
            t = 2 * a + half
            copy(t).wait()
            rows = jnp.zeros((N, N), F32)
            for k in range(T):
                m = buf[t, k] * pattern[t, k].astype(F32)
                rows = rows + m
                cols[t + k + 1] += jnp.sum(m.reshape(N // 8, 8, N), axis=0)
                h = m.astype(BF16)
                place = slice((k + half) * N, (k + half + 1) * N)
                high[a, half * N : (half + 1) * N, place] = h
                low[a, half * N : (half + 1) * N, place] = (m - h.astype(F32)).astype(BF16)
            own[pl.ds(t, 1), :] = reg[pl.ds(t, 1), :] + jnp.sum(rows.T, axis=0, keepdims=True)
        return carry

    lax.fori_loop(0, T // 2, step, 0)
    inflow = jnp.sum(cols[...], axis=1)
    own[...] += inflow[:T]
    ahead[...] = inflow[T:]


def sums(pattern, weights, reg):
    return call(
        sums_kernel,
        (shape(*BAND, dtype=BF16), shape(*BAND, dtype=BF16), shape(T, N), shape(T, N)),
        [SMEM, pl.BlockSpec(memory_space=pl.ANY), VMEM],
        [pltpu.VMEM((T, T, N, N), F32), pltpu.VMEM((2 * T, 8, N), F32), pltpu.SemaphoreType.DMA((T,))],
        flops=8 * T * T * N * N,
        moved=4 * T * T * N * N,
    )(pattern, weights, reg)


def put_pieces(pieces, t, value):
    h = value.astype(BF16)
    pieces[0:R, t * N : (t + 1) * N] = h
    pieces[R : 2 * R, t * N : (t + 1) * N] = (value - h.astype(F32)).astype(BF16)


def product(pieces, cols, high, low, mult):
    both = mult(pieces[:, cols], high)
    return (both[:R] + mult(pieces[0:R, cols], low)) + both[R:]


def to_next(pieces, high, low, out):
    for b in range(T // 2):
        total = None
        for a in range(b, T // 2):
            at = slice((7 + 2 * b - 2 * a) * N, (9 + 2 * b - 2 * a) * N)
            term = product(pieces, slice(a * 2 * N, (a + 1) * 2 * N), high[a, :, at], low[a, :, at], dot)
            total = term if total is None else total + term
        out[2 * b] = total[:, :N]
        out[2 * b + 1] = total[:, N:]


def within(pieces, high, low, out):
    out[0] = jnp.zeros((R, N), F32)
    for p in range(T // 2):
        total = None
        width = 2 * N if p < T // 2 - 1 else N
        for a in range(p + 1):
            at = slice(2 * (p - a) * N, 2 * (p - a) * N + width)
            term = product(pieces, slice(a * 2 * N, (a + 1) * 2 * N), high[a, :, at], low[a, :, at], dot)
            total = term if total is None else total + term
        out[2 * p + 1] = total[:, :N]
        if width > N:
            out[2 * p + 2] = total[:, N:]
    for a in range(T // 2):
        at = slice(0, (7 - 2 * a) * N)
        term = product(pieces, slice((2 * a + 1) * N, T * N), high[a, :, at], low[a, :, at], dot_t)
        out[2 * a] += term[:, :N]
        out[2 * a + 1] += term[:, N:]


def from_next(pieces, high, low, out):
    for a in range(T // 2):
        at = slice((7 - 2 * a) * N, (T + 1) * N)
        term = product(pieces, slice(0, (2 * a + 2) * N), high[a, :, at], low[a, :, at], dot_t)
        out[2 * a] += term[:, :N]
        out[2 * a + 1] += term[:, N:]


def moments(first, second):
    high = low = jnp.zeros((R, N), F32)
    for t in range(T):
        high, err = two_sum(high, first[t] * second[t])
        low = low + err
    return high, low


PIECES = pltpu.VMEM((2 * R, T * N), BF16)
ONE_WAY = 2 * 3 * 40 * R * N * N


def start_kernel(rhs, own, arrived, high, low, diag, vec, out, pieces):
    diag[...] = own[...] + arrived[...]
    for t in range(T):
        value = rhs[t] / diag[t : t + 1, :]
        vec[t] = value
        put_pieces(pieces, t, value)
    to_next(pieces, high, low, out)


def start(rhs, own, arrived, high, low):
    return call(
        start_kernel,
        (shape(T, N), shape(T, R, N), shape(T, R, N)),
        [VMEM] * 5,
        [PIECES],
        flops=ONE_WAY,
    )(rhs, own, arrived, high, low)


def contrib_kernel(vec, high, low, out, pieces):
    for t in range(T):
        put_pieces(pieces, t, vec[t])
    to_next(pieces, high, low, out)


def contrib(vec, high, low):
    return call(contrib_kernel, shape(T, R, N), [VMEM] * 3, [PIECES], flops=ONE_WAY)(vec, high, low)


def local_kernel(count, *refs):
    vecs, (image, high, low, out, found, pieces) = refs[:count], refs[count:]
    for t in range(T):
        put_pieces(pieces, t, vecs[-1][t])
    within(pieces, high, low, out)
    for i, vec in enumerate(vecs):
        h, l = moments(vec, image)
        found[i, 0] = h
        found[i, 1] = l


def local(vecs, image, high, low):
    return call(
        functools.partial(local_kernel, len(vecs)),
        (shape(T, R, N), shape(len(vecs), 2, R, N)),
        [VMEM] * (len(vecs) + 3),
        [PIECES],
        flops=2 * ONE_WAY,
    )(*vecs, image, high, low)


def finish_first_kernel(rhs_next, own_next, ahead, high, low, partial, out, pieces):
    scale = own_next[...] + ahead[...]
    for t in range(T):
        put_pieces(pieces, t, rhs_next[t] / scale[t : t + 1, :])
    out[...] = partial[...]
    from_next(pieces, high, low, out)


def finish_first(rhs_next, own_next, ahead, high, low, partial):
    return call(finish_first_kernel, shape(T, R, N), [VMEM] * 6, [PIECES], flops=ONE_WAY)(
        rhs_next, own_next, ahead, high, low, partial
    )


def finish_kernel(vec_next, high, low, partial, out, pieces):
    for t in range(T):
        put_pieces(pieces, t, vec_next[t])
    out[...] = partial[...]
    from_next(pieces, high, low, out)


def finish(vec_next, high, low, partial):
    return call(finish_kernel, shape(T, R, N), [VMEM] * 4, [PIECES], flops=ONE_WAY)(vec_next, high, low, partial)


def fold(found):
    high, low = (jnp.concatenate([f[i] for f in found], axis=0).T for i in range(2))
    value = (high[:N], low[:N])
    size = N
    while size > 8:
        size //= 2
        value = dd_add(tuple(v[:size] for v in value), tuple(v[size:] for v in value))
    for turn in (4, 2, 1):
        value = dd_add(value, tuple(pltpu.roll(v, turn, 0) for v in value))
    return value


def gram_kernel(v0, v1, v2, image, m0, m1, m2, out):
    last = [moments(v, image) for v in (v0, v1, v2)]
    every = [(m[i, 0], m[i, 1]) for m in (m0, m1, m2) for i in range(m.shape[0])] + last + last[-1:]
    out[...] = jnp.zeros_like(out)
    for q in range(5):
        h, l = fold(every[2 * q : 2 * q + 2])
        out[q : q + 1, :] = h[0:1]
        out[8 + q : 9 + q, :] = l[0:1]


def gram(vecs, image, found):
    return call(gram_kernel, shape(16, 2 * R), [VMEM] * 7)(*vecs, image, *found)


def solve(matrix, right):
    (a00, a01, a02), (a10, a11, a12), (a20, a21, a22) = matrix
    b0, b1, b2 = right
    inv0 = 1.0 / a00
    f1, f2 = a10 * inv0, a20 * inv0
    c11, c12, e1 = a11 - f1 * a01, a12 - f1 * a02, b1 - f1 * b0
    c21, c22, e2 = a21 - f2 * a01, a22 - f2 * a02, b2 - f2 * b0
    inv1 = 1.0 / c11
    g = c21 * inv1
    x2 = (e2 - g * e1) / (c22 - g * c12)
    x1 = (e1 - c12 * x2) * inv1
    x0 = (b0 - a01 * x1 - a02 * x2) * inv0
    return x0, x1, x2


def result_kernel(sums_ref, v0, v1, v2, y0, y1, y2, y3, sol, res):
    flat = []
    for q in range(5):
        h, l = sums_ref[q : q + 1, :], sums_ref[8 + q : 9 + q, :]
        flat += [(h, l), (pltpu.roll(h, R, 1), pltpu.roll(l, R, 1))]
    g00, g01, g11, g02, g12, g22, g03, g13, g23 = flat[:9]
    full = ((g00, g01, g02, g03), (g01, g11, g12, g13), (g02, g12, g22, g23))
    minus = lambda a, b: dd_add(a, (-b[0], -b[1]))
    matrix = [[minus(row[j], row[j + 1]) for j in range(3)] for row in full]
    right = [row[1] for row in full]
    near = [[m[0] + m[1] for m in row] for row in matrix]
    coef = [jnp.zeros_like(g00[0])] * 3
    for _ in range(3):
        left = []
        for row, value in zip(matrix, right):
            for m, c in zip(row, coef):
                p, e = two_prod(m[0], c)
                value = minus(value, (p, e + m[1] * c))
            left.append(value[0] + value[1])
        coef = [c + s for c, s in zip(coef, solve(near, left))]
    rows = jnp.concatenate([c[:, :N] for c in coef] + [jnp.zeros((N - 3, N), F32)], axis=0).T
    d0, d1, d2 = (jnp.broadcast_to(rows[:R, i : i + 1], (R, N)) for i in range(3))
    for t in range(T):
        sol[t] = v0[t] + (d0 * v0[t] + d1 * v1[t] + d2 * v2[t])
        first, second = y1[t], y2[t]
        res[t] = first - (d0 * (y0[t] - first) + d1 * (first - second) + d2 * (second - y3[t]))


def result(total, vecs, images):
    return call(result_kernel, (shape(T, R, N), shape(T, R, N)), [VMEM] * 8)(total, *vecs, *images)


def shift(value, steps):
    count = lax.axis_size("tm")
    return lax.ppermute(value, "tm", [(i, (i + steps) % count) for i in range(count)])


def pair_add(values):
    total = (values[0][:8], values[0][8:])
    for value in values[1:]:
        total = dd_add(total, (value[:8], value[8:]))
    return jnp.concatenate(total, axis=0)


def sum_all(value):
    count = lax.axis_size("tm")
    run = 4
    others = [
        lax.ppermute(value, "tm", [(i, i - i % run + (i + s) % run) for i in range(count)]) for s in range(1, run)
    ]
    value = pair_add([value] + others)
    groups = [[i for i in range(j, count, run)] for j in range(run)]
    size = count // run
    spread = lax.all_to_all(
        jnp.broadcast_to(value[None], (size,) + value.shape), "tm", 0, 0, axis_index_groups=groups
    )
    return pair_add([spread[i] for i in range(size)])


def shards(weights, pattern, shift_reg, rhs):
    rhs_next = shift(rhs, -1)
    high, low, own, ahead = sums(pattern, weights, shift_reg)
    arrived = shift(ahead, 1)
    own_next = shift(own, -1)
    diag, vec, out = start(rhs, own, arrived, high, low)
    arrived = shift(out, 1)
    vecs, images, found = [vec], [rhs], []
    partial, part = local(vecs, rhs, high, low)
    found.append(part)
    partial = finish_first(rhs_next, own_next, ahead, high, low, partial)
    for step in range(1, 3):
        image = partial + arrived
        vec = image / diag[:, None, :]
        vec_next = shift(vec, -1)
        out = contrib(vec, high, low)
        arrived = shift(out, 1)
        vecs.append(vec)
        images.append(image)
        partial, part = local(vecs, image, high, low)
        found.append(part)
        partial = finish(vec_next, high, low, partial)
    image = partial + arrived
    images.append(image)
    total = sum_all(gram(vecs, image, found))
    return result(total, vecs, images)


def solution(mesh):
    return jax.shard_map(
        shards,
        mesh=mesh,
        in_specs=(P("tm", None, None, None), P("tm", None), P("tm", None), P("tm", "scen", None)),
        out_specs=(P("tm", "scen", None), P("tm", "scen", None)),
        check_vma=False,
    )
```

time: 968 us -> 80.3 us (0.08)
  blocking collectives: 770 us -> 15.3 us
  waiting for transfers between devices: 109 us -> 24.2 us
  matrix products: 50.2 us -> 0 us
  other arithmetic: 14.9 us -> 0.17 us
  Pallas kernels: 0 us -> 12.4 us
    psum x5 -> x0, blocking collectives: 770 us -> none  [the longest x3 465 us: precond_sum(): return lax.psum(inner(residual, precond), 'tm')]
    ppermute x7 -> x11, waiting for transfers between devices: 109 us -> 24.2 us  [the longest x8 19.9 us: shift(): lax.ppermute(value, 'tm', [(i, (i + steps) % count) for i in range(count)])]
    dot_general x48 -> x0, matrix products: 50.2 us -> none  [the longest x24 29.6 us: forward_terms(): jnp.einsum('trj,tij->tri', extended[lo:lo + count], masked[:, k], precisi...]
    all_to_all x0 -> x1, blocking collectives: none -> 15.3 us  [sum_all(): lax.all_to_all(jnp.broadcast_to(value[None], (size,) + value.shape), 'tm'...]
    pallas_call x0 -> x12, Pallas kernels: none -> 12.4 us  [the longest x3 3.43 us: local(): call(functools.partial(local_kernel, len(vecs)), (shape(T, R, N), shape(l...]
    ppermute x7 -> x11, starting transfers between devices: 17.1 us -> 23.7 us  [the longest x8 21.6 us: shift(): lax.ppermute(value, 'tm', [(i, (i + steps) % count) for i in range(count)])]
  transfers between devices with their start and end apart: 7 -> 11, of which waited for: 4 -> 10; matrix products, arithmetic and copies ran while one was open for 3% -> 0% of each run, Pallas kernels for 0% -> 10%
where the time goes in v1:
time: 80.3 us; the launch traced here: 80.1 us
  waiting for transfers between devices  24.2 us (30%)
  starting transfers between devices  23.7 us (30%)
  blocking collectives  15.3 us (19%)
  Pallas kernels  12.4 us (15%)
  local copies, waits for them, and re-layouts  3.57 us (4%)
    ppermute x8, starting transfers between devices, shift(): lax.ppermute(value, 'tm', [(i, (i + steps) % count) for i in range(count)])  21.6 us
    ppermute x8, waiting for transfers between devices, shift(): lax.ppermute(value, 'tm', [(i, (i + steps) % count) for i in range(count)])  19.9 us
    all_to_all x1, blocking collectives, sum_all(): lax.all_to_all(jnp.broadcast_to(value[None], (size,) + value.shape), 'tm'...  15.3 us
    ppermute x3, waiting for transfers between devices, sum_all(): lax.ppermute(value, 'tm', [(i, i - i % run + (i + s) % run) for i in rang...  4.3 us
    unnamed x8, local copies, waits for them, and re-layouts  3.56 us
    pallas_call x3, Pallas kernels, local(): call(functools.partial(local_kernel, len(vecs)), (shape(T, R, N), shape(l...  3.43 us
    pallas_call x1, Pallas kernels, sums(): call(sums_kernel, (shape(*BAND, dtype=BF16), shape(*BAND, dtype=BF16), sh...  2.75 us
    ppermute x3, starting transfers between devices, sum_all(): lax.ppermute(value, 'tm', [(i, i - i % run + (i + s) % run) for i in rang...  2.09 us
  transfers between devices with their start and end apart: 11, of which 10 were waited for; matrix products, arithmetic and copies ran while one was open for 0% of the time, Pallas kernels for 10%

profile of v1, /device:TPU:4, one launch (start us, length us, event | category | flops | bytes accessed | tf_op | source)
XLA Modules:
  0.0 80.1 jit_solution(6902064762699526692)
XLA Ops:
  0.6 2.2 %copy-done = f32[8,8,128,128]{3,2,1,0:T(8,128)S(1)} copy-done((f32[8,8,128,128]{3,2,1,0:T(8,128)S(1)}, f32[8,8,128,128]{3,2,1,0:T(8,128)}, u32[]{:S(2)}) %copy-start) | copy-done | bytes 4194328
  4.2 2.8 %shard_map.59 = (bf16[4,256,1152]{2,1,0:T(8,128)(2,1)S(1)}, bf16[4,256,1152]{2,1,0:T(8,128)(2,1)S(1)}, f32[8,128]{1,0:T(8,128)S(1)}, f32[8,128]{1,0:T(8,128)S(1)}) custom-call(s32[8,8]{1,0:T(8,128)S(1)} %copy-done.2, f32[8,8,128,128]{3,2,1,0:T(8,128)S(1)} %copy-done, f32[8,128]{1,0:T(8,128)S(1)} %copy-done.3), custom_call_target="tpu_custom_call" | custom-call | flops 8388608 | bytes 4194304 | tf_op jit(solution)/shard_map/pallas_call | solution.py:106
  7.0 1.7 %collective-permute-start = (f32[8,128]{1,0:T(8,128)S(1)}, f32[8,128]{1,0:T(8,128)S(1)}, u32[]{:S(2)}, u32[]{:S(2)}) collective-permute-start(f32[8,128]{1,0:T(8,128)S(1)} %get-tuple-element.16.ahead), channel_id=1, source_target_pairs={{0,1},{1,2},{2,3},{3,4},{4,5},{5,6},{6,7},{7,8},{8,9},{9,10},{10,1... | collective-permute-start | bytes 12296 | tf_op jit(solution)/shard_map/ppermute | solution.py:327
  8.6 7.5 %collective-permute-start.1 = (f32[8,64,128]{2,1,0:T(8,128)S(1)}, f32[8,64,128]{2,1,0:T(8,128)S(1)}, u32[]{:S(2)}, u32[]{:S(2)}) collective-permute-start(f32[8,64,128]{2,1,0:T(8,128)S(1)} %copy-done.1), channel_id=1, source_target_pairs={{0,63},{1,0},{2,1},{3,2},{4,3},{5,4},{6,5},{7,6},{8,7},{9,8},{10,9... | collective-permute-start | bytes 786440 | tf_op jit(solution)/shard_map/ppermute | solution.py:327
  16.1 1.5 %collective-permute-done.arrived = f32[8,128]{1,0:T(8,128)S(1)} collective-permute-done((f32[8,128]{1,0:T(8,128)S(1)}, f32[8,128]{1,0:T(8,128)S(1)}, u32[]{:S(2)}, u32[]{:S(2)}) %collective-permute-start) | collective-permute-done | bytes 4128 | tf_op jit(solution)/shard_map/ppermute | solution.py:327
  18.2 6.2 %collective-permute-start.2 = (f32[8,128]{1,0:T(8,128)S(1)}, f32[8,128]{1,0:T(8,128)S(1)}, u32[]{:S(2)}, u32[]{:S(2)}) collective-permute-start(f32[8,128]{1,0:T(8,128)S(1)} %get-tuple-element.15.own), channel_id=1, source_target_pairs={{0,63},{1,0},{2,1},{3,2},{4,3},{5,4},{6,5},{7,6},{8,7},{9,8},{10,9... | collective-permute-start | bytes 12296 | tf_op jit(solution)/shard_map/ppermute | solution.py:327
  24.5 1.1 %shard_map.61 = (f32[8,64,128]{2,1,0:T(8,128)S(1)}, f32[1,2,64,128]{3,2,1,0:T(8,128)S(1)}) custom-call(f32[8,64,128]{2,1,0:T(8,128)S(1)} %get-tuple-element.19.refs_0_.v0, f32[8,64,128]{2,1,0:T(8,128)S(1)} %copy-done.1, bf16[4,256,1152]{2,1,0:T(8,128)(2,1)S(1)} %get-tuple-element.17.high.refs_2_.refs_3_.refs_4_, ...), custom_call_target="tpu_custom_call" | custom-call | flops 503316480 | tf_op jit(solution)/shard_map/pallas_call | solution.py:218
  25.8 0.9 %shard_map.62 = f32[8,64,128]{2,1,0:T(8,128)S(1)} custom-call(f32[8,64,128]{2,1,0:T(8,128)S(1)} %collective-permute-done.1.rhs_next, f32[8,128]{1,0:T(8,128)S(1)} %collective-permute-done.2.own_next, f32[8,128]{1,0:T(8,128)S(1)} %get-tuple-element.16.ahead, bf16[4,256,1152]{2,1,0:T(8,128)(2,1)S(1)} %get-tuple-element.17.high.refs_2_.refs_3_.refs_4_, ...), custom_call_target="tpu_custom_call" | custom-call | flops 251658240 | tf_op jit(solution)/shard_map/pallas_call | solution.py:236
  26.7 2.9 %collective-permute-done.3 = f32[8,64,128]{2,1,0:T(8,128)S(1)} collective-permute-done((f32[8,64,128]{2,1,0:T(8,128)S(1)}, f32[8,64,128]{2,1,0:T(8,128)S(1)}, u32[]{:S(2)}, u32[]{:S(2)}) %collective-permute-start.3) | collective-permute-done | bytes 262176 | tf_op jit(solution)/shard_map/ppermute | solution.py:327
  29.7 3.7 %collective-permute-start.4 = (f32[8,64,128]{2,1,0:T(8,128)S(1)}, f32[8,64,128]{2,1,0:T(8,128)S(1)}, u32[]{:S(2)}, u32[]{:S(2)}) collective-permute-start(f32[8,64,128]{2,1,0:T(8,128)S(1)} %get-tuple-element.34.refs_1_.vec.v1), channel_id=1, source_target_pairs={{0,63},{1,0},{2,1},{3,2},{4,3},{5,4},{6,5},{7,6},{8,7},{9,8},{10,9... | collective-permute-start | bytes 786440 | tf_op jit(solution)/shard_map/ppermute | solution.py:327
  34.0 1.1 %shard_map.63 = (f32[8,64,128]{2,1,0:T(8,128)S(1)}, f32[2,2,64,128]{3,2,1,0:T(8,128)S(1)}) custom-call(f32[8,64,128]{2,1,0:T(8,128)S(1)} %get-tuple-element.19.refs_0_.v0, f32[8,64,128]{2,1,0:T(8,128)S(1)} %get-tuple-element.34.refs_1_.vec.v1, f32[8,64,128]{2,1,0:T(8,128)S(1)} %get-tuple-element.35.refs_2_.y1, ...), custom_call_target="tpu_custom_call" | custom-call | flops 503316480 | tf_op jit(solution)/shard_map/pallas_call | solution.py:218
  35.2 2.1 %collective-permute-done.4.vec_next = f32[8,64,128]{2,1,0:T(8,128)S(1)} collective-permute-done((f32[8,64,128]{2,1,0:T(8,128)S(1)}, f32[8,64,128]{2,1,0:T(8,128)S(1)}, u32[]{:S(2)}, u32[]{:S(2)}) %collective-permute-start.4) | collective-permute-done | bytes 262176 | tf_op jit(solution)/shard_map/ppermute | solution.py:327
  37.3 0.9 %shard_map.64 = f32[8,64,128]{2,1,0:T(8,128)S(1)} custom-call(f32[8,64,128]{2,1,0:T(8,128)S(1)} %collective-permute-done.4.vec_next, bf16[4,256,1152]{2,1,0:T(8,128)(2,1)S(1)} %get-tuple-element.17.high.refs_2_.refs_3_.refs_4_, bf16[4,256,1152]{2,1,0:T(8,128)(2,1)S(1)} %get-tuple-element.18.low.refs_3_.refs_4_.refs_5_, ...), custom_call_target="tpu_custom_call" | custom-call | flops 251658240 | tf_op jit(solution)/shard_map/pallas_call | solution.py:249
  38.2 6.4 %collective-permute-done.5 = f32[8,64,128]{2,1,0:T(8,128)S(1)} collective-permute-done((f32[8,64,128]{2,1,0:T(8,128)S(1)}, f32[8,64,128]{2,1,0:T(8,128)S(1)}, u32[]{:S(2)}, u32[]{:S(2)}) %collective-permute-start.5) | collective-permute-done | bytes 262176 | tf_op jit(solution)/shard_map/ppermute | solution.py:327
  45.6 2.0 %collective-permute-start.7 = (f32[8,64,128]{2,1,0:T(8,128)S(1)}, f32[8,64,128]{2,1,0:T(8,128)S(1)}, u32[]{:S(2)}, u32[]{:S(2)}) collective-permute-start(f32[8,64,128]{2,1,0:T(8,128)S(1)} %shard_map.68), channel_id=1, source_target_pairs={{0,1},{1,2},{2,3},{3,4},{4,5},{5,6},{6,7},{7,8},{8,9},{9,10},{10,1... | collective-permute-start | bytes 786440 | tf_op jit(solution)/shard_map/ppermute | solution.py:327
  47.6 1.2 %shard_map.66 = (f32[8,64,128]{2,1,0:T(8,128)S(1)}, f32[3,2,64,128]{3,2,1,0:T(8,128)S(1)}) custom-call(f32[8,64,128]{2,1,0:T(8,128)S(1)} %get-tuple-element.19.refs_0_.v0, f32[8,64,128]{2,1,0:T(8,128)S(1)} %get-tuple-element.34.refs_1_.vec.v1, f32[8,64,128]{2,1,0:T(8,128)S(1)} %get-tuple-element.32.refs_2_.vec.v2, ...), custom_call_target="tpu_custom_call" | custom-call | flops 503316480 | tf_op jit(solution)/shard_map/pallas_call | solution.py:218
  48.8 2.3 %collective-permute-done.6.vec_next = f32[8,64,128]{2,1,0:T(8,128)S(1)} collective-permute-done((f32[8,64,128]{2,1,0:T(8,128)S(1)}, f32[8,64,128]{2,1,0:T(8,128)S(1)}, u32[]{:S(2)}, u32[]{:S(2)}) %collective-permute-start.6) | collective-permute-done | bytes 262176 | tf_op jit(solution)/shard_map/ppermute | solution.py:327
  52.0 4.5 %collective-permute-done.7 = f32[8,64,128]{2,1,0:T(8,128)S(1)} collective-permute-done((f32[8,64,128]{2,1,0:T(8,128)S(1)}, f32[8,64,128]{2,1,0:T(8,128)S(1)}, u32[]{:S(2)}, u32[]{:S(2)}) %collective-permute-start.7) | collective-permute-done | bytes 262176 | tf_op jit(solution)/shard_map/ppermute | solution.py:327
  57.2 1.9 %collective-permute-start.8 = (f32[16,128]{1,0:T(8,128)S(1)}, f32[16,128]{1,0:T(8,128)S(1)}, u32[]{:S(2)}, u32[]{:S(2)}) collective-permute-start(f32[16,128]{1,0:T(8,128)S(1)} %shard_map.69), channel_id=1, source_target_pairs={{0,1},{1,2},{2,3},{3,0},{4,5},{5,6},{6,7},{7,4},{8,9},{9,10},{10,1... | collective-permute-start | bytes 24584 | tf_op jit(solution)/shard_map/ppermute | solution.py:341
  59.1 1.6 %collective-permute-done.10 = f32[16,128]{1,0:T(8,128)S(1)} collective-permute-done((f32[16,128]{1,0:T(8,128)S(1)}, f32[16,128]{1,0:T(8,128)S(1)}, u32[]{:S(2)}, u32[]{:S(2)}) %collective-permute-start.10) | collective-permute-done | bytes 8224 | tf_op jit(solution)/shard_map/ppermute | solution.py:341
  60.7 1.6 %collective-permute-done.9 = f32[16,128]{1,0:T(8,128)S(1)} collective-permute-done((f32[16,128]{1,0:T(8,128)S(1)}, f32[16,128]{1,0:T(8,128)S(1)}, u32[]{:S(2)}, u32[]{:S(2)}) %collective-permute-start.9) | collective-permute-done | bytes 8224 | tf_op jit(solution)/shard_map/ppermute | solution.py:341
  62.3 1.1 %collective-permute-done.8 = f32[16,128]{1,0:T(8,128)S(1)} collective-permute-done((f32[16,128]{1,0:T(8,128)S(1)}, f32[16,128]{1,0:T(8,128)S(1)}, u32[]{:S(2)}, u32[]{:S(2)}) %collective-permute-start.8) | collective-permute-done | bytes 8224 | tf_op jit(solution)/shard_map/ppermute | solution.py:341
  63.4 15.3 %all_to_all.5 = f32[16,16,128]{2,1,0:T(8,128)S(1)} all-to-all(f32[16,16,128]{2,1,0:T(8,128)S(1)} %broadcast_in_dim.2), channel_id=1, replica_groups={{0,4,8,12,16,20,24,28,32,36,40,44,48,52,56,60},{1,5,9,13,17,21,25,29,33..., dimensions={0} | all-to-all | bytes 262144 | tf_op jit(solution)/shard_map/all_to_all | solution.py:346
  78.8 1.3 %shard_map.70 = (f32[8,64,128]{2,1,0:T(8,128)}, f32[8,64,128]{2,1,0:T(8,128)}) custom-call(f32[16,128]{1,0:T(8,128)S(1)} %pad_maximum_fusion.1.sums_ref, f32[8,64,128]{2,1,0:T(8,128)S(1)} %get-tuple-element.19.refs_0_.v0, f32[8,64,128]{2,1,0:T(8,128)S(1)} %get-tuple-element.34.refs_1_.vec.v1, f32[8,64,128]{2,1,0:T(8,128)S(1)} %get-tuple-element.32.refs_2_.vec.v2, ...), custom_call_target="tpu_custom_call" | custom-call | tf_op jit(solution)/shard_map/pallas_call | solution.py:322
  (27 shorter events, 5.6 us)
Async XLA Ops:
  0.6 2.2 %copy-start = (f32[8,8,128,128]{3,2,1,0:T(8,128)S(1)}, f32[8,8,128,128]{3,2,1,0:T(8,128)}, u32[]{:S(2)}) copy-start(f32[8,8,128,128]{3,2,1,0:T(8,128)} %weights.1) | copy-start | bytes 12582916
  2.8 0.7 copy-start.2
  3.5 0.7 copy-start.3
  4.2 4.4 %copy-start.1 = (f32[8,64,128]{2,1,0:T(8,128)S(1)}, f32[8,64,128]{2,1,0:T(8,128)}, u32[]{:S(2)}) copy-start(f32[8,64,128]{2,1,0:T(8,128)} %y0.1) | copy-start | bytes 786436
  7.0 10.6 %collective-permute-start = (f32[8,128]{1,0:T(8,128)S(1)}, f32[8,128]{1,0:T(8,128)S(1)}, u32[]{:S(2)}, u32[]{:S(2)}) collective-permute-start(f32[8,128]{1,0:T(8,128)S(1)} %get-tuple-element.16.ahead), channel_id=1, source_target_pairs={{0,1},{1,2},{2,3},{3,4},{4,5},{5,6},{6,7},{7,8},{8,9},{9,10},{10,1... | collective-permute-start | bytes 12296 | tf_op jit(solution)/shard_map/ppermute | solution.py:327
  8.6 17.2 %collective-permute-start.1 = (f32[8,64,128]{2,1,0:T(8,128)S(1)}, f32[8,64,128]{2,1,0:T(8,128)S(1)}, u32[]{:S(2)}, u32[]{:S(2)}) collective-permute-start(f32[8,64,128]{2,1,0:T(8,128)S(1)} %copy-done.1), channel_id=1, source_target_pairs={{0,63},{1,0},{2,1},{3,2},{4,3},{5,4},{6,5},{7,6},{8,7},{9,8},{10,9... | collective-permute-start | bytes 786440 | tf_op jit(solution)/shard_map/ppermute | solution.py:327
  18.1 11.5 %collective-permute-start.3 = (f32[8,64,128]{2,1,0:T(8,128)S(1)}, f32[8,64,128]{2,1,0:T(8,128)S(1)}, u32[]{:S(2)}, u32[]{:S(2)}) collective-permute-start(f32[8,64,128]{2,1,0:T(8,128)S(1)} %get-tuple-element.21), channel_id=1, source_target_pairs={{0,1},{1,2},{2,3},{3,4},{4,5},{5,6},{6,7},{7,8},{8,9},{9,10},{10,1... | collective-permute-start | bytes 786440 | tf_op jit(solution)/shard_map/ppermute | solution.py:327
  18.2 7.6 %collective-permute-start.2 = (f32[8,128]{1,0:T(8,128)S(1)}, f32[8,128]{1,0:T(8,128)S(1)}, u32[]{:S(2)}, u32[]{:S(2)}) collective-permute-start(f32[8,128]{1,0:T(8,128)S(1)} %get-tuple-element.15.own), channel_id=1, source_target_pairs={{0,63},{1,0},{2,1},{3,2},{4,3},{5,4},{6,5},{7,6},{8,7},{9,8},{10,9... | collective-permute-start | bytes 12296 | tf_op jit(solution)/shard_map/ppermute | solution.py:327
  29.7 7.6 %collective-permute-start.4 = (f32[8,64,128]{2,1,0:T(8,128)S(1)}, f32[8,64,128]{2,1,0:T(8,128)S(1)}, u32[]{:S(2)}, u32[]{:S(2)}) collective-permute-start(f32[8,64,128]{2,1,0:T(8,128)S(1)} %get-tuple-element.34.refs_1_.vec.v1), channel_id=1, source_target_pairs={{0,63},{1,0},{2,1},{3,2},{4,3},{5,4},{6,5},{7,6},{8,7},{9,8},{10,9... | collective-permute-start | bytes 786440 | tf_op jit(solution)/shard_map/ppermute | solution.py:327
  33.9 10.7 %collective-permute-start.5 = (f32[8,64,128]{2,1,0:T(8,128)S(1)}, f32[8,64,128]{2,1,0:T(8,128)S(1)}, u32[]{:S(2)}, u32[]{:S(2)}) collective-permute-start(f32[8,64,128]{2,1,0:T(8,128)S(1)} %shard_map.65), channel_id=1, source_target_pairs={{0,1},{1,2},{2,3},{3,4},{4,5},{5,6},{6,7},{7,8},{8,9},{9,10},{10,1... | collective-permute-start | bytes 786440 | tf_op jit(solution)/shard_map/ppermute | solution.py:327
  44.7 6.4 %collective-permute-start.6 = (f32[8,64,128]{2,1,0:T(8,128)S(1)}, f32[8,64,128]{2,1,0:T(8,128)S(1)}, u32[]{:S(2)}, u32[]{:S(2)}) collective-permute-start(f32[8,64,128]{2,1,0:T(8,128)S(1)} %get-tuple-element.32.refs_2_.vec.v2), channel_id=1, source_target_pairs={{0,63},{1,0},{2,1},{3,2},{4,3},{5,4},{6,5},{7,6},{8,7},{9,8},{10,9... | collective-permute-start | bytes 786440 | tf_op jit(solution)/shard_map/ppermute | solution.py:327
  45.6 10.9 %collective-permute-start.7 = (f32[8,64,128]{2,1,0:T(8,128)S(1)}, f32[8,64,128]{2,1,0:T(8,128)S(1)}, u32[]{:S(2)}, u32[]{:S(2)}) collective-permute-start(f32[8,64,128]{2,1,0:T(8,128)S(1)} %shard_map.68), channel_id=1, source_target_pairs={{0,1},{1,2},{2,3},{3,4},{4,5},{5,6},{6,7},{7,8},{8,9},{9,10},{10,1... | collective-permute-start | bytes 786440 | tf_op jit(solution)/shard_map/ppermute | solution.py:327
  57.0 3.7 %collective-permute-start.10 = (f32[16,128]{1,0:T(8,128)S(1)}, f32[16,128]{1,0:T(8,128)S(1)}, u32[]{:S(2)}, u32[]{:S(2)}) collective-permute-start(f32[16,128]{1,0:T(8,128)S(1)} %shard_map.69), channel_id=1, source_target_pairs={{0,3},{1,0},{2,1},{3,2},{4,7},{5,4},{6,5},{7,6},{8,11},{9,8},{10,9... | collective-permute-start | bytes 24584 | tf_op jit(solution)/shard_map/ppermute | solution.py:341
  57.1 5.2 %collective-permute-start.9 = (f32[16,128]{1,0:T(8,128)S(1)}, f32[16,128]{1,0:T(8,128)S(1)}, u32[]{:S(2)}, u32[]{:S(2)}) collective-permute-start(f32[16,128]{1,0:T(8,128)S(1)} %shard_map.69), channel_id=1, source_target_pairs={{0,2},{1,3},{2,0},{3,1},{4,6},{5,7},{6,4},{7,5},{8,10},{9,11},{10,... | collective-permute-start | bytes 24584 | tf_op jit(solution)/shard_map/ppermute | solution.py:341
  57.2 6.2 %collective-permute-start.8 = (f32[16,128]{1,0:T(8,128)S(1)}, f32[16,128]{1,0:T(8,128)S(1)}, u32[]{:S(2)}, u32[]{:S(2)}) collective-permute-start(f32[16,128]{1,0:T(8,128)S(1)} %shard_map.69), channel_id=1, source_target_pairs={{0,1},{1,2},{2,3},{3,0},{4,5},{5,6},{6,7},{7,4},{8,9},{9,10},{10,1... | collective-permute-start | bytes 24584 | tf_op jit(solution)/shard_map/ppermute | solution.py:341

commit v2 on v1

--- a/solution.py
+++ b/solution.py
@@ -14,7 +14,7 @@
 T = 8
 R = 64
 VMEM = pl.BlockSpec(memory_space=pltpu.VMEM)
-SMEM = pl.BlockSpec(memory_space=pltpu.SMEM)
+HBM = pl.BlockSpec(memory_space=pltpu.HBM)
 
 BAND = (T // 2, 2 * N, (T + 1) * N)
 
@@ -31,6 +31,10 @@
     )
 
 
+def in_hbm(value):
+    return pltpu.with_memory_space_constraint(value, pltpu.HBM)
+
+
 def shape(*dims, dtype=F32):
     return jax.ShapeDtypeStruct(dims, dtype)
 
@@ -67,18 +71,63 @@
     return p, ((ah * bh - p) + ah * bl + al * bh) + al * bl
 
 
-def sums_kernel(pattern, weights, reg, high, low, own, ahead, buf, cols, sems):
+def ahead_kernel(pattern, weights, ahead, mask, buf, cols, sems):
+    head = pltpu.make_async_copy(pattern, mask, sems.at[T])
+    head.start()
+    copies = []
+    for t in range(T):
+        some = slice(T - 1 - t, T)
+        copies.append(pltpu.make_async_copy(weights.at[t, some], buf.at[t, some], sems.at[t]))
+    for copy in copies:
+        copy.start()
+    cols[...] = jnp.zeros_like(cols)
+    head.wait()
+    for t in range(T):
+        copies[t].wait()
+
+        def step(k, carry):
+            m = buf[t, k] * mask[t, k].astype(F32)
+            cols[t + k + 1 - T] += jnp.sum(m.reshape(N // 8, 8, N), axis=0)
+            return carry
+
+        lax.fori_loop(T - 1 - t, T, step, 0)
+    ahead[...] = jnp.sum(cols[...], axis=1)
+
+
+def ahead_sums(pattern, weights):
+    pattern, weights = in_hbm(pattern), in_hbm(weights)
+    return call(
+        ahead_kernel,
+        shape(T, N),
+        [HBM, HBM],
+        [
+            pltpu.SMEM((T, T), jnp.int32),
+            pltpu.VMEM((T, T, N, N), F32),
+            pltpu.VMEM((T, 8, N), F32),
+            pltpu.SemaphoreType.DMA((T + 1,)),
+        ],
+        flops=4 * T * T * N * N,
+        moved=4 * T * T * N * N,
+    )(pattern, weights)
+
+
+def band_kernel(pattern, weights, reg, high, low, own, mask, buf, cols, extra, sems):
     def copy(t):
         return pltpu.make_async_copy(weights.at[t], buf.at[t], sems.at[t])
 
+    head = pltpu.make_async_copy(pattern, mask, sems.at[T])
+    tail = pltpu.make_async_copy(reg, extra, sems.at[T + 1])
+    head.start()
     for t in range(T):
         copy(t).start()
+    tail.start()
     cols[...] = jnp.zeros_like(cols)
     zero = jnp.zeros((N, N), BF16)
     for a in range(T // 2):
         for piece in (high, low):
             piece[a, N : 2 * N, 0:N] = zero
             piece[a, 0:N, T * N : (T + 1) * N] = zero
+    head.wait()
 
     def step(a, carry):
         for half in range(2):
@@ -86,30 +135,36 @@
             copy(t).wait()
             rows = jnp.zeros((N, N), F32)
             for k in range(T):
-                m = buf[t, k] * pattern[t, k].astype(F32)
+                m = buf[t, k] * mask[t, k].astype(F32)
                 rows = rows + m
                 cols[t + k + 1] += jnp.sum(m.reshape(N // 8, 8, N), axis=0)
                 h = m.astype(BF16)
                 place = slice((k + half) * N, (k + half + 1) * N)
                 high[a, half * N : (half + 1) * N, place] = h
                 low[a, half * N : (half + 1) * N, place] = (m - h.astype(F32)).astype(BF16)
-            own[pl.ds(t, 1), :] = reg[pl.ds(t, 1), :] + jnp.sum(rows.T, axis=0, keepdims=True)
+            own[pl.ds(t, 1), :] = jnp.sum(rows.T, axis=0, keepdims=True)
         return carry
 
     lax.fori_loop(0, T // 2, step, 0)
-    inflow = jnp.sum(cols[...], axis=1)
-    own[...] += inflow[:T]
-    ahead[...] = inflow[T:]
-
-
-def sums(pattern, weights, reg):
+    tail.wait()
+    own[...] += jnp.sum(cols[:T], axis=1) + extra[...]
+
+
+def band_pieces(pattern, weights, reg):
+    pattern, weights, reg = in_hbm(pattern), in_hbm(weights), in_hbm(reg)
     return call(
-        sums_kernel,
-        (shape(*BAND, dtype=BF16), shape(*BAND, dtype=BF16), shape(T, N), shape(T, N)),
-        [SMEM, pl.BlockSpec(memory_space=pl.ANY), VMEM],
-        [pltpu.VMEM((T, T, N, N), F32), pltpu.VMEM((2 * T, 8, N), F32), pltpu.SemaphoreType.DMA((T,))],
-        flops=8 * T * T * N * N,
-        moved=4 * T * T * N * N,
+        band_kernel,
+        (shape(*BAND, dtype=BF16), shape(*BAND, dtype=BF16), shape(T, N)),
+        [HBM, HBM, HBM],
+        [
+            pltpu.SMEM((T, T), jnp.int32),
+            pltpu.VMEM((T, T, N, N), F32),
+            pltpu.VMEM((2 * T, 8, N), F32),
+            pltpu.VMEM((T, N), F32),
+            pltpu.SemaphoreType.DMA((T + 2,)),
+        ],
+        flops=2048 * T * T * N * N,
+        moved=8 * T * T * N * N,
     )(pattern, weights, reg)
 
 
@@ -174,25 +229,6 @@
 ONE_WAY = 2 * 3 * 40 * R * N * N
 
 
-def start_kernel(rhs, own, arrived, high, low, diag, vec, out, pieces):
-    diag[...] = own[...] + arrived[...]
-    for t in range(T):
-        value = rhs[t] / diag[t : t + 1, :]
-        vec[t] = value
-        put_pieces(pieces, t, value)
-    to_next(pieces, high, low, out)
-
-
-def start(rhs, own, arrived, high, low):
-    return call(
-        start_kernel,
-        (shape(T, N), shape(T, R, N), shape(T, R, N)),
-        [VMEM] * 5,
-        [PIECES],
-        flops=ONE_WAY,
-    )(rhs, own, arrived, high, low)
-
-
 def contrib_kernel(vec, high, low, out, pieces):
     for t in range(T):
         put_pieces(pieces, t, vec[t])
@@ -222,20 +258,6 @@
         [PIECES],
         flops=2 * ONE_WAY,
     )(*vecs, image, high, low)
-
-
-def finish_first_kernel(rhs_next, own_next, ahead, high, low, partial, out, pieces):
-    scale = own_next[...] + ahead[...]
-    for t in range(T):
-        put_pieces(pieces, t, rhs_next[t] / scale[t : t + 1, :])
-    out[...] = partial[...]
-    from_next(pieces, high, low, out)
-
-
-def finish_first(rhs_next, own_next, ahead, high, low, partial):
-    return call(finish_first_kernel, shape(T, R, N), [VMEM] * 6, [PIECES], flops=ONE_WAY)(
-        rhs_next, own_next, ahead, high, low, partial
-    )
 
 
 def finish_kernel(vec_next, high, low, partial, out, pieces):
@@ -261,8 +283,14 @@
     return value
 
 
-def gram_kernel(v0, v1, v2, image, m0, m1, m2, out):
-    last = [moments(v, image) for v in (v0, v1, v2)]
+def gram_kernel(v0, v1, v2, n0, n1, n2, sent, partial, high, low, m0, m1, m2, image, out, pieces):
+    for t in range(T):
+        put_pieces(pieces, t, n2[t])
+    image[...] = partial[...]
+    from_next(pieces, high, low, image)
+    last = [
+        dd_add(moments(v, image), moments(n, sent)) for v, n in ((v0, n0), (v1, n1), (v2, n2))
+    ]
     every = [(m[i, 0], m[i, 1]) for m in (m0, m1, m2) for i in range(m.shape[0])] + last + last[-1:]
     out[...] = jnp.zeros_like(out)
     for q in range(5):
@@ -271,8 +299,10 @@
         out[8 + q : 9 + q, :] = l[0:1]
 
 
-def gram(vecs, image, found):
-    return call(gram_kernel, shape(16, 2 * R), [VMEM] * 7)(*vecs, image, *found)
+def gram(vecs, ahead, sent, partial, high, low, found):
+    return call(gram_kernel, (shape(T, R, N), shape(16, 2 * R)), [VMEM] * 13, [PIECES], flops=ONE_WAY)(
+        *vecs, *ahead, sent, partial, high, low, *found
+    )
 
 
 def solve(matrix, right):
@@ -290,7 +320,7 @@
     return x0, x1, x2
 
 
-def result_kernel(sums_ref, v0, v1, v2, y0, y1, y2, y3, sol, res):
+def result_kernel(sums_ref, v0, v1, v2, y0, y1, y2, y3, arrived, sol, res):
     flat = []
     for q in range(5):
         h, l = sums_ref[q : q + 1, :], sums_ref[8 + q : 9 + q, :]
@@ -315,11 +345,11 @@
     for t in range(T):
         sol[t] = v0[t] + (d0 * v0[t] + d1 * v1[t] + d2 * v2[t])
         first, second = y1[t], y2[t]
-        res[t] = first - (d0 * (y0[t] - first) + d1 * (first - second) + d2 * (second - y3[t]))
-
-
-def result(total, vecs, images):
-    return call(result_kernel, (shape(T, R, N), shape(T, R, N)), [VMEM] * 8)(total, *vecs, *images)
+        res[t] = first - (d0 * (y0[t] - first) + d1 * (first - second) + d2 * (second - (y3[t] + arrived[t])))
+
+
+def result(total, vecs, images, arrived):
+    return call(result_kernel, (shape(T, R, N), shape(T, R, N)), [VMEM] * 9)(total, *vecs, *images, arrived)
 
 
 def shift(value, steps):
@@ -334,47 +364,40 @@
     return jnp.concatenate(total, axis=0)
 
 
-def sum_all(value):
+def sum_all(value, beside):
     count = lax.axis_size("tm")
     run = 4
     others = [
         lax.ppermute(value, "tm", [(i, i - i % run + (i + s) % run) for i in range(count)]) for s in range(1, run)
     ]
-    value = pair_add([value] + others)
+    value, beside = lax.optimization_barrier((pair_add([value] + others), beside))
     groups = [[i for i in range(j, count, run)] for j in range(run)]
     size = count // run
     spread = lax.all_to_all(
         jnp.broadcast_to(value[None], (size,) + value.shape), "tm", 0, 0, axis_index_groups=groups
     )
-    return pair_add([spread[i] for i in range(size)])
+    return pair_add([spread[i] for i in range(size)]), beside
 
 
 def shards(weights, pattern, shift_reg, rhs):
-    rhs_next = shift(rhs, -1)
-    high, low, own, ahead = sums(pattern, weights, shift_reg)
-    arrived = shift(ahead, 1)
-    own_next = shift(own, -1)
-    diag, vec, out = start(rhs, own, arrived, high, low)
-    arrived = shift(out, 1)
-    vecs, images, found = [vec], [rhs], []
-    partial, part = local(vecs, rhs, high, low)
-    found.append(part)
-    partial = finish_first(rhs_next, own_next, ahead, high, low, partial)
-    for step in range(1, 3):
-        image = partial + arrived
-        vec = image / diag[:, None, :]
-        vec_next = shift(vec, -1)
-        out = contrib(vec, high, low)
-        arrived = shift(out, 1)
-        vecs.append(vec)
-        images.append(image)
-        partial, part = local(vecs, image, high, low)
+    inflow = shift(ahead_sums(pattern, weights), 1)
+    high, low, own = band_pieces(pattern, weights, shift_reg)
+    diag = own + inflow
+    vec = rhs / diag[:, None, :]
+    vecs, images, found, ahead = [vec], [rhs], [], []
+    for step in range(3):
+        ahead.append(shift(vec, -1))
+        sent = contrib(vec, high, low)
+        arrived = shift(sent, 1)
+        partial, part = local(vecs, images[-1], high, low)
         found.append(part)
-        partial = finish(vec_next, high, low, partial)
-    image = partial + arrived
-    images.append(image)
-    total = sum_all(gram(vecs, image, found))
-    return result(total, vecs, images)
+        if step < 2:
+            images.append(finish(ahead[-1], high, low, partial) + arrived)
+            vec = images[-1] / diag[:, None, :]
+            vecs.append(vec)
+    image, total = gram(vecs, ahead, sent, partial, high, low, found)
+    total, arrived = sum_all(total, arrived)
+    return result(total, vecs, images + [image], arrived)
 
 
 def solution(mesh):

time: 80.3 us -> 77.8 us (0.969)
  starting transfers between devices: 23.7 us -> 10.6 us
  waiting for transfers between devices: 24.2 us -> 36.2 us
  local copies, waits for them, and re-layouts: 3.57 us -> 0.02 us
  Pallas kernels: 12.4 us -> 14.6 us
    ppermute x8 -> x7, waiting for transfers between devices: 19.9 us -> 34.5 us  [shift(): lax.ppermute(value, 'tm', [(i, (i + steps) % count) for i in range(count)])]
    ppermute x8 -> x7, starting transfers between devices: 21.6 us -> 7.31 us  [shift(): lax.ppermute(value, 'tm', [(i, (i + steps) % count) for i in range(count)])]
    unnamed x8 -> x2, local copies, waits for them, and re-layouts: 3.56 us -> 0.01 us
    ppermute x3, waiting for transfers between devices: 4.3 us -> 1.71 us  [sum_all(): lax.ppermute(value, 'tm', [(i, i - i % run + (i + s) % run) for i in rang...]
    pallas_call x5 -> x4, Pallas kernels: 5.99 us -> 7.5 us  [the longest x1 2.85 us: band_pieces(): call(band_kernel, (shape(*BAND, dtype=BF16), shape(*BAND, dtype=BF16), sh...]
    ppermute x3, starting transfers between devices: 2.09 us -> 3.3 us  [sum_all(): lax.ppermute(value, 'tm', [(i, i - i % run + (i + s) % run) for i in rang...]
    pallas_call x2 -> x3, Pallas kernels: 1.12 us -> 1.71 us  [contrib(): call(contrib_kernel, shape(T, R, N), [VMEM] * 3, [PIECES], flops=ONE_WAY)]
  transfers between devices with their start and end apart: 11 -> 10, of which waited for: 10 -> 10; matrix products, arithmetic and copies ran while one was open for 0% -> 0% of each run, Pallas kernels for 10% -> 13%
where the time goes in v2:
time: 77.8 us; the launch traced here: 77.6 us
  waiting for transfers between devices  36.2 us (47%)
  blocking collectives  15.2 us (20%)
  Pallas kernels  14.6 us (19%)
  starting transfers between devices  10.6 us (14%)
    ppermute x7, waiting for transfers between devices, shift(): lax.ppermute(value, 'tm', [(i, (i + steps) % count) for i in range(count)])  34.5 us
    all_to_all x1, blocking collectives, sum_all(): lax.all_to_all(jnp.broadcast_to(value[None], (size,) + value.shape), 'tm'...  15.2 us
    ppermute x7, starting transfers between devices, shift(): lax.ppermute(value, 'tm', [(i, (i + steps) % count) for i in range(count)])  7.31 us
    pallas_call x3, Pallas kernels, local(): call(functools.partial(local_kernel, len(vecs)), (shape(T, R, N), shape(l...  3.52 us
    ppermute x3, starting transfers between devices, sum_all(): lax.ppermute(value, 'tm', [(i, i - i % run + (i + s) % run) for i in rang...  3.3 us
    pallas_call x1, Pallas kernels, band_pieces(): call(band_kernel, (shape(*BAND, dtype=BF16), shape(*BAND, dtype=BF16), sh...  2.85 us
    pallas_call x1, Pallas kernels, ahead_sums(): call(ahead_kernel, shape(T, N), [HBM, HBM], [pltpu.SMEM((T, T), jnp.int32...  1.95 us
    pallas_call x2, Pallas kernels, finish(): call(finish_kernel, shape(T, R, N), [VMEM] * 4, [PIECES], flops=ONE_WAY)  1.9 us
  transfers between devices with their start and end apart: 10, of which 10 were waited for; matrix products, arithmetic and copies ran while one was open for 0% of the time, Pallas kernels for 13%

profile of v2, /device:TPU:4, one launch (start us, length us, event | category | flops | bytes accessed | tf_op | source)
XLA Modules:
  0.0 77.6 jit_solution(15285802828832901130)
XLA Ops:
  0.6 1.9 %shard_map.60 = f32[8,128]{1,0:T(8,128)S(1)} custom-call(s32[8,8]{1,0:T(8,128)} %pattern.3, f32[8,8,128,128]{3,2,1,0:T(8,128)} %weights.3), custom_call_target="tpu_custom_call" | custom-call | flops 4194304 | bytes 4194304 | tf_op jit(solution)/shard_map/pallas_call | solution.py:99
  2.6 1.7 %collective-permute-start = (f32[8,128]{1,0:T(8,128)S(1)}, f32[8,128]{1,0:T(8,128)S(1)}, u32[]{:S(2)}, u32[]{:S(2)}) collective-permute-start(f32[8,128]{1,0:T(8,128)S(1)} %shard_map.60), channel_id=1, source_target_pairs={{0,1},{1,2},{2,3},{3,4},{4,5},{5,6},{6,7},{7,8},{8,9},{9,10},{10,1... | collective-permute-start | bytes 12296 | tf_op jit(solution)/shard_map/ppermute | solution.py:357
  4.3 2.8 %shard_map.59 = (bf16[4,256,1152]{2,1,0:T(8,128)(2,1)S(1)}, bf16[4,256,1152]{2,1,0:T(8,128)(2,1)S(1)}, f32[8,128]{1,0:T(8,128)S(1)}) custom-call(s32[8,8]{1,0:T(8,128)} %pattern.3, f32[8,8,128,128]{3,2,1,0:T(8,128)} %weights.3, f32[8,128]{1,0:T(8,128)} %reg.1), custom_call_target="tpu_custom_call" | custom-call | flops 2147483648 | bytes 8388608 | tf_op jit(solution)/shard_map/pallas_call | solution.py:155
  7.1 6.1 %collective-permute-done = f32[8,128]{1,0:T(8,128)S(1)} collective-permute-done((f32[8,128]{1,0:T(8,128)S(1)}, f32[8,128]{1,0:T(8,128)S(1)}, u32[]{:S(2)}, u32[]{:S(2)}) %collective-permute-start) | collective-permute-done | bytes 4128 | tf_op jit(solution)/shard_map/ppermute | solution.py:357
  13.2 2.1 %collective-permute-start.1 = (f32[8,64,128]{2,1,0:T(8,128)S(1)}, f32[8,64,128]{2,1,0:T(8,128)S(1)}, u32[]{:S(2)}, u32[]{:S(2)}) collective-permute-start(f32[8,64,128]{2,1,0:T(8,128)S(1)} %broadcast_divide_fusion.2.refs_0_.vec.v0), channel_id=1, source_target_pairs={{0,63},{1,0},{2,1},{3,2},{4,3},{5,4},{6,5},{7,6},{8,7},{9,8},{10,9... | collective-permute-start | bytes 786440 | tf_op jit(solution)/shard_map/ppermute | solution.py:357
  16.0 1.1 %shard_map.61 = (f32[8,64,128]{2,1,0:T(8,128)S(1)}, f32[1,2,64,128]{3,2,1,0:T(8,128)S(1)}) custom-call(f32[8,64,128]{2,1,0:T(8,128)S(1)} %broadcast_divide_fusion.2.refs_0_.vec.v0, f32[8,64,128]{2,1,0:T(8,128)S(1)} %copy-done, bf16[4,256,1152]{2,1,0:T(8,128)(2,1)S(1)} %get-tuple-element.16.refs_2_.high.refs_3_.refs_4_, ...), custom_call_target="tpu_custom_call" | custom-call | flops 503316480 | tf_op jit(solution)/shard_map/pallas_call | solution.py:254
  17.1 3.4 %collective-permute-done.1.vec_next.n0 = f32[8,64,128]{2,1,0:T(8,128)S(1)} collective-permute-done((f32[8,64,128]{2,1,0:T(8,128)S(1)}, f32[8,64,128]{2,1,0:T(8,128)S(1)}, u32[]{:S(2)}, u32[]{:S(2)}) %collective-permute-start.1) | collective-permute-done | bytes 262176 | tf_op jit(solution)/shard_map/ppermute | solution.py:357
  20.5 0.9 %shard_map.62 = f32[8,64,128]{2,1,0:T(8,128)S(1)} custom-call(f32[8,64,128]{2,1,0:T(8,128)S(1)} %collective-permute-done.1.vec_next.n0, bf16[4,256,1152]{2,1,0:T(8,128)(2,1)S(1)} %get-tuple-element.16.refs_2_.high.refs_3_.refs_4_, bf16[4,256,1152]{2,1,0:T(8,128)(2,1)S(1)} %get-tuple-element.17.refs_3_.low.refs_4_.refs_5_, ...), custom_call_target="tpu_custom_call" | custom-call | flops 251658240 | tf_op jit(solution)/shard_map/pallas_call | solution.py:271
  21.4 5.8 %collective-permute-done.2 = f32[8,64,128]{2,1,0:T(8,128)S(1)} collective-permute-done((f32[8,64,128]{2,1,0:T(8,128)S(1)}, f32[8,64,128]{2,1,0:T(8,128)S(1)}, u32[]{:S(2)}, u32[]{:S(2)}) %collective-permute-start.2) | collective-permute-done | bytes 262176 | tf_op jit(solution)/shard_map/ppermute | solution.py:357
  27.3 0.7 collective-permute-start.3
  28.6 1.5 %collective-permute-start.4 = (f32[8,64,128]{2,1,0:T(8,128)S(1)}, f32[8,64,128]{2,1,0:T(8,128)S(1)}, u32[]{:S(2)}, u32[]{:S(2)}) collective-permute-start(f32[8,64,128]{2,1,0:T(8,128)S(1)} %shard_map.66), channel_id=1, source_target_pairs={{0,1},{1,2},{2,3},{3,4},{4,5},{5,6},{6,7},{7,8},{8,9},{9,10},{10,1... | collective-permute-start | bytes 786440 | tf_op jit(solution)/shard_map/ppermute | solution.py:357
  30.1 1.2 %shard_map.64 = (f32[8,64,128]{2,1,0:T(8,128)S(1)}, f32[2,2,64,128]{3,2,1,0:T(8,128)S(1)}) custom-call(f32[8,64,128]{2,1,0:T(8,128)S(1)} %broadcast_divide_fusion.2.refs_0_.vec.v0, f32[8,64,128]{2,1,0:T(8,128)S(1)} %get-tuple-element.34.refs_1_.vec.v1, f32[8,64,128]{2,1,0:T(8,128)S(1)} %get-tuple-element.35.refs_2_.y1, ...), custom_call_target="tpu_custom_call" | custom-call | flops 503316480 | tf_op jit(solution)/shard_map/pallas_call | solution.py:254
  31.3 2.5 %collective-permute-done.3.vec_next.n1 = f32[8,64,128]{2,1,0:T(8,128)S(1)} collective-permute-done((f32[8,64,128]{2,1,0:T(8,128)S(1)}, f32[8,64,128]{2,1,0:T(8,128)S(1)}, u32[]{:S(2)}, u32[]{:S(2)}) %collective-permute-start.3) | collective-permute-done | bytes 262176 | tf_op jit(solution)/shard_map/ppermute | solution.py:357
  33.8 1.0 %shard_map.65 = f32[8,64,128]{2,1,0:T(8,128)S(1)} custom-call(f32[8,64,128]{2,1,0:T(8,128)S(1)} %collective-permute-done.3.vec_next.n1, bf16[4,256,1152]{2,1,0:T(8,128)(2,1)S(1)} %get-tuple-element.16.refs_2_.high.refs_3_.refs_4_, bf16[4,256,1152]{2,1,0:T(8,128)(2,1)S(1)} %get-tuple-element.17.refs_3_.low.refs_4_.refs_5_, ...), custom_call_target="tpu_custom_call" | custom-call | flops 251658240 | tf_op jit(solution)/shard_map/pallas_call | solution.py:271
  34.7 4.5 %collective-permute-done.4 = f32[8,64,128]{2,1,0:T(8,128)S(1)} collective-permute-done((f32[8,64,128]{2,1,0:T(8,128)S(1)}, f32[8,64,128]{2,1,0:T(8,128)S(1)}, u32[]{:S(2)}, u32[]{:S(2)}) %collective-permute-start.4) | collective-permute-done | bytes 262176 | tf_op jit(solution)/shard_map/ppermute | solution.py:357
  40.3 1.2 %shard_map.68 = (f32[8,64,128]{2,1,0:T(8,128)S(1)}, f32[3,2,64,128]{3,2,1,0:T(8,128)S(1)}) custom-call(f32[8,64,128]{2,1,0:T(8,128)S(1)} %broadcast_divide_fusion.2.refs_0_.vec.v0, f32[8,64,128]{2,1,0:T(8,128)S(1)} %get-tuple-element.34.refs_1_.vec.v1, f32[8,64,128]{2,1,0:T(8,128)S(1)} %get-tuple-element.32.vec.refs_2_.v2, ...), custom_call_target="tpu_custom_call" | custom-call | flops 503316480 | tf_op jit(solution)/shard_map/pallas_call | solution.py:254
  41.5 4.2 %collective-permute-done.5.n2 = f32[8,64,128]{2,1,0:T(8,128)S(1)} collective-permute-done((f32[8,64,128]{2,1,0:T(8,128)S(1)}, f32[8,64,128]{2,1,0:T(8,128)S(1)}, u32[]{:S(2)}, u32[]{:S(2)}) %collective-permute-start.5) | collective-permute-done | bytes 262176 | tf_op jit(solution)/shard_map/ppermute | solution.py:357
  45.7 1.4 %shard_map.69 = (f32[8,64,128]{2,1,0:T(8,128)S(1)}, f32[16,128]{1,0:T(8,128)S(1)}) custom-call(f32[8,64,128]{2,1,0:T(8,128)S(1)} %broadcast_divide_fusion.2.refs_0_.vec.v0, f32[8,64,128]{2,1,0:T(8,128)S(1)} %get-tuple-element.34.refs_1_.vec.v1, f32[8,64,128]{2,1,0:T(8,128)S(1)} %get-tuple-element.32.vec.refs_2_.v2, ...), custom_call_target="tpu_custom_call" | custom-call | flops 251658240 | tf_op jit(solution)/shard_map/pallas_call | solution.py:303
  47.5 2.9 %collective-permute-start.8 = (f32[16,128]{1,0:T(8,128)S(1)}, f32[16,128]{1,0:T(8,128)S(1)}, u32[]{:S(2)}, u32[]{:S(2)}) collective-permute-start(f32[16,128]{1,0:T(8,128)S(1)} %get-tuple-element.24), channel_id=1, source_target_pairs={{0,3},{1,0},{2,1},{3,2},{4,7},{5,4},{6,5},{7,6},{8,11},{9,8},{10,9... | collective-permute-start | bytes 24584 | tf_op jit(solution)/shard_map/ppermute | solution.py:371
  50.5 0.9 %collective-permute-start.9 = (f32[8,64,128]{2,1,0:T(8,128)S(1)}, f32[8,64,128]{2,1,0:T(8,128)S(1)}, u32[]{:S(2)}, u32[]{:S(2)}) collective-permute-start(f32[8,64,128]{2,1,0:T(8,128)S(1)} %shard_map.67.sent), channel_id=1, source_target_pairs={{0,1},{1,2},{2,3},{3,4},{4,5},{5,6},{6,7},{7,8},{8,9},{9,10},{10,1... | collective-permute-start | bytes 786440 | tf_op jit(solution)/shard_map/ppermute | solution.py:357
  51.3 0.8 collective-permute-done.6
  53.0 8.0 %collective-permute-done.9.arrived = f32[8,64,128]{2,1,0:T(8,128)S(1)} collective-permute-done((f32[8,64,128]{2,1,0:T(8,128)S(1)}, f32[8,64,128]{2,1,0:T(8,128)S(1)}, u32[]{:S(2)}, u32[]{:S(2)}) %collective-permute-start.9) | collective-permute-done | bytes 262176 | tf_op jit(solution)/shard_map/ppermute | solution.py:357
  61.1 15.2 %all_to_all.5 = f32[16,16,128]{2,1,0:T(8,128)S(1)} all-to-all(f32[16,16,128]{2,1,0:T(8,128)S(1)} %broadcast_in_dim.2), channel_id=1, replica_groups={{0,4,8,12,16,20,24,28,32,36,40,44,48,52,56,60},{1,5,9,13,17,21,25,29,33..., dimensions={0} | all-to-all | bytes 262144 | tf_op jit(solution)/shard_map/all_to_all | solution.py:376
  76.3 1.3 %shard_map.70 = (f32[8,64,128]{2,1,0:T(8,128)}, f32[8,64,128]{2,1,0:T(8,128)}) custom-call(f32[16,128]{1,0:T(8,128)S(1)} %pad_maximum_fusion.1.sums_ref, f32[8,64,128]{2,1,0:T(8,128)S(1)} %broadcast_divide_fusion.2.refs_0_.vec.v0, f32[8,64,128]{2,1,0:T(8,128)S(1)} %get-tuple-element.34.refs_1_.vec.v1, f32[8,64,128]{2,1,0:T(8,128)S(1)} %get-tuple-element.32.vec.refs_2_.v2, ...), custom_call_target="tpu_custom_call" | custom-call | tf_op jit(solution)/shard_map/pallas_call | solution.py:352
  (20 shorter events, 3.7 us)
Async XLA Ops:
  2.6 10.6 %copy-start = (f32[8,64,128]{2,1,0:T(8,128)S(1)}, f32[8,64,128]{2,1,0:T(8,128)}, u32[]{:S(2)}) copy-start(f32[8,64,128]{2,1,0:T(8,128)} %y0.1) | copy-start | bytes 786436
  2.6 10.6 %collective-permute-start = (f32[8,128]{1,0:T(8,128)S(1)}, f32[8,128]{1,0:T(8,128)S(1)}, u32[]{:S(2)}, u32[]{:S(2)}) collective-permute-start(f32[8,128]{1,0:T(8,128)S(1)} %shard_map.60), channel_id=1, source_target_pairs={{0,1},{1,2},{2,3},{3,4},{4,5},{5,6},{6,7},{7,8},{8,9},{9,10},{10,1... | collective-permute-start | bytes 12296 | tf_op jit(solution)/shard_map/ppermute | solution.py:357
  13.2 7.3 %collective-permute-start.1 = (f32[8,64,128]{2,1,0:T(8,128)S(1)}, f32[8,64,128]{2,1,0:T(8,128)S(1)}, u32[]{:S(2)}, u32[]{:S(2)}) collective-permute-start(f32[8,64,128]{2,1,0:T(8,128)S(1)} %broadcast_divide_fusion.2.refs_0_.vec.v0), channel_id=1, source_target_pairs={{0,63},{1,0},{2,1},{3,2},{4,3},{5,4},{6,5},{7,6},{8,7},{9,8},{10,9... | collective-permute-start | bytes 786440 | tf_op jit(solution)/shard_map/ppermute | solution.py:357
  15.9 11.4 %collective-permute-start.2 = (f32[8,64,128]{2,1,0:T(8,128)S(1)}, f32[8,64,128]{2,1,0:T(8,128)S(1)}, u32[]{:S(2)}, u32[]{:S(2)}) collective-permute-start(f32[8,64,128]{2,1,0:T(8,128)S(1)} %shard_map.63), channel_id=1, source_target_pairs={{0,1},{1,2},{2,3},{3,4},{4,5},{5,6},{6,7},{7,8},{8,9},{9,10},{10,1... | collective-permute-start | bytes 786440 | tf_op jit(solution)/shard_map/ppermute | solution.py:357
  27.3 6.4 %collective-permute-start.3 = (f32[8,64,128]{2,1,0:T(8,128)S(1)}, f32[8,64,128]{2,1,0:T(8,128)S(1)}, u32[]{:S(2)}, u32[]{:S(2)}) collective-permute-start(f32[8,64,128]{2,1,0:T(8,128)S(1)} %get-tuple-element.34.refs_1_.vec.v1), channel_id=1, source_target_pairs={{0,63},{1,0},{2,1},{3,2},{4,3},{5,4},{6,5},{7,6},{8,7},{9,8},{10,9... | collective-permute-start | bytes 786440 | tf_op jit(solution)/shard_map/ppermute | solution.py:357
  28.6 10.7 %collective-permute-start.4 = (f32[8,64,128]{2,1,0:T(8,128)S(1)}, f32[8,64,128]{2,1,0:T(8,128)S(1)}, u32[]{:S(2)}, u32[]{:S(2)}) collective-permute-start(f32[8,64,128]{2,1,0:T(8,128)S(1)} %shard_map.66), channel_id=1, source_target_pairs={{0,1},{1,2},{2,3},{3,4},{4,5},{5,6},{6,7},{7,8},{8,9},{9,10},{10,1... | collective-permute-start | bytes 786440 | tf_op jit(solution)/shard_map/ppermute | solution.py:357
  39.3 6.4 %collective-permute-start.5 = (f32[8,64,128]{2,1,0:T(8,128)S(1)}, f32[8,64,128]{2,1,0:T(8,128)S(1)}, u32[]{:S(2)}, u32[]{:S(2)}) collective-permute-start(f32[8,64,128]{2,1,0:T(8,128)S(1)} %get-tuple-element.32.vec.refs_2_.v2), channel_id=1, source_target_pairs={{0,63},{1,0},{2,1},{3,2},{4,3},{5,4},{6,5},{7,6},{8,7},{9,8},{10,9... | collective-permute-start | bytes 786440 | tf_op jit(solution)/shard_map/ppermute | solution.py:357
  47.1 4.9 %collective-permute-start.6 = (f32[16,128]{1,0:T(8,128)S(1)}, f32[16,128]{1,0:T(8,128)S(1)}, u32[]{:S(2)}, u32[]{:S(2)}) collective-permute-start(f32[16,128]{1,0:T(8,128)S(1)} %get-tuple-element.24), channel_id=1, source_target_pairs={{0,1},{1,2},{2,3},{3,0},{4,5},{5,6},{6,7},{7,4},{8,9},{9,10},{10,1... | collective-permute-start | bytes 24584 | tf_op jit(solution)/shard_map/ppermute | solution.py:371
  47.2 5.5 %collective-permute-start.7 = (f32[16,128]{1,0:T(8,128)S(1)}, f32[16,128]{1,0:T(8,128)S(1)}, u32[]{:S(2)}, u32[]{:S(2)}) collective-permute-start(f32[16,128]{1,0:T(8,128)S(1)} %get-tuple-element.24), channel_id=1, source_target_pairs={{0,2},{1,3},{2,0},{3,1},{4,6},{5,7},{6,4},{7,5},{8,10},{9,11},{10,... | collective-permute-start | bytes 24584 | tf_op jit(solution)/shard_map/ppermute | solution.py:371
  47.5 5.5 %collective-permute-start.8 = (f32[16,128]{1,0:T(8,128)S(1)}, f32[16,128]{1,0:T(8,128)S(1)}, u32[]{:S(2)}, u32[]{:S(2)}) collective-permute-start(f32[16,128]{1,0:T(8,128)S(1)} %get-tuple-element.24), channel_id=1, source_target_pairs={{0,3},{1,0},{2,1},{3,2},{4,7},{5,4},{6,5},{7,6},{8,11},{9,8},{10,9... | collective-permute-start | bytes 24584 | tf_op jit(solution)/shard_map/ppermute | solution.py:371
  50.5 10.6 %collective-permute-start.9 = (f32[8,64,128]{2,1,0:T(8,128)S(1)}, f32[8,64,128]{2,1,0:T(8,128)S(1)}, u32[]{:S(2)}, u32[]{:S(2)}) collective-permute-start(f32[8,64,128]{2,1,0:T(8,128)S(1)} %shard_map.67.sent), channel_id=1, source_target_pairs={{0,1},{1,2},{2,3},{3,4},{4,5},{5,6},{6,7},{7,8},{8,9},{9,10},{10,1... | collective-permute-start | bytes 786440 | tf_op jit(solution)/shard_map/ppermute | solution.py:357

commit v3 on v2

--- a/solution.py
+++ b/solution.py
@@ -283,14 +283,12 @@
     return value
 
 
-def gram_kernel(v0, v1, v2, n0, n1, n2, sent, partial, high, low, m0, m1, m2, image, out, pieces):
-    for t in range(T):
-        put_pieces(pieces, t, n2[t])
-    image[...] = partial[...]
+def gram_kernel(v0, v1, v2, ahead, arrived, partial, high, low, m0, m1, m2, image, out, pieces):
+    for t in range(T):
+        put_pieces(pieces, t, ahead[t])
+        image[t] = partial[t] + arrived[t]
     from_next(pieces, high, low, image)
-    last = [
-        dd_add(moments(v, image), moments(n, sent)) for v, n in ((v0, n0), (v1, n1), (v2, n2))
-    ]
+    last = [moments(v, image) for v in (v0, v1, v2)]
     every = [(m[i, 0], m[i, 1]) for m in (m0, m1, m2) for i in range(m.shape[0])] + last + last[-1:]
     out[...] = jnp.zeros_like(out)
     for q in range(5):
@@ -299,9 +297,9 @@
         out[8 + q : 9 + q, :] = l[0:1]
 
 
-def gram(vecs, ahead, sent, partial, high, low, found):
-    return call(gram_kernel, (shape(T, R, N), shape(16, 2 * R)), [VMEM] * 13, [PIECES], flops=ONE_WAY)(
-        *vecs, *ahead, sent, partial, high, low, *found
+def gram(vecs, ahead, arrived, partial, high, low, found):
+    return call(gram_kernel, (shape(T, R, N), shape(16, 2 * R)), [VMEM] * 11, [PIECES], flops=ONE_WAY)(
+        *vecs, ahead, arrived, partial, high, low, *found
     )
 
 
@@ -320,7 +318,7 @@
     return x0, x1, x2
 
 
-def result_kernel(sums_ref, v0, v1, v2, y0, y1, y2, y3, arrived, sol, res):
+def result_kernel(sums_ref, v0, v1, v2, y0, y1, y2, y3, sol, res):
     flat = []
     for q in range(5):
         h, l = sums_ref[q : q + 1, :], sums_ref[8 + q : 9 + q, :]
@@ -345,11 +343,11 @@
     for t in range(T):
         sol[t] = v0[t] + (d0 * v0[t] + d1 * v1[t] + d2 * v2[t])
         first, second = y1[t], y2[t]
-        res[t] = first - (d0 * (y0[t] - first) + d1 * (first - second) + d2 * (second - (y3[t] + arrived[t])))
-
-
-def result(total, vecs, images, arrived):
-    return call(result_kernel, (shape(T, R, N), shape(T, R, N)), [VMEM] * 9)(total, *vecs, *images, arrived)
+        res[t] = first - (d0 * (y0[t] - first) + d1 * (first - second) + d2 * (second - y3[t]))
+
+
+def result(total, vecs, images):
+    return call(result_kernel, (shape(T, R, N), shape(T, R, N)), [VMEM] * 8)(total, *vecs, *images)
 
 
 def shift(value, steps):
@@ -364,40 +362,46 @@
     return jnp.concatenate(total, axis=0)
 
 
-def sum_all(value, beside):
+def sum_all(value):
     count = lax.axis_size("tm")
     run = 4
     others = [
         lax.ppermute(value, "tm", [(i, i - i % run + (i + s) % run) for i in range(count)]) for s in range(1, run)
     ]
-    value, beside = lax.optimization_barrier((pair_add([value] + others), beside))
+    value = pair_add([value] + others)
     groups = [[i for i in range(j, count, run)] for j in range(run)]
     size = count // run
     spread = lax.all_to_all(
         jnp.broadcast_to(value[None], (size,) + value.shape), "tm", 0, 0, axis_index_groups=groups
     )
-    return pair_add([spread[i] for i in range(size)]), beside
+    return pair_add([spread[i] for i in range(size)])
+
+
+def exchange(vec, sent):
+    count = lax.axis_size("tm")
+    even = lax.axis_index("tm") % 2 == 0
+    one = lax.ppermute(jnp.where(even, sent, vec), "tm", [(i, i ^ 1) for i in range(count)])
+    two = lax.ppermute(
+        jnp.where(even, vec, sent), "tm", [(i, (i + (1 if i % 2 else -1)) % count) for i in range(count)]
+    )
+    return jnp.where(even, one, two), jnp.where(even, two, one)
 
 
 def shards(weights, pattern, shift_reg, rhs):
     inflow = shift(ahead_sums(pattern, weights), 1)
     high, low, own = band_pieces(pattern, weights, shift_reg)
     diag = own + inflow
-    vec = rhs / diag[:, None, :]
-    vecs, images, found, ahead = [vec], [rhs], [], []
+    vecs, images, found = [rhs / diag[:, None, :]], [rhs], []
     for step in range(3):
-        ahead.append(shift(vec, -1))
-        sent = contrib(vec, high, low)
-        arrived = shift(sent, 1)
+        vec = vecs[-1]
+        ahead, arrived = exchange(vec, contrib(vec, high, low))
         partial, part = local(vecs, images[-1], high, low)
         found.append(part)
         if step < 2:
-            images.append(finish(ahead[-1], high, low, partial) + arrived)
-            vec = images[-1] / diag[:, None, :]
-            vecs.append(vec)
-    image, total = gram(vecs, ahead, sent, partial, high, low, found)
-    total, arrived = sum_all(total, arrived)
-    return result(total, vecs, images + [image], arrived)
+            images.append(finish(ahead, high, low, partial) + arrived)
+            vecs.append(images[-1] / diag[:, None, :])
+    image, total = gram(vecs, ahead, arrived, partial, high, low, found)
+    return result(sum_all(total), vecs, images + [image])
 
 
 def solution(mesh):

time: 77.8 us -> 76.7 us (0.986)
  waiting for transfers between devices: 36.2 us -> 28.1 us
  starting transfers between devices: 10.6 us -> 14.8 us
  local copies, waits for them, and re-layouts: 0.02 us -> 3.1 us
    ppermute x7 -> x1, waiting for transfers between devices: 34.5 us -> 4.66 us  [shift(): lax.ppermute(value, 'tm', [(i, (i + steps) % count) for i in range(count)])]
    ppermute x0 -> x6, waiting for transfers between devices: none -> 18.6 us  [the longest x3 18.4 us: exchange(): lax.ppermute(jnp.where(even, vec, sent), 'tm', [(i, (i + (1 if i % 2 else...]
    ppermute x0 -> x6, starting transfers between devices: none -> 11 us  [the longest x3 11 us: exchange(): lax.ppermute(jnp.where(even, vec, sent), 'tm', [(i, (i + (1 if i % 2 else...]
    ppermute x7 -> x1, starting transfers between devices: 7.31 us -> 1.65 us  [shift(): lax.ppermute(value, 'tm', [(i, (i + steps) % count) for i in range(count)])]
    ppermute x3, waiting for transfers between devices: 1.71 us -> 4.86 us  [sum_all(): lax.ppermute(value, 'tm', [(i, i - i % run + (i + s) % run) for i in rang...]
    unnamed x2 -> x6, local copies, waits for them, and re-layouts: 0.01 us -> 3.09 us
    ppermute x3, starting transfers between devices: 3.3 us -> 2.14 us  [sum_all(): lax.ppermute(value, 'tm', [(i, i - i % run + (i + s) % run) for i in rang...]
  transfers between devices with their start and end apart: 10 -> 10, of which waited for: 10 -> 8; matrix products, arithmetic and copies ran while one was open for 0% -> 0% of each run, Pallas kernels for 13% -> 8%
where the time goes in v3:
time: 76.7 us; the launch traced here: 76.5 us
  waiting for transfers between devices  28.1 us (37%)
  blocking collectives  15 us (20%)
  starting transfers between devices  14.8 us (19%)
  Pallas kernels  14.2 us (19%)
  local copies, waits for them, and re-layouts  3.1 us (4%)
  between operations  0.82 us (1%)
    ppermute x3, waiting for transfers between devices, exchange(): lax.ppermute(jnp.where(even, vec, sent), 'tm', [(i, (i + (1 if i % 2 else...  18.4 us
    all_to_all x1, blocking collectives, sum_all(): lax.all_to_all(jnp.broadcast_to(value[None], (size,) + value.shape), 'tm'...  15 us
    ppermute x3, starting transfers between devices, exchange(): lax.ppermute(jnp.where(even, vec, sent), 'tm', [(i, (i + (1 if i % 2 else...  11 us
    ppermute x3, waiting for transfers between devices, sum_all(): lax.ppermute(value, 'tm', [(i, i - i % run + (i + s) % run) for i in rang...  4.86 us
    ppermute x1, waiting for transfers between devices, shift(): lax.ppermute(value, 'tm', [(i, (i + steps) % count) for i in range(count)])  4.66 us
    pallas_call x3, Pallas kernels, local(): call(functools.partial(local_kernel, len(vecs)), (shape(T, R, N), shape(l...  3.4 us
    unnamed x6, local copies, waits for them, and re-layouts  3.09 us
    pallas_call x1, Pallas kernels, band_pieces(): call(band_kernel, (shape(*BAND, dtype=BF16), shape(*BAND, dtype=BF16), sh...  2.85 us
  transfers between devices with their start and end apart: 10, of which 8 were waited for; matrix products, arithmetic and copies ran while one was open for 0% of the time, Pallas kernels for 8%

profile of v3, /device:TPU:4, one launch (start us, length us, event | category | flops | bytes accessed | tf_op | source)
XLA Modules:
  0.0 76.5 jit_solution(788988098464283762)
XLA Ops:
  0.6 1.9 %shard_map.60 = f32[8,128]{1,0:T(8,128)S(1)} custom-call(s32[8,8]{1,0:T(8,128)} %pattern.3, f32[8,8,128,128]{3,2,1,0:T(8,128)} %weights.3), custom_call_target="tpu_custom_call" | custom-call | flops 4194304 | bytes 4194304 | tf_op jit(solution)/shard_map/pallas_call | solution.py:99
  2.6 1.7 %collective-permute-start = (f32[8,128]{1,0:T(8,128)S(1)}, f32[8,128]{1,0:T(8,128)S(1)}, u32[]{:S(2)}, u32[]{:S(2)}) collective-permute-start(f32[8,128]{1,0:T(8,128)S(1)} %shard_map.60), channel_id=1, source_target_pairs={{0,1},{1,2},{2,3},{3,4},{4,5},{5,6},{6,7},{7,8},{8,9},{9,10},{10,1... | collective-permute-start | bytes 12296 | tf_op jit(solution)/shard_map/ppermute | solution.py:355
  4.3 2.8 %shard_map.59 = (bf16[4,256,1152]{2,1,0:T(8,128)(2,1)S(1)}, bf16[4,256,1152]{2,1,0:T(8,128)(2,1)S(1)}, f32[8,128]{1,0:T(8,128)S(1)}) custom-call(s32[8,8]{1,0:T(8,128)} %pattern.3, f32[8,8,128,128]{3,2,1,0:T(8,128)} %weights.3, f32[8,128]{1,0:T(8,128)} %reg.1), custom_call_target="tpu_custom_call" | custom-call | flops 2147483648 | bytes 8388608 | tf_op jit(solution)/shard_map/pallas_call | solution.py:155
  7.1 1.4 %copy-done = bf16[4,256,1152]{2,1,0:T(8,128)(2,1)} copy-done((bf16[4,256,1152]{2,1,0:T(8,128)(2,1)}, bf16[4,256,1152]{2,1,0:T(8,128)(2,1)S(1)}, u32[]{:S(2)}) %copy-start) | copy-done | bytes 2359320
  8.5 4.7 %collective-permute-done = f32[8,128]{1,0:T(8,128)S(1)} collective-permute-done((f32[8,128]{1,0:T(8,128)S(1)}, f32[8,128]{1,0:T(8,128)S(1)}, u32[]{:S(2)}, u32[]{:S(2)}) %collective-permute-start) | collective-permute-done | bytes 4128 | tf_op jit(solution)/shard_map/ppermute | solution.py:355
  13.2 1.7 %copy-done.1 = bf16[4,256,1152]{2,1,0:T(8,128)(2,1)S(1)} copy-done((bf16[4,256,1152]{2,1,0:T(8,128)(2,1)S(1)}, bf16[4,256,1152]{2,1,0:T(8,128)(2,1)}, u32[]{:S(2)}) %copy-start.1) | copy-done | bytes 2359320
  15.5 2.8 %collective-permute-start.2 = (f32[8,64,128]{2,1,0:T(8,128)S(1)}, f32[8,64,128]{2,1,0:T(8,128)S(1)}, u32[]{:S(2)}, u32[]{:S(2)}) collective-permute-start(f32[8,64,128]{2,1,0:T(8,128)S(1)} %get-tuple-element.38), channel_id=1, source_target_pairs={{0,63},{1,2},{2,1},{3,4},{4,3},{5,6},{6,5},{7,8},{8,7},{9,10},{10,... | collective-permute-start | bytes 786440 | tf_op jit(solution)/shard_map/ppermute | solution.py:384
  18.4 1.1 %shard_map.62 = (f32[8,64,128]{2,1,0:T(8,128)S(1)}, f32[1,2,64,128]{3,2,1,0:T(8,128)S(1)}) custom-call(f32[8,64,128]{2,1,0:T(8,128)S(1)} %broadcast_divide_fusion.2.vec.refs_0_.v0, f32[8,64,128]{2,1,0:T(8,128)S(1)} %copy-done.2, bf16[4,256,1152]{2,1,0:T(8,128)(2,1)S(1)} %get-tuple-element.14.high.refs_2_.refs_3_.refs_4_, bf16[4,256,1152]{2,1,0:T(8,128)(2,1)S(1)} %copy-done.1), custom_call_target="tpu_custom_call" | custom-call | flops 503316480 | tf_op jit(solution)/shard_map/pallas_call | solution.py:254
  19.4 7.6 %collective-permute-done.2 = f32[8,64,128]{2,1,0:T(8,128)S(1)} collective-permute-done((f32[8,64,128]{2,1,0:T(8,128)S(1)}, f32[8,64,128]{2,1,0:T(8,128)S(1)}, u32[]{:S(2)}, u32[]{:S(2)}) %collective-permute-start.2) | collective-permute-done | bytes 262176 | tf_op jit(solution)/shard_map/ppermute | solution.py:384
  27.1 0.9 %shard_map.63 = f32[8,64,128]{2,1,0:T(8,128)S(1)} custom-call(f32[8,64,128]{2,1,0:T(8,128)S(1)} %broadcast_select_fusion.7.vec_next, bf16[4,256,1152]{2,1,0:T(8,128)(2,1)S(1)} %get-tuple-element.14.high.refs_2_.refs_3_.refs_4_, bf16[4,256,1152]{2,1,0:T(8,128)(2,1)S(1)} %copy-done.1, f32[8,64,128]{2,1,0:T(8,128)S(1)} %get-tuple-element.16.partial), custom_call_target="tpu_custom_call" | custom-call | flops 251658240 | tf_op jit(solution)/shard_map/pallas_call | solution.py:271
  28.7 3.7 %collective-permute-start.4 = (f32[8,64,128]{2,1,0:T(8,128)S(1)}, f32[8,64,128]{2,1,0:T(8,128)S(1)}, u32[]{:S(2)}, u32[]{:S(2)}) collective-permute-start(f32[8,64,128]{2,1,0:T(8,128)S(1)} %get-tuple-element.36), channel_id=1, source_target_pairs={{0,63},{1,2},{2,1},{3,4},{4,3},{5,6},{6,5},{7,8},{8,7},{9,10},{10,... | collective-permute-start | bytes 786440 | tf_op jit(solution)/shard_map/ppermute | solution.py:384
  32.4 1.1 %shard_map.65 = (f32[8,64,128]{2,1,0:T(8,128)S(1)}, f32[2,2,64,128]{3,2,1,0:T(8,128)S(1)}) custom-call(f32[8,64,128]{2,1,0:T(8,128)S(1)} %broadcast_divide_fusion.2.vec.refs_0_.v0, f32[8,64,128]{2,1,0:T(8,128)S(1)} %get-tuple-element.30.vec.refs_1_.v1, f32[8,64,128]{2,1,0:T(8,128)S(1)} %get-tuple-element.31.refs_2_.y1, ...), custom_call_target="tpu_custom_call" | custom-call | flops 503316480 | tf_op jit(solution)/shard_map/pallas_call | solution.py:254
  33.5 5.8 %collective-permute-done.4 = f32[8,64,128]{2,1,0:T(8,128)S(1)} collective-permute-done((f32[8,64,128]{2,1,0:T(8,128)S(1)}, f32[8,64,128]{2,1,0:T(8,128)S(1)}, u32[]{:S(2)}, u32[]{:S(2)}) %collective-permute-start.4) | collective-permute-done | bytes 262176 | tf_op jit(solution)/shard_map/ppermute | solution.py:384
  39.4 0.9 %shard_map.66 = f32[8,64,128]{2,1,0:T(8,128)S(1)} custom-call(f32[8,64,128]{2,1,0:T(8,128)S(1)} %broadcast_select_fusion.4.vec_next, bf16[4,256,1152]{2,1,0:T(8,128)(2,1)S(1)} %get-tuple-element.14.high.refs_2_.refs_3_.refs_4_, bf16[4,256,1152]{2,1,0:T(8,128)(2,1)S(1)} %copy-done.1, f32[8,64,128]{2,1,0:T(8,128)S(1)} %get-tuple-element.17.partial), custom_call_target="tpu_custom_call" | custom-call | flops 251658240 | tf_op jit(solution)/shard_map/pallas_call | solution.py:271
  41.0 4.5 %collective-permute-start.6 = (f32[8,64,128]{2,1,0:T(8,128)S(1)}, f32[8,64,128]{2,1,0:T(8,128)S(1)}, u32[]{:S(2)}, u32[]{:S(2)}) collective-permute-start(f32[8,64,128]{2,1,0:T(8,128)S(1)} %get-tuple-element.34), channel_id=1, source_target_pairs={{0,63},{1,2},{2,1},{3,4},{4,3},{5,6},{6,5},{7,8},{8,7},{9,10},{10,... | collective-permute-start | bytes 786440 | tf_op jit(solution)/shard_map/ppermute | solution.py:384
  45.5 1.2 %shard_map.68 = (f32[8,64,128]{2,1,0:T(8,128)S(1)}, f32[3,2,64,128]{3,2,1,0:T(8,128)S(1)}) custom-call(f32[8,64,128]{2,1,0:T(8,128)S(1)} %broadcast_divide_fusion.2.vec.refs_0_.v0, f32[8,64,128]{2,1,0:T(8,128)S(1)} %get-tuple-element.30.vec.refs_1_.v1, f32[8,64,128]{2,1,0:T(8,128)S(1)} %get-tuple-element.28.vec.refs_2_.v2, ...), custom_call_target="tpu_custom_call" | custom-call | flops 503316480 | tf_op jit(solution)/shard_map/pallas_call | solution.py:254
  46.7 5.0 %collective-permute-done.6 = f32[8,64,128]{2,1,0:T(8,128)S(1)} collective-permute-done((f32[8,64,128]{2,1,0:T(8,128)S(1)}, f32[8,64,128]{2,1,0:T(8,128)S(1)}, u32[]{:S(2)}, u32[]{:S(2)}) %collective-permute-start.6) | collective-permute-done | bytes 262176 | tf_op jit(solution)/shard_map/ppermute | solution.py:384
  51.9 1.2 %shard_map.69 = (f32[8,64,128]{2,1,0:T(8,128)S(1)}, f32[16,128]{1,0:T(8,128)S(1)}) custom-call(f32[8,64,128]{2,1,0:T(8,128)S(1)} %broadcast_divide_fusion.2.vec.refs_0_.v0, f32[8,64,128]{2,1,0:T(8,128)S(1)} %get-tuple-element.30.vec.refs_1_.v1, f32[8,64,128]{2,1,0:T(8,128)S(1)} %get-tuple-element.28.vec.refs_2_.v2, ...), custom_call_target="tpu_custom_call" | custom-call | flops 251658240 | tf_op jit(solution)/shard_map/pallas_call | solution.py:301
  53.2 2.1 %collective-permute-start.8 = (f32[16,128]{1,0:T(8,128)S(1)}, f32[16,128]{1,0:T(8,128)S(1)}, u32[]{:S(2)}, u32[]{:S(2)}) collective-permute-start(f32[16,128]{1,0:T(8,128)S(1)} %get-tuple-element.22), channel_id=1, source_target_pairs={{0,2},{1,3},{2,0},{3,1},{4,6},{5,7},{6,4},{7,5},{8,10},{9,11},{10,... | collective-permute-start | bytes 24584 | tf_op jit(solution)/shard_map/ppermute | solution.py:369
  55.2 1.6 %collective-permute-done.9 = f32[16,128]{1,0:T(8,128)S(1)} collective-permute-done((f32[16,128]{1,0:T(8,128)S(1)}, f32[16,128]{1,0:T(8,128)S(1)}, u32[]{:S(2)}, u32[]{:S(2)}) %collective-permute-start.9) | collective-permute-done | bytes 8224 | tf_op jit(solution)/shard_map/ppermute | solution.py:369
  56.8 1.6 %collective-permute-done.8 = f32[16,128]{1,0:T(8,128)S(1)} collective-permute-done((f32[16,128]{1,0:T(8,128)S(1)}, f32[16,128]{1,0:T(8,128)S(1)}, u32[]{:S(2)}, u32[]{:S(2)}) %collective-permute-start.8) | collective-permute-done | bytes 8224 | tf_op jit(solution)/shard_map/ppermute | solution.py:369
  58.4 1.7 %collective-permute-done.7 = f32[16,128]{1,0:T(8,128)S(1)} collective-permute-done((f32[16,128]{1,0:T(8,128)S(1)}, f32[16,128]{1,0:T(8,128)S(1)}, u32[]{:S(2)}, u32[]{:S(2)}) %collective-permute-start.7) | collective-permute-done | bytes 8224 | tf_op jit(solution)/shard_map/ppermute | solution.py:369
  60.1 15.0 %all_to_all.5 = f32[16,16,128]{2,1,0:T(8,128)S(1)} all-to-all(f32[16,16,128]{2,1,0:T(8,128)S(1)} %broadcast_in_dim.2), channel_id=1, replica_groups={{0,4,8,12,16,20,24,28,32,36,40,44,48,52,56,60},{1,5,9,13,17,21,25,29,33..., dimensions={0} | all-to-all | bytes 262144 | tf_op jit(solution)/shard_map/all_to_all | solution.py:374
  75.2 1.3 %shard_map.70 = (f32[8,64,128]{2,1,0:T(8,128)}, f32[8,64,128]{2,1,0:T(8,128)}) custom-call(f32[16,128]{1,0:T(8,128)S(1)} %pad_maximum_fusion.1.sums_ref, f32[8,64,128]{2,1,0:T(8,128)S(1)} %broadcast_divide_fusion.2.vec.refs_0_.v0, f32[8,64,128]{2,1,0:T(8,128)S(1)} %get-tuple-element.30.vec.refs_1_.v1, f32[8,64,128]{2,1,0:T(8,128)S(1)} %get-tuple-element.28.vec.refs_2_.v2, ...), custom_call_target="tpu_custom_call" | custom-call | tf_op jit(solution)/shard_map/pallas_call | solution.py:350
  (30 shorter events, 2.4 us)
Async XLA Ops:
  2.6 10.6 %copy-start.2 = (f32[8,64,128]{2,1,0:T(8,128)S(1)}, f32[8,64,128]{2,1,0:T(8,128)}, u32[]{:S(2)}) copy-start(f32[8,64,128]{2,1,0:T(8,128)} %y0.1) | copy-start | bytes 786436
  2.6 10.6 %collective-permute-start = (f32[8,128]{1,0:T(8,128)S(1)}, f32[8,128]{1,0:T(8,128)S(1)}, u32[]{:S(2)}, u32[]{:S(2)}) collective-permute-start(f32[8,128]{1,0:T(8,128)S(1)} %shard_map.60), channel_id=1, source_target_pairs={{0,1},{1,2},{2,3},{3,4},{4,5},{5,6},{6,7},{7,8},{8,9},{9,10},{10,1... | collective-permute-start | bytes 12296 | tf_op jit(solution)/shard_map/ppermute | solution.py:355
  7.1 1.4 %copy-start = (bf16[4,256,1152]{2,1,0:T(8,128)(2,1)}, bf16[4,256,1152]{2,1,0:T(8,128)(2,1)S(1)}, u32[]{:S(2)}) copy-start(bf16[4,256,1152]{2,1,0:T(8,128)(2,1)S(1)} %get-tuple-element.15.low.refs_3_.refs_4_.refs_5_) | copy-start | bytes 7077892
  13.2 1.7 %copy-start.1 = (bf16[4,256,1152]{2,1,0:T(8,128)(2,1)S(1)}, bf16[4,256,1152]{2,1,0:T(8,128)(2,1)}, u32[]{:S(2)}) copy-start(bf16[4,256,1152]{2,1,0:T(8,128)(2,1)} %copy-done) | copy-start | bytes 7077892
  15.5 11.5 %collective-permute-start.2 = (f32[8,64,128]{2,1,0:T(8,128)S(1)}, f32[8,64,128]{2,1,0:T(8,128)S(1)}, u32[]{:S(2)}, u32[]{:S(2)}) collective-permute-start(f32[8,64,128]{2,1,0:T(8,128)S(1)} %get-tuple-element.38), channel_id=1, source_target_pairs={{0,63},{1,2},{2,1},{3,4},{4,3},{5,6},{6,5},{7,8},{8,7},{9,10},{10,... | collective-permute-start | bytes 786440 | tf_op jit(solution)/shard_map/ppermute | solution.py:384
  18.4 8.7 %collective-permute-start.1 = (f32[8,64,128]{2,1,0:T(8,128)S(1)}, f32[8,64,128]{2,1,0:T(8,128)S(1)}, u32[]{:S(2)}, u32[]{:S(2)}) collective-permute-start(f32[8,64,128]{2,1,0:T(8,128)S(1)} %get-tuple-element.39), channel_id=1, source_target_pairs={{0,1},{1,0},{2,3},{3,2},{4,5},{5,4},{6,7},{7,6},{8,9},{9,8},{10,11... | collective-permute-start | bytes 786440 | tf_op jit(solution)/shard_map/ppermute | solution.py:383
  28.7 10.7 %collective-permute-start.4 = (f32[8,64,128]{2,1,0:T(8,128)S(1)}, f32[8,64,128]{2,1,0:T(8,128)S(1)}, u32[]{:S(2)}, u32[]{:S(2)}) collective-permute-start(f32[8,64,128]{2,1,0:T(8,128)S(1)} %get-tuple-element.36), channel_id=1, source_target_pairs={{0,63},{1,2},{2,1},{3,4},{4,3},{5,6},{6,5},{7,8},{8,7},{9,10},{10,... | collective-permute-start | bytes 786440 | tf_op jit(solution)/shard_map/ppermute | solution.py:384
  32.4 7.0 %collective-permute-start.3 = (f32[8,64,128]{2,1,0:T(8,128)S(1)}, f32[8,64,128]{2,1,0:T(8,128)S(1)}, u32[]{:S(2)}, u32[]{:S(2)}) collective-permute-start(f32[8,64,128]{2,1,0:T(8,128)S(1)} %get-tuple-element.37), channel_id=1, source_target_pairs={{0,1},{1,0},{2,3},{3,2},{4,5},{5,4},{6,7},{7,6},{8,9},{9,8},{10,11... | collective-permute-start | bytes 786440 | tf_op jit(solution)/shard_map/ppermute | solution.py:383
  41.0 10.7 %collective-permute-start.6 = (f32[8,64,128]{2,1,0:T(8,128)S(1)}, f32[8,64,128]{2,1,0:T(8,128)S(1)}, u32[]{:S(2)}, u32[]{:S(2)}) collective-permute-start(f32[8,64,128]{2,1,0:T(8,128)S(1)} %get-tuple-element.34), channel_id=1, source_target_pairs={{0,63},{1,2},{2,1},{3,4},{4,3},{5,6},{6,5},{7,8},{8,7},{9,10},{10,... | collective-permute-start | bytes 786440 | tf_op jit(solution)/shard_map/ppermute | solution.py:384
  45.5 6.4 %collective-permute-start.5 = (f32[8,64,128]{2,1,0:T(8,128)S(1)}, f32[8,64,128]{2,1,0:T(8,128)S(1)}, u32[]{:S(2)}, u32[]{:S(2)}) collective-permute-start(f32[8,64,128]{2,1,0:T(8,128)S(1)} %get-tuple-element.35), channel_id=1, source_target_pairs={{0,1},{1,0},{2,3},{3,2},{4,5},{5,4},{6,7},{7,6},{8,9},{9,8},{10,11... | collective-permute-start | bytes 786440 | tf_op jit(solution)/shard_map/ppermute | solution.py:383
  53.1 3.7 %collective-permute-start.9 = (f32[16,128]{1,0:T(8,128)S(1)}, f32[16,128]{1,0:T(8,128)S(1)}, u32[]{:S(2)}, u32[]{:S(2)}) collective-permute-start(f32[16,128]{1,0:T(8,128)S(1)} %get-tuple-element.22), channel_id=1, source_target_pairs={{0,3},{1,0},{2,1},{3,2},{4,7},{5,4},{6,5},{7,6},{8,11},{9,8},{10,9... | collective-permute-start | bytes 24584 | tf_op jit(solution)/shard_map/ppermute | solution.py:369
  53.2 5.2 %collective-permute-start.8 = (f32[16,128]{1,0:T(8,128)S(1)}, f32[16,128]{1,0:T(8,128)S(1)}, u32[]{:S(2)}, u32[]{:S(2)}) collective-permute-start(f32[16,128]{1,0:T(8,128)S(1)} %get-tuple-element.22), channel_id=1, source_target_pairs={{0,2},{1,3},{2,0},{3,1},{4,6},{5,7},{6,4},{7,5},{8,10},{9,11},{10,... | collective-permute-start | bytes 24584 | tf_op jit(solution)/shard_map/ppermute | solution.py:369
  55.2 4.9 %collective-permute-start.7 = (f32[16,128]{1,0:T(8,128)S(1)}, f32[16,128]{1,0:T(8,128)S(1)}, u32[]{:S(2)}, u32[]{:S(2)}) collective-permute-start(f32[16,128]{1,0:T(8,128)S(1)} %get-tuple-element.22), channel_id=1, source_target_pairs={{0,1},{1,2},{2,3},{3,0},{4,5},{5,6},{6,7},{7,4},{8,9},{9,10},{10,1... | collective-permute-start | bytes 24584 | tf_op jit(solution)/shard_map/ppermute | solution.py:369

commit v4 on v3

--- a/solution.py
+++ b/solution.py
@@ -209,10 +209,20 @@
         out[2 * a + 1] += term[:, N:]
 
 
+def turned_rows(a):
+    return slice(a * (a + 1) * N, (a + 1) * (a + 2) * N)
+
+
+def turn(high, low, turned_high, turned_low):
+    for piece, out in ((high, turned_high), (low, turned_low)):
+        for a in range(T // 2):
+            out[turned_rows(a), :] = piece[a, :, (7 - 2 * a) * N :].T
+
+
 def from_next(pieces, high, low, out):
     for a in range(T // 2):
-        at = slice((7 - 2 * a) * N, (T + 1) * N)
-        term = product(pieces, slice(0, (2 * a + 2) * N), high[a, :, at], low[a, :, at], dot_t)
+        rows = turned_rows(a)
+        term = product(pieces, slice(0, (2 * a + 2) * N), high[rows, :], low[rows, :], dot)
         out[2 * a] += term[:, :N]
         out[2 * a + 1] += term[:, N:]
 
@@ -229,18 +239,45 @@
 ONE_WAY = 2 * 3 * 40 * R * N * N
 
 
-def contrib_kernel(vec, high, low, out, pieces):
+def choose(flag, first, second):
+    return jnp.where(jnp.broadcast_to(flag[0:1, :], (R, N)) > 0, first, second)
+
+
+def hand_out(flag, vec, high, low, one, two, sent, pieces):
     for t in range(T):
         put_pieces(pieces, t, vec[t])
-    to_next(pieces, high, low, out)
-
-
-def contrib(vec, high, low):
-    return call(contrib_kernel, shape(T, R, N), [VMEM] * 3, [PIECES], flops=ONE_WAY)(vec, high, low)
+    to_next(pieces, high, low, sent)
+    for t in range(T):
+        one[t] = choose(flag, sent[t], vec[t])
+        two[t] = choose(flag, vec[t], sent[t])
+
+
+BLOCKS = shape(T, R, N)
+SENT = pltpu.VMEM((T, R, N), F32)
+TURNED = shape((T // 2) * (T // 2 + 1) * N, 2 * N, dtype=BF16)
+
+
+def first_kernel(flag, rhs, own, inflow, high, low, diag, vec, one, two, sent, pieces):
+    diag[...] = own[...] + inflow[...]
+    for t in range(T):
+        vec[t] = rhs[t] / diag[t : t + 1, :]
+    hand_out(flag, vec, high, low, one, two, sent, pieces)
+
+
+def first(flag, rhs, own, inflow, high, low):
+    return call(
+        first_kernel,
+        (shape(T, N), BLOCKS, BLOCKS, BLOCKS),
+        [VMEM] * 6,
+        [SENT, PIECES],
+        flops=ONE_WAY,
+    )(flag, rhs, own, inflow, high, low)
 
 
 def local_kernel(count, *refs):
-    vecs, (image, high, low, out, found, pieces) = refs[:count], refs[count:]
+    vecs, (image, high, low, out, found, *turned, pieces) = refs[:count], refs[count:]
+    if turned:
+        turn(high, low, *turned)
     for t in range(T):
         put_pieces(pieces, t, vecs[-1][t])
     within(pieces, high, low, out)
@@ -251,24 +288,32 @@
 
 
 def local(vecs, image, high, low):
+    turned = (TURNED, TURNED) if len(vecs) == 1 else ()
     return call(
         functools.partial(local_kernel, len(vecs)),
-        (shape(T, R, N), shape(len(vecs), 2, R, N)),
+        (BLOCKS, shape(len(vecs), 2, R, N)) + turned,
         [VMEM] * (len(vecs) + 3),
         [PIECES],
         flops=2 * ONE_WAY,
     )(*vecs, image, high, low)
 
 
-def finish_kernel(vec_next, high, low, partial, out, pieces):
-    for t in range(T):
-        put_pieces(pieces, t, vec_next[t])
-    out[...] = partial[...]
-    from_next(pieces, high, low, out)
-
-
-def finish(vec_next, high, low, partial):
-    return call(finish_kernel, shape(T, R, N), [VMEM] * 4, [PIECES], flops=ONE_WAY)(vec_next, high, low, partial)
+def add_received(flag, got_one, got_two, partial, turned_high, turned_low, image, pieces):
+    for t in range(T):
+        put_pieces(pieces, t, choose(flag, got_one[t], got_two[t]))
+        image[t] = partial[t] + choose(flag, got_two[t], got_one[t])
+    from_next(pieces, turned_high, turned_low, image)
+
+
+def step_kernel(flag, got_one, got_two, partial, diag, high, low, turned_high, turned_low, image, vec, one, two, sent, pieces):
+    add_received(flag, got_one, got_two, partial, turned_high, turned_low, image, pieces)
+    for t in range(T):
+        vec[t] = image[t] / diag[t : t + 1, :]
+    hand_out(flag, vec, high, low, one, two, sent, pieces)
+
+
+def next_step(*args):
+    return call(step_kernel, (BLOCKS,) * 4, [VMEM] * 9, [SENT, PIECES], flops=2 * ONE_WAY)(*args)
 
 
 def fold(found):
@@ -278,16 +323,15 @@
     while size > 8:
         size //= 2
         value = dd_add(tuple(v[:size] for v in value), tuple(v[size:] for v in value))
-    for turn in (4, 2, 1):
-        value = dd_add(value, tuple(pltpu.roll(v, turn, 0) for v in value))
+    for turn_by in (4, 2, 1):
+        value = dd_add(value, tuple(pltpu.roll(v, turn_by, 0) for v in value))
     return value
 
 
-def gram_kernel(v0, v1, v2, ahead, arrived, partial, high, low, m0, m1, m2, image, out, pieces):
-    for t in range(T):
-        put_pieces(pieces, t, ahead[t])
-        image[t] = partial[t] + arrived[t]
-    from_next(pieces, high, low, image)
+def gram_kernel(
+    flag, got_one, got_two, partial, turned_high, turned_low, v0, v1, v2, m0, m1, m2, image, out, pieces
+):
+    add_received(flag, got_one, got_two, partial, turned_high, turned_low, image, pieces)
     last = [moments(v, image) for v in (v0, v1, v2)]
     every = [(m[i, 0], m[i, 1]) for m in (m0, m1, m2) for i in range(m.shape[0])] + last + last[-1:]
     out[...] = jnp.zeros_like(out)
@@ -297,10 +341,8 @@
         out[8 + q : 9 + q, :] = l[0:1]
 
 
-def gram(vecs, ahead, arrived, partial, high, low, found):
-    return call(gram_kernel, (shape(T, R, N), shape(16, 2 * R)), [VMEM] * 11, [PIECES], flops=ONE_WAY)(
-        *vecs, ahead, arrived, partial, high, low, *found
-    )
+def gram(*args):
+    return call(gram_kernel, (BLOCKS, shape(16, 2 * R)), [VMEM] * 12, [PIECES], flops=ONE_WAY)(*args)
 
 
 def solve(matrix, right):
@@ -377,30 +419,29 @@
     return pair_add([spread[i] for i in range(size)])
 
 
-def exchange(vec, sent):
+def swaps(one, two):
     count = lax.axis_size("tm")
-    even = lax.axis_index("tm") % 2 == 0
-    one = lax.ppermute(jnp.where(even, sent, vec), "tm", [(i, i ^ 1) for i in range(count)])
-    two = lax.ppermute(
-        jnp.where(even, vec, sent), "tm", [(i, (i + (1 if i % 2 else -1)) % count) for i in range(count)]
-    )
-    return jnp.where(even, one, two), jnp.where(even, two, one)
+    one = lax.ppermute(one, "tm", [(i, i ^ 1) for i in range(count)])
+    return one, lax.ppermute(two, "tm", [(i, (i + (1 if i % 2 else -1)) % count) for i in range(count)])
 
 
 def shards(weights, pattern, shift_reg, rhs):
+    flag = jnp.broadcast_to((1 - lax.axis_index("tm") % 2).astype(F32), (8, N))
+    flag, pattern = lax.optimization_barrier((flag, pattern))
     inflow = shift(ahead_sums(pattern, weights), 1)
     high, low, own = band_pieces(pattern, weights, shift_reg)
-    diag = own + inflow
-    vecs, images, found = [rhs / diag[:, None, :]], [rhs], []
+    diag, vec, *leaving = first(flag, rhs, own, inflow, high, low)
+    vecs, images, found = [vec], [rhs], []
     for step in range(3):
-        vec = vecs[-1]
-        ahead, arrived = exchange(vec, contrib(vec, high, low))
-        partial, part = local(vecs, images[-1], high, low)
+        got = swaps(*leaving)
+        partial, part, *extra = local(vecs, images[-1], high, low)
         found.append(part)
+        turned = extra or turned
         if step < 2:
-            images.append(finish(ahead, high, low, partial) + arrived)
-            vecs.append(images[-1] / diag[:, None, :])
-    image, total = gram(vecs, ahead, arrived, partial, high, low, found)
+            image, vec, *leaving = next_step(flag, *got, partial, diag, high, low, *turned)
+            images.append(image)
+            vecs.append(vec)
+    image, total = gram(flag, *got, partial, *turned, *vecs, *found)
     return result(sum_all(total), vecs, images + [image])
 
 

time: 76.7 us -> 72.8 us (0.949)
  local copies, waits for them, and re-layouts: 3.1 us -> 0.02 us
  Pallas kernels: 14.2 us -> 13.1 us
  waiting for transfers between devices: 28.1 us -> 28.9 us
    unnamed x6 -> x2, local copies, waits for them, and re-layouts: 3.09 us -> 0.01 us
    ppermute x1, waiting for transfers between devices: 4.66 us -> 6.09 us  [shift(): lax.ppermute(value, 'tm', [(i, (i + steps) % count) for i in range(count)])]
    pallas_call x9 -> x7, Pallas kernels: 8.1 us -> 7.01 us  [the longest x3 3.56 us: local(): call(functools.partial(local_kernel, len(vecs)), (BLOCKS, shape(len(vecs)...]
  transfers between devices with their start and end apart: 10 -> 10, of which waited for: 8 -> 10; matrix products, arithmetic and copies ran while one was open for 0% -> 0% of each run, Pallas kernels for 8% -> 9%
where the time goes in v4:
time: 72.8 us; the launch traced here: 72.7 us
  waiting for transfers between devices  28.9 us (40%)
  blocking collectives  15 us (21%)
  starting transfers between devices  14.7 us (20%)
  Pallas kernels  13.1 us (18%)
  between operations  0.78 us (1%)
    all_to_all x1, blocking collectives, sum_all(): lax.all_to_all(jnp.broadcast_to(value[None], (size,) + value.shape), 'tm'...  15 us
    ppermute x3, waiting for transfers between devices, swaps(): lax.ppermute(two, 'tm', [(i, (i + (1 if i % 2 else -1)) % count) for i in...  13 us
    ppermute x3, starting transfers between devices, swaps(): lax.ppermute(two, 'tm', [(i, (i + (1 if i % 2 else -1)) % count) for i in...  10.7 us
    ppermute x1, waiting for transfers between devices, shift(): lax.ppermute(value, 'tm', [(i, (i + steps) % count) for i in range(count)])  6.09 us
    ppermute x3, waiting for transfers between devices, swaps(): one = lax.ppermute(one, 'tm', [(i, i ^ 1) for i in range(count)])  5.59 us
    ppermute x3, waiting for transfers between devices, sum_all(): lax.ppermute(value, 'tm', [(i, i - i % run + (i + s) % run) for i in rang...  4.3 us
    pallas_call x3, Pallas kernels, local(): call(functools.partial(local_kernel, len(vecs)), (BLOCKS, shape(len(vecs)...  3.56 us
    pallas_call x1, Pallas kernels, band_pieces(): call(band_kernel, (shape(*BAND, dtype=BF16), shape(*BAND, dtype=BF16), sh...  2.85 us
  transfers between devices with their start and end apart: 10, of which 10 were waited for; matrix products, arithmetic and copies ran while one was open for 0% of the time, Pallas kernels for 9%

profile of v4, /device:TPU:4, one launch (start us, length us, event | category | flops | bytes accessed | tf_op | source)
XLA Modules:
  0.0 72.7 jit_solution(15303971612335546402)
XLA Ops:
  0.7 1.9 %shard_map.60 = f32[8,128]{1,0:T(8,128)S(1)} custom-call(s32[8,8]{1,0:T(8,128)} %pattern.1, f32[8,8,128,128]{3,2,1,0:T(8,128)} %weights.3), custom_call_target="tpu_custom_call" | custom-call | flops 4194304 | bytes 4194304 | tf_op jit(solution)/shard_map/pallas_call | solution.py:99
  2.6 1.7 %collective-permute-start = (f32[8,128]{1,0:T(8,128)S(1)}, f32[8,128]{1,0:T(8,128)S(1)}, u32[]{:S(2)}, u32[]{:S(2)}) collective-permute-start(f32[8,128]{1,0:T(8,128)S(1)} %shard_map.60), channel_id=1, source_target_pairs={{0,1},{1,2},{2,3},{3,4},{4,5},{5,6},{6,7},{7,8},{8,9},{9,10},{10,1... | collective-permute-start | bytes 12296 | tf_op jit(solution)/shard_map/ppermute | solution.py:397
  4.3 2.8 %shard_map.59 = (bf16[4,256,1152]{2,1,0:T(8,128)(2,1)S(1)}, bf16[4,256,1152]{2,1,0:T(8,128)(2,1)S(1)}, f32[8,128]{1,0:T(8,128)S(1)}) custom-call(s32[8,8]{1,0:T(8,128)} %pattern.1, f32[8,8,128,128]{3,2,1,0:T(8,128)} %weights.3, f32[8,128]{1,0:T(8,128)} %reg.1), custom_call_target="tpu_custom_call" | custom-call | flops 2147483648 | bytes 8388608 | tf_op jit(solution)/shard_map/pallas_call | solution.py:155
  7.1 6.1 %collective-permute-done.inflow = f32[8,128]{1,0:T(8,128)S(1)} collective-permute-done((f32[8,128]{1,0:T(8,128)S(1)}, f32[8,128]{1,0:T(8,128)S(1)}, u32[]{:S(2)}, u32[]{:S(2)}) %collective-permute-start) | collective-permute-done | bytes 4128 | tf_op jit(solution)/shard_map/ppermute | solution.py:397
  13.9 3.3 %collective-permute-start.2 = (f32[8,64,128]{2,1,0:T(8,128)S(1)}, f32[8,64,128]{2,1,0:T(8,128)S(1)}, u32[]{:S(2)}, u32[]{:S(2)}) collective-permute-start(f32[8,64,128]{2,1,0:T(8,128)S(1)} %get-tuple-element.35), channel_id=1, source_target_pairs={{0,63},{1,2},{2,1},{3,4},{4,3},{5,6},{6,5},{7,8},{8,7},{9,10},{10,... | collective-permute-start | bytes 786440 | tf_op jit(solution)/shard_map/ppermute | solution.py:425
  17.2 1.2 %shard_map.62 = (f32[8,64,128]{2,1,0:T(8,128)S(1)}, f32[1,2,64,128]{3,2,1,0:T(8,128)S(1)}, bf16[2560,256]{1,0:T(8,128)(2,1)S(1)}, bf16[2560,256]{1,0:T(8,128)(2,1)S(1)}) custom-call(f32[8,64,128]{2,1,0:T(8,128)S(1)} %get-tuple-element.36.refs_0_.v0, f32[8,64,128]{2,1,0:T(8,128)S(1)} %copy-done, ...), custom_call_target="tpu_custom_call" | custom-call | flops 503316480 | tf_op jit(solution)/shard_map/pallas_call | solution.py:292
  18.4 2.7 %collective-permute-done.1.got_one = f32[8,64,128]{2,1,0:T(8,128)S(1)} collective-permute-done((f32[8,64,128]{2,1,0:T(8,128)S(1)}, f32[8,64,128]{2,1,0:T(8,128)S(1)}, u32[]{:S(2)}, u32[]{:S(2)}) %collective-permute-start.1) | collective-permute-done | bytes 262176 | tf_op jit(solution)/shard_map/ppermute | solution.py:424
  21.1 4.3 %collective-permute-done.2.got_two = f32[8,64,128]{2,1,0:T(8,128)S(1)} collective-permute-done((f32[8,64,128]{2,1,0:T(8,128)S(1)}, f32[8,64,128]{2,1,0:T(8,128)S(1)}, u32[]{:S(2)}, u32[]{:S(2)}) %collective-permute-start.2) | collective-permute-done | bytes 262176 | tf_op jit(solution)/shard_map/ppermute | solution.py:425
  25.4 1.0 %shard_map.63 = (f32[8,64,128]{2,1,0:T(8,128)S(1)}, f32[8,64,128]{2,1,0:T(8,128)S(1)}, f32[8,64,128]{2,1,0:T(8,128)S(1)}, f32[8,64,128]{2,1,0:T(8,128)S(1)}) custom-call(f32[8,128]{1,0:T(8,128)S(1)} %broadcast_in_dim.4.flag, f32[8,64,128]{2,1,0:T(8,128)S(1)} %collective-permute-done.1.got_one, f32[8,64,128]{2,1,0:T(8,128)S(1)} %collective-permute-done.2.got_two, ...), custom_call_target="tpu_custom_call" | custom-call | flops 503316480 | tf_op jit(solution)/shard_map/pallas_call | solution.py:316
  26.5 3.6 %collective-permute-start.4 = (f32[8,64,128]{2,1,0:T(8,128)S(1)}, f32[8,64,128]{2,1,0:T(8,128)S(1)}, u32[]{:S(2)}, u32[]{:S(2)}) collective-permute-start(f32[8,64,128]{2,1,0:T(8,128)S(1)} %get-tuple-element.42), channel_id=1, source_target_pairs={{0,63},{1,2},{2,1},{3,4},{4,3},{5,6},{6,5},{7,8},{8,7},{9,10},{10,... | collective-permute-start | bytes 786440 | tf_op jit(solution)/shard_map/ppermute | solution.py:425
  30.1 1.2 %shard_map.64 = (f32[8,64,128]{2,1,0:T(8,128)S(1)}, f32[2,2,64,128]{3,2,1,0:T(8,128)S(1)}) custom-call(f32[8,64,128]{2,1,0:T(8,128)S(1)} %get-tuple-element.36.refs_0_.v0, f32[8,64,128]{2,1,0:T(8,128)S(1)} %get-tuple-element.43.refs_1_.v1, f32[8,64,128]{2,1,0:T(8,128)S(1)} %get-tuple-element.44.refs_2_.y1, ...), custom_call_target="tpu_custom_call" | custom-call | flops 503316480 | tf_op jit(solution)/shard_map/pallas_call | solution.py:292
  31.3 1.6 %collective-permute-done.3.got_one = f32[8,64,128]{2,1,0:T(8,128)S(1)} collective-permute-done((f32[8,64,128]{2,1,0:T(8,128)S(1)}, f32[8,64,128]{2,1,0:T(8,128)S(1)}, u32[]{:S(2)}, u32[]{:S(2)}) %collective-permute-start.3) | collective-permute-done | bytes 262176 | tf_op jit(solution)/shard_map/ppermute | solution.py:424
  32.9 4.3 %collective-permute-done.4.got_two = f32[8,64,128]{2,1,0:T(8,128)S(1)} collective-permute-done((f32[8,64,128]{2,1,0:T(8,128)S(1)}, f32[8,64,128]{2,1,0:T(8,128)S(1)}, u32[]{:S(2)}, u32[]{:S(2)}) %collective-permute-start.4) | collective-permute-done | bytes 262176 | tf_op jit(solution)/shard_map/ppermute | solution.py:425
  37.2 1.0 %shard_map.65 = (f32[8,64,128]{2,1,0:T(8,128)S(1)}, f32[8,64,128]{2,1,0:T(8,128)S(1)}, f32[8,64,128]{2,1,0:T(8,128)S(1)}, f32[8,64,128]{2,1,0:T(8,128)S(1)}) custom-call(f32[8,128]{1,0:T(8,128)S(1)} %broadcast_in_dim.4.flag, f32[8,64,128]{2,1,0:T(8,128)S(1)} %collective-permute-done.3.got_one, f32[8,64,128]{2,1,0:T(8,128)S(1)} %collective-permute-done.4.got_two, ...), custom_call_target="tpu_custom_call" | custom-call | flops 503316480 | tf_op jit(solution)/shard_map/pallas_call | solution.py:316
  38.3 3.8 %collective-permute-start.6 = (f32[8,64,128]{2,1,0:T(8,128)S(1)}, f32[8,64,128]{2,1,0:T(8,128)S(1)}, u32[]{:S(2)}, u32[]{:S(2)}) collective-permute-start(f32[8,64,128]{2,1,0:T(8,128)S(1)} %get-tuple-element.47), channel_id=1, source_target_pairs={{0,63},{1,2},{2,1},{3,4},{4,3},{5,6},{6,5},{7,8},{8,7},{9,10},{10,... | collective-permute-start | bytes 786440 | tf_op jit(solution)/shard_map/ppermute | solution.py:425
  42.1 1.2 %shard_map.66 = (f32[8,64,128]{2,1,0:T(8,128)S(1)}, f32[3,2,64,128]{3,2,1,0:T(8,128)S(1)}) custom-call(f32[8,64,128]{2,1,0:T(8,128)S(1)} %get-tuple-element.36.refs_0_.v0, f32[8,64,128]{2,1,0:T(8,128)S(1)} %get-tuple-element.43.refs_1_.v1, f32[8,64,128]{2,1,0:T(8,128)S(1)} %get-tuple-element.48.refs_2_.v2, f32[8,64,128]{2,1,0:T(8,128)S(1)} %get-tuple-element.49.refs_3_.y2, ...), custom_call_target="tpu_custom_call" | custom-call | flops 503316480 | tf_op jit(solution)/shard_map/pallas_call | solution.py:292
  43.3 1.3 %collective-permute-done.5.got_one = f32[8,64,128]{2,1,0:T(8,128)S(1)} collective-permute-done((f32[8,64,128]{2,1,0:T(8,128)S(1)}, f32[8,64,128]{2,1,0:T(8,128)S(1)}, u32[]{:S(2)}, u32[]{:S(2)}) %collective-permute-start.5) | collective-permute-done | bytes 262176 | tf_op jit(solution)/shard_map/ppermute | solution.py:424
  44.7 4.3 %collective-permute-done.6.got_two = f32[8,64,128]{2,1,0:T(8,128)S(1)} collective-permute-done((f32[8,64,128]{2,1,0:T(8,128)S(1)}, f32[8,64,128]{2,1,0:T(8,128)S(1)}, u32[]{:S(2)}, u32[]{:S(2)}) %collective-permute-start.6) | collective-permute-done | bytes 262176 | tf_op jit(solution)/shard_map/ppermute | solution.py:425
  50.0 1.9 %collective-permute-start.7 = (f32[16,128]{1,0:T(8,128)S(1)}, f32[16,128]{1,0:T(8,128)S(1)}, u32[]{:S(2)}, u32[]{:S(2)}) collective-permute-start(f32[16,128]{1,0:T(8,128)S(1)} %get-tuple-element.54), channel_id=1, source_target_pairs={{0,1},{1,2},{2,3},{3,0},{4,5},{5,6},{6,7},{7,4},{8,9},{9,10},{10,1... | collective-permute-start | bytes 24584 | tf_op jit(solution)/shard_map/ppermute | solution.py:411
  52.0 1.6 %collective-permute-done.9 = f32[16,128]{1,0:T(8,128)S(1)} collective-permute-done((f32[16,128]{1,0:T(8,128)S(1)}, f32[16,128]{1,0:T(8,128)S(1)}, u32[]{:S(2)}, u32[]{:S(2)}) %collective-permute-start.9) | collective-permute-done | bytes 8224 | tf_op jit(solution)/shard_map/ppermute | solution.py:411
  53.6 1.6 %collective-permute-done.8 = f32[16,128]{1,0:T(8,128)S(1)} collective-permute-done((f32[16,128]{1,0:T(8,128)S(1)}, f32[16,128]{1,0:T(8,128)S(1)}, u32[]{:S(2)}, u32[]{:S(2)}) %collective-permute-start.8) | collective-permute-done | bytes 8224 | tf_op jit(solution)/shard_map/ppermute | solution.py:411
  55.2 1.1 %collective-permute-done.7 = f32[16,128]{1,0:T(8,128)S(1)} collective-permute-done((f32[16,128]{1,0:T(8,128)S(1)}, f32[16,128]{1,0:T(8,128)S(1)}, u32[]{:S(2)}, u32[]{:S(2)}) %collective-permute-start.7) | collective-permute-done | bytes 8224 | tf_op jit(solution)/shard_map/ppermute | solution.py:411
  56.3 15.0 %all_to_all.5 = f32[16,16,128]{2,1,0:T(8,128)S(1)} all-to-all(f32[16,16,128]{2,1,0:T(8,128)S(1)} %broadcast_in_dim.10), channel_id=1, replica_groups={{0,4,8,12,16,20,24,28,32,36,40,44,48,52,56,60},{1,5,9,13,17,21,25,29,33..., dimensions={0} | all-to-all | bytes 262144 | tf_op jit(solution)/shard_map/all_to_all | solution.py:416
  71.4 1.3 %shard_map.68 = (f32[8,64,128]{2,1,0:T(8,128)}, f32[8,64,128]{2,1,0:T(8,128)}) custom-call(f32[16,128]{1,0:T(8,128)S(1)} %pad_maximum_fusion.1.sums_ref, f32[8,64,128]{2,1,0:T(8,128)S(1)} %get-tuple-element.36.refs_0_.v0, f32[8,64,128]{2,1,0:T(8,128)S(1)} %get-tuple-element.43.refs_1_.v1, f32[8,64,128]{2,1,0:T(8,128)S(1)} %get-tuple-element.48.refs_2_.v2, ...), custom_call_target="tpu_custom_call" | custom-call | tf_op jit(solution)/shard_map/pallas_call | solution.py:392
  (15 shorter events, 2.0 us)
Async XLA Ops:
  2.6 10.6 %copy-start = (f32[8,64,128]{2,1,0:T(8,128)S(1)}, f32[8,64,128]{2,1,0:T(8,128)}, u32[]{:S(2)}) copy-start(f32[8,64,128]{2,1,0:T(8,128)} %y0.1) | copy-start | bytes 786436
  2.6 10.6 %collective-permute-start = (f32[8,128]{1,0:T(8,128)S(1)}, f32[8,128]{1,0:T(8,128)S(1)}, u32[]{:S(2)}, u32[]{:S(2)}) collective-permute-start(f32[8,128]{1,0:T(8,128)S(1)} %shard_map.60), channel_id=1, source_target_pairs={{0,1},{1,2},{2,3},{3,4},{4,5},{5,6},{6,7},{7,8},{8,9},{9,10},{10,1... | collective-permute-start | bytes 12296 | tf_op jit(solution)/shard_map/ppermute | solution.py:397
  13.8 7.3 %collective-permute-start.1 = (f32[8,64,128]{2,1,0:T(8,128)S(1)}, f32[8,64,128]{2,1,0:T(8,128)S(1)}, u32[]{:S(2)}, u32[]{:S(2)}) collective-permute-start(f32[8,64,128]{2,1,0:T(8,128)S(1)} %get-tuple-element.34), channel_id=1, source_target_pairs={{0,1},{1,0},{2,3},{3,2},{4,5},{5,4},{6,7},{7,6},{8,9},{9,8},{10,11... | collective-permute-start | bytes 786440 | tf_op jit(solution)/shard_map/ppermute | solution.py:424
  13.9 11.5 %collective-permute-start.2 = (f32[8,64,128]{2,1,0:T(8,128)S(1)}, f32[8,64,128]{2,1,0:T(8,128)S(1)}, u32[]{:S(2)}, u32[]{:S(2)}) collective-permute-start(f32[8,64,128]{2,1,0:T(8,128)S(1)} %get-tuple-element.35), channel_id=1, source_target_pairs={{0,63},{1,2},{2,1},{3,4},{4,3},{5,6},{6,5},{7,8},{8,7},{9,10},{10,... | collective-permute-start | bytes 786440 | tf_op jit(solution)/shard_map/ppermute | solution.py:425
  26.4 6.5 %collective-permute-start.3 = (f32[8,64,128]{2,1,0:T(8,128)S(1)}, f32[8,64,128]{2,1,0:T(8,128)S(1)}, u32[]{:S(2)}, u32[]{:S(2)}) collective-permute-start(f32[8,64,128]{2,1,0:T(8,128)S(1)} %get-tuple-element.41), channel_id=1, source_target_pairs={{0,1},{1,0},{2,3},{3,2},{4,5},{5,4},{6,7},{7,6},{8,9},{9,8},{10,11... | collective-permute-start | bytes 786440 | tf_op jit(solution)/shard_map/ppermute | solution.py:424
  26.5 10.7 %collective-permute-start.4 = (f32[8,64,128]{2,1,0:T(8,128)S(1)}, f32[8,64,128]{2,1,0:T(8,128)S(1)}, u32[]{:S(2)}, u32[]{:S(2)}) collective-permute-start(f32[8,64,128]{2,1,0:T(8,128)S(1)} %get-tuple-element.42), channel_id=1, source_target_pairs={{0,63},{1,2},{2,1},{3,4},{4,3},{5,6},{6,5},{7,8},{8,7},{9,10},{10,... | collective-permute-start | bytes 786440 | tf_op jit(solution)/shard_map/ppermute | solution.py:425
  38.2 6.5 %collective-permute-start.5 = (f32[8,64,128]{2,1,0:T(8,128)S(1)}, f32[8,64,128]{2,1,0:T(8,128)S(1)}, u32[]{:S(2)}, u32[]{:S(2)}) collective-permute-start(f32[8,64,128]{2,1,0:T(8,128)S(1)} %get-tuple-element.46), channel_id=1, source_target_pairs={{0,1},{1,0},{2,3},{3,2},{4,5},{5,4},{6,7},{7,6},{8,9},{9,8},{10,11... | collective-permute-start | bytes 786440 | tf_op jit(solution)/shard_map/ppermute | solution.py:424
  38.3 10.7 %collective-permute-start.6 = (f32[8,64,128]{2,1,0:T(8,128)S(1)}, f32[8,64,128]{2,1,0:T(8,128)S(1)}, u32[]{:S(2)}, u32[]{:S(2)}) collective-permute-start(f32[8,64,128]{2,1,0:T(8,128)S(1)} %get-tuple-element.47), channel_id=1, source_target_pairs={{0,63},{1,2},{2,1},{3,4},{4,3},{5,6},{6,5},{7,8},{8,7},{9,10},{10,... | collective-permute-start | bytes 786440 | tf_op jit(solution)/shard_map/ppermute | solution.py:425
  49.8 3.7 %collective-permute-start.9 = (f32[16,128]{1,0:T(8,128)S(1)}, f32[16,128]{1,0:T(8,128)S(1)}, u32[]{:S(2)}, u32[]{:S(2)}) collective-permute-start(f32[16,128]{1,0:T(8,128)S(1)} %get-tuple-element.54), channel_id=1, source_target_pairs={{0,3},{1,0},{2,1},{3,2},{4,7},{5,4},{6,5},{7,6},{8,11},{9,8},{10,9... | collective-permute-start | bytes 24584 | tf_op jit(solution)/shard_map/ppermute | solution.py:411
  49.9 5.2 %collective-permute-start.8 = (f32[16,128]{1,0:T(8,128)S(1)}, f32[16,128]{1,0:T(8,128)S(1)}, u32[]{:S(2)}, u32[]{:S(2)}) collective-permute-start(f32[16,128]{1,0:T(8,128)S(1)} %get-tuple-element.54), channel_id=1, source_target_pairs={{0,2},{1,3},{2,0},{3,1},{4,6},{5,7},{6,4},{7,5},{8,10},{9,11},{10,... | collective-permute-start | bytes 24584 | tf_op jit(solution)/shard_map/ppermute | solution.py:411
  50.0 6.2 %collective-permute-start.7 = (f32[16,128]{1,0:T(8,128)S(1)}, f32[16,128]{1,0:T(8,128)S(1)}, u32[]{:S(2)}, u32[]{:S(2)}) collective-permute-start(f32[16,128]{1,0:T(8,128)S(1)} %get-tuple-element.54), channel_id=1, source_target_pairs={{0,1},{1,2},{2,3},{3,0},{4,5},{5,6},{6,7},{7,4},{8,9},{9,10},{10,1... | collective-permute-start | bytes 24584 | tf_op jit(solution)/shard_map/ppermute | solution.py:411

commit v5 on v4

--- a/solution.py
+++ b/solution.py
@@ -316,10 +316,12 @@
     return call(step_kernel, (BLOCKS,) * 4, [VMEM] * 9, [SENT, PIECES], flops=2 * ONE_WAY)(*args)
 
 
-def fold(found):
-    high, low = (jnp.concatenate([f[i] for f in found], axis=0).T for i in range(2))
-    value = (high[:N], low[:N])
-    size = N
+PAIRS = 5
+
+
+def fold(high, low):
+    value = (high, low)
+    size = high.shape[0]
     while size > 8:
         size //= 2
         value = dd_add(tuple(v[:size] for v in value), tuple(v[size:] for v in value))
@@ -334,15 +336,14 @@
     add_received(flag, got_one, got_two, partial, turned_high, turned_low, image, pieces)
     last = [moments(v, image) for v in (v0, v1, v2)]
     every = [(m[i, 0], m[i, 1]) for m in (m0, m1, m2) for i in range(m.shape[0])] + last + last[-1:]
-    out[...] = jnp.zeros_like(out)
-    for q in range(5):
-        h, l = fold(every[2 * q : 2 * q + 2])
-        out[q : q + 1, :] = h[0:1]
-        out[8 + q : 9 + q, :] = l[0:1]
+    for q in range(PAIRS):
+        pair = every[2 * q : 2 * q + 2]
+        h, l = fold(*(jnp.concatenate([f[i] for f in pair], axis=0).T for i in range(2)))
+        out[:, q * N : (q + 1) * N] = (h + l)[0:1]
 
 
 def gram(*args):
-    return call(gram_kernel, (BLOCKS, shape(16, 2 * R)), [VMEM] * 12, [PIECES], flops=ONE_WAY)(*args)
+    return call(gram_kernel, (BLOCKS, shape(1, PAIRS * N)), [VMEM] * 12, [PIECES], flops=ONE_WAY)(*args)
 
 
 def solve(matrix, right):
@@ -360,10 +361,11 @@
     return x0, x1, x2
 
 
-def result_kernel(sums_ref, v0, v1, v2, y0, y1, y2, y3, sol, res):
+def result_kernel(parts, v0, v1, v2, y0, y1, y2, y3, sol, res):
     flat = []
-    for q in range(5):
-        h, l = sums_ref[q : q + 1, :], sums_ref[8 + q : 9 + q, :]
+    for q in range(PAIRS):
+        part = parts[:, q * N : (q + 1) * N]
+        h, l = (v[0:1] for v in fold(part, jnp.zeros_like(part)))
         flat += [(h, l), (pltpu.roll(h, R, 1), pltpu.roll(l, R, 1))]
     g00, g01, g11, g02, g12, g22, g03, g13, g23 = flat[:9]
     full = ((g00, g01, g02, g03), (g01, g11, g12, g13), (g02, g12, g22, g23))
@@ -388,8 +390,8 @@
         res[t] = first - (d0 * (y0[t] - first) + d1 * (first - second) + d2 * (second - y3[t]))
 
 
-def result(total, vecs, images):
-    return call(result_kernel, (shape(T, R, N), shape(T, R, N)), [VMEM] * 8)(total, *vecs, *images)
+def result(parts, vecs, images):
+    return call(result_kernel, (shape(T, R, N), shape(T, R, N)), [VMEM] * 8)(parts, *vecs, *images)
 
 
 def shift(value, steps):
@@ -397,26 +399,10 @@
     return lax.ppermute(value, "tm", [(i, (i + steps) % count) for i in range(count)])
 
 
-def pair_add(values):
-    total = (values[0][:8], values[0][8:])
-    for value in values[1:]:
-        total = dd_add(total, (value[:8], value[8:]))
-    return jnp.concatenate(total, axis=0)
-
-
-def sum_all(value):
+def all_parts(value):
     count = lax.axis_size("tm")
-    run = 4
-    others = [
-        lax.ppermute(value, "tm", [(i, i - i % run + (i + s) % run) for i in range(count)]) for s in range(1, run)
-    ]
-    value = pair_add([value] + others)
-    groups = [[i for i in range(j, count, run)] for j in range(run)]
-    size = count // run
-    spread = lax.all_to_all(
-        jnp.broadcast_to(value[None], (size,) + value.shape), "tm", 0, 0, axis_index_groups=groups
-    )
-    return pair_add([spread[i] for i in range(size)])
+    spread = lax.all_to_all(jnp.broadcast_to(value[None], (count,) + value.shape), "tm", 0, 0)
+    return spread.reshape(count, value.shape[1])
 
 
 def swaps(one, two):
@@ -441,8 +427,8 @@
             image, vec, *leaving = next_step(flag, *got, partial, diag, high, low, *turned)
             images.append(image)
             vecs.append(vec)
-    image, total = gram(flag, *got, partial, *turned, *vecs, *found)
-    return result(sum_all(total), vecs, images + [image])
+    image, part = gram(flag, *got, partial, *turned, *vecs, *found)
+    return result(all_parts(part), vecs, images + [image])
 
 
 def solution(mesh):

time: 72.8 us -> 68.7 us (0.944)
  waiting for transfers between devices: 28.9 us -> 24.7 us
  blocking collectives: 15 us -> 17.3 us
  starting transfers between devices: 14.7 us -> 12.6 us
    ppermute x3 -> x0, waiting for transfers between devices: 4.3 us -> none  [sum_all(): lax.ppermute(value, 'tm', [(i, i - i % run + (i + s) % run) for i in rang...]
    all_to_all x1, blocking collectives: 15 us -> 17.3 us  [all_parts(): lax.all_to_all(jnp.broadcast_to(value[None], (count,) + value.shape), 'tm...]
    ppermute x3 -> x0, starting transfers between devices: 2.09 us -> none  [sum_all(): lax.ppermute(value, 'tm', [(i, i - i % run + (i + s) % run) for i in rang...]
  transfers between devices with their start and end apart: 10 -> 7, of which waited for: 10 -> 7; matrix products, arithmetic and copies ran while one was open for 0% -> 0% of each run, Pallas kernels for 9% -> 9%
where the time goes in v5:
time: 68.7 us; the launch traced here: 68.6 us
  waiting for transfers between devices  24.7 us (36%)
  blocking collectives  17.3 us (25%)
  Pallas kernels  13.1 us (19%)
  starting transfers between devices  12.6 us (18%)
  between operations  0.77 us (1%)
    all_to_all x1, blocking collectives, all_parts(): lax.all_to_all(jnp.broadcast_to(value[None], (count,) + value.shape), 'tm...  17.3 us
    ppermute x3, waiting for transfers between devices, swaps(): lax.ppermute(two, 'tm', [(i, (i + (1 if i % 2 else -1)) % count) for i in...  13 us
    ppermute x3, starting transfers between devices, swaps(): lax.ppermute(two, 'tm', [(i, (i + (1 if i % 2 else -1)) % count) for i in...  10.7 us
    ppermute x1, waiting for transfers between devices, shift(): lax.ppermute(value, 'tm', [(i, (i + steps) % count) for i in range(count)])  6.09 us
    ppermute x3, waiting for transfers between devices, swaps(): one = lax.ppermute(one, 'tm', [(i, i ^ 1) for i in range(count)])  5.6 us
    pallas_call x3, Pallas kernels, local(): call(functools.partial(local_kernel, len(vecs)), (BLOCKS, shape(len(vecs)...  3.55 us
    pallas_call x1, Pallas kernels, band_pieces(): call(band_kernel, (shape(*BAND, dtype=BF16), shape(*BAND, dtype=BF16), sh...  2.85 us
    pallas_call x2, Pallas kernels, next_step(): call(step_kernel, (BLOCKS,) * 4, [VMEM] * 9, [SENT, PIECES], flops=2 * ON...  2.01 us
  transfers between devices with their start and end apart: 7, of which 7 were waited for; matrix products, arithmetic and copies ran while one was open for 0% of the time, Pallas kernels for 9%

profile of v5, /device:TPU:4, one launch (start us, length us, event | category | flops | bytes accessed | tf_op | source)
XLA Modules:
  0.0 68.6 jit_solution(12197081947123605594)
XLA Ops:
  0.7 1.9 %shard_map.60 = f32[8,128]{1,0:T(8,128)S(1)} custom-call(s32[8,8]{1,0:T(8,128)} %pattern.1, f32[8,8,128,128]{3,2,1,0:T(8,128)} %weights.3), custom_call_target="tpu_custom_call" | custom-call | flops 4194304 | bytes 4194304 | tf_op jit(solution)/shard_map/pallas_call | solution.py:99
  2.6 1.7 %collective-permute-start = (f32[8,128]{1,0:T(8,128)S(1)}, f32[8,128]{1,0:T(8,128)S(1)}, u32[]{:S(2)}, u32[]{:S(2)}) collective-permute-start(f32[8,128]{1,0:T(8,128)S(1)} %shard_map.60), channel_id=1, source_target_pairs={{0,1},{1,2},{2,3},{3,4},{4,5},{5,6},{6,7},{7,8},{8,9},{9,10},{10,1... | collective-permute-start | bytes 12296 | tf_op jit(solution)/shard_map/ppermute | solution.py:399
  4.3 2.8 %shard_map.59 = (bf16[4,256,1152]{2,1,0:T(8,128)(2,1)S(1)}, bf16[4,256,1152]{2,1,0:T(8,128)(2,1)S(1)}, f32[8,128]{1,0:T(8,128)S(1)}) custom-call(s32[8,8]{1,0:T(8,128)} %pattern.1, f32[8,8,128,128]{3,2,1,0:T(8,128)} %weights.3, f32[8,128]{1,0:T(8,128)} %reg.1), custom_call_target="tpu_custom_call" | custom-call | flops 2147483648 | bytes 8388608 | tf_op jit(solution)/shard_map/pallas_call | solution.py:155
  7.1 6.1 %collective-permute-done.inflow = f32[8,128]{1,0:T(8,128)S(1)} collective-permute-done((f32[8,128]{1,0:T(8,128)S(1)}, f32[8,128]{1,0:T(8,128)S(1)}, u32[]{:S(2)}, u32[]{:S(2)}) %collective-permute-start) | collective-permute-done | bytes 4128 | tf_op jit(solution)/shard_map/ppermute | solution.py:399
  13.2 0.6 shard_map.61
  13.8 0.1 collective-permute-start.1
  13.9 3.3 %collective-permute-start.2 = (f32[8,64,128]{2,1,0:T(8,128)S(1)}, f32[8,64,128]{2,1,0:T(8,128)S(1)}, u32[]{:S(2)}, u32[]{:S(2)}) collective-permute-start(f32[8,64,128]{2,1,0:T(8,128)S(1)} %get-tuple-element.35), channel_id=1, source_target_pairs={{0,63},{1,2},{2,1},{3,4},{4,3},{5,6},{6,5},{7,8},{8,7},{9,10},{10,... | collective-permute-start | bytes 786440 | tf_op jit(solution)/shard_map/ppermute | solution.py:411
  17.2 1.1 %shard_map.62 = (f32[8,64,128]{2,1,0:T(8,128)S(1)}, f32[1,2,64,128]{3,2,1,0:T(8,128)S(1)}, bf16[2560,256]{1,0:T(8,128)(2,1)S(1)}, bf16[2560,256]{1,0:T(8,128)(2,1)S(1)}) custom-call(f32[8,64,128]{2,1,0:T(8,128)S(1)} %get-tuple-element.36.refs_0_.v0, f32[8,64,128]{2,1,0:T(8,128)S(1)} %copy-done, ...), custom_call_target="tpu_custom_call" | custom-call | flops 503316480 | tf_op jit(solution)/shard_map/pallas_call | solution.py:292
  18.4 2.7 %collective-permute-done.1.got_one = f32[8,64,128]{2,1,0:T(8,128)S(1)} collective-permute-done((f32[8,64,128]{2,1,0:T(8,128)S(1)}, f32[8,64,128]{2,1,0:T(8,128)S(1)}, u32[]{:S(2)}, u32[]{:S(2)}) %collective-permute-start.1) | collective-permute-done | bytes 262176 | tf_op jit(solution)/shard_map/ppermute | solution.py:410
  21.1 4.3 %collective-permute-done.2.got_two = f32[8,64,128]{2,1,0:T(8,128)S(1)} collective-permute-done((f32[8,64,128]{2,1,0:T(8,128)S(1)}, f32[8,64,128]{2,1,0:T(8,128)S(1)}, u32[]{:S(2)}, u32[]{:S(2)}) %collective-permute-start.2) | collective-permute-done | bytes 262176 | tf_op jit(solution)/shard_map/ppermute | solution.py:411
  25.4 1.0 %shard_map.63 = (f32[8,64,128]{2,1,0:T(8,128)S(1)}, f32[8,64,128]{2,1,0:T(8,128)S(1)}, f32[8,64,128]{2,1,0:T(8,128)S(1)}, f32[8,64,128]{2,1,0:T(8,128)S(1)}) custom-call(f32[8,128]{1,0:T(8,128)S(1)} %broadcast_in_dim.11.flag, f32[8,64,128]{2,1,0:T(8,128)S(1)} %collective-permute-done.1.got_one, f32[8,64,128]{2,1,0:T(8,128)S(1)} %collective-permute-done.2.got_two, ...), custom_call_target="tpu_custom_call" | custom-call | flops 503316480 | tf_op jit(solution)/shard_map/pallas_call | solution.py:316
  26.5 3.6 %collective-permute-start.4 = (f32[8,64,128]{2,1,0:T(8,128)S(1)}, f32[8,64,128]{2,1,0:T(8,128)S(1)}, u32[]{:S(2)}, u32[]{:S(2)}) collective-permute-start(f32[8,64,128]{2,1,0:T(8,128)S(1)} %get-tuple-element.42), channel_id=1, source_target_pairs={{0,63},{1,2},{2,1},{3,4},{4,3},{5,6},{6,5},{7,8},{8,7},{9,10},{10,... | collective-permute-start | bytes 786440 | tf_op jit(solution)/shard_map/ppermute | solution.py:411
  30.1 1.2 %shard_map.64 = (f32[8,64,128]{2,1,0:T(8,128)S(1)}, f32[2,2,64,128]{3,2,1,0:T(8,128)S(1)}) custom-call(f32[8,64,128]{2,1,0:T(8,128)S(1)} %get-tuple-element.36.refs_0_.v0, f32[8,64,128]{2,1,0:T(8,128)S(1)} %get-tuple-element.43.refs_1_.v1, f32[8,64,128]{2,1,0:T(8,128)S(1)} %get-tuple-element.44.refs_2_.y1, ...), custom_call_target="tpu_custom_call" | custom-call | flops 503316480 | tf_op jit(solution)/shard_map/pallas_call | solution.py:292
  31.3 1.6 %collective-permute-done.3.got_one = f32[8,64,128]{2,1,0:T(8,128)S(1)} collective-permute-done((f32[8,64,128]{2,1,0:T(8,128)S(1)}, f32[8,64,128]{2,1,0:T(8,128)S(1)}, u32[]{:S(2)}, u32[]{:S(2)}) %collective-permute-start.3) | collective-permute-done | bytes 262176 | tf_op jit(solution)/shard_map/ppermute | solution.py:410
  32.9 4.3 %collective-permute-done.4.got_two = f32[8,64,128]{2,1,0:T(8,128)S(1)} collective-permute-done((f32[8,64,128]{2,1,0:T(8,128)S(1)}, f32[8,64,128]{2,1,0:T(8,128)S(1)}, u32[]{:S(2)}, u32[]{:S(2)}) %collective-permute-start.4) | collective-permute-done | bytes 262176 | tf_op jit(solution)/shard_map/ppermute | solution.py:411
  37.2 1.0 %shard_map.65 = (f32[8,64,128]{2,1,0:T(8,128)S(1)}, f32[8,64,128]{2,1,0:T(8,128)S(1)}, f32[8,64,128]{2,1,0:T(8,128)S(1)}, f32[8,64,128]{2,1,0:T(8,128)S(1)}) custom-call(f32[8,128]{1,0:T(8,128)S(1)} %broadcast_in_dim.11.flag, f32[8,64,128]{2,1,0:T(8,128)S(1)} %collective-permute-done.3.got_one, f32[8,64,128]{2,1,0:T(8,128)S(1)} %collective-permute-done.4.got_two, ...), custom_call_target="tpu_custom_call" | custom-call | flops 503316480 | tf_op jit(solution)/shard_map/pallas_call | solution.py:316
  38.2 0.1 collective-permute-start.5
  38.3 3.8 %collective-permute-start.6 = (f32[8,64,128]{2,1,0:T(8,128)S(1)}, f32[8,64,128]{2,1,0:T(8,128)S(1)}, u32[]{:S(2)}, u32[]{:S(2)}) collective-permute-start(f32[8,64,128]{2,1,0:T(8,128)S(1)} %get-tuple-element.47), channel_id=1, source_target_pairs={{0,63},{1,2},{2,1},{3,4},{4,3},{5,6},{6,5},{7,8},{8,7},{9,10},{10,... | collective-permute-start | bytes 786440 | tf_op jit(solution)/shard_map/ppermute | solution.py:411
  42.1 1.2 %shard_map.66 = (f32[8,64,128]{2,1,0:T(8,128)S(1)}, f32[3,2,64,128]{3,2,1,0:T(8,128)S(1)}) custom-call(f32[8,64,128]{2,1,0:T(8,128)S(1)} %get-tuple-element.36.refs_0_.v0, f32[8,64,128]{2,1,0:T(8,128)S(1)} %get-tuple-element.43.refs_1_.v1, f32[8,64,128]{2,1,0:T(8,128)S(1)} %get-tuple-element.48.refs_2_.v2, f32[8,64,128]{2,1,0:T(8,128)S(1)} %get-tuple-element.49.refs_3_.y2, ...), custom_call_target="tpu_custom_call" | custom-call | flops 503316480 | tf_op jit(solution)/shard_map/pallas_call | solution.py:292
  43.3 1.3 %collective-permute-done.5.got_one = f32[8,64,128]{2,1,0:T(8,128)S(1)} collective-permute-done((f32[8,64,128]{2,1,0:T(8,128)S(1)}, f32[8,64,128]{2,1,0:T(8,128)S(1)}, u32[]{:S(2)}, u32[]{:S(2)}) %collective-permute-start.5) | collective-permute-done | bytes 262176 | tf_op jit(solution)/shard_map/ppermute | solution.py:410
  44.7 4.3 %collective-permute-done.6.got_two = f32[8,64,128]{2,1,0:T(8,128)S(1)} collective-permute-done((f32[8,64,128]{2,1,0:T(8,128)S(1)}, f32[8,64,128]{2,1,0:T(8,128)S(1)}, u32[]{:S(2)}, u32[]{:S(2)}) %collective-permute-start.6) | collective-permute-done | bytes 262176 | tf_op jit(solution)/shard_map/ppermute | solution.py:411
  49.0 0.9 %shard_map.67 = (f32[8,64,128]{2,1,0:T(8,128)S(1)}, f32[1,640]{1,0:T(1,128)S(1)}) custom-call(f32[8,128]{1,0:T(8,128)S(1)} %broadcast_in_dim.11.flag, f32[8,64,128]{2,1,0:T(8,128)S(1)} %collective-permute-done.5.got_one, f32[8,64,128]{2,1,0:T(8,128)S(1)} %collective-permute-done.6.got_two, f32[8,64,128]{2,1,0:T(8,128)S(1)} %get-tuple-element.50.partial, ...), custom_call_target="tpu_custom_call" | custom-call | flops 251658240 | tf_op jit(solution)/shard_map/pallas_call | solution.py:346
  50.0 17.3 %all_to_all.5 = f32[64,1,640]{2,1,0:T(1,128)S(1)} all-to-all(f32[64,1,640]{2,1,0:T(1,128)S(1)} %broadcast_in_dim.13), channel_id=1, replica_groups=mesh['scen'=4,'tm'=64] {'tm'}, dimensions={0} | all-to-all | bytes 327680 | tf_op jit(solution)/shard_map/all_to_all | solution.py:404
  67.3 1.3 %shard_map.68 = (f32[8,64,128]{2,1,0:T(8,128)}, f32[8,64,128]{2,1,0:T(8,128)}) custom-call(f32[64,640]{1,0:T(8,128)S(1)} %bitcast.3, f32[8,64,128]{2,1,0:T(8,128)S(1)} %get-tuple-element.36.refs_0_.v0, f32[8,64,128]{2,1,0:T(8,128)S(1)} %get-tuple-element.43.refs_1_.v1, f32[8,64,128]{2,1,0:T(8,128)S(1)} %get-tuple-element.48.refs_2_.v2, ...), custom_call_target="tpu_custom_call" | custom-call | tf_op jit(solution)/shard_map/pallas_call | solution.py:394
  (7 shorter events, 0.2 us)
Async XLA Ops:
  2.6 10.6 %copy-start = (f32[8,64,128]{2,1,0:T(8,128)S(1)}, f32[8,64,128]{2,1,0:T(8,128)}, u32[]{:S(2)}) copy-start(f32[8,64,128]{2,1,0:T(8,128)} %y0.1) | copy-start | bytes 786436
  2.6 10.6 %collective-permute-start = (f32[8,128]{1,0:T(8,128)S(1)}, f32[8,128]{1,0:T(8,128)S(1)}, u32[]{:S(2)}, u32[]{:S(2)}) collective-permute-start(f32[8,128]{1,0:T(8,128)S(1)} %shard_map.60), channel_id=1, source_target_pairs={{0,1},{1,2},{2,3},{3,4},{4,5},{5,6},{6,7},{7,8},{8,9},{9,10},{10,1... | collective-permute-start | bytes 12296 | tf_op jit(solution)/shard_map/ppermute | solution.py:399
  13.8 7.3 %collective-permute-start.1 = (f32[8,64,128]{2,1,0:T(8,128)S(1)}, f32[8,64,128]{2,1,0:T(8,128)S(1)}, u32[]{:S(2)}, u32[]{:S(2)}) collective-permute-start(f32[8,64,128]{2,1,0:T(8,128)S(1)} %get-tuple-element.34), channel_id=1, source_target_pairs={{0,1},{1,0},{2,3},{3,2},{4,5},{5,4},{6,7},{7,6},{8,9},{9,8},{10,11... | collective-permute-start | bytes 786440 | tf_op jit(solution)/shard_map/ppermute | solution.py:410
  13.9 11.5 %collective-permute-start.2 = (f32[8,64,128]{2,1,0:T(8,128)S(1)}, f32[8,64,128]{2,1,0:T(8,128)S(1)}, u32[]{:S(2)}, u32[]{:S(2)}) collective-permute-start(f32[8,64,128]{2,1,0:T(8,128)S(1)} %get-tuple-element.35), channel_id=1, source_target_pairs={{0,63},{1,2},{2,1},{3,4},{4,3},{5,6},{6,5},{7,8},{8,7},{9,10},{10,... | collective-permute-start | bytes 786440 | tf_op jit(solution)/shard_map/ppermute | solution.py:411
  26.4 6.5 %collective-permute-start.3 = (f32[8,64,128]{2,1,0:T(8,128)S(1)}, f32[8,64,128]{2,1,0:T(8,128)S(1)}, u32[]{:S(2)}, u32[]{:S(2)}) collective-permute-start(f32[8,64,128]{2,1,0:T(8,128)S(1)} %get-tuple-element.41), channel_id=1, source_target_pairs={{0,1},{1,0},{2,3},{3,2},{4,5},{5,4},{6,7},{7,6},{8,9},{9,8},{10,11... | collective-permute-start | bytes 786440 | tf_op jit(solution)/shard_map/ppermute | solution.py:410
  26.5 10.7 %collective-permute-start.4 = (f32[8,64,128]{2,1,0:T(8,128)S(1)}, f32[8,64,128]{2,1,0:T(8,128)S(1)}, u32[]{:S(2)}, u32[]{:S(2)}) collective-permute-start(f32[8,64,128]{2,1,0:T(8,128)S(1)} %get-tuple-element.42), channel_id=1, source_target_pairs={{0,63},{1,2},{2,1},{3,4},{4,3},{5,6},{6,5},{7,8},{8,7},{9,10},{10,... | collective-permute-start | bytes 786440 | tf_op jit(solution)/shard_map/ppermute | solution.py:411
  38.2 6.5 %collective-permute-start.5 = (f32[8,64,128]{2,1,0:T(8,128)S(1)}, f32[8,64,128]{2,1,0:T(8,128)S(1)}, u32[]{:S(2)}, u32[]{:S(2)}) collective-permute-start(f32[8,64,128]{2,1,0:T(8,128)S(1)} %get-tuple-element.46), channel_id=1, source_target_pairs={{0,1},{1,0},{2,3},{3,2},{4,5},{5,4},{6,7},{7,6},{8,9},{9,8},{10,11... | collective-permute-start | bytes 786440 | tf_op jit(solution)/shard_map/ppermute | solution.py:410
  38.3 10.7 %collective-permute-start.6 = (f32[8,64,128]{2,1,0:T(8,128)S(1)}, f32[8,64,128]{2,1,0:T(8,128)S(1)}, u32[]{:S(2)}, u32[]{:S(2)}) collective-permute-start(f32[8,64,128]{2,1,0:T(8,128)S(1)} %get-tuple-element.47), channel_id=1, source_target_pairs={{0,63},{1,2},{2,1},{3,4},{4,3},{5,6},{6,5},{7,8},{8,7},{9,10},{10,... | collective-permute-start | bytes 786440 | tf_op jit(solution)/shard_map/ppermute | solution.py:411

commit v6 on v5

--- a/solution.py
+++ b/solution.py
@@ -243,25 +243,23 @@
     return jnp.where(jnp.broadcast_to(flag[0:1, :], (R, N)) > 0, first, second)
 
 
-def hand_out(flag, vec, high, low, one, two, sent, pieces):
+def hand_out(flag, vec, high, low, two, sent, pieces):
     for t in range(T):
         put_pieces(pieces, t, vec[t])
     to_next(pieces, high, low, sent)
     for t in range(T):
-        one[t] = choose(flag, sent[t], vec[t])
         two[t] = choose(flag, vec[t], sent[t])
 
 
 BLOCKS = shape(T, R, N)
-SENT = pltpu.VMEM((T, R, N), F32)
 TURNED = shape((T // 2) * (T // 2 + 1) * N, 2 * N, dtype=BF16)
 
 
-def first_kernel(flag, rhs, own, inflow, high, low, diag, vec, one, two, sent, pieces):
+def first_kernel(flag, rhs, own, inflow, high, low, diag, vec, two, sent, pieces):
     diag[...] = own[...] + inflow[...]
     for t in range(T):
         vec[t] = rhs[t] / diag[t : t + 1, :]
-    hand_out(flag, vec, high, low, one, two, sent, pieces)
+    hand_out(flag, vec, high, low, two, sent, pieces)
 
 
 def first(flag, rhs, own, inflow, high, low):
@@ -269,13 +267,15 @@
         first_kernel,
         (shape(T, N), BLOCKS, BLOCKS, BLOCKS),
         [VMEM] * 6,
-        [SENT, PIECES],
+        [PIECES],
         flops=ONE_WAY,
     )(flag, rhs, own, inflow, high, low)
 
 
 def local_kernel(count, *refs):
-    vecs, (image, high, low, out, found, *turned, pieces) = refs[:count], refs[count:]
+    vecs, (image, high, low, flag, sent, out, found, one, *turned, pieces) = refs[:count], refs[count:]
+    for t in range(T):
+        one[t] = choose(flag, sent[t], vecs[-1][t])
     if turned:
         turn(high, low, *turned)
     for t in range(T):
@@ -287,15 +287,15 @@
         found[i, 1] = l
 
 
-def local(vecs, image, high, low):
+def local(vecs, *args):
     turned = (TURNED, TURNED) if len(vecs) == 1 else ()
     return call(
         functools.partial(local_kernel, len(vecs)),
-        (BLOCKS, shape(len(vecs), 2, R, N)) + turned,
-        [VMEM] * (len(vecs) + 3),
+        (BLOCKS, shape(len(vecs), 2, R, N), BLOCKS) + turned,
+        [VMEM] * (len(vecs) + 5),
         [PIECES],
         flops=2 * ONE_WAY,
-    )(*vecs, image, high, low)
+    )(*vecs, *args)
 
 
 def add_received(flag, got_one, got_two, partial, turned_high, turned_low, image, pieces):
@@ -305,15 +305,15 @@
     from_next(pieces, turned_high, turned_low, image)
 
 
-def step_kernel(flag, got_one, got_two, partial, diag, high, low, turned_high, turned_low, image, vec, one, two, sent, pieces):
+def step_kernel(flag, got_one, got_two, partial, diag, high, low, turned_high, turned_low, image, vec, two, sent, pieces):
     add_received(flag, got_one, got_two, partial, turned_high, turned_low, image, pieces)
     for t in range(T):
         vec[t] = image[t] / diag[t : t + 1, :]
-    hand_out(flag, vec, high, low, one, two, sent, pieces)
+    hand_out(flag, vec, high, low, two, sent, pieces)
 
 
 def next_step(*args):
-    return call(step_kernel, (BLOCKS,) * 4, [VMEM] * 9, [SENT, PIECES], flops=2 * ONE_WAY)(*args)
+    return call(step_kernel, (BLOCKS,) * 4, [VMEM] * 9, [PIECES], flops=2 * ONE_WAY)(*args)
 
 
 PAIRS = 5
@@ -405,10 +405,13 @@
     return spread.reshape(count, value.shape[1])
 
 
-def swaps(one, two):
+def swap_within(value):
+    return lax.ppermute(value, "tm", [(i, i ^ 1) for i in range(lax.axis_size("tm"))])
+
+
+def swap_across(value):
     count = lax.axis_size("tm")
-    one = lax.ppermute(one, "tm", [(i, i ^ 1) for i in range(count)])
-    return one, lax.ppermute(two, "tm", [(i, (i + (1 if i % 2 else -1)) % count) for i in range(count)])
+    return lax.ppermute(value, "tm", [(i, (i + (1 if i % 2 else -1)) % count) for i in range(count)])
 
 
 def shards(weights, pattern, shift_reg, rhs):
@@ -416,15 +419,16 @@
     flag, pattern = lax.optimization_barrier((flag, pattern))
     inflow = shift(ahead_sums(pattern, weights), 1)
     high, low, own = band_pieces(pattern, weights, shift_reg)
-    diag, vec, *leaving = first(flag, rhs, own, inflow, high, low)
+    diag, vec, two, sent = first(flag, rhs, own, inflow, high, low)
     vecs, images, found = [vec], [rhs], []
     for step in range(3):
-        got = swaps(*leaving)
-        partial, part, *extra = local(vecs, images[-1], high, low)
+        got_two = swap_across(two)
+        partial, part, one, *extra = local(vecs, images[-1], high, low, flag, sent)
+        got = swap_within(one), got_two
         found.append(part)
         turned = extra or turned
         if step < 2:
-            image, vec, *leaving = next_step(flag, *got, partial, diag, high, low, *turned)
+            image, vec, two, sent = next_step(flag, *got, partial, diag, high, low, *turned)
             images.append(image)
             vecs.append(vec)
     image, part = gram(flag, *got, partial, *turned, *vecs, *found)

time: 68.7 us -> 70.4 us (1.025)
  waiting for transfers between devices: 24.7 us -> 27.9 us
  starting transfers between devices: 12.6 us -> 10.5 us
    ppermute x6, waiting for transfers between devices: 18.6 us -> 21.8 us  [the longest x3 18.8 us: swap_across(): lax.ppermute(value, 'tm', [(i, (i + (1 if i % 2 else -1)) % count) for i...]
    ppermute x6, starting transfers between devices: 11 us -> 8.8 us  [the longest x3 8.52 us: swap_across(): lax.ppermute(value, 'tm', [(i, (i + (1 if i % 2 else -1)) % count) for i...]
  transfers between devices with their start and end apart: 7 -> 7, of which waited for: 7 -> 5; matrix products, arithmetic and copies ran while one was open for 0% -> 0% of each run, Pallas kernels for 9% -> 7%
where the time goes in v6:
time: 70.4 us; the launch traced here: 70.2 us
  waiting for transfers between devices  27.9 us (40%)
  blocking collectives  17.9 us (25%)
  Pallas kernels  13.1 us (19%)
  starting transfers between devices  10.5 us (15%)
  between operations  0.77 us (1%)
    ppermute x3, waiting for transfers between devices, swap_across(): lax.ppermute(value, 'tm', [(i, (i + (1 if i % 2 else -1)) % count) for i...  18.8 us
    all_to_all x1, blocking collectives, all_parts(): lax.all_to_all(jnp.broadcast_to(value[None], (count,) + value.shape), 'tm...  17.9 us
    ppermute x3, starting transfers between devices, swap_across(): lax.ppermute(value, 'tm', [(i, (i + (1 if i % 2 else -1)) % count) for i...  8.52 us
    ppermute x1, waiting for transfers between devices, shift(): lax.ppermute(value, 'tm', [(i, (i + steps) % count) for i in range(count)])  6.09 us
    pallas_call x3, Pallas kernels, local(): call(functools.partial(local_kernel, len(vecs)), (BLOCKS, shape(len(vecs)...  3.55 us
    ppermute x3, waiting for transfers between devices, swap_within(): lax.ppermute(value, 'tm', [(i, i ^ 1) for i in range(lax.axis_size('tm'))])  3.03 us
    pallas_call x1, Pallas kernels, band_pieces(): call(band_kernel, (shape(*BAND, dtype=BF16), shape(*BAND, dtype=BF16), sh...  2.85 us
    pallas_call x2, Pallas kernels, next_step(): call(step_kernel, (BLOCKS,) * 4, [VMEM] * 9, [PIECES], flops=2 * ONE_WAY)  2.01 us
  transfers between devices with their start and end apart: 7, of which 5 were waited for; matrix products, arithmetic and copies ran while one was open for 0% of the time, Pallas kernels for 7%

profile of v6, /device:TPU:4, one launch (start us, length us, event | category | flops | bytes accessed | tf_op | source)
XLA Modules:
  0.0 70.2 jit_solution(12674194234746061401)
XLA Ops:
  0.7 1.9 %shard_map.60 = f32[8,128]{1,0:T(8,128)S(1)} custom-call(s32[8,8]{1,0:T(8,128)} %pattern.1, f32[8,8,128,128]{3,2,1,0:T(8,128)} %weights.3), custom_call_target="tpu_custom_call" | custom-call | flops 4194304 | bytes 4194304 | tf_op jit(solution)/shard_map/pallas_call | solution.py:99
  2.6 1.7 %collective-permute-start = (f32[8,128]{1,0:T(8,128)S(1)}, f32[8,128]{1,0:T(8,128)S(1)}, u32[]{:S(2)}, u32[]{:S(2)}) collective-permute-start(f32[8,128]{1,0:T(8,128)S(1)} %shard_map.60), channel_id=1, source_target_pairs={{0,1},{1,2},{2,3},{3,4},{4,5},{5,6},{6,7},{7,8},{8,9},{9,10},{10,1... | collective-permute-start | bytes 12296 | tf_op jit(solution)/shard_map/ppermute | solution.py:399
  4.3 2.8 %shard_map.59 = (bf16[4,256,1152]{2,1,0:T(8,128)(2,1)S(1)}, bf16[4,256,1152]{2,1,0:T(8,128)(2,1)S(1)}, f32[8,128]{1,0:T(8,128)S(1)}) custom-call(s32[8,8]{1,0:T(8,128)} %pattern.1, f32[8,8,128,128]{3,2,1,0:T(8,128)} %weights.3, f32[8,128]{1,0:T(8,128)} %reg.1), custom_call_target="tpu_custom_call" | custom-call | flops 2147483648 | bytes 8388608 | tf_op jit(solution)/shard_map/pallas_call | solution.py:155
  7.1 6.1 %collective-permute-done.inflow = f32[8,128]{1,0:T(8,128)S(1)} collective-permute-done((f32[8,128]{1,0:T(8,128)S(1)}, f32[8,128]{1,0:T(8,128)S(1)}, u32[]{:S(2)}, u32[]{:S(2)}) %collective-permute-start) | collective-permute-done | bytes 4128 | tf_op jit(solution)/shard_map/ppermute | solution.py:399
  13.2 0.6 shard_map.61
  13.8 2.1 %collective-permute-start.2 = (f32[8,64,128]{2,1,0:T(8,128)S(1)}, f32[8,64,128]{2,1,0:T(8,128)S(1)}, u32[]{:S(2)}, u32[]{:S(2)}) collective-permute-start(f32[8,64,128]{2,1,0:T(8,128)S(1)} %get-tuple-element.40), channel_id=1, source_target_pairs={{0,63},{1,2},{2,1},{3,4},{4,3},{5,6},{6,5},{7,8},{8,7},{9,10},{10,... | collective-permute-start | bytes 786440 | tf_op jit(solution)/shard_map/ppermute | solution.py:414
  15.9 1.1 %shard_map.62 = (f32[8,64,128]{2,1,0:T(8,128)S(1)}, f32[1,2,64,128]{3,2,1,0:T(8,128)S(1)}, f32[8,64,128]{2,1,0:T(8,128)S(1)}, bf16[2560,256]{1,0:T(8,128)(2,1)S(1)}, bf16[2560,256]{1,0:T(8,128)(2,1)S(1)}) custom-call(f32[8,64,128]{2,1,0:T(8,128)S(1)} %get-tuple-element.37.refs_0_.v0, f32[8,64,128]{2,1,0:T(8,128)S(1)} %copy-done, ...), custom_call_target="tpu_custom_call" | custom-call | flops 503316480 | tf_op jit(solution)/shard_map/pallas_call | solution.py:292
  17.1 0.1 collective-permute-start.1
  17.2 8.1 %collective-permute-done.2.got_two = f32[8,64,128]{2,1,0:T(8,128)S(1)} collective-permute-done((f32[8,64,128]{2,1,0:T(8,128)S(1)}, f32[8,64,128]{2,1,0:T(8,128)S(1)}, u32[]{:S(2)}, u32[]{:S(2)}) %collective-permute-start.2) | collective-permute-done | bytes 262176 | tf_op jit(solution)/shard_map/ppermute | solution.py:414
  25.3 1.0 %shard_map.63 = (f32[8,64,128]{2,1,0:T(8,128)S(1)}, f32[8,64,128]{2,1,0:T(8,128)S(1)}, f32[8,64,128]{2,1,0:T(8,128)S(1)}, f32[8,64,128]{2,1,0:T(8,128)S(1)}) custom-call(f32[8,128]{1,0:T(8,128)S(1)} %broadcast_in_dim.11.flag.refs_4_.refs_5_.refs_6_, f32[8,64,128]{2,1,0:T(8,128)S(1)} %collective-permute-done.1.got_one, ...), custom_call_target="tpu_custom_call" | custom-call | flops 503316480 | tf_op jit(solution)/shard_map/pallas_call | solution.py:316
  26.3 3.1 %collective-permute-start.4 = (f32[8,64,128]{2,1,0:T(8,128)S(1)}, f32[8,64,128]{2,1,0:T(8,128)S(1)}, u32[]{:S(2)}, u32[]{:S(2)}) collective-permute-start(f32[8,64,128]{2,1,0:T(8,128)S(1)} %get-tuple-element.49), channel_id=1, source_target_pairs={{0,63},{1,2},{2,1},{3,4},{4,3},{5,6},{6,5},{7,8},{8,7},{9,10},{10,... | collective-permute-start | bytes 786440 | tf_op jit(solution)/shard_map/ppermute | solution.py:414
  29.4 1.2 %shard_map.64 = (f32[8,64,128]{2,1,0:T(8,128)S(1)}, f32[2,2,64,128]{3,2,1,0:T(8,128)S(1)}, f32[8,64,128]{2,1,0:T(8,128)S(1)}) custom-call(f32[8,64,128]{2,1,0:T(8,128)S(1)} %get-tuple-element.37.refs_0_.v0, f32[8,64,128]{2,1,0:T(8,128)S(1)} %get-tuple-element.45.refs_1_.v1, f32[8,64,128]{2,1,0:T(8,128)S(1)} %get-tuple-element.46.refs_2_.y1, ...), custom_call_target="tpu_custom_call" | custom-call | flops 503316480 | tf_op jit(solution)/shard_map/pallas_call | solution.py:292
  30.6 0.1 collective-permute-start.3
  30.7 6.3 %collective-permute-done.4.got_two = f32[8,64,128]{2,1,0:T(8,128)S(1)} collective-permute-done((f32[8,64,128]{2,1,0:T(8,128)S(1)}, f32[8,64,128]{2,1,0:T(8,128)S(1)}, u32[]{:S(2)}, u32[]{:S(2)}) %collective-permute-start.4) | collective-permute-done | bytes 262176 | tf_op jit(solution)/shard_map/ppermute | solution.py:414
  37.0 1.0 %shard_map.65 = (f32[8,64,128]{2,1,0:T(8,128)S(1)}, f32[8,64,128]{2,1,0:T(8,128)S(1)}, f32[8,64,128]{2,1,0:T(8,128)S(1)}, f32[8,64,128]{2,1,0:T(8,128)S(1)}) custom-call(f32[8,128]{1,0:T(8,128)S(1)} %broadcast_in_dim.11.flag.refs_4_.refs_5_.refs_6_, f32[8,64,128]{2,1,0:T(8,128)S(1)} %collective-permute-done.3.got_one, ...), custom_call_target="tpu_custom_call" | custom-call | flops 503316480 | tf_op jit(solution)/shard_map/pallas_call | solution.py:316
  38.0 1.2 %shard_map.66 = (f32[8,64,128]{2,1,0:T(8,128)S(1)}, f32[3,2,64,128]{3,2,1,0:T(8,128)S(1)}, f32[8,64,128]{2,1,0:T(8,128)S(1)}) custom-call(f32[8,64,128]{2,1,0:T(8,128)S(1)} %get-tuple-element.37.refs_0_.v0, f32[8,64,128]{2,1,0:T(8,128)S(1)} %get-tuple-element.45.refs_1_.v1, f32[8,64,128]{2,1,0:T(8,128)S(1)} %get-tuple-element.51.refs_2_.v2, ...), custom_call_target="tpu_custom_call" | custom-call | flops 503316480 | tf_op jit(solution)/shard_map/pallas_call | solution.py:292
  39.3 0.1 collective-permute-start.5
  39.4 3.4 %collective-permute-start.6 = (f32[8,64,128]{2,1,0:T(8,128)S(1)}, f32[8,64,128]{2,1,0:T(8,128)S(1)}, u32[]{:S(2)}, u32[]{:S(2)}) collective-permute-start(f32[8,64,128]{2,1,0:T(8,128)S(1)} %get-tuple-element.55), channel_id=1, source_target_pairs={{0,63},{1,2},{2,1},{3,4},{4,3},{5,6},{6,5},{7,8},{8,7},{9,10},{10,... | collective-permute-start | bytes 786440 | tf_op jit(solution)/shard_map/ppermute | solution.py:414
  42.7 3.0 %collective-permute-done.5.got_one = f32[8,64,128]{2,1,0:T(8,128)S(1)} collective-permute-done((f32[8,64,128]{2,1,0:T(8,128)S(1)}, f32[8,64,128]{2,1,0:T(8,128)S(1)}, u32[]{:S(2)}, u32[]{:S(2)}) %collective-permute-start.5) | collective-permute-done | bytes 262176 | tf_op jit(solution)/shard_map/ppermute | solution.py:409
  45.7 4.3 %collective-permute-done.6.got_two = f32[8,64,128]{2,1,0:T(8,128)S(1)} collective-permute-done((f32[8,64,128]{2,1,0:T(8,128)S(1)}, f32[8,64,128]{2,1,0:T(8,128)S(1)}, u32[]{:S(2)}, u32[]{:S(2)}) %collective-permute-start.6) | collective-permute-done | bytes 262176 | tf_op jit(solution)/shard_map/ppermute | solution.py:414
  50.1 0.9 %shard_map.67 = (f32[8,64,128]{2,1,0:T(8,128)S(1)}, f32[1,640]{1,0:T(1,128)S(1)}) custom-call(f32[8,128]{1,0:T(8,128)S(1)} %broadcast_in_dim.11.flag.refs_4_.refs_5_.refs_6_, f32[8,64,128]{2,1,0:T(8,128)S(1)} %collective-permute-done.5.got_one, f32[8,64,128]{2,1,0:T(8,128)S(1)} %collective-permute-done.6.got_two, ...), custom_call_target="tpu_custom_call" | custom-call | flops 251658240 | tf_op jit(solution)/shard_map/pallas_call | solution.py:346
  51.0 0.1 broadcast_in_dim.13
  51.1 17.9 %all_to_all.5 = f32[64,1,640]{2,1,0:T(1,128)S(1)} all-to-all(f32[64,1,640]{2,1,0:T(1,128)S(1)} %broadcast_in_dim.13), channel_id=1, replica_groups=mesh['scen'=4,'tm'=64] {'tm'}, dimensions={0} | all-to-all | bytes 327680 | tf_op jit(solution)/shard_map/all_to_all | solution.py:404
  68.9 1.3 %shard_map.68 = (f32[8,64,128]{2,1,0:T(8,128)}, f32[8,64,128]{2,1,0:T(8,128)}) custom-call(f32[64,640]{1,0:T(8,128)S(1)} %bitcast.3, f32[8,64,128]{2,1,0:T(8,128)S(1)} %get-tuple-element.37.refs_0_.v0, f32[8,64,128]{2,1,0:T(8,128)S(1)} %get-tuple-element.45.refs_1_.v1, f32[8,64,128]{2,1,0:T(8,128)S(1)} %get-tuple-element.51.refs_2_.v2, ...), custom_call_target="tpu_custom_call" | custom-call | tf_op jit(solution)/shard_map/pallas_call | solution.py:394
  (7 shorter events, 0.1 us)
Async XLA Ops:
  2.6 10.6 %copy-start = (f32[8,64,128]{2,1,0:T(8,128)S(1)}, f32[8,64,128]{2,1,0:T(8,128)}, u32[]{:S(2)}) copy-start(f32[8,64,128]{2,1,0:T(8,128)} %y0.1) | copy-start | bytes 786436
  2.6 10.6 %collective-permute-start = (f32[8,128]{1,0:T(8,128)S(1)}, f32[8,128]{1,0:T(8,128)S(1)}, u32[]{:S(2)}, u32[]{:S(2)}) collective-permute-start(f32[8,128]{1,0:T(8,128)S(1)} %shard_map.60), channel_id=1, source_target_pairs={{0,1},{1,2},{2,3},{3,4},{4,5},{5,6},{6,7},{7,8},{8,9},{9,10},{10,1... | collective-permute-start | bytes 12296 | tf_op jit(solution)/shard_map/ppermute | solution.py:399
  13.8 11.5 %collective-permute-start.2 = (f32[8,64,128]{2,1,0:T(8,128)S(1)}, f32[8,64,128]{2,1,0:T(8,128)S(1)}, u32[]{:S(2)}, u32[]{:S(2)}) collective-permute-start(f32[8,64,128]{2,1,0:T(8,128)S(1)} %get-tuple-element.40), channel_id=1, source_target_pairs={{0,63},{1,2},{2,1},{3,4},{4,3},{5,6},{6,5},{7,8},{8,7},{9,10},{10,... | collective-permute-start | bytes 786440 | tf_op jit(solution)/shard_map/ppermute | solution.py:414
  17.1 8.2 %collective-permute-start.1 = (f32[8,64,128]{2,1,0:T(8,128)S(1)}, f32[8,64,128]{2,1,0:T(8,128)S(1)}, u32[]{:S(2)}, u32[]{:S(2)}) collective-permute-start(f32[8,64,128]{2,1,0:T(8,128)S(1)} %get-tuple-element.39), channel_id=1, source_target_pairs={{0,1},{1,0},{2,3},{3,2},{4,5},{5,4},{6,7},{7,6},{8,9},{9,8},{10,11... | collective-permute-start | bytes 786440 | tf_op jit(solution)/shard_map/ppermute | solution.py:409
  26.3 10.7 %collective-permute-start.4 = (f32[8,64,128]{2,1,0:T(8,128)S(1)}, f32[8,64,128]{2,1,0:T(8,128)S(1)}, u32[]{:S(2)}, u32[]{:S(2)}) collective-permute-start(f32[8,64,128]{2,1,0:T(8,128)S(1)} %get-tuple-element.49), channel_id=1, source_target_pairs={{0,63},{1,2},{2,1},{3,4},{4,3},{5,6},{6,5},{7,8},{8,7},{9,10},{10,... | collective-permute-start | bytes 786440 | tf_op jit(solution)/shard_map/ppermute | solution.py:414
  30.6 6.5 %collective-permute-start.3 = (f32[8,64,128]{2,1,0:T(8,128)S(1)}, f32[8,64,128]{2,1,0:T(8,128)S(1)}, u32[]{:S(2)}, u32[]{:S(2)}) collective-permute-start(f32[8,64,128]{2,1,0:T(8,128)S(1)} %get-tuple-element.48), channel_id=1, source_target_pairs={{0,1},{1,0},{2,3},{3,2},{4,5},{5,4},{6,7},{7,6},{8,9},{9,8},{10,11... | collective-permute-start | bytes 786440 | tf_op jit(solution)/shard_map/ppermute | solution.py:409
  39.3 6.5 %collective-permute-start.5 = (f32[8,64,128]{2,1,0:T(8,128)S(1)}, f32[8,64,128]{2,1,0:T(8,128)S(1)}, u32[]{:S(2)}, u32[]{:S(2)}) collective-permute-start(f32[8,64,128]{2,1,0:T(8,128)S(1)} %get-tuple-element.54), channel_id=1, source_target_pairs={{0,1},{1,0},{2,3},{3,2},{4,5},{5,4},{6,7},{7,6},{8,9},{9,8},{10,11... | collective-permute-start | bytes 786440 | tf_op jit(solution)/shard_map/ppermute | solution.py:409
  39.4 10.7 %collective-permute-start.6 = (f32[8,64,128]{2,1,0:T(8,128)S(1)}, f32[8,64,128]{2,1,0:T(8,128)S(1)}, u32[]{:S(2)}, u32[]{:S(2)}) collective-permute-start(f32[8,64,128]{2,1,0:T(8,128)S(1)} %get-tuple-element.55), channel_id=1, source_target_pairs={{0,63},{1,2},{2,1},{3,4},{4,3},{5,6},{6,5},{7,8},{8,7},{9,10},{10,... | collective-permute-start | bytes 786440 | tf_op jit(solution)/shard_map/ppermute | solution.py:414

commit v7 on v5

--- a/solution.py
+++ b/solution.py
@@ -71,39 +71,44 @@
     return p, ((ah * bh - p) + ah * bl + al * bh) + al * bl
 
 
-def ahead_kernel(pattern, weights, ahead, mask, buf, cols, sems):
-    head = pltpu.make_async_copy(pattern, mask, sems.at[T])
-    head.start()
-    copies = []
-    for t in range(T):
-        some = slice(T - 1 - t, T)
-        copies.append(pltpu.make_async_copy(weights.at[t, some], buf.at[t, some], sems.at[t]))
-    for copy in copies:
-        copy.start()
-    cols[...] = jnp.zeros_like(cols)
-    head.wait()
-    for t in range(T):
-        copies[t].wait()
-
-        def step(k, carry):
-            m = buf[t, k] * mask[t, k].astype(F32)
-            cols[t + k + 1 - T] += jnp.sum(m.reshape(N // 8, 8, N), axis=0)
-            return carry
-
-        lax.fori_loop(T - 1 - t, T, step, 0)
-    ahead[...] = jnp.sum(cols[...], axis=1)
-
-
-def ahead_sums(pattern, weights):
+def on_parity(parity):
+    return pl.when(lax.axis_index("tm") % 2 == parity)
+
+
+def ahead_kernel(parity, pattern, weights, ahead, mask, buf, cols, sems):
+    @on_parity(parity)
+    def _():
+        head = pltpu.make_async_copy(pattern, mask, sems.at[T])
+        head.start()
+        copies = []
+        for t in range(T):
+            some = slice(T - 1 - t, T)
+            copies.append(pltpu.make_async_copy(weights.at[t, some], buf.at[t, some], sems.at[t]))
+        for copy in copies:
+            copy.start()
+        for t in range(T):
+            copies[t].wait()
+            for k in range(T - 1 - t, T):
+                cols[t, k] = jnp.sum(buf[t, k].reshape(N // 8, 8, N), axis=0)
+        head.wait()
+        for b in range(T):
+            total = jnp.zeros((8, N), F32)
+            for t in range(b, T):
+                k = T - 1 - t + b
+                total = total + cols[t, k] * mask[t, k].astype(F32)
+            ahead[b : b + 1, :] = jnp.sum(total, axis=0, keepdims=True)
+
+
+def ahead_sums(parity, pattern, weights):
     pattern, weights = in_hbm(pattern), in_hbm(weights)
     return call(
-        ahead_kernel,
+        functools.partial(ahead_kernel, parity),
         shape(T, N),
         [HBM, HBM],
         [
             pltpu.SMEM((T, T), jnp.int32),
             pltpu.VMEM((T, T, N, N), F32),
-            pltpu.VMEM((T, 8, N), F32),
+            pltpu.VMEM((T, T, 8, N), F32),
             pltpu.SemaphoreType.DMA((T + 1,)),
         ],
         flops=4 * T * T * N * N,
@@ -257,21 +262,37 @@
 TURNED = shape((T // 2) * (T // 2 + 1) * N, 2 * N, dtype=BF16)
 
 
-def first_kernel(flag, rhs, own, inflow, high, low, diag, vec, one, two, sent, pieces):
-    diag[...] = own[...] + inflow[...]
+def first_odd_kernel(rhs, own, inflow, high, low, sent, pieces):
+    @on_parity(1)
+    def _():
+        diag = own[...] + inflow[...]
+        for t in range(T):
+            put_pieces(pieces, t, rhs[t] / diag[t : t + 1, :])
+        to_next(pieces, high, low, sent)
+
+
+def first_odd(*args):
+    return call(first_odd_kernel, BLOCKS, [VMEM] * 5, [PIECES], flops=ONE_WAY)(*args)
+
+
+def first_even_kernel(rhs, own, inflow_odd, inflow_even, high, low, diag, vec, one, pieces):
+    diag[...] = own[...] + (inflow_odd[...] + inflow_even[...])
     for t in range(T):
         vec[t] = rhs[t] / diag[t : t + 1, :]
-    hand_out(flag, vec, high, low, one, two, sent, pieces)
-
-
-def first(flag, rhs, own, inflow, high, low):
-    return call(
-        first_kernel,
-        (shape(T, N), BLOCKS, BLOCKS, BLOCKS),
-        [VMEM] * 6,
-        [SENT, PIECES],
-        flops=ONE_WAY,
-    )(flag, rhs, own, inflow, high, low)
+
+    @on_parity(0)
+    def _():
+        for t in range(T):
+            put_pieces(pieces, t, vec[t])
+        to_next(pieces, high, low, one)
+
+    @on_parity(1)
+    def _():
+        one[...] = vec[...]
+
+
+def first_even(*args):
+    return call(first_even_kernel, (shape(T, N), BLOCKS, BLOCKS), [VMEM] * 6, [PIECES], flops=ONE_WAY)(*args)
 
 
 def local_kernel(count, *refs):
@@ -298,22 +319,39 @@
     )(*vecs, image, high, low)
 
 
-def add_received(flag, got_one, got_two, partial, turned_high, turned_low, image, pieces):
-    for t in range(T):
-        put_pieces(pieces, t, choose(flag, got_one[t], got_two[t]))
-        image[t] = partial[t] + choose(flag, got_two[t], got_one[t])
+def add_received(flag, got_one, got_even, got_odd, partial, turned_high, turned_low, image, pieces):
+    for t in range(T):
+        put_pieces(pieces, t, choose(flag, got_one[t], got_odd[t]))
+        image[t] = partial[t] + choose(flag, got_even[t], got_one[t])
     from_next(pieces, turned_high, turned_low, image)
 
 
-def step_kernel(flag, got_one, got_two, partial, diag, high, low, turned_high, turned_low, image, vec, one, two, sent, pieces):
-    add_received(flag, got_one, got_two, partial, turned_high, turned_low, image, pieces)
+def step_kernel(
+    flag,
+    got_one,
+    got_even,
+    got_odd,
+    partial,
+    diag,
+    high,
+    low,
+    turned_high,
+    turned_low,
+    image,
+    vec,
+    one,
+    two,
+    sent,
+    pieces,
+):
+    add_received(flag, got_one, got_even, got_odd, partial, turned_high, turned_low, image, pieces)
     for t in range(T):
         vec[t] = image[t] / diag[t : t + 1, :]
     hand_out(flag, vec, high, low, one, two, sent, pieces)
 
 
 def next_step(*args):
-    return call(step_kernel, (BLOCKS,) * 4, [VMEM] * 9, [SENT, PIECES], flops=2 * ONE_WAY)(*args)
+    return call(step_kernel, (BLOCKS,) * 4, [VMEM] * 10, [SENT, PIECES], flops=2 * ONE_WAY)(*args)
 
 
 PAIRS = 5
@@ -331,9 +369,9 @@
 
 
 def gram_kernel(
-    flag, got_one, got_two, partial, turned_high, turned_low, v0, v1, v2, m0, m1, m2, image, out, pieces
+    flag, got_one, got_even, got_odd, partial, turned_high, turned_low, v0, v1, v2, m0, m1, m2, image, out, pieces
 ):
-    add_received(flag, got_one, got_two, partial, turned_high, turned_low, image, pieces)
+    add_received(flag, got_one, got_even, got_odd, partial, turned_high, turned_low, image, pieces)
     last = [moments(v, image) for v in (v0, v1, v2)]
     every = [(m[i, 0], m[i, 1]) for m in (m0, m1, m2) for i in range(m.shape[0])] + last + last[-1:]
     for q in range(PAIRS):
@@ -343,7 +381,7 @@
 
 
 def gram(*args):
-    return call(gram_kernel, (BLOCKS, shape(1, PAIRS * N)), [VMEM] * 12, [PIECES], flops=ONE_WAY)(*args)
+    return call(gram_kernel, (BLOCKS, shape(1, PAIRS * N)), [VMEM] * 13, [PIECES], flops=ONE_WAY)(*args)
 
 
 def solve(matrix, right):
@@ -394,9 +432,9 @@
     return call(result_kernel, (shape(T, R, N), shape(T, R, N)), [VMEM] * 8)(parts, *vecs, *images)
 
 
-def shift(value, steps):
+def shift(value, steps, parity):
     count = lax.axis_size("tm")
-    return lax.ppermute(value, "tm", [(i, (i + steps) % count) for i in range(count)])
+    return lax.ppermute(value, "tm", [(i, (i + steps) % count) for i in range(parity, count, 2)])
 
 
 def all_parts(value):
@@ -405,26 +443,34 @@
     return spread.reshape(count, value.shape[1])
 
 
-def swaps(one, two):
+def swap_within(value):
+    return lax.ppermute(value, "tm", [(i, i ^ 1) for i in range(lax.axis_size("tm"))])
+
+
+def swap_across(value):
     count = lax.axis_size("tm")
-    one = lax.ppermute(one, "tm", [(i, i ^ 1) for i in range(count)])
-    return one, lax.ppermute(two, "tm", [(i, (i + (1 if i % 2 else -1)) % count) for i in range(count)])
+    return lax.ppermute(value, "tm", [(i, (i + (1 if i % 2 else -1)) % count) for i in range(count)])
 
 
 def shards(weights, pattern, shift_reg, rhs):
     flag = jnp.broadcast_to((1 - lax.axis_index("tm") % 2).astype(F32), (8, N))
     flag, pattern = lax.optimization_barrier((flag, pattern))
-    inflow = shift(ahead_sums(pattern, weights), 1)
+    inflow_even = shift(ahead_sums(1, pattern, weights), 1, 1)
+    inflow_odd = shift(ahead_sums(0, pattern, weights), 1, 0)
     high, low, own = band_pieces(pattern, weights, shift_reg)
-    diag, vec, *leaving = first(flag, rhs, own, inflow, high, low)
+    got_even = shift(first_odd(rhs, own, inflow_odd, high, low), 1, 1)
+    diag, vec, one = first_even(rhs, own, inflow_odd, inflow_even, high, low)
+    got_odd = shift(vec, -1, 0)
+    got = swap_within(one), got_even, got_odd
     vecs, images, found = [vec], [rhs], []
     for step in range(3):
-        got = swaps(*leaving)
         partial, part, *extra = local(vecs, images[-1], high, low)
         found.append(part)
         turned = extra or turned
         if step < 2:
-            image, vec, *leaving = next_step(flag, *got, partial, diag, high, low, *turned)
+            image, vec, one, two = next_step(flag, *got, partial, diag, high, low, *turned)
+            got_two = swap_across(two)
+            got = swap_within(one), got_two, got_two
             images.append(image)
             vecs.append(vec)
     image, part = gram(flag, *got, partial, *turned, *vecs, *found)

time: 68.7 us -> 75.1 us (1.093)
  starting transfers between devices: 12.6 us -> 23 us
  waiting for transfers between devices: 24.7 us -> 16.9 us
  blocking collectives: 17.3 us -> 20.8 us
    ppermute x7 -> x9, starting transfers between devices: 12.6 us -> 23 us  [the longest x2 12.6 us: swap_across(): lax.ppermute(value, 'tm', [(i, (i + (1 if i % 2 else -1)) % count) for i...]
    ppermute x7 -> x9, waiting for transfers between devices: 24.7 us -> 16.9 us  [the longest x4 9.77 us: shift(): lax.ppermute(value, 'tm', [(i, (i + steps) % count) for i in range(parity...]
    all_to_all x1, blocking collectives: 17.3 us -> 20.8 us  [all_parts(): lax.all_to_all(jnp.broadcast_to(value[None], (count,) + value.shape), 'tm...]
    pallas_call x5 -> x7, Pallas kernels: 5.41 us -> 5.44 us  [the longest x2 2.01 us: next_step(): call(step_kernel, (BLOCKS,) * 4, [VMEM] * 10, [SENT, PIECES], flops=2 * O...]
  transfers between devices with their start and end apart: 7 -> 9, of which waited for: 7 -> 5; matrix products, arithmetic and copies ran while one was open for 0% -> 0% of each run, Pallas kernels for 9% -> 10%
where the time goes in v7:
time: 75.1 us; the launch traced here: 74.9 us
  starting transfers between devices  23 us (31%)
  blocking collectives  20.8 us (28%)
  waiting for transfers between devices  16.9 us (23%)
  Pallas kernels  13.2 us (18%)
  between operations  0.84 us (1%)
    all_to_all x1, blocking collectives, all_parts(): lax.all_to_all(jnp.broadcast_to(value[None], (count,) + value.shape), 'tm...  20.8 us
    ppermute x2, starting transfers between devices, swap_across(): lax.ppermute(value, 'tm', [(i, (i + (1 if i % 2 else -1)) % count) for i...  12.6 us
    ppermute x4, starting transfers between devices, shift(): lax.ppermute(value, 'tm', [(i, (i + steps) % count) for i in range(parity...  9.91 us
    ppermute x4, waiting for transfers between devices, shift(): lax.ppermute(value, 'tm', [(i, (i + steps) % count) for i in range(parity...  9.77 us
    ppermute x2, waiting for transfers between devices, swap_across(): lax.ppermute(value, 'tm', [(i, (i + (1 if i % 2 else -1)) % count) for i...  7.15 us
    pallas_call x3, Pallas kernels, local(): call(functools.partial(local_kernel, len(vecs)), (BLOCKS, shape(len(vecs)...  3.56 us
    pallas_call x1, Pallas kernels, band_pieces(): call(band_kernel, (shape(*BAND, dtype=BF16), shape(*BAND, dtype=BF16), sh...  2.85 us
    pallas_call x2, Pallas kernels, next_step(): call(step_kernel, (BLOCKS,) * 4, [VMEM] * 10, [SENT, PIECES], flops=2 * O...  2.01 us
  transfers between devices with their start and end apart: 9, of which 5 were waited for; matrix products, arithmetic and copies ran while one was open for 0% of the time, Pallas kernels for 10%

profile of v7, /device:TPU:4, one launch (start us, length us, event | category | flops | bytes accessed | tf_op | source)
XLA Modules:
  0.0 74.9 jit_solution(14059189919229288054)
XLA Ops:
  0.7 1.8 %shard_map.60 = f32[8,128]{1,0:T(8,128)S(1)} custom-call(s32[8,8]{1,0:T(8,128)} %pattern.2, f32[8,8,128,128]{3,2,1,0:T(8,128)} %weights.5), custom_call_target="tpu_custom_call" | custom-call | flops 4194304 | bytes 4194304 | tf_op jit(solution)/shard_map/pallas_call | solution.py:104
  2.5 1.7 %collective-permute-start = (f32[8,128]{1,0:T(8,128)S(1)}, f32[8,128]{1,0:T(8,128)S(1)}, u32[]{:S(2)}, u32[]{:S(2)}) collective-permute-start(f32[8,128]{1,0:T(8,128)S(1)} %shard_map.60), channel_id=1, source_target_pairs={{0,1},{2,3},{4,5},{6,7},{8,9},{10,11},{12,13},{14,15},{16,17},{18,... | collective-permute-start | bytes 12296 | tf_op jit(solution)/shard_map/ppermute | solution.py:437
  4.2 0.1 shard_map.61
  4.4 1.4 %collective-permute-start.1 = (f32[8,128]{1,0:T(8,128)S(1)}, f32[8,128]{1,0:T(8,128)S(1)}, u32[]{:S(2)}, u32[]{:S(2)}) collective-permute-start(f32[8,128]{1,0:T(8,128)S(1)} %shard_map.61), channel_id=1, source_target_pairs={{1,2},{3,4},{5,6},{7,8},{9,10},{11,12},{13,14},{15,16},{17,18},{19... | collective-permute-start | bytes 12296 | tf_op jit(solution)/shard_map/ppermute | solution.py:437
  5.8 2.9 %shard_map.59 = (bf16[4,256,1152]{2,1,0:T(8,128)(2,1)S(1)}, bf16[4,256,1152]{2,1,0:T(8,128)(2,1)S(1)}, f32[8,128]{1,0:T(8,128)S(1)}) custom-call(s32[8,8]{1,0:T(8,128)} %pattern.2, f32[8,8,128,128]{3,2,1,0:T(8,128)} %weights.5, f32[8,128]{1,0:T(8,128)} %reg.1), custom_call_target="tpu_custom_call" | custom-call | flops 2147483648 | bytes 8388608 | tf_op jit(solution)/shard_map/pallas_call | solution.py:160
  8.7 1.3 %collective-permute-start.3 = (f32[8,64,128]{2,1,0:T(8,128)S(1)}, f32[8,64,128]{2,1,0:T(8,128)S(1)}, u32[]{:S(2)}, u32[]{:S(2)}) collective-permute-start(f32[8,64,128]{2,1,0:T(8,128)S(1)} %shard_map.63), channel_id=1, source_target_pairs={{1,2},{3,4},{5,6},{7,8},{9,10},{11,12},{13,14},{15,16},{17,18},{19... | collective-permute-start | bytes 786440 | tf_op jit(solution)/shard_map/ppermute | solution.py:437
  10.0 5.8 %collective-permute-done.1.inflow_even = f32[8,128]{1,0:T(8,128)S(1)} collective-permute-done((f32[8,128]{1,0:T(8,128)S(1)}, f32[8,128]{1,0:T(8,128)S(1)}, u32[]{:S(2)}, u32[]{:S(2)}) %collective-permute-start.1) | collective-permute-done | bytes 4128 | tf_op jit(solution)/shard_map/ppermute | solution.py:437
  15.8 0.6 shard_map.62
  16.6 5.5 %collective-permute-start.4 = (f32[8,64,128]{2,1,0:T(8,128)S(1)}, f32[8,64,128]{2,1,0:T(8,128)S(1)}, u32[]{:S(2)}, u32[]{:S(2)}) collective-permute-start(f32[8,64,128]{2,1,0:T(8,128)S(1)} %get-tuple-element.34.refs_0_.v0), channel_id=1, source_target_pairs={{0,63},{2,1},{4,3},{6,5},{8,7},{10,9},{12,11},{14,13},{16,15},{18,... | collective-permute-start | bytes 786440 | tf_op jit(solution)/shard_map/ppermute | solution.py:437
  22.0 1.2 %shard_map.64 = (f32[8,64,128]{2,1,0:T(8,128)S(1)}, f32[1,2,64,128]{3,2,1,0:T(8,128)S(1)}, bf16[2560,256]{1,0:T(8,128)(2,1)S(1)}, bf16[2560,256]{1,0:T(8,128)(2,1)S(1)}) custom-call(f32[8,64,128]{2,1,0:T(8,128)S(1)} %get-tuple-element.34.refs_0_.v0, f32[8,64,128]{2,1,0:T(8,128)S(1)} %copy-done, ...), custom_call_target="tpu_custom_call" | custom-call | flops 503316480 | tf_op jit(solution)/shard_map/pallas_call | solution.py:313
  23.2 2.2 %collective-permute-done.3.got_even = f32[8,64,128]{2,1,0:T(8,128)S(1)} collective-permute-done((f32[8,64,128]{2,1,0:T(8,128)S(1)}, f32[8,64,128]{2,1,0:T(8,128)S(1)}, u32[]{:S(2)}, u32[]{:S(2)}) %collective-permute-start.3) | collective-permute-done | bytes 262176 | tf_op jit(solution)/shard_map/ppermute | solution.py:437
  25.4 1.8 %collective-permute-done.4.got_odd = f32[8,64,128]{2,1,0:T(8,128)S(1)} collective-permute-done((f32[8,64,128]{2,1,0:T(8,128)S(1)}, f32[8,64,128]{2,1,0:T(8,128)S(1)}, u32[]{:S(2)}, u32[]{:S(2)}) %collective-permute-start.4) | collective-permute-done | bytes 262176 | tf_op jit(solution)/shard_map/ppermute | solution.py:437
  27.1 1.0 %shard_map.65 = (f32[8,64,128]{2,1,0:T(8,128)S(1)}, f32[8,64,128]{2,1,0:T(8,128)S(1)}, f32[8,64,128]{2,1,0:T(8,128)S(1)}, f32[8,64,128]{2,1,0:T(8,128)S(1)}) custom-call(f32[8,128]{1,0:T(8,128)S(1)} %broadcast_in_dim.11.flag, f32[8,64,128]{2,1,0:T(8,128)S(1)} %collective-permute-done.2.got_one, f32[8,64,128]{2,1,0:T(8,128)S(1)} %collective-permute-done.3.got_even, ...), custom_call_target="tpu_custom_call" | custom-call | flops 503316480 | tf_op jit(solution)/shard_map/pallas_call | solution.py:354
  28.1 0.3 collective-permute-start.5
  28.5 6.6 %collective-permute-start.6 = (f32[8,64,128]{2,1,0:T(8,128)S(1)}, f32[8,64,128]{2,1,0:T(8,128)S(1)}, u32[]{:S(2)}, u32[]{:S(2)}) collective-permute-start(f32[8,64,128]{2,1,0:T(8,128)S(1)} %get-tuple-element.40), channel_id=1, source_target_pairs={{0,63},{1,2},{2,1},{3,4},{4,3},{5,6},{6,5},{7,8},{8,7},{9,10},{10,... | collective-permute-start | bytes 786440 | tf_op jit(solution)/shard_map/ppermute | solution.py:452
  35.0 1.2 %shard_map.66 = (f32[8,64,128]{2,1,0:T(8,128)S(1)}, f32[2,2,64,128]{3,2,1,0:T(8,128)S(1)}) custom-call(f32[8,64,128]{2,1,0:T(8,128)S(1)} %get-tuple-element.34.refs_0_.v0, f32[8,64,128]{2,1,0:T(8,128)S(1)} %get-tuple-element.41.refs_1_.v1, f32[8,64,128]{2,1,0:T(8,128)S(1)} %get-tuple-element.42.refs_2_.y1, ...), custom_call_target="tpu_custom_call" | custom-call | flops 503316480 | tf_op jit(solution)/shard_map/pallas_call | solution.py:313
  36.2 3.8 %collective-permute-done.6.got_even.got_odd = f32[8,64,128]{2,1,0:T(8,128)S(1)} collective-permute-done((f32[8,64,128]{2,1,0:T(8,128)S(1)}, f32[8,64,128]{2,1,0:T(8,128)S(1)}, u32[]{:S(2)}, u32[]{:S(2)}) %collective-permute-start.6) | collective-permute-done | bytes 262176 | tf_op jit(solution)/shard_map/ppermute | solution.py:452
  40.0 1.0 %shard_map.67 = (f32[8,64,128]{2,1,0:T(8,128)S(1)}, f32[8,64,128]{2,1,0:T(8,128)S(1)}, f32[8,64,128]{2,1,0:T(8,128)S(1)}, f32[8,64,128]{2,1,0:T(8,128)S(1)}) custom-call(f32[8,128]{1,0:T(8,128)S(1)} %broadcast_in_dim.11.flag, f32[8,64,128]{2,1,0:T(8,128)S(1)} %collective-permute-done.5.got_one, f32[8,64,128]{2,1,0:T(8,128)S(1)} %collective-permute-done.6.got_even.got_odd, ...), custom_call_target="tpu_custom_call" | custom-call | flops 503316480 | tf_op jit(solution)/shard_map/pallas_call | solution.py:354
  41.1 6.0 %collective-permute-start.8 = (f32[8,64,128]{2,1,0:T(8,128)S(1)}, f32[8,64,128]{2,1,0:T(8,128)S(1)}, u32[]{:S(2)}, u32[]{:S(2)}) collective-permute-start(f32[8,64,128]{2,1,0:T(8,128)S(1)} %get-tuple-element.45), channel_id=1, source_target_pairs={{0,63},{1,2},{2,1},{3,4},{4,3},{5,6},{6,5},{7,8},{8,7},{9,10},{10,... | collective-permute-start | bytes 786440 | tf_op jit(solution)/shard_map/ppermute | solution.py:452
  47.1 1.2 %shard_map.68 = (f32[8,64,128]{2,1,0:T(8,128)S(1)}, f32[3,2,64,128]{3,2,1,0:T(8,128)S(1)}) custom-call(f32[8,64,128]{2,1,0:T(8,128)S(1)} %get-tuple-element.34.refs_0_.v0, f32[8,64,128]{2,1,0:T(8,128)S(1)} %get-tuple-element.41.refs_1_.v1, f32[8,64,128]{2,1,0:T(8,128)S(1)} %get-tuple-element.46.refs_2_.v2, f32[8,64,128]{2,1,0:T(8,128)S(1)} %get-tuple-element.47.refs_3_.y2, ...), custom_call_target="tpu_custom_call" | custom-call | flops 503316480 | tf_op jit(solution)/shard_map/pallas_call | solution.py:313
  48.4 3.4 %collective-permute-done.8.got_even.got_odd = f32[8,64,128]{2,1,0:T(8,128)S(1)} collective-permute-done((f32[8,64,128]{2,1,0:T(8,128)S(1)}, f32[8,64,128]{2,1,0:T(8,128)S(1)}, u32[]{:S(2)}, u32[]{:S(2)}) %collective-permute-start.8) | collective-permute-done | bytes 262176 | tf_op jit(solution)/shard_map/ppermute | solution.py:452
  51.8 0.9 %shard_map.69 = (f32[8,64,128]{2,1,0:T(8,128)S(1)}, f32[1,640]{1,0:T(1,128)S(1)}) custom-call(f32[8,128]{1,0:T(8,128)S(1)} %broadcast_in_dim.11.flag, f32[8,64,128]{2,1,0:T(8,128)S(1)} %collective-permute-done.7.got_one, f32[8,64,128]{2,1,0:T(8,128)S(1)} %collective-permute-done.8.got_even.got_odd, ...), custom_call_target="tpu_custom_call" | custom-call | flops 251658240 | tf_op jit(solution)/shard_map/pallas_call | solution.py:384
  52.7 20.8 %all_to_all.5 = f32[64,1,640]{2,1,0:T(1,128)S(1)} all-to-all(f32[64,1,640]{2,1,0:T(1,128)S(1)} %broadcast_in_dim.13), channel_id=1, replica_groups=mesh['scen'=4,'tm'=64] {'tm'}, dimensions={0} | all-to-all | bytes 327680 | tf_op jit(solution)/shard_map/all_to_all | solution.py:442
  73.6 1.3 %shard_map.70 = (f32[8,64,128]{2,1,0:T(8,128)}, f32[8,64,128]{2,1,0:T(8,128)}) custom-call(f32[64,640]{1,0:T(8,128)S(1)} %bitcast.3, f32[8,64,128]{2,1,0:T(8,128)S(1)} %get-tuple-element.34.refs_0_.v0, f32[8,64,128]{2,1,0:T(8,128)S(1)} %get-tuple-element.41.refs_1_.v1, f32[8,64,128]{2,1,0:T(8,128)S(1)} %get-tuple-element.46.refs_2_.v2, ...), custom_call_target="tpu_custom_call" | custom-call | tf_op jit(solution)/shard_map/pallas_call | solution.py:432
  (13 shorter events, 0.3 us)
Async XLA Ops:
  2.5 6.2 %collective-permute-start = (f32[8,128]{1,0:T(8,128)S(1)}, f32[8,128]{1,0:T(8,128)S(1)}, u32[]{:S(2)}, u32[]{:S(2)}) collective-permute-start(f32[8,128]{1,0:T(8,128)S(1)} %shard_map.60), channel_id=1, source_target_pairs={{0,1},{2,3},{4,5},{6,7},{8,9},{10,11},{12,13},{14,15},{16,17},{18,... | collective-permute-start | bytes 12296 | tf_op jit(solution)/shard_map/ppermute | solution.py:437
  4.3 4.3 %copy-start = (f32[8,64,128]{2,1,0:T(8,128)S(1)}, f32[8,64,128]{2,1,0:T(8,128)}, u32[]{:S(2)}) copy-start(f32[8,64,128]{2,1,0:T(8,128)} %y0.1) | copy-start | bytes 786436
  4.4 11.5 %collective-permute-start.1 = (f32[8,128]{1,0:T(8,128)S(1)}, f32[8,128]{1,0:T(8,128)S(1)}, u32[]{:S(2)}, u32[]{:S(2)}) collective-permute-start(f32[8,128]{1,0:T(8,128)S(1)} %shard_map.61), channel_id=1, source_target_pairs={{1,2},{3,4},{5,6},{7,8},{9,10},{11,12},{13,14},{15,16},{17,18},{19... | collective-permute-start | bytes 12296 | tf_op jit(solution)/shard_map/ppermute | solution.py:437
  8.7 16.7 %collective-permute-start.3 = (f32[8,64,128]{2,1,0:T(8,128)S(1)}, f32[8,64,128]{2,1,0:T(8,128)S(1)}, u32[]{:S(2)}, u32[]{:S(2)}) collective-permute-start(f32[8,64,128]{2,1,0:T(8,128)S(1)} %shard_map.63), channel_id=1, source_target_pairs={{1,2},{3,4},{5,6},{7,8},{9,10},{11,12},{13,14},{15,16},{17,18},{19... | collective-permute-start | bytes 786440 | tf_op jit(solution)/shard_map/ppermute | solution.py:437
  16.5 8.9 %collective-permute-start.2 = (f32[8,64,128]{2,1,0:T(8,128)S(1)}, f32[8,64,128]{2,1,0:T(8,128)S(1)}, u32[]{:S(2)}, u32[]{:S(2)}) collective-permute-start(f32[8,64,128]{2,1,0:T(8,128)S(1)} %get-tuple-element.33), channel_id=1, source_target_pairs={{0,1},{1,0},{2,3},{3,2},{4,5},{5,4},{6,7},{7,6},{8,9},{9,8},{10,11... | collective-permute-start | bytes 786440 | tf_op jit(solution)/shard_map/ppermute | solution.py:447
  16.6 10.6 %collective-permute-start.4 = (f32[8,64,128]{2,1,0:T(8,128)S(1)}, f32[8,64,128]{2,1,0:T(8,128)S(1)}, u32[]{:S(2)}, u32[]{:S(2)}) collective-permute-start(f32[8,64,128]{2,1,0:T(8,128)S(1)} %get-tuple-element.34.refs_0_.v0), channel_id=1, source_target_pairs={{0,63},{2,1},{4,3},{6,5},{8,7},{10,9},{12,11},{14,13},{16,15},{18,... | collective-permute-start | bytes 786440 | tf_op jit(solution)/shard_map/ppermute | solution.py:437
  28.1 8.1 %collective-permute-start.5 = (f32[8,64,128]{2,1,0:T(8,128)S(1)}, f32[8,64,128]{2,1,0:T(8,128)S(1)}, u32[]{:S(2)}, u32[]{:S(2)}) collective-permute-start(f32[8,64,128]{2,1,0:T(8,128)S(1)} %get-tuple-element.39), channel_id=1, source_target_pairs={{0,1},{1,0},{2,3},{3,2},{4,5},{5,4},{6,7},{7,6},{8,9},{9,8},{10,11... | collective-permute-start | bytes 786440 | tf_op jit(solution)/shard_map/ppermute | solution.py:447
  28.5 11.5 %collective-permute-start.6 = (f32[8,64,128]{2,1,0:T(8,128)S(1)}, f32[8,64,128]{2,1,0:T(8,128)S(1)}, u32[]{:S(2)}, u32[]{:S(2)}) collective-permute-start(f32[8,64,128]{2,1,0:T(8,128)S(1)} %get-tuple-element.40), channel_id=1, source_target_pairs={{0,63},{1,2},{2,1},{3,4},{4,3},{5,6},{6,5},{7,8},{8,7},{9,10},{10,... | collective-permute-start | bytes 786440 | tf_op jit(solution)/shard_map/ppermute | solution.py:452
  41.0 7.4 %collective-permute-start.7 = (f32[8,64,128]{2,1,0:T(8,128)S(1)}, f32[8,64,128]{2,1,0:T(8,128)S(1)}, u32[]{:S(2)}, u32[]{:S(2)}) collective-permute-start(f32[8,64,128]{2,1,0:T(8,128)S(1)} %get-tuple-element.44), channel_id=1, source_target_pairs={{0,1},{1,0},{2,3},{3,2},{4,5},{5,4},{6,7},{7,6},{8,9},{9,8},{10,11... | collective-permute-start | bytes 786440 | tf_op jit(solution)/shard_map/ppermute | solution.py:447
  41.1 10.7 %collective-permute-start.8 = (f32[8,64,128]{2,1,0:T(8,128)S(1)}, f32[8,64,128]{2,1,0:T(8,128)S(1)}, u32[]{:S(2)}, u32[]{:S(2)}) collective-permute-start(f32[8,64,128]{2,1,0:T(8,128)S(1)} %get-tuple-element.45), channel_id=1, source_target_pairs={{0,63},{1,2},{2,1},{3,4},{4,3},{5,6},{6,5},{7,8},{8,7},{9,10},{10,... | collective-permute-start | bytes 786440 | tf_op jit(solution)/shard_map/ppermute | solution.py:452

commit v8 on v5

--- a/solution.py
+++ b/solution.py
@@ -80,18 +80,17 @@
         copies.append(pltpu.make_async_copy(weights.at[t, some], buf.at[t, some], sems.at[t]))
     for copy in copies:
         copy.start()
-    cols[...] = jnp.zeros_like(cols)
+    for t in range(T):
+        copies[t].wait()
+        for k in range(T - 1 - t, T):
+            cols[t, k] = jnp.sum(buf[t, k].reshape(N // 8, 8, N), axis=0)
     head.wait()
-    for t in range(T):
-        copies[t].wait()
-
-        def step(k, carry):
-            m = buf[t, k] * mask[t, k].astype(F32)
-            cols[t + k + 1 - T] += jnp.sum(m.reshape(N // 8, 8, N), axis=0)
-            return carry
-
-        lax.fori_loop(T - 1 - t, T, step, 0)
-    ahead[...] = jnp.sum(cols[...], axis=1)
+    for b in range(T):
+        total = jnp.zeros((8, N), F32)
+        for t in range(b, T):
+            k = T - 1 - t + b
+            total = total + cols[t, k] * mask[t, k].astype(F32)
+        ahead[b : b + 1, :] = jnp.sum(total, axis=0, keepdims=True)
 
 
 def ahead_sums(pattern, weights):
@@ -103,7 +102,7 @@
         [
             pltpu.SMEM((T, T), jnp.int32),
             pltpu.VMEM((T, T, N, N), F32),
-            pltpu.VMEM((T, 8, N), F32),
+            pltpu.VMEM((T, T, 8, N), F32),
             pltpu.SemaphoreType.DMA((T + 1,)),
         ],
         flops=4 * T * T * N * N,
@@ -257,29 +256,49 @@
 TURNED = shape((T // 2) * (T // 2 + 1) * N, 2 * N, dtype=BF16)
 
 
-def first_kernel(flag, rhs, own, inflow, high, low, diag, vec, one, two, sent, pieces):
+def on_parity(parity):
+    return pl.when(lax.axis_index("tm") % 2 == parity)
+
+
+def first_kernel(rhs, own, inflow, high, low, diag, vec, two, pieces):
     diag[...] = own[...] + inflow[...]
-    for t in range(T):
-        vec[t] = rhs[t] / diag[t : t + 1, :]
-    hand_out(flag, vec, high, low, one, two, sent, pieces)
-
-
-def first(flag, rhs, own, inflow, high, low):
-    return call(
-        first_kernel,
-        (shape(T, N), BLOCKS, BLOCKS, BLOCKS),
-        [VMEM] * 6,
-        [SENT, PIECES],
-        flops=ONE_WAY,
-    )(flag, rhs, own, inflow, high, low)
+
+    @on_parity(0)
+    def _():
+        for t in range(T):
+            value = rhs[t] / diag[t : t + 1, :]
+            vec[t] = value
+            two[t] = value
+
+    @on_parity(1)
+    def _():
+        for t in range(T):
+            value = rhs[t] / diag[t : t + 1, :]
+            vec[t] = value
+            put_pieces(pieces, t, value)
+        to_next(pieces, high, low, two)
+
+
+def first(*args):
+    return call(first_kernel, (shape(T, N), BLOCKS, BLOCKS), [VMEM] * 5, [PIECES], flops=ONE_WAY)(*args)
 
 
 def local_kernel(count, *refs):
-    vecs, (image, high, low, out, found, *turned, pieces) = refs[:count], refs[count:]
-    if turned:
+    vecs, (image, high, low, out, found, *more, pieces) = refs[:count], refs[count:]
+    for t in range(T):
+        put_pieces(pieces, t, vecs[-1][t])
+    if more:
+        one, *turned = more
+
+        @on_parity(0)
+        def _():
+            to_next(pieces, high, low, one)
+
+        @on_parity(1)
+        def _():
+            one[...] = vecs[0][...]
+
         turn(high, low, *turned)
-    for t in range(T):
-        put_pieces(pieces, t, vecs[-1][t])
     within(pieces, high, low, out)
     for i, vec in enumerate(vecs):
         h, l = moments(vec, image)
@@ -288,10 +307,10 @@
 
 
 def local(vecs, image, high, low):
-    turned = (TURNED, TURNED) if len(vecs) == 1 else ()
+    more = (BLOCKS, TURNED, TURNED) if len(vecs) == 1 else ()
     return call(
         functools.partial(local_kernel, len(vecs)),
-        (BLOCKS, shape(len(vecs), 2, R, N)) + turned,
+        (BLOCKS, shape(len(vecs), 2, R, N)) + more,
         [VMEM] * (len(vecs) + 3),
         [PIECES],
         flops=2 * ONE_WAY,
@@ -405,10 +424,13 @@
     return spread.reshape(count, value.shape[1])
 
 
-def swaps(one, two):
+def swap_within(value):
+    return lax.ppermute(value, "tm", [(i, i ^ 1) for i in range(lax.axis_size("tm"))])
+
+
+def swap_across(value):
     count = lax.axis_size("tm")
-    one = lax.ppermute(one, "tm", [(i, i ^ 1) for i in range(count)])
-    return one, lax.ppermute(two, "tm", [(i, (i + (1 if i % 2 else -1)) % count) for i in range(count)])
+    return lax.ppermute(value, "tm", [(i, (i + (1 if i % 2 else -1)) % count) for i in range(count)])
 
 
 def shards(weights, pattern, shift_reg, rhs):
@@ -416,17 +438,18 @@
     flag, pattern = lax.optimization_barrier((flag, pattern))
     inflow = shift(ahead_sums(pattern, weights), 1)
     high, low, own = band_pieces(pattern, weights, shift_reg)
-    diag, vec, *leaving = first(flag, rhs, own, inflow, high, low)
-    vecs, images, found = [vec], [rhs], []
-    for step in range(3):
-        got = swaps(*leaving)
-        partial, part, *extra = local(vecs, images[-1], high, low)
+    diag, vec, two = first(rhs, own, inflow, high, low)
+    got_two = swap_across(two)
+    partial, part, one, *turned = local([vec], rhs, high, low)
+    got = swap_within(one), got_two
+    vecs, images, found = [vec], [rhs], [part]
+    for step in range(2):
+        image, vec, one, two = next_step(flag, *got, partial, diag, high, low, *turned)
+        got = swap_within(one), swap_across(two)
+        images.append(image)
+        vecs.append(vec)
+        partial, part = local(vecs, image, high, low)
         found.append(part)
-        turned = extra or turned
-        if step < 2:
-            image, vec, *leaving = next_step(flag, *got, partial, diag, high, low, *turned)
-            images.append(image)
-            vecs.append(vec)
     image, part = gram(flag, *got, partial, *turned, *vecs, *found)
     return result(all_parts(part), vecs, images + [image])
 

time: 68.7 us -> 68.5 us (level)
  starting transfers between devices: 12.6 us -> 10.9 us
  waiting for transfers between devices: 24.7 us -> 26 us
    ppermute x6, starting transfers between devices: 11 us -> 9.22 us  [the longest x3 8.66 us: swap_across(): lax.ppermute(value, 'tm', [(i, (i + (1 if i % 2 else -1)) % count) for i...]
    ppermute x6, waiting for transfers between devices: 18.6 us -> 19.9 us  [the longest x3 15.8 us: swap_across(): lax.ppermute(value, 'tm', [(i, (i + (1 if i % 2 else -1)) % count) for i...]
  transfers between devices with their start and end apart: 7 -> 7, of which waited for: 7 -> 7; matrix products, arithmetic and copies ran while one was open for 0% -> 0% of each run, Pallas kernels for 9% -> 10%
where the time goes in v8:
time: 68.5 us; the launch traced here: 68.4 us
  waiting for transfers between devices  26 us (38%)
  blocking collectives  17.6 us (26%)
  Pallas kernels  13.1 us (19%)
  starting transfers between devices  10.9 us (16%)
  between operations  0.76 us (1%)
    all_to_all x1, blocking collectives, all_parts(): lax.all_to_all(jnp.broadcast_to(value[None], (count,) + value.shape), 'tm...  17.6 us
    ppermute x3, waiting for transfers between devices, swap_across(): lax.ppermute(value, 'tm', [(i, (i + (1 if i % 2 else -1)) % count) for i...  15.8 us
    ppermute x3, starting transfers between devices, swap_across(): lax.ppermute(value, 'tm', [(i, (i + (1 if i % 2 else -1)) % count) for i...  8.66 us
    ppermute x1, waiting for transfers between devices, shift(): lax.ppermute(value, 'tm', [(i, (i + steps) % count) for i in range(count)])  6.09 us
    pallas_call x3, Pallas kernels, local(): call(functools.partial(local_kernel, len(vecs)), (BLOCKS, shape(len(vecs)...  4.17 us
    ppermute x3, waiting for transfers between devices, swap_within(): lax.ppermute(value, 'tm', [(i, i ^ 1) for i in range(lax.axis_size('tm'))])  4.07 us
    pallas_call x1, Pallas kernels, band_pieces(): call(band_kernel, (shape(*BAND, dtype=BF16), shape(*BAND, dtype=BF16), sh...  2.85 us
    pallas_call x2, Pallas kernels, next_step(): call(step_kernel, (BLOCKS,) * 4, [VMEM] * 9, [SENT, PIECES], flops=2 * ON...  2.02 us
  transfers between devices with their start and end apart: 7, of which 7 were waited for; matrix products, arithmetic and copies ran while one was open for 0% of the time, Pallas kernels for 10%

profile of v8, /device:TPU:4, one launch (start us, length us, event | category | flops | bytes accessed | tf_op | source)
XLA Modules:
  0.0 68.4 jit_solution(7398453581612185680)
XLA Ops:
  0.7 1.8 %shard_map.60 = f32[8,128]{1,0:T(8,128)S(1)} custom-call(s32[8,8]{1,0:T(8,128)} %pattern.1, f32[8,8,128,128]{3,2,1,0:T(8,128)} %weights.3), custom_call_target="tpu_custom_call" | custom-call | flops 4194304 | bytes 4194304 | tf_op jit(solution)/shard_map/pallas_call | solution.py:98
  2.5 1.7 %collective-permute-start = (f32[8,128]{1,0:T(8,128)S(1)}, f32[8,128]{1,0:T(8,128)S(1)}, u32[]{:S(2)}, u32[]{:S(2)}) collective-permute-start(f32[8,128]{1,0:T(8,128)S(1)} %shard_map.60), channel_id=1, source_target_pairs={{0,1},{1,2},{2,3},{3,4},{4,5},{5,6},{6,7},{7,8},{8,9},{9,10},{10,1... | collective-permute-start | bytes 12296 | tf_op jit(solution)/shard_map/ppermute | solution.py:418
  4.2 2.8 %shard_map.59 = (bf16[4,256,1152]{2,1,0:T(8,128)(2,1)S(1)}, bf16[4,256,1152]{2,1,0:T(8,128)(2,1)S(1)}, f32[8,128]{1,0:T(8,128)S(1)}) custom-call(s32[8,8]{1,0:T(8,128)} %pattern.1, f32[8,8,128,128]{3,2,1,0:T(8,128)} %weights.3, f32[8,128]{1,0:T(8,128)} %reg.1), custom_call_target="tpu_custom_call" | custom-call | flops 2147483648 | bytes 8388608 | tf_op jit(solution)/shard_map/pallas_call | solution.py:154
  7.0 6.1 %collective-permute-done.inflow = f32[8,128]{1,0:T(8,128)S(1)} collective-permute-done((f32[8,128]{1,0:T(8,128)S(1)}, f32[8,128]{1,0:T(8,128)S(1)}, u32[]{:S(2)}, u32[]{:S(2)}) %collective-permute-start) | collective-permute-done | bytes 4128 | tf_op jit(solution)/shard_map/ppermute | solution.py:418
  13.2 2.6 %collective-permute-start.2 = (f32[8,64,128]{2,1,0:T(8,128)S(1)}, f32[8,64,128]{2,1,0:T(8,128)S(1)}, u32[]{:S(2)}, u32[]{:S(2)}) collective-permute-start(f32[8,64,128]{2,1,0:T(8,128)S(1)} %get-tuple-element.36), channel_id=1, source_target_pairs={{0,63},{1,2},{2,1},{3,4},{4,3},{5,6},{6,5},{7,8},{8,7},{9,10},{10,... | collective-permute-start | bytes 786440 | tf_op jit(solution)/shard_map/ppermute | solution.py:433
  15.8 1.8 %shard_map.62 = (f32[8,64,128]{2,1,0:T(8,128)S(1)}, f32[1,2,64,128]{3,2,1,0:T(8,128)S(1)}, f32[8,64,128]{2,1,0:T(8,128)S(1)}, bf16[2560,256]{1,0:T(8,128)(2,1)S(1)}, bf16[2560,256]{1,0:T(8,128)(2,1)S(1)}) custom-call(f32[8,64,128]{2,1,0:T(8,128)S(1)} %get-tuple-element.34.refs_0_.v0, f32[8,64,128]{2,1,0:T(8,128)S(1)} %copy-done, ...), custom_call_target="tpu_custom_call" | custom-call | flops 503316480 | tf_op jit(solution)/shard_map/pallas_call | solution.py:311
  17.6 0.1 collective-permute-start.1
  17.7 7.0 %collective-permute-done.2.got_two = f32[8,64,128]{2,1,0:T(8,128)S(1)} collective-permute-done((f32[8,64,128]{2,1,0:T(8,128)S(1)}, f32[8,64,128]{2,1,0:T(8,128)S(1)}, u32[]{:S(2)}, u32[]{:S(2)}) %collective-permute-start.2) | collective-permute-done | bytes 262176 | tf_op jit(solution)/shard_map/ppermute | solution.py:433
  24.7 1.0 %shard_map.63 = (f32[8,64,128]{2,1,0:T(8,128)S(1)}, f32[8,64,128]{2,1,0:T(8,128)S(1)}, f32[8,64,128]{2,1,0:T(8,128)S(1)}, f32[8,64,128]{2,1,0:T(8,128)S(1)}) custom-call(f32[8,128]{1,0:T(8,128)S(1)} %broadcast_in_dim.11.flag, f32[8,64,128]{2,1,0:T(8,128)S(1)} %collective-permute-done.1.got_one, f32[8,64,128]{2,1,0:T(8,128)S(1)} %collective-permute-done.2.got_two, ...), custom_call_target="tpu_custom_call" | custom-call | flops 503316480 | tf_op jit(solution)/shard_map/pallas_call | solution.py:335
  25.7 0.4 collective-permute-start.3
  26.1 3.0 %collective-permute-start.4 = (f32[8,64,128]{2,1,0:T(8,128)S(1)}, f32[8,64,128]{2,1,0:T(8,128)S(1)}, u32[]{:S(2)}, u32[]{:S(2)}) collective-permute-start(f32[8,64,128]{2,1,0:T(8,128)S(1)} %get-tuple-element.42), channel_id=1, source_target_pairs={{0,63},{1,2},{2,1},{3,4},{4,3},{5,6},{6,5},{7,8},{8,7},{9,10},{10,... | collective-permute-start | bytes 786440 | tf_op jit(solution)/shard_map/ppermute | solution.py:433
  29.1 1.2 %shard_map.64 = (f32[8,64,128]{2,1,0:T(8,128)S(1)}, f32[2,2,64,128]{3,2,1,0:T(8,128)S(1)}) custom-call(f32[8,64,128]{2,1,0:T(8,128)S(1)} %get-tuple-element.34.refs_0_.v0, f32[8,64,128]{2,1,0:T(8,128)S(1)} %get-tuple-element.43.refs_1_.v1, f32[8,64,128]{2,1,0:T(8,128)S(1)} %get-tuple-element.44.refs_2_.y1, ...), custom_call_target="tpu_custom_call" | custom-call | flops 503316480 | tf_op jit(solution)/shard_map/pallas_call | solution.py:311
  30.3 1.9 %collective-permute-done.3.got_one = f32[8,64,128]{2,1,0:T(8,128)S(1)} collective-permute-done((f32[8,64,128]{2,1,0:T(8,128)S(1)}, f32[8,64,128]{2,1,0:T(8,128)S(1)}, u32[]{:S(2)}, u32[]{:S(2)}) %collective-permute-start.3) | collective-permute-done | bytes 262176 | tf_op jit(solution)/shard_map/ppermute | solution.py:428
  32.2 4.5 %collective-permute-done.4.got_two = f32[8,64,128]{2,1,0:T(8,128)S(1)} collective-permute-done((f32[8,64,128]{2,1,0:T(8,128)S(1)}, f32[8,64,128]{2,1,0:T(8,128)S(1)}, u32[]{:S(2)}, u32[]{:S(2)}) %collective-permute-start.4) | collective-permute-done | bytes 262176 | tf_op jit(solution)/shard_map/ppermute | solution.py:433
  36.7 1.0 %shard_map.65 = (f32[8,64,128]{2,1,0:T(8,128)S(1)}, f32[8,64,128]{2,1,0:T(8,128)S(1)}, f32[8,64,128]{2,1,0:T(8,128)S(1)}, f32[8,64,128]{2,1,0:T(8,128)S(1)}) custom-call(f32[8,128]{1,0:T(8,128)S(1)} %broadcast_in_dim.11.flag, f32[8,64,128]{2,1,0:T(8,128)S(1)} %collective-permute-done.3.got_one, f32[8,64,128]{2,1,0:T(8,128)S(1)} %collective-permute-done.4.got_two, ...), custom_call_target="tpu_custom_call" | custom-call | flops 503316480 | tf_op jit(solution)/shard_map/pallas_call | solution.py:335
  37.7 0.1 collective-permute-start.5
  37.8 3.1 %collective-permute-start.6 = (f32[8,64,128]{2,1,0:T(8,128)S(1)}, f32[8,64,128]{2,1,0:T(8,128)S(1)}, u32[]{:S(2)}, u32[]{:S(2)}) collective-permute-start(f32[8,64,128]{2,1,0:T(8,128)S(1)} %get-tuple-element.47), channel_id=1, source_target_pairs={{0,63},{1,2},{2,1},{3,4},{4,3},{5,6},{6,5},{7,8},{8,7},{9,10},{10,... | collective-permute-start | bytes 786440 | tf_op jit(solution)/shard_map/ppermute | solution.py:433
  40.9 1.2 %shard_map.66 = (f32[8,64,128]{2,1,0:T(8,128)S(1)}, f32[3,2,64,128]{3,2,1,0:T(8,128)S(1)}) custom-call(f32[8,64,128]{2,1,0:T(8,128)S(1)} %get-tuple-element.34.refs_0_.v0, f32[8,64,128]{2,1,0:T(8,128)S(1)} %get-tuple-element.43.refs_1_.v1, f32[8,64,128]{2,1,0:T(8,128)S(1)} %get-tuple-element.48.refs_2_.v2, f32[8,64,128]{2,1,0:T(8,128)S(1)} %get-tuple-element.49.refs_3_.y2, ...), custom_call_target="tpu_custom_call" | custom-call | flops 503316480 | tf_op jit(solution)/shard_map/pallas_call | solution.py:311
  42.1 2.1 %collective-permute-done.5.got_one = f32[8,64,128]{2,1,0:T(8,128)S(1)} collective-permute-done((f32[8,64,128]{2,1,0:T(8,128)S(1)}, f32[8,64,128]{2,1,0:T(8,128)S(1)}, u32[]{:S(2)}, u32[]{:S(2)}) %collective-permute-start.5) | collective-permute-done | bytes 262176 | tf_op jit(solution)/shard_map/ppermute | solution.py:428
  44.2 4.3 %collective-permute-done.6.got_two = f32[8,64,128]{2,1,0:T(8,128)S(1)} collective-permute-done((f32[8,64,128]{2,1,0:T(8,128)S(1)}, f32[8,64,128]{2,1,0:T(8,128)S(1)}, u32[]{:S(2)}, u32[]{:S(2)}) %collective-permute-start.6) | collective-permute-done | bytes 262176 | tf_op jit(solution)/shard_map/ppermute | solution.py:433
  48.5 0.9 %shard_map.67 = (f32[8,64,128]{2,1,0:T(8,128)S(1)}, f32[1,640]{1,0:T(1,128)S(1)}) custom-call(f32[8,128]{1,0:T(8,128)S(1)} %broadcast_in_dim.11.flag, f32[8,64,128]{2,1,0:T(8,128)S(1)} %collective-permute-done.5.got_one, f32[8,64,128]{2,1,0:T(8,128)S(1)} %collective-permute-done.6.got_two, f32[8,64,128]{2,1,0:T(8,128)S(1)} %get-tuple-element.50.partial, ...), custom_call_target="tpu_custom_call" | custom-call | flops 251658240 | tf_op jit(solution)/shard_map/pallas_call | solution.py:365
  49.4 0.1 broadcast_in_dim.13
  49.5 17.6 %all_to_all.5 = f32[64,1,640]{2,1,0:T(1,128)S(1)} all-to-all(f32[64,1,640]{2,1,0:T(1,128)S(1)} %broadcast_in_dim.13), channel_id=1, replica_groups=mesh['scen'=4,'tm'=64] {'tm'}, dimensions={0} | all-to-all | bytes 327680 | tf_op jit(solution)/shard_map/all_to_all | solution.py:423
  67.1 1.3 %shard_map.68 = (f32[8,64,128]{2,1,0:T(8,128)}, f32[8,64,128]{2,1,0:T(8,128)}) custom-call(f32[64,640]{1,0:T(8,128)S(1)} %bitcast.3, f32[8,64,128]{2,1,0:T(8,128)S(1)} %get-tuple-element.34.refs_0_.v0, f32[8,64,128]{2,1,0:T(8,128)S(1)} %get-tuple-element.43.refs_1_.v1, f32[8,64,128]{2,1,0:T(8,128)S(1)} %get-tuple-element.48.refs_2_.v2, ...), custom_call_target="tpu_custom_call" | custom-call | tf_op jit(solution)/shard_map/pallas_call | solution.py:413
  (7 shorter events, 0.2 us)
Async XLA Ops:
  2.5 10.6 %copy-start = (f32[8,64,128]{2,1,0:T(8,128)S(1)}, f32[8,64,128]{2,1,0:T(8,128)}, u32[]{:S(2)}) copy-start(f32[8,64,128]{2,1,0:T(8,128)} %y0.1) | copy-start | bytes 786436
  2.5 10.6 %collective-permute-start = (f32[8,128]{1,0:T(8,128)S(1)}, f32[8,128]{1,0:T(8,128)S(1)}, u32[]{:S(2)}, u32[]{:S(2)}) collective-permute-start(f32[8,128]{1,0:T(8,128)S(1)} %shard_map.60), channel_id=1, source_target_pairs={{0,1},{1,2},{2,3},{3,4},{4,5},{5,6},{6,7},{7,8},{8,9},{9,10},{10,1... | collective-permute-start | bytes 12296 | tf_op jit(solution)/shard_map/ppermute | solution.py:418
  13.2 11.5 %collective-permute-start.2 = (f32[8,64,128]{2,1,0:T(8,128)S(1)}, f32[8,64,128]{2,1,0:T(8,128)S(1)}, u32[]{:S(2)}, u32[]{:S(2)}) collective-permute-start(f32[8,64,128]{2,1,0:T(8,128)S(1)} %get-tuple-element.36), channel_id=1, source_target_pairs={{0,63},{1,2},{2,1},{3,4},{4,3},{5,6},{6,5},{7,8},{8,7},{9,10},{10,... | collective-permute-start | bytes 786440 | tf_op jit(solution)/shard_map/ppermute | solution.py:433
  17.6 7.2 %collective-permute-start.1 = (f32[8,64,128]{2,1,0:T(8,128)S(1)}, f32[8,64,128]{2,1,0:T(8,128)S(1)}, u32[]{:S(2)}, u32[]{:S(2)}) collective-permute-start(f32[8,64,128]{2,1,0:T(8,128)S(1)} %get-tuple-element.35), channel_id=1, source_target_pairs={{0,1},{1,0},{2,3},{3,2},{4,5},{5,4},{6,7},{7,6},{8,9},{9,8},{10,11... | collective-permute-start | bytes 786440 | tf_op jit(solution)/shard_map/ppermute | solution.py:428
  25.7 6.5 %collective-permute-start.3 = (f32[8,64,128]{2,1,0:T(8,128)S(1)}, f32[8,64,128]{2,1,0:T(8,128)S(1)}, u32[]{:S(2)}, u32[]{:S(2)}) collective-permute-start(f32[8,64,128]{2,1,0:T(8,128)S(1)} %get-tuple-element.41), channel_id=1, source_target_pairs={{0,1},{1,0},{2,3},{3,2},{4,5},{5,4},{6,7},{7,6},{8,9},{9,8},{10,11... | collective-permute-start | bytes 786440 | tf_op jit(solution)/shard_map/ppermute | solution.py:428
  26.1 10.6 %collective-permute-start.4 = (f32[8,64,128]{2,1,0:T(8,128)S(1)}, f32[8,64,128]{2,1,0:T(8,128)S(1)}, u32[]{:S(2)}, u32[]{:S(2)}) collective-permute-start(f32[8,64,128]{2,1,0:T(8,128)S(1)} %get-tuple-element.42), channel_id=1, source_target_pairs={{0,63},{1,2},{2,1},{3,4},{4,3},{5,6},{6,5},{7,8},{8,7},{9,10},{10,... | collective-permute-start | bytes 786440 | tf_op jit(solution)/shard_map/ppermute | solution.py:433
  37.7 6.5 %collective-permute-start.5 = (f32[8,64,128]{2,1,0:T(8,128)S(1)}, f32[8,64,128]{2,1,0:T(8,128)S(1)}, u32[]{:S(2)}, u32[]{:S(2)}) collective-permute-start(f32[8,64,128]{2,1,0:T(8,128)S(1)} %get-tuple-element.46), channel_id=1, source_target_pairs={{0,1},{1,0},{2,3},{3,2},{4,5},{5,4},{6,7},{7,6},{8,9},{9,8},{10,11... | collective-permute-start | bytes 786440 | tf_op jit(solution)/shard_map/ppermute | solution.py:428
  37.8 10.7 %collective-permute-start.6 = (f32[8,64,128]{2,1,0:T(8,128)S(1)}, f32[8,64,128]{2,1,0:T(8,128)S(1)}, u32[]{:S(2)}, u32[]{:S(2)}) collective-permute-start(f32[8,64,128]{2,1,0:T(8,128)S(1)} %get-tuple-element.47), channel_id=1, source_target_pairs={{0,63},{1,2},{2,1},{3,4},{4,3},{5,6},{6,5},{7,8},{8,7},{9,10},{10,... | collective-permute-start | bytes 786440 | tf_op jit(solution)/shard_map/ppermute | solution.py:433

commit v9 on v8

--- a/solution.py
+++ b/solution.py
@@ -185,8 +185,8 @@
             at = slice((7 + 2 * b - 2 * a) * N, (9 + 2 * b - 2 * a) * N)
             term = product(pieces, slice(a * 2 * N, (a + 1) * 2 * N), high[a, :, at], low[a, :, at], dot)
             total = term if total is None else total + term
-        out[2 * b] = total[:, :N]
-        out[2 * b + 1] = total[:, N:]
+        out[2 * b, 0:R] = total[:, :N]
+        out[2 * b + 1, 0:R] = total[:, N:]
 
 
 def within(pieces, high, low, out):
@@ -260,45 +260,74 @@
     return pl.when(lax.axis_index("tm") % 2 == parity)
 
 
-def first_kernel(rhs, own, inflow, high, low, diag, vec, two, pieces):
-    diag[...] = own[...] + inflow[...]
-
+EXTRA = 8
+
+
+def first_kernel(rhs, own, inflow, high, low, two, pieces):
     @on_parity(0)
     def _():
         for t in range(T):
-            value = rhs[t] / diag[t : t + 1, :]
-            vec[t] = value
-            two[t] = value
+            two[t, 0:R] = rhs[t]
+            two[t, R:] = jnp.broadcast_to(own[t : t + 1, :], (EXTRA, N))
 
     @on_parity(1)
     def _():
+        diag = own[...] + inflow[...]
         for t in range(T):
-            value = rhs[t] / diag[t : t + 1, :]
-            vec[t] = value
-            put_pieces(pieces, t, value)
+            put_pieces(pieces, t, rhs[t] / diag[t : t + 1, :])
+            two[t, R:] = jnp.ones((EXTRA, N), F32)
         to_next(pieces, high, low, two)
 
 
 def first(*args):
-    return call(first_kernel, (shape(T, N), BLOCKS, BLOCKS), [VMEM] * 5, [PIECES], flops=ONE_WAY)(*args)
+    return call(first_kernel, shape(T, R + EXTRA, N), [VMEM] * 5, [PIECES], flops=ONE_WAY)(*args)
+
+
+def start_kernel(rhs, own, inflow_odd, inflow_even, high, low, diag, vec, one, out, found, *rest):
+    *turned, pieces = rest
+
+    @on_parity(0)
+    def _():
+        diag[...] = own[...] + inflow_even[...]
+
+    @on_parity(1)
+    def _():
+        diag[...] = own[...] + inflow_odd[...]
+
+    for t in range(T):
+        value = rhs[t] / diag[t : t + 1, :]
+        vec[t] = value
+        put_pieces(pieces, t, value)
+
+    @on_parity(0)
+    def _():
+        to_next(pieces, high, low, one)
+
+    @on_parity(1)
+    def _():
+        one[...] = vec[...]
+
+    turn(high, low, *turned)
+    within(pieces, high, low, out)
+    h, l = moments(vec, rhs)
+    found[0, 0] = h
+    found[0, 1] = l
+
+
+def start(*args):
+    return call(
+        start_kernel,
+        (shape(T, N), BLOCKS, BLOCKS, BLOCKS, shape(1, 2, R, N), TURNED, TURNED),
+        [VMEM] * 6,
+        [PIECES],
+        flops=3 * ONE_WAY,
+    )(*args)
 
 
 def local_kernel(count, *refs):
-    vecs, (image, high, low, out, found, *more, pieces) = refs[:count], refs[count:]
+    vecs, (image, high, low, out, found, pieces) = refs[:count], refs[count:]
     for t in range(T):
         put_pieces(pieces, t, vecs[-1][t])
-    if more:
-        one, *turned = more
-
-        @on_parity(0)
-        def _():
-            to_next(pieces, high, low, one)
-
-        @on_parity(1)
-        def _():
-            one[...] = vecs[0][...]
-
-        turn(high, low, *turned)
     within(pieces, high, low, out)
     for i, vec in enumerate(vecs):
         h, l = moments(vec, image)
@@ -307,10 +336,9 @@
 
 
 def local(vecs, image, high, low):
-    more = (BLOCKS, TURNED, TURNED) if len(vecs) == 1 else ()
     return call(
         functools.partial(local_kernel, len(vecs)),
-        (BLOCKS, shape(len(vecs), 2, R, N)) + more,
+        (BLOCKS, shape(len(vecs), 2, R, N)),
         [VMEM] * (len(vecs) + 3),
         [PIECES],
         flops=2 * ONE_WAY,
@@ -324,11 +352,33 @@
     from_next(pieces, turned_high, turned_low, image)
 
 
-def step_kernel(flag, got_one, got_two, partial, diag, high, low, turned_high, turned_low, image, vec, one, two, sent, pieces):
-    add_received(flag, got_one, got_two, partial, turned_high, turned_low, image, pieces)
+def move_on(flag, diag, high, low, image, vec, one, two, sent, pieces):
     for t in range(T):
         vec[t] = image[t] / diag[t : t + 1, :]
     hand_out(flag, vec, high, low, one, two, sent, pieces)
+
+
+def second_kernel(
+    flag, ahead, got_one, got_two, partial, turned_high, turned_low, diag, high, low, image, vec, one, two, sent, pieces
+):
+    for t in range(T):
+        value = got_two[t, 0:R]
+        made = value / (got_two[t, R : R + 1] + ahead[t : t + 1, :])
+        put_pieces(pieces, t, choose(flag, got_one[t], made))
+        image[t] = partial[t] + choose(flag, value, got_one[t])
+    from_next(pieces, turned_high, turned_low, image)
+    move_on(flag, diag, high, low, image, vec, one, two, sent, pieces)
+
+
+def second_step(*args):
+    return call(second_kernel, (BLOCKS,) * 4, [VMEM] * 10, [SENT, PIECES], flops=2 * ONE_WAY)(*args)
+
+
+def step_kernel(
+    flag, got_one, got_two, partial, turned_high, turned_low, diag, high, low, image, vec, one, two, sent, pieces
+):
+    add_received(flag, got_one, got_two, partial, turned_high, turned_low, image, pieces)
+    move_on(flag, diag, high, low, image, vec, one, two, sent, pieces)
 
 
 def next_step(*args):
@@ -413,11 +463,6 @@
     return call(result_kernel, (shape(T, R, N), shape(T, R, N)), [VMEM] * 8)(parts, *vecs, *images)
 
 
-def shift(value, steps):
-    count = lax.axis_size("tm")
-    return lax.ppermute(value, "tm", [(i, (i + steps) % count) for i in range(count)])
-
-
 def all_parts(value):
     count = lax.axis_size("tm")
     spread = lax.all_to_all(jnp.broadcast_to(value[None], (count,) + value.shape), "tm", 0, 0)
@@ -436,15 +481,16 @@
 def shards(weights, pattern, shift_reg, rhs):
     flag = jnp.broadcast_to((1 - lax.axis_index("tm") % 2).astype(F32), (8, N))
     flag, pattern = lax.optimization_barrier((flag, pattern))
-    inflow = shift(ahead_sums(pattern, weights), 1)
+    ahead = ahead_sums(pattern, weights)
+    inflow_odd, inflow_even = swap_within(ahead), swap_across(ahead)
     high, low, own = band_pieces(pattern, weights, shift_reg)
-    diag, vec, two = first(rhs, own, inflow, high, low)
-    got_two = swap_across(two)
-    partial, part, one, *turned = local([vec], rhs, high, low)
+    got_two = swap_across(first(rhs, own, inflow_odd, high, low))
+    diag, vec, one, partial, part, *turned = start(rhs, own, inflow_odd, inflow_even, high, low)
     got = swap_within(one), got_two
     vecs, images, found = [vec], [rhs], [part]
     for step in range(2):
-        image, vec, one, two = next_step(flag, *got, partial, diag, high, low, *turned)
+        given = (flag, *got) if step else (flag, ahead, *got)
+        image, vec, one, two = (next_step if step else second_step)(*given, partial, *turned, diag, high, low)
         got = swap_within(one), swap_across(two)
         images.append(image)
         vecs.append(vec)

time: 68.5 us -> 68.9 us (level)
  starting transfers between devices: 10.9 us -> 16.1 us
  waiting for transfers between devices: 26 us -> 23.1 us
  blocking collectives: 17.6 us -> 15.6 us
    ppermute x3 -> x4, waiting for transfers between devices: 4.07 us -> 12.6 us  [swap_within(): lax.ppermute(value, 'tm', [(i, i ^ 1) for i in range(lax.axis_size('tm'))])]
    ppermute x3 -> x4, starting transfers between devices: 8.66 us -> 15.5 us  [swap_across(): lax.ppermute(value, 'tm', [(i, (i + (1 if i % 2 else -1)) % count) for i...]
    ppermute x1 -> x0, waiting for transfers between devices: 6.09 us -> none  [shift(): lax.ppermute(value, 'tm', [(i, (i + steps) % count) for i in range(count)])]
    ppermute x3 -> x4, waiting for transfers between devices: 15.8 us -> 10.5 us  [swap_across(): lax.ppermute(value, 'tm', [(i, (i + (1 if i % 2 else -1)) % count) for i...]
    pallas_call x1 -> x3, Pallas kernels: 0.05 us -> 2.81 us  [the longest x1 1.79 us: start(): call(start_kernel, (shape(T, N), BLOCKS, BLOCKS, BLOCKS, shape(1, 2, R, N...]
    all_to_all x1, blocking collectives: 17.6 us -> 15.6 us  [all_parts(): lax.all_to_all(jnp.broadcast_to(value[None], (count,) + value.shape), 'tm...]
    pallas_call x3 -> x2, Pallas kernels: 4.17 us -> 2.4 us  [local(): call(functools.partial(local_kernel, len(vecs)), (BLOCKS, shape(len(vecs)...]
    ppermute x1 -> x0, starting transfers between devices: 1.65 us -> none  [shift(): lax.ppermute(value, 'tm', [(i, (i + steps) % count) for i in range(count)])]
  transfers between devices with their start and end apart: 7 -> 8, of which waited for: 7 -> 7; matrix products, arithmetic and copies ran while one was open for 0% -> 0% of each run, Pallas kernels for 10% -> 10%
where the time goes in v9:
time: 68.9 us; the launch traced here: 68.7 us
  waiting for transfers between devices  23.1 us (34%)
  starting transfers between devices  16.1 us (23%)
  blocking collectives  15.6 us (23%)
  Pallas kernels  13 us (19%)
  between operations  0.76 us (1%)
    all_to_all x1, blocking collectives, all_parts(): lax.all_to_all(jnp.broadcast_to(value[None], (count,) + value.shape), 'tm...  15.6 us
    ppermute x4, starting transfers between devices, swap_across(): lax.ppermute(value, 'tm', [(i, (i + (1 if i % 2 else -1)) % count) for i...  15.5 us
    ppermute x4, waiting for transfers between devices, swap_within(): lax.ppermute(value, 'tm', [(i, i ^ 1) for i in range(lax.axis_size('tm'))])  12.6 us
    ppermute x4, waiting for transfers between devices, swap_across(): lax.ppermute(value, 'tm', [(i, (i + (1 if i % 2 else -1)) % count) for i...  10.5 us
    pallas_call x1, Pallas kernels, band_pieces(): call(band_kernel, (shape(*BAND, dtype=BF16), shape(*BAND, dtype=BF16), sh...  2.85 us
    pallas_call x2, Pallas kernels, local(): call(functools.partial(local_kernel, len(vecs)), (BLOCKS, shape(len(vecs)...  2.4 us
    pallas_call x1, Pallas kernels, ahead_sums(): call(ahead_kernel, shape(T, N), [HBM, HBM], [pltpu.SMEM((T, T), jnp.int32...  1.83 us
    pallas_call x1, Pallas kernels, start(): call(start_kernel, (shape(T, N), BLOCKS, BLOCKS, BLOCKS, shape(1, 2, R, N...  1.79 us
  transfers between devices with their start and end apart: 8, of which 7 were waited for; matrix products, arithmetic and copies ran while one was open for 0% of the time, Pallas kernels for 10%

profile of v9, /device:TPU:4, one launch (start us, length us, event | category | flops | bytes accessed | tf_op | source)
XLA Modules:
  0.0 68.7 jit_solution(3570337972587483096)
XLA Ops:
  0.7 1.8 %shard_map.59.ahead = f32[8,128]{1,0:T(8,128)S(1)} custom-call(s32[8,8]{1,0:T(8,128)} %pattern.1, f32[8,8,128,128]{3,2,1,0:T(8,128)} %weights.3), custom_call_target="tpu_custom_call" | custom-call | flops 4194304 | bytes 4194304 | tf_op jit(solution)/shard_map/pallas_call | solution.py:98
  2.5 9.0 %collective-permute-start.1 = (f32[8,128]{1,0:T(8,128)S(1)}, f32[8,128]{1,0:T(8,128)S(1)}, u32[]{:S(2)}, u32[]{:S(2)}) collective-permute-start(f32[8,128]{1,0:T(8,128)S(1)} %shard_map.59.ahead), channel_id=1, source_target_pairs={{0,63},{1,2},{2,1},{3,4},{4,3},{5,6},{6,5},{7,8},{8,7},{9,10},{10,... | collective-permute-start | bytes 12296 | tf_op jit(solution)/shard_map/ppermute | solution.py:478
  11.5 2.8 %shard_map.60 = (bf16[4,256,1152]{2,1,0:T(8,128)(2,1)S(1)}, bf16[4,256,1152]{2,1,0:T(8,128)(2,1)S(1)}, f32[8,128]{1,0:T(8,128)S(1)}) custom-call(s32[8,8]{1,0:T(8,128)} %pattern.1, f32[8,8,128,128]{3,2,1,0:T(8,128)} %weights.3, f32[8,128]{1,0:T(8,128)} %reg.1), custom_call_target="tpu_custom_call" | custom-call | flops 2147483648 | bytes 8388608 | tf_op jit(solution)/shard_map/pallas_call | solution.py:154
  14.4 0.7 %collective-permute-done.inflow_odd.inflow = f32[8,128]{1,0:T(8,128)S(1)} collective-permute-done((f32[8,128]{1,0:T(8,128)S(1)}, f32[8,128]{1,0:T(8,128)S(1)}, u32[]{:S(2)}, u32[]{:S(2)}) %collective-permute-start) | collective-permute-done | bytes 4128 | tf_op jit(solution)/shard_map/ppermute | solution.py:473
  15.2 1.1 %collective-permute-start.3 = (f32[8,72,128]{2,1,0:T(8,128)S(1)}, f32[8,72,128]{2,1,0:T(8,128)S(1)}, u32[]{:S(2)}, u32[]{:S(2)}) collective-permute-start(f32[8,72,128]{2,1,0:T(8,128)S(1)} %shard_map.62), channel_id=1, source_target_pairs={{0,63},{1,2},{2,1},{3,4},{4,3},{5,6},{6,5},{7,8},{8,7},{9,10},{10,... | collective-permute-start | bytes 884744 | tf_op jit(solution)/shard_map/ppermute | solution.py:478
  16.3 1.8 %shard_map.61 = (f32[8,128]{1,0:T(8,128)S(1)}, f32[8,64,128]{2,1,0:T(8,128)S(1)}, f32[8,64,128]{2,1,0:T(8,128)S(1)}, f32[8,64,128]{2,1,0:T(8,128)S(1)}, f32[1,2,...) custom-call(f32[8,64,128]{2,1,0:T(8,128)S(1)} %copy-done, ...), custom_call_target="tpu_custom_call" | custom-call | flops 754974720 | tf_op jit(solution)/shard_map/pallas_call | solution.py:318
  18.1 0.4 collective-permute-start.2
  18.5 6.9 %collective-permute-done.2.got_one = f32[8,64,128]{2,1,0:T(8,128)S(1)} collective-permute-done((f32[8,64,128]{2,1,0:T(8,128)S(1)}, f32[8,64,128]{2,1,0:T(8,128)S(1)}, u32[]{:S(2)}, u32[]{:S(2)}) %collective-permute-start.2) | collective-permute-done | bytes 262176 | tf_op jit(solution)/shard_map/ppermute | solution.py:473
  25.4 1.8 %collective-permute-done.3.got_two = f32[8,72,128]{2,1,0:T(8,128)S(1)} collective-permute-done((f32[8,72,128]{2,1,0:T(8,128)S(1)}, f32[8,72,128]{2,1,0:T(8,128)S(1)}, u32[]{:S(2)}, u32[]{:S(2)}) %collective-permute-start.3) | collective-permute-done | bytes 294944 | tf_op jit(solution)/shard_map/ppermute | solution.py:478
  27.2 1.0 %shard_map.63 = (f32[8,64,128]{2,1,0:T(8,128)S(1)}, f32[8,64,128]{2,1,0:T(8,128)S(1)}, f32[8,64,128]{2,1,0:T(8,128)S(1)}, f32[8,64,128]{2,1,0:T(8,128)S(1)}) custom-call(f32[8,128]{1,0:T(8,128)S(1)} %broadcast_in_dim.11.flag, f32[8,128]{1,0:T(8,128)S(1)} %shard_map.59.ahead, f32[8,64,128]{2,1,0:T(8,128)S(1)} %collective-permute-done.2.got_one, ...), custom_call_target="tpu_custom_call" | custom-call | flops 503316480 | tf_op jit(solution)/shard_map/pallas_call | solution.py:374
  28.2 0.1 collective-permute-start.4
  28.3 2.7 %collective-permute-start.5 = (f32[8,64,128]{2,1,0:T(8,128)S(1)}, f32[8,64,128]{2,1,0:T(8,128)S(1)}, u32[]{:S(2)}, u32[]{:S(2)}) collective-permute-start(f32[8,64,128]{2,1,0:T(8,128)S(1)} %get-tuple-element.39), channel_id=1, source_target_pairs={{0,63},{1,2},{2,1},{3,4},{4,3},{5,6},{6,5},{7,8},{8,7},{9,10},{10,... | collective-permute-start | bytes 786440 | tf_op jit(solution)/shard_map/ppermute | solution.py:478
  31.0 1.2 %shard_map.64 = (f32[8,64,128]{2,1,0:T(8,128)S(1)}, f32[2,2,64,128]{3,2,1,0:T(8,128)S(1)}) custom-call(f32[8,64,128]{2,1,0:T(8,128)S(1)} %get-tuple-element.40.refs_0_.v0, f32[8,64,128]{2,1,0:T(8,128)S(1)} %get-tuple-element.41.refs_1_.v1, f32[8,64,128]{2,1,0:T(8,128)S(1)} %get-tuple-element.42.refs_2_.y1, ...), custom_call_target="tpu_custom_call" | custom-call | flops 503316480 | tf_op jit(solution)/shard_map/pallas_call | solution.py:339
  32.2 2.5 %collective-permute-done.4.got_one = f32[8,64,128]{2,1,0:T(8,128)S(1)} collective-permute-done((f32[8,64,128]{2,1,0:T(8,128)S(1)}, f32[8,64,128]{2,1,0:T(8,128)S(1)}, u32[]{:S(2)}, u32[]{:S(2)}) %collective-permute-start.4) | collective-permute-done | bytes 262176 | tf_op jit(solution)/shard_map/ppermute | solution.py:473
  34.7 4.3 %collective-permute-done.5.got_two = f32[8,64,128]{2,1,0:T(8,128)S(1)} collective-permute-done((f32[8,64,128]{2,1,0:T(8,128)S(1)}, f32[8,64,128]{2,1,0:T(8,128)S(1)}, u32[]{:S(2)}, u32[]{:S(2)}) %collective-permute-start.5) | collective-permute-done | bytes 262176 | tf_op jit(solution)/shard_map/ppermute | solution.py:478
  39.0 1.0 %shard_map.65 = (f32[8,64,128]{2,1,0:T(8,128)S(1)}, f32[8,64,128]{2,1,0:T(8,128)S(1)}, f32[8,64,128]{2,1,0:T(8,128)S(1)}, f32[8,64,128]{2,1,0:T(8,128)S(1)}) custom-call(f32[8,128]{1,0:T(8,128)S(1)} %broadcast_in_dim.11.flag, f32[8,64,128]{2,1,0:T(8,128)S(1)} %collective-permute-done.4.got_one, f32[8,64,128]{2,1,0:T(8,128)S(1)} %collective-permute-done.5.got_two, ...), custom_call_target="tpu_custom_call" | custom-call | flops 503316480 | tf_op jit(solution)/shard_map/pallas_call | solution.py:385
  40.0 0.1 collective-permute-start.6
  40.1 2.7 %collective-permute-start.7 = (f32[8,64,128]{2,1,0:T(8,128)S(1)}, f32[8,64,128]{2,1,0:T(8,128)S(1)}, u32[]{:S(2)}, u32[]{:S(2)}) collective-permute-start(f32[8,64,128]{2,1,0:T(8,128)S(1)} %get-tuple-element.45), channel_id=1, source_target_pairs={{0,63},{1,2},{2,1},{3,4},{4,3},{5,6},{6,5},{7,8},{8,7},{9,10},{10,... | collective-permute-start | bytes 786440 | tf_op jit(solution)/shard_map/ppermute | solution.py:478
  42.8 1.2 %shard_map.66 = (f32[8,64,128]{2,1,0:T(8,128)S(1)}, f32[3,2,64,128]{3,2,1,0:T(8,128)S(1)}) custom-call(f32[8,64,128]{2,1,0:T(8,128)S(1)} %get-tuple-element.40.refs_0_.v0, f32[8,64,128]{2,1,0:T(8,128)S(1)} %get-tuple-element.41.refs_1_.v1, f32[8,64,128]{2,1,0:T(8,128)S(1)} %get-tuple-element.46.refs_2_.v2, f32[8,64,128]{2,1,0:T(8,128)S(1)} %get-tuple-element.47.refs_3_.y2, ...), custom_call_target="tpu_custom_call" | custom-call | flops 503316480 | tf_op jit(solution)/shard_map/pallas_call | solution.py:339
  44.0 2.5 %collective-permute-done.6.got_one = f32[8,64,128]{2,1,0:T(8,128)S(1)} collective-permute-done((f32[8,64,128]{2,1,0:T(8,128)S(1)}, f32[8,64,128]{2,1,0:T(8,128)S(1)}, u32[]{:S(2)}, u32[]{:S(2)}) %collective-permute-start.6) | collective-permute-done | bytes 262176 | tf_op jit(solution)/shard_map/ppermute | solution.py:473
  46.5 4.3 %collective-permute-done.7.got_two = f32[8,64,128]{2,1,0:T(8,128)S(1)} collective-permute-done((f32[8,64,128]{2,1,0:T(8,128)S(1)}, f32[8,64,128]{2,1,0:T(8,128)S(1)}, u32[]{:S(2)}, u32[]{:S(2)}) %collective-permute-start.7) | collective-permute-done | bytes 262176 | tf_op jit(solution)/shard_map/ppermute | solution.py:478
  50.8 0.8 %shard_map.67 = (f32[8,64,128]{2,1,0:T(8,128)S(1)}, f32[1,640]{1,0:T(1,128)S(1)}) custom-call(f32[8,128]{1,0:T(8,128)S(1)} %broadcast_in_dim.11.flag, f32[8,64,128]{2,1,0:T(8,128)S(1)} %collective-permute-done.6.got_one, f32[8,64,128]{2,1,0:T(8,128)S(1)} %collective-permute-done.7.got_two, f32[8,64,128]{2,1,0:T(8,128)S(1)} %get-tuple-element.48.partial, ...), custom_call_target="tpu_custom_call" | custom-call | flops 251658240 | tf_op jit(solution)/shard_map/pallas_call | solution.py:415
  51.8 15.6 %all_to_all.5 = f32[64,1,640]{2,1,0:T(1,128)S(1)} all-to-all(f32[64,1,640]{2,1,0:T(1,128)S(1)} %broadcast_in_dim.13), channel_id=1, replica_groups=mesh['scen'=4,'tm'=64] {'tm'}, dimensions={0} | all-to-all | bytes 327680 | tf_op jit(solution)/shard_map/all_to_all | solution.py:468
  67.4 1.3 %shard_map.68 = (f32[8,64,128]{2,1,0:T(8,128)}, f32[8,64,128]{2,1,0:T(8,128)}) custom-call(f32[64,640]{1,0:T(8,128)S(1)} %bitcast.3, f32[8,64,128]{2,1,0:T(8,128)S(1)} %get-tuple-element.40.refs_0_.v0, f32[8,64,128]{2,1,0:T(8,128)S(1)} %get-tuple-element.41.refs_1_.v1, f32[8,64,128]{2,1,0:T(8,128)S(1)} %get-tuple-element.46.refs_2_.v2, ...), custom_call_target="tpu_custom_call" | custom-call | tf_op jit(solution)/shard_map/pallas_call | solution.py:463
  (9 shorter events, 0.1 us)
Async XLA Ops:
  2.5 12.6 %copy-start = (f32[8,64,128]{2,1,0:T(8,128)S(1)}, f32[8,64,128]{2,1,0:T(8,128)}, u32[]{:S(2)}) copy-start(f32[8,64,128]{2,1,0:T(8,128)} %y0.1) | copy-start | bytes 786436
  2.5 13.8 %collective-permute-start.1 = (f32[8,128]{1,0:T(8,128)S(1)}, f32[8,128]{1,0:T(8,128)S(1)}, u32[]{:S(2)}, u32[]{:S(2)}) collective-permute-start(f32[8,128]{1,0:T(8,128)S(1)} %shard_map.59.ahead), channel_id=1, source_target_pairs={{0,63},{1,2},{2,1},{3,4},{4,3},{5,6},{6,5},{7,8},{8,7},{9,10},{10,... | collective-permute-start | bytes 12296 | tf_op jit(solution)/shard_map/ppermute | solution.py:478
  11.5 3.6 %collective-permute-start = (f32[8,128]{1,0:T(8,128)S(1)}, f32[8,128]{1,0:T(8,128)S(1)}, u32[]{:S(2)}, u32[]{:S(2)}) collective-permute-start(f32[8,128]{1,0:T(8,128)S(1)} %shard_map.59.ahead), channel_id=1, source_target_pairs={{0,1},{1,0},{2,3},{3,2},{4,5},{5,4},{6,7},{7,6},{8,9},{9,8},{10,11... | collective-permute-start | bytes 12296 | tf_op jit(solution)/shard_map/ppermute | solution.py:473
  15.2 12.1 %collective-permute-start.3 = (f32[8,72,128]{2,1,0:T(8,128)S(1)}, f32[8,72,128]{2,1,0:T(8,128)S(1)}, u32[]{:S(2)}, u32[]{:S(2)}) collective-permute-start(f32[8,72,128]{2,1,0:T(8,128)S(1)} %shard_map.62), channel_id=1, source_target_pairs={{0,63},{1,2},{2,1},{3,4},{4,3},{5,6},{6,5},{7,8},{8,7},{9,10},{10,... | collective-permute-start | bytes 884744 | tf_op jit(solution)/shard_map/ppermute | solution.py:478
  18.1 7.3 %collective-permute-start.2 = (f32[8,64,128]{2,1,0:T(8,128)S(1)}, f32[8,64,128]{2,1,0:T(8,128)S(1)}, u32[]{:S(2)}, u32[]{:S(2)}) collective-permute-start(f32[8,64,128]{2,1,0:T(8,128)S(1)} %get-tuple-element.33), channel_id=1, source_target_pairs={{0,1},{1,0},{2,3},{3,2},{4,5},{5,4},{6,7},{7,6},{8,9},{9,8},{10,11... | collective-permute-start | bytes 786440 | tf_op jit(solution)/shard_map/ppermute | solution.py:473
  28.2 6.5 %collective-permute-start.4 = (f32[8,64,128]{2,1,0:T(8,128)S(1)}, f32[8,64,128]{2,1,0:T(8,128)S(1)}, u32[]{:S(2)}, u32[]{:S(2)}) collective-permute-start(f32[8,64,128]{2,1,0:T(8,128)S(1)} %get-tuple-element.38), channel_id=1, source_target_pairs={{0,1},{1,0},{2,3},{3,2},{4,5},{5,4},{6,7},{7,6},{8,9},{9,8},{10,11... | collective-permute-start | bytes 786440 | tf_op jit(solution)/shard_map/ppermute | solution.py:473
  28.3 10.7 %collective-permute-start.5 = (f32[8,64,128]{2,1,0:T(8,128)S(1)}, f32[8,64,128]{2,1,0:T(8,128)S(1)}, u32[]{:S(2)}, u32[]{:S(2)}) collective-permute-start(f32[8,64,128]{2,1,0:T(8,128)S(1)} %get-tuple-element.39), channel_id=1, source_target_pairs={{0,63},{1,2},{2,1},{3,4},{4,3},{5,6},{6,5},{7,8},{8,7},{9,10},{10,... | collective-permute-start | bytes 786440 | tf_op jit(solution)/shard_map/ppermute | solution.py:478
  40.0 6.5 %collective-permute-start.6 = (f32[8,64,128]{2,1,0:T(8,128)S(1)}, f32[8,64,128]{2,1,0:T(8,128)S(1)}, u32[]{:S(2)}, u32[]{:S(2)}) collective-permute-start(f32[8,64,128]{2,1,0:T(8,128)S(1)} %get-tuple-element.44), channel_id=1, source_target_pairs={{0,1},{1,0},{2,3},{3,2},{4,5},{5,4},{6,7},{7,6},{8,9},{9,8},{10,11... | collective-permute-start | bytes 786440 | tf_op jit(solution)/shard_map/ppermute | solution.py:473
  40.1 10.7 %collective-permute-start.7 = (f32[8,64,128]{2,1,0:T(8,128)S(1)}, f32[8,64,128]{2,1,0:T(8,128)S(1)}, u32[]{:S(2)}, u32[]{:S(2)}) collective-permute-start(f32[8,64,128]{2,1,0:T(8,128)S(1)} %get-tuple-element.45), channel_id=1, source_target_pairs={{0,63},{1,2},{2,1},{3,4},{4,3},{5,6},{6,5},{7,8},{8,7},{9,10},{10,... | collective-permute-start | bytes 786440 | tf_op jit(solution)/shard_map/ppermute | solution.py:478

commit v10 on v8

--- a/solution.py
+++ b/solution.py
@@ -420,7 +420,11 @@
 
 def all_parts(value):
     count = lax.axis_size("tm")
-    spread = lax.all_to_all(jnp.broadcast_to(value[None], (count,) + value.shape), "tm", 0, 0)
+    half, quarter = count // 2, count // 8
+    turns = [*range(half + quarter, count), *range(half - quarter, half + quarter), *range(half - quarter)]
+    spread = lax.all_to_all(
+        jnp.broadcast_to(value[None], (count,) + value.shape), "tm", 0, 0, axis_index_groups=[turns]
+    )
     return spread.reshape(count, value.shape[1])
 
 

time: 68.5 us -> 67.4 us (0.984)
  blocking collectives: 17.6 us -> 16.4 us
    all_to_all x1, blocking collectives: 17.6 us -> 16.4 us  [all_parts(): lax.all_to_all(jnp.broadcast_to(value[None], (count,) + value.shape), 'tm...]
where the time goes in v10:
time: 67.4 us; the launch traced here: 67.2 us
  waiting for transfers between devices  26 us (39%)
  blocking collectives  16.4 us (24%)
  Pallas kernels  13.1 us (19%)
  starting transfers between devices  10.9 us (16%)
  between operations  0.76 us (1%)
    all_to_all x1, blocking collectives, all_parts(): lax.all_to_all(jnp.broadcast_to(value[None], (count,) + value.shape), 'tm...  16.4 us
    ppermute x3, waiting for transfers between devices, swap_across(): lax.ppermute(value, 'tm', [(i, (i + (1 if i % 2 else -1)) % count) for i...  15.8 us
    ppermute x3, starting transfers between devices, swap_across(): lax.ppermute(value, 'tm', [(i, (i + (1 if i % 2 else -1)) % count) for i...  8.66 us
    ppermute x1, waiting for transfers between devices, shift(): lax.ppermute(value, 'tm', [(i, (i + steps) % count) for i in range(count)])  6.09 us
    pallas_call x3, Pallas kernels, local(): call(functools.partial(local_kernel, len(vecs)), (BLOCKS, shape(len(vecs)...  4.17 us
    ppermute x3, waiting for transfers between devices, swap_within(): lax.ppermute(value, 'tm', [(i, i ^ 1) for i in range(lax.axis_size('tm'))])  4.07 us
    pallas_call x1, Pallas kernels, band_pieces(): call(band_kernel, (shape(*BAND, dtype=BF16), shape(*BAND, dtype=BF16), sh...  2.85 us
    pallas_call x2, Pallas kernels, next_step(): call(step_kernel, (BLOCKS,) * 4, [VMEM] * 9, [SENT, PIECES], flops=2 * ON...  2.02 us
  transfers between devices with their start and end apart: 7, of which 7 were waited for; matrix products, arithmetic and copies ran while one was open for 0% of the time, Pallas kernels for 10%

profile of v10, /device:TPU:4, one launch (start us, length us, event | category | flops | bytes accessed | tf_op | source)
XLA Modules:
  0.0 67.2 jit_solution(17738578350477457450)
XLA Ops:
  0.7 1.8 %shard_map.60 = f32[8,128]{1,0:T(8,128)S(1)} custom-call(s32[8,8]{1,0:T(8,128)} %pattern.1, f32[8,8,128,128]{3,2,1,0:T(8,128)} %weights.3), custom_call_target="tpu_custom_call" | custom-call | flops 4194304 | bytes 4194304 | tf_op jit(solution)/shard_map/pallas_call | solution.py:98
  2.5 1.7 %collective-permute-start = (f32[8,128]{1,0:T(8,128)S(1)}, f32[8,128]{1,0:T(8,128)S(1)}, u32[]{:S(2)}, u32[]{:S(2)}) collective-permute-start(f32[8,128]{1,0:T(8,128)S(1)} %shard_map.60), channel_id=1, source_target_pairs={{0,1},{1,2},{2,3},{3,4},{4,5},{5,6},{6,7},{7,8},{8,9},{9,10},{10,1... | collective-permute-start | bytes 12296 | tf_op jit(solution)/shard_map/ppermute | solution.py:418
  4.2 2.8 %shard_map.59 = (bf16[4,256,1152]{2,1,0:T(8,128)(2,1)S(1)}, bf16[4,256,1152]{2,1,0:T(8,128)(2,1)S(1)}, f32[8,128]{1,0:T(8,128)S(1)}) custom-call(s32[8,8]{1,0:T(8,128)} %pattern.1, f32[8,8,128,128]{3,2,1,0:T(8,128)} %weights.3, f32[8,128]{1,0:T(8,128)} %reg.1), custom_call_target="tpu_custom_call" | custom-call | flops 2147483648 | bytes 8388608 | tf_op jit(solution)/shard_map/pallas_call | solution.py:154
  7.0 6.1 %collective-permute-done.inflow = f32[8,128]{1,0:T(8,128)S(1)} collective-permute-done((f32[8,128]{1,0:T(8,128)S(1)}, f32[8,128]{1,0:T(8,128)S(1)}, u32[]{:S(2)}, u32[]{:S(2)}) %collective-permute-start) | collective-permute-done | bytes 4128 | tf_op jit(solution)/shard_map/ppermute | solution.py:418
  13.2 2.6 %collective-permute-start.2 = (f32[8,64,128]{2,1,0:T(8,128)S(1)}, f32[8,64,128]{2,1,0:T(8,128)S(1)}, u32[]{:S(2)}, u32[]{:S(2)}) collective-permute-start(f32[8,64,128]{2,1,0:T(8,128)S(1)} %get-tuple-element.36), channel_id=1, source_target_pairs={{0,63},{1,2},{2,1},{3,4},{4,3},{5,6},{6,5},{7,8},{8,7},{9,10},{10,... | collective-permute-start | bytes 786440 | tf_op jit(solution)/shard_map/ppermute | solution.py:437
  15.8 1.8 %shard_map.62 = (f32[8,64,128]{2,1,0:T(8,128)S(1)}, f32[1,2,64,128]{3,2,1,0:T(8,128)S(1)}, f32[8,64,128]{2,1,0:T(8,128)S(1)}, bf16[2560,256]{1,0:T(8,128)(2,1)S(1)}, bf16[2560,256]{1,0:T(8,128)(2,1)S(1)}) custom-call(f32[8,64,128]{2,1,0:T(8,128)S(1)} %get-tuple-element.34.refs_0_.v0, f32[8,64,128]{2,1,0:T(8,128)S(1)} %copy-done, ...), custom_call_target="tpu_custom_call" | custom-call | flops 503316480 | tf_op jit(solution)/shard_map/pallas_call | solution.py:311
  17.6 0.1 collective-permute-start.1
  17.7 7.0 %collective-permute-done.2.got_two = f32[8,64,128]{2,1,0:T(8,128)S(1)} collective-permute-done((f32[8,64,128]{2,1,0:T(8,128)S(1)}, f32[8,64,128]{2,1,0:T(8,128)S(1)}, u32[]{:S(2)}, u32[]{:S(2)}) %collective-permute-start.2) | collective-permute-done | bytes 262176 | tf_op jit(solution)/shard_map/ppermute | solution.py:437
  24.7 1.0 %shard_map.63 = (f32[8,64,128]{2,1,0:T(8,128)S(1)}, f32[8,64,128]{2,1,0:T(8,128)S(1)}, f32[8,64,128]{2,1,0:T(8,128)S(1)}, f32[8,64,128]{2,1,0:T(8,128)S(1)}) custom-call(f32[8,128]{1,0:T(8,128)S(1)} %broadcast_in_dim.11.flag, f32[8,64,128]{2,1,0:T(8,128)S(1)} %collective-permute-done.1.got_one, f32[8,64,128]{2,1,0:T(8,128)S(1)} %collective-permute-done.2.got_two, ...), custom_call_target="tpu_custom_call" | custom-call | flops 503316480 | tf_op jit(solution)/shard_map/pallas_call | solution.py:335
  25.7 0.4 collective-permute-start.3
  26.1 3.0 %collective-permute-start.4 = (f32[8,64,128]{2,1,0:T(8,128)S(1)}, f32[8,64,128]{2,1,0:T(8,128)S(1)}, u32[]{:S(2)}, u32[]{:S(2)}) collective-permute-start(f32[8,64,128]{2,1,0:T(8,128)S(1)} %get-tuple-element.42), channel_id=1, source_target_pairs={{0,63},{1,2},{2,1},{3,4},{4,3},{5,6},{6,5},{7,8},{8,7},{9,10},{10,... | collective-permute-start | bytes 786440 | tf_op jit(solution)/shard_map/ppermute | solution.py:437
  29.1 1.2 %shard_map.64 = (f32[8,64,128]{2,1,0:T(8,128)S(1)}, f32[2,2,64,128]{3,2,1,0:T(8,128)S(1)}) custom-call(f32[8,64,128]{2,1,0:T(8,128)S(1)} %get-tuple-element.34.refs_0_.v0, f32[8,64,128]{2,1,0:T(8,128)S(1)} %get-tuple-element.43.refs_1_.v1, f32[8,64,128]{2,1,0:T(8,128)S(1)} %get-tuple-element.44.refs_2_.y1, ...), custom_call_target="tpu_custom_call" | custom-call | flops 503316480 | tf_op jit(solution)/shard_map/pallas_call | solution.py:311
  30.3 1.9 %collective-permute-done.3.got_one = f32[8,64,128]{2,1,0:T(8,128)S(1)} collective-permute-done((f32[8,64,128]{2,1,0:T(8,128)S(1)}, f32[8,64,128]{2,1,0:T(8,128)S(1)}, u32[]{:S(2)}, u32[]{:S(2)}) %collective-permute-start.3) | collective-permute-done | bytes 262176 | tf_op jit(solution)/shard_map/ppermute | solution.py:432
  32.2 4.5 %collective-permute-done.4.got_two = f32[8,64,128]{2,1,0:T(8,128)S(1)} collective-permute-done((f32[8,64,128]{2,1,0:T(8,128)S(1)}, f32[8,64,128]{2,1,0:T(8,128)S(1)}, u32[]{:S(2)}, u32[]{:S(2)}) %collective-permute-start.4) | collective-permute-done | bytes 262176 | tf_op jit(solution)/shard_map/ppermute | solution.py:437
  36.7 1.0 %shard_map.65 = (f32[8,64,128]{2,1,0:T(8,128)S(1)}, f32[8,64,128]{2,1,0:T(8,128)S(1)}, f32[8,64,128]{2,1,0:T(8,128)S(1)}, f32[8,64,128]{2,1,0:T(8,128)S(1)}) custom-call(f32[8,128]{1,0:T(8,128)S(1)} %broadcast_in_dim.11.flag, f32[8,64,128]{2,1,0:T(8,128)S(1)} %collective-permute-done.3.got_one, f32[8,64,128]{2,1,0:T(8,128)S(1)} %collective-permute-done.4.got_two, ...), custom_call_target="tpu_custom_call" | custom-call | flops 503316480 | tf_op jit(solution)/shard_map/pallas_call | solution.py:335
  37.7 0.1 collective-permute-start.5
  37.8 3.1 %collective-permute-start.6 = (f32[8,64,128]{2,1,0:T(8,128)S(1)}, f32[8,64,128]{2,1,0:T(8,128)S(1)}, u32[]{:S(2)}, u32[]{:S(2)}) collective-permute-start(f32[8,64,128]{2,1,0:T(8,128)S(1)} %get-tuple-element.47), channel_id=1, source_target_pairs={{0,63},{1,2},{2,1},{3,4},{4,3},{5,6},{6,5},{7,8},{8,7},{9,10},{10,... | collective-permute-start | bytes 786440 | tf_op jit(solution)/shard_map/ppermute | solution.py:437
  40.9 1.2 %shard_map.66 = (f32[8,64,128]{2,1,0:T(8,128)S(1)}, f32[3,2,64,128]{3,2,1,0:T(8,128)S(1)}) custom-call(f32[8,64,128]{2,1,0:T(8,128)S(1)} %get-tuple-element.34.refs_0_.v0, f32[8,64,128]{2,1,0:T(8,128)S(1)} %get-tuple-element.43.refs_1_.v1, f32[8,64,128]{2,1,0:T(8,128)S(1)} %get-tuple-element.48.refs_2_.v2, f32[8,64,128]{2,1,0:T(8,128)S(1)} %get-tuple-element.49.refs_3_.y2, ...), custom_call_target="tpu_custom_call" | custom-call | flops 503316480 | tf_op jit(solution)/shard_map/pallas_call | solution.py:311
  42.1 2.1 %collective-permute-done.5.got_one = f32[8,64,128]{2,1,0:T(8,128)S(1)} collective-permute-done((f32[8,64,128]{2,1,0:T(8,128)S(1)}, f32[8,64,128]{2,1,0:T(8,128)S(1)}, u32[]{:S(2)}, u32[]{:S(2)}) %collective-permute-start.5) | collective-permute-done | bytes 262176 | tf_op jit(solution)/shard_map/ppermute | solution.py:432
  44.2 4.3 %collective-permute-done.6.got_two = f32[8,64,128]{2,1,0:T(8,128)S(1)} collective-permute-done((f32[8,64,128]{2,1,0:T(8,128)S(1)}, f32[8,64,128]{2,1,0:T(8,128)S(1)}, u32[]{:S(2)}, u32[]{:S(2)}) %collective-permute-start.6) | collective-permute-done | bytes 262176 | tf_op jit(solution)/shard_map/ppermute | solution.py:437
  48.5 0.9 %shard_map.67 = (f32[8,64,128]{2,1,0:T(8,128)S(1)}, f32[1,640]{1,0:T(1,128)S(1)}) custom-call(f32[8,128]{1,0:T(8,128)S(1)} %broadcast_in_dim.11.flag, f32[8,64,128]{2,1,0:T(8,128)S(1)} %collective-permute-done.5.got_one, f32[8,64,128]{2,1,0:T(8,128)S(1)} %collective-permute-done.6.got_two, f32[8,64,128]{2,1,0:T(8,128)S(1)} %get-tuple-element.50.partial, ...), custom_call_target="tpu_custom_call" | custom-call | flops 251658240 | tf_op jit(solution)/shard_map/pallas_call | solution.py:365
  49.4 0.1 broadcast_in_dim.13
  49.5 16.4 %all_to_all.5 = f32[64,1,640]{2,1,0:T(1,128)S(1)} all-to-all(f32[64,1,640]{2,1,0:T(1,128)S(1)} %broadcast_in_dim.13), channel_id=1, replica_groups={{40,41,42,43,44,45,46,47,48,49,50,51,52,53,54,55,56,57,58,59,60,61,62,6..., dimensions={0} | all-to-all | bytes 327680 | tf_op jit(solution)/shard_map/all_to_all | solution.py:425
  65.9 1.3 %shard_map.68 = (f32[8,64,128]{2,1,0:T(8,128)}, f32[8,64,128]{2,1,0:T(8,128)}) custom-call(f32[64,640]{1,0:T(8,128)S(1)} %bitcast.3, f32[8,64,128]{2,1,0:T(8,128)S(1)} %get-tuple-element.34.refs_0_.v0, f32[8,64,128]{2,1,0:T(8,128)S(1)} %get-tuple-element.43.refs_1_.v1, f32[8,64,128]{2,1,0:T(8,128)S(1)} %get-tuple-element.48.refs_2_.v2, ...), custom_call_target="tpu_custom_call" | custom-call | tf_op jit(solution)/shard_map/pallas_call | solution.py:413
  (7 shorter events, 0.2 us)
Async XLA Ops:
  2.5 10.6 %copy-start = (f32[8,64,128]{2,1,0:T(8,128)S(1)}, f32[8,64,128]{2,1,0:T(8,128)}, u32[]{:S(2)}) copy-start(f32[8,64,128]{2,1,0:T(8,128)} %y0.1) | copy-start | bytes 786436
  2.5 10.6 %collective-permute-start = (f32[8,128]{1,0:T(8,128)S(1)}, f32[8,128]{1,0:T(8,128)S(1)}, u32[]{:S(2)}, u32[]{:S(2)}) collective-permute-start(f32[8,128]{1,0:T(8,128)S(1)} %shard_map.60), channel_id=1, source_target_pairs={{0,1},{1,2},{2,3},{3,4},{4,5},{5,6},{6,7},{7,8},{8,9},{9,10},{10,1... | collective-permute-start | bytes 12296 | tf_op jit(solution)/shard_map/ppermute | solution.py:418
  13.2 11.5 %collective-permute-start.2 = (f32[8,64,128]{2,1,0:T(8,128)S(1)}, f32[8,64,128]{2,1,0:T(8,128)S(1)}, u32[]{:S(2)}, u32[]{:S(2)}) collective-permute-start(f32[8,64,128]{2,1,0:T(8,128)S(1)} %get-tuple-element.36), channel_id=1, source_target_pairs={{0,63},{1,2},{2,1},{3,4},{4,3},{5,6},{6,5},{7,8},{8,7},{9,10},{10,... | collective-permute-start | bytes 786440 | tf_op jit(solution)/shard_map/ppermute | solution.py:437
  17.6 7.2 %collective-permute-start.1 = (f32[8,64,128]{2,1,0:T(8,128)S(1)}, f32[8,64,128]{2,1,0:T(8,128)S(1)}, u32[]{:S(2)}, u32[]{:S(2)}) collective-permute-start(f32[8,64,128]{2,1,0:T(8,128)S(1)} %get-tuple-element.35), channel_id=1, source_target_pairs={{0,1},{1,0},{2,3},{3,2},{4,5},{5,4},{6,7},{7,6},{8,9},{9,8},{10,11... | collective-permute-start | bytes 786440 | tf_op jit(solution)/shard_map/ppermute | solution.py:432
  25.7 6.5 %collective-permute-start.3 = (f32[8,64,128]{2,1,0:T(8,128)S(1)}, f32[8,64,128]{2,1,0:T(8,128)S(1)}, u32[]{:S(2)}, u32[]{:S(2)}) collective-permute-start(f32[8,64,128]{2,1,0:T(8,128)S(1)} %get-tuple-element.41), channel_id=1, source_target_pairs={{0,1},{1,0},{2,3},{3,2},{4,5},{5,4},{6,7},{7,6},{8,9},{9,8},{10,11... | collective-permute-start | bytes 786440 | tf_op jit(solution)/shard_map/ppermute | solution.py:432
  26.1 10.6 %collective-permute-start.4 = (f32[8,64,128]{2,1,0:T(8,128)S(1)}, f32[8,64,128]{2,1,0:T(8,128)S(1)}, u32[]{:S(2)}, u32[]{:S(2)}) collective-permute-start(f32[8,64,128]{2,1,0:T(8,128)S(1)} %get-tuple-element.42), channel_id=1, source_target_pairs={{0,63},{1,2},{2,1},{3,4},{4,3},{5,6},{6,5},{7,8},{8,7},{9,10},{10,... | collective-permute-start | bytes 786440 | tf_op jit(solution)/shard_map/ppermute | solution.py:437
  37.7 6.5 %collective-permute-start.5 = (f32[8,64,128]{2,1,0:T(8,128)S(1)}, f32[8,64,128]{2,1,0:T(8,128)S(1)}, u32[]{:S(2)}, u32[]{:S(2)}) collective-permute-start(f32[8,64,128]{2,1,0:T(8,128)S(1)} %get-tuple-element.46), channel_id=1, source_target_pairs={{0,1},{1,0},{2,3},{3,2},{4,5},{5,4},{6,7},{7,6},{8,9},{9,8},{10,11... | collective-permute-start | bytes 786440 | tf_op jit(solution)/shard_map/ppermute | solution.py:432
  37.8 10.7 %collective-permute-start.6 = (f32[8,64,128]{2,1,0:T(8,128)S(1)}, f32[8,64,128]{2,1,0:T(8,128)S(1)}, u32[]{:S(2)}, u32[]{:S(2)}) collective-permute-start(f32[8,64,128]{2,1,0:T(8,128)S(1)} %get-tuple-element.47), channel_id=1, source_target_pairs={{0,63},{1,2},{2,1},{3,4},{4,3},{5,6},{6,5},{7,8},{8,7},{9,10},{10,... | collective-permute-start | bytes 786440 | tf_op jit(solution)/shard_map/ppermute | solution.py:437

commit v11 on v10

--- a/solution.py
+++ b/solution.py
@@ -420,8 +420,10 @@
 
 def all_parts(value):
     count = lax.axis_size("tm")
-    half, quarter = count // 2, count // 8
-    turns = [*range(half + quarter, count), *range(half - quarter, half + quarter), *range(half - quarter)]
+    half, eighth = count // 2, count // 8
+    last = [half - 1, half]
+    near = [i for i in range(half - eighth, half + eighth) if i not in last]
+    turns = [*range(half + eighth, count), *near, *last, *range(half - eighth)]
     spread = lax.all_to_all(
         jnp.broadcast_to(value[None], (count,) + value.shape), "tm", 0, 0, axis_index_groups=[turns]
     )

time: 67.4 us -> 67.2 us (level)
  no operation moved by 1% of the time
where the time goes in v11:
time: 67.2 us; the launch traced here: 67.1 us
  waiting for transfers between devices  26 us (39%)
  blocking collectives  16.2 us (24%)
  Pallas kernels  13.1 us (19%)
  starting transfers between devices  10.9 us (16%)
  between operations  0.76 us (1%)
    all_to_all x1, blocking collectives, all_parts(): lax.all_to_all(jnp.broadcast_to(value[None], (count,) + value.shape), 'tm...  16.2 us
    ppermute x3, waiting for transfers between devices, swap_across(): lax.ppermute(value, 'tm', [(i, (i + (1 if i % 2 else -1)) % count) for i...  15.8 us
    ppermute x3, starting transfers between devices, swap_across(): lax.ppermute(value, 'tm', [(i, (i + (1 if i % 2 else -1)) % count) for i...  8.66 us
    ppermute x1, waiting for transfers between devices, shift(): lax.ppermute(value, 'tm', [(i, (i + steps) % count) for i in range(count)])  6.09 us
    pallas_call x3, Pallas kernels, local(): call(functools.partial(local_kernel, len(vecs)), (BLOCKS, shape(len(vecs)...  4.17 us
    ppermute x3, waiting for transfers between devices, swap_within(): lax.ppermute(value, 'tm', [(i, i ^ 1) for i in range(lax.axis_size('tm'))])  4.07 us
    pallas_call x1, Pallas kernels, band_pieces(): call(band_kernel, (shape(*BAND, dtype=BF16), shape(*BAND, dtype=BF16), sh...  2.85 us
    pallas_call x2, Pallas kernels, next_step(): call(step_kernel, (BLOCKS,) * 4, [VMEM] * 9, [SENT, PIECES], flops=2 * ON...  2.02 us
  transfers between devices with their start and end apart: 7, of which 7 were waited for; matrix products, arithmetic and copies ran while one was open for 0% of the time, Pallas kernels for 10%

profile of v11, /device:TPU:4, one launch (start us, length us, event | category | flops | bytes accessed | tf_op | source)
XLA Modules:
  0.0 67.1 jit_solution(16546419989844691954)
XLA Ops:
  0.7 1.8 %shard_map.60 = f32[8,128]{1,0:T(8,128)S(1)} custom-call(s32[8,8]{1,0:T(8,128)} %pattern.1, f32[8,8,128,128]{3,2,1,0:T(8,128)} %weights.3), custom_call_target="tpu_custom_call" | custom-call | flops 4194304 | bytes 4194304 | tf_op jit(solution)/shard_map/pallas_call | solution.py:98
  2.5 1.7 %collective-permute-start = (f32[8,128]{1,0:T(8,128)S(1)}, f32[8,128]{1,0:T(8,128)S(1)}, u32[]{:S(2)}, u32[]{:S(2)}) collective-permute-start(f32[8,128]{1,0:T(8,128)S(1)} %shard_map.60), channel_id=1, source_target_pairs={{0,1},{1,2},{2,3},{3,4},{4,5},{5,6},{6,7},{7,8},{8,9},{9,10},{10,1... | collective-permute-start | bytes 12296 | tf_op jit(solution)/shard_map/ppermute | solution.py:418
  4.2 2.8 %shard_map.59 = (bf16[4,256,1152]{2,1,0:T(8,128)(2,1)S(1)}, bf16[4,256,1152]{2,1,0:T(8,128)(2,1)S(1)}, f32[8,128]{1,0:T(8,128)S(1)}) custom-call(s32[8,8]{1,0:T(8,128)} %pattern.1, f32[8,8,128,128]{3,2,1,0:T(8,128)} %weights.3, f32[8,128]{1,0:T(8,128)} %reg.1), custom_call_target="tpu_custom_call" | custom-call | flops 2147483648 | bytes 8388608 | tf_op jit(solution)/shard_map/pallas_call | solution.py:154
  7.0 6.1 %collective-permute-done.inflow = f32[8,128]{1,0:T(8,128)S(1)} collective-permute-done((f32[8,128]{1,0:T(8,128)S(1)}, f32[8,128]{1,0:T(8,128)S(1)}, u32[]{:S(2)}, u32[]{:S(2)}) %collective-permute-start) | collective-permute-done | bytes 4128 | tf_op jit(solution)/shard_map/ppermute | solution.py:418
  13.2 2.6 %collective-permute-start.2 = (f32[8,64,128]{2,1,0:T(8,128)S(1)}, f32[8,64,128]{2,1,0:T(8,128)S(1)}, u32[]{:S(2)}, u32[]{:S(2)}) collective-permute-start(f32[8,64,128]{2,1,0:T(8,128)S(1)} %get-tuple-element.36), channel_id=1, source_target_pairs={{0,63},{1,2},{2,1},{3,4},{4,3},{5,6},{6,5},{7,8},{8,7},{9,10},{10,... | collective-permute-start | bytes 786440 | tf_op jit(solution)/shard_map/ppermute | solution.py:439
  15.8 1.8 %shard_map.62 = (f32[8,64,128]{2,1,0:T(8,128)S(1)}, f32[1,2,64,128]{3,2,1,0:T(8,128)S(1)}, f32[8,64,128]{2,1,0:T(8,128)S(1)}, bf16[2560,256]{1,0:T(8,128)(2,1)S(1)}, bf16[2560,256]{1,0:T(8,128)(2,1)S(1)}) custom-call(f32[8,64,128]{2,1,0:T(8,128)S(1)} %get-tuple-element.34.refs_0_.v0, f32[8,64,128]{2,1,0:T(8,128)S(1)} %copy-done, ...), custom_call_target="tpu_custom_call" | custom-call | flops 503316480 | tf_op jit(solution)/shard_map/pallas_call | solution.py:311
  17.6 0.1 collective-permute-start.1
  17.7 7.0 %collective-permute-done.2.got_two = f32[8,64,128]{2,1,0:T(8,128)S(1)} collective-permute-done((f32[8,64,128]{2,1,0:T(8,128)S(1)}, f32[8,64,128]{2,1,0:T(8,128)S(1)}, u32[]{:S(2)}, u32[]{:S(2)}) %collective-permute-start.2) | collective-permute-done | bytes 262176 | tf_op jit(solution)/shard_map/ppermute | solution.py:439
  24.7 1.0 %shard_map.63 = (f32[8,64,128]{2,1,0:T(8,128)S(1)}, f32[8,64,128]{2,1,0:T(8,128)S(1)}, f32[8,64,128]{2,1,0:T(8,128)S(1)}, f32[8,64,128]{2,1,0:T(8,128)S(1)}) custom-call(f32[8,128]{1,0:T(8,128)S(1)} %broadcast_in_dim.11.flag, f32[8,64,128]{2,1,0:T(8,128)S(1)} %collective-permute-done.1.got_one, f32[8,64,128]{2,1,0:T(8,128)S(1)} %collective-permute-done.2.got_two, ...), custom_call_target="tpu_custom_call" | custom-call | flops 503316480 | tf_op jit(solution)/shard_map/pallas_call | solution.py:335
  25.7 0.4 collective-permute-start.3
  26.1 3.0 %collective-permute-start.4 = (f32[8,64,128]{2,1,0:T(8,128)S(1)}, f32[8,64,128]{2,1,0:T(8,128)S(1)}, u32[]{:S(2)}, u32[]{:S(2)}) collective-permute-start(f32[8,64,128]{2,1,0:T(8,128)S(1)} %get-tuple-element.42), channel_id=1, source_target_pairs={{0,63},{1,2},{2,1},{3,4},{4,3},{5,6},{6,5},{7,8},{8,7},{9,10},{10,... | collective-permute-start | bytes 786440 | tf_op jit(solution)/shard_map/ppermute | solution.py:439
  29.1 1.2 %shard_map.64 = (f32[8,64,128]{2,1,0:T(8,128)S(1)}, f32[2,2,64,128]{3,2,1,0:T(8,128)S(1)}) custom-call(f32[8,64,128]{2,1,0:T(8,128)S(1)} %get-tuple-element.34.refs_0_.v0, f32[8,64,128]{2,1,0:T(8,128)S(1)} %get-tuple-element.43.refs_1_.v1, f32[8,64,128]{2,1,0:T(8,128)S(1)} %get-tuple-element.44.refs_2_.y1, ...), custom_call_target="tpu_custom_call" | custom-call | flops 503316480 | tf_op jit(solution)/shard_map/pallas_call | solution.py:311
  30.3 1.9 %collective-permute-done.3.got_one = f32[8,64,128]{2,1,0:T(8,128)S(1)} collective-permute-done((f32[8,64,128]{2,1,0:T(8,128)S(1)}, f32[8,64,128]{2,1,0:T(8,128)S(1)}, u32[]{:S(2)}, u32[]{:S(2)}) %collective-permute-start.3) | collective-permute-done | bytes 262176 | tf_op jit(solution)/shard_map/ppermute | solution.py:434
  32.2 4.5 %collective-permute-done.4.got_two = f32[8,64,128]{2,1,0:T(8,128)S(1)} collective-permute-done((f32[8,64,128]{2,1,0:T(8,128)S(1)}, f32[8,64,128]{2,1,0:T(8,128)S(1)}, u32[]{:S(2)}, u32[]{:S(2)}) %collective-permute-start.4) | collective-permute-done | bytes 262176 | tf_op jit(solution)/shard_map/ppermute | solution.py:439
  36.7 1.0 %shard_map.65 = (f32[8,64,128]{2,1,0:T(8,128)S(1)}, f32[8,64,128]{2,1,0:T(8,128)S(1)}, f32[8,64,128]{2,1,0:T(8,128)S(1)}, f32[8,64,128]{2,1,0:T(8,128)S(1)}) custom-call(f32[8,128]{1,0:T(8,128)S(1)} %broadcast_in_dim.11.flag, f32[8,64,128]{2,1,0:T(8,128)S(1)} %collective-permute-done.3.got_one, f32[8,64,128]{2,1,0:T(8,128)S(1)} %collective-permute-done.4.got_two, ...), custom_call_target="tpu_custom_call" | custom-call | flops 503316480 | tf_op jit(solution)/shard_map/pallas_call | solution.py:335
  37.7 0.1 collective-permute-start.5
  37.8 3.1 %collective-permute-start.6 = (f32[8,64,128]{2,1,0:T(8,128)S(1)}, f32[8,64,128]{2,1,0:T(8,128)S(1)}, u32[]{:S(2)}, u32[]{:S(2)}) collective-permute-start(f32[8,64,128]{2,1,0:T(8,128)S(1)} %get-tuple-element.47), channel_id=1, source_target_pairs={{0,63},{1,2},{2,1},{3,4},{4,3},{5,6},{6,5},{7,8},{8,7},{9,10},{10,... | collective-permute-start | bytes 786440 | tf_op jit(solution)/shard_map/ppermute | solution.py:439
  40.9 1.2 %shard_map.66 = (f32[8,64,128]{2,1,0:T(8,128)S(1)}, f32[3,2,64,128]{3,2,1,0:T(8,128)S(1)}) custom-call(f32[8,64,128]{2,1,0:T(8,128)S(1)} %get-tuple-element.34.refs_0_.v0, f32[8,64,128]{2,1,0:T(8,128)S(1)} %get-tuple-element.43.refs_1_.v1, f32[8,64,128]{2,1,0:T(8,128)S(1)} %get-tuple-element.48.refs_2_.v2, f32[8,64,128]{2,1,0:T(8,128)S(1)} %get-tuple-element.49.refs_3_.y2, ...), custom_call_target="tpu_custom_call" | custom-call | flops 503316480 | tf_op jit(solution)/shard_map/pallas_call | solution.py:311
  42.1 2.1 %collective-permute-done.5.got_one = f32[8,64,128]{2,1,0:T(8,128)S(1)} collective-permute-done((f32[8,64,128]{2,1,0:T(8,128)S(1)}, f32[8,64,128]{2,1,0:T(8,128)S(1)}, u32[]{:S(2)}, u32[]{:S(2)}) %collective-permute-start.5) | collective-permute-done | bytes 262176 | tf_op jit(solution)/shard_map/ppermute | solution.py:434
  44.2 4.3 %collective-permute-done.6.got_two = f32[8,64,128]{2,1,0:T(8,128)S(1)} collective-permute-done((f32[8,64,128]{2,1,0:T(8,128)S(1)}, f32[8,64,128]{2,1,0:T(8,128)S(1)}, u32[]{:S(2)}, u32[]{:S(2)}) %collective-permute-start.6) | collective-permute-done | bytes 262176 | tf_op jit(solution)/shard_map/ppermute | solution.py:439
  48.5 0.9 %shard_map.67 = (f32[8,64,128]{2,1,0:T(8,128)S(1)}, f32[1,640]{1,0:T(1,128)S(1)}) custom-call(f32[8,128]{1,0:T(8,128)S(1)} %broadcast_in_dim.11.flag, f32[8,64,128]{2,1,0:T(8,128)S(1)} %collective-permute-done.5.got_one, f32[8,64,128]{2,1,0:T(8,128)S(1)} %collective-permute-done.6.got_two, f32[8,64,128]{2,1,0:T(8,128)S(1)} %get-tuple-element.50.partial, ...), custom_call_target="tpu_custom_call" | custom-call | flops 251658240 | tf_op jit(solution)/shard_map/pallas_call | solution.py:365
  49.4 0.1 broadcast_in_dim.13
  49.5 16.2 %all_to_all.5 = f32[64,1,640]{2,1,0:T(1,128)S(1)} all-to-all(f32[64,1,640]{2,1,0:T(1,128)S(1)} %broadcast_in_dim.13), channel_id=1, replica_groups={{40,41,42,43,44,45,46,47,48,49,50,51,52,53,54,55,56,57,58,59,60,61,62,6..., dimensions={0} | all-to-all | bytes 327680 | tf_op jit(solution)/shard_map/all_to_all | solution.py:427
  65.7 1.3 %shard_map.68 = (f32[8,64,128]{2,1,0:T(8,128)}, f32[8,64,128]{2,1,0:T(8,128)}) custom-call(f32[64,640]{1,0:T(8,128)S(1)} %bitcast.3, f32[8,64,128]{2,1,0:T(8,128)S(1)} %get-tuple-element.34.refs_0_.v0, f32[8,64,128]{2,1,0:T(8,128)S(1)} %get-tuple-element.43.refs_1_.v1, f32[8,64,128]{2,1,0:T(8,128)S(1)} %get-tuple-element.48.refs_2_.v2, ...), custom_call_target="tpu_custom_call" | custom-call | tf_op jit(solution)/shard_map/pallas_call | solution.py:413
  (7 shorter events, 0.2 us)
Async XLA Ops:
  2.5 10.6 %copy-start = (f32[8,64,128]{2,1,0:T(8,128)S(1)}, f32[8,64,128]{2,1,0:T(8,128)}, u32[]{:S(2)}) copy-start(f32[8,64,128]{2,1,0:T(8,128)} %y0.1) | copy-start | bytes 786436
  2.5 10.6 %collective-permute-start = (f32[8,128]{1,0:T(8,128)S(1)}, f32[8,128]{1,0:T(8,128)S(1)}, u32[]{:S(2)}, u32[]{:S(2)}) collective-permute-start(f32[8,128]{1,0:T(8,128)S(1)} %shard_map.60), channel_id=1, source_target_pairs={{0,1},{1,2},{2,3},{3,4},{4,5},{5,6},{6,7},{7,8},{8,9},{9,10},{10,1... | collective-permute-start | bytes 12296 | tf_op jit(solution)/shard_map/ppermute | solution.py:418
  13.2 11.5 %collective-permute-start.2 = (f32[8,64,128]{2,1,0:T(8,128)S(1)}, f32[8,64,128]{2,1,0:T(8,128)S(1)}, u32[]{:S(2)}, u32[]{:S(2)}) collective-permute-start(f32[8,64,128]{2,1,0:T(8,128)S(1)} %get-tuple-element.36), channel_id=1, source_target_pairs={{0,63},{1,2},{2,1},{3,4},{4,3},{5,6},{6,5},{7,8},{8,7},{9,10},{10,... | collective-permute-start | bytes 786440 | tf_op jit(solution)/shard_map/ppermute | solution.py:439
  17.6 7.2 %collective-permute-start.1 = (f32[8,64,128]{2,1,0:T(8,128)S(1)}, f32[8,64,128]{2,1,0:T(8,128)S(1)}, u32[]{:S(2)}, u32[]{:S(2)}) collective-permute-start(f32[8,64,128]{2,1,0:T(8,128)S(1)} %get-tuple-element.35), channel_id=1, source_target_pairs={{0,1},{1,0},{2,3},{3,2},{4,5},{5,4},{6,7},{7,6},{8,9},{9,8},{10,11... | collective-permute-start | bytes 786440 | tf_op jit(solution)/shard_map/ppermute | solution.py:434
  25.7 6.5 %collective-permute-start.3 = (f32[8,64,128]{2,1,0:T(8,128)S(1)}, f32[8,64,128]{2,1,0:T(8,128)S(1)}, u32[]{:S(2)}, u32[]{:S(2)}) collective-permute-start(f32[8,64,128]{2,1,0:T(8,128)S(1)} %get-tuple-element.41), channel_id=1, source_target_pairs={{0,1},{1,0},{2,3},{3,2},{4,5},{5,4},{6,7},{7,6},{8,9},{9,8},{10,11... | collective-permute-start | bytes 786440 | tf_op jit(solution)/shard_map/ppermute | solution.py:434
  26.1 10.6 %collective-permute-start.4 = (f32[8,64,128]{2,1,0:T(8,128)S(1)}, f32[8,64,128]{2,1,0:T(8,128)S(1)}, u32[]{:S(2)}, u32[]{:S(2)}) collective-permute-start(f32[8,64,128]{2,1,0:T(8,128)S(1)} %get-tuple-element.42), channel_id=1, source_target_pairs={{0,63},{1,2},{2,1},{3,4},{4,3},{5,6},{6,5},{7,8},{8,7},{9,10},{10,... | collective-permute-start | bytes 786440 | tf_op jit(solution)/shard_map/ppermute | solution.py:439
  37.7 6.5 %collective-permute-start.5 = (f32[8,64,128]{2,1,0:T(8,128)S(1)}, f32[8,64,128]{2,1,0:T(8,128)S(1)}, u32[]{:S(2)}, u32[]{:S(2)}) collective-permute-start(f32[8,64,128]{2,1,0:T(8,128)S(1)} %get-tuple-element.46), channel_id=1, source_target_pairs={{0,1},{1,0},{2,3},{3,2},{4,5},{5,4},{6,7},{7,6},{8,9},{9,8},{10,11... | collective-permute-start | bytes 786440 | tf_op jit(solution)/shard_map/ppermute | solution.py:434
  37.8 10.7 %collective-permute-start.6 = (f32[8,64,128]{2,1,0:T(8,128)S(1)}, f32[8,64,128]{2,1,0:T(8,128)S(1)}, u32[]{:S(2)}, u32[]{:S(2)}) collective-permute-start(f32[8,64,128]{2,1,0:T(8,128)S(1)} %get-tuple-element.47), channel_id=1, source_target_pairs={{0,63},{1,2},{2,1},{3,4},{4,3},{5,6},{6,5},{7,8},{8,7},{9,10},{10,... | collective-permute-start | bytes 786440 | tf_op jit(solution)/shard_map/ppermute | solution.py:439

commit v12 on v10

--- a/solution.py
+++ b/solution.py
@@ -37,6 +37,10 @@
 
 def shape(*dims, dtype=F32):
     return jax.ShapeDtypeStruct(dims, dtype)
+
+
+BLOCKS = shape(T, R, N)
+TURNED = shape((T // 2) * (T // 2 + 1) * N, 2 * N, dtype=BF16)
 
 
 def dot(a, b):
@@ -110,7 +114,7 @@
     )(pattern, weights)
 
 
-def band_kernel(pattern, weights, reg, high, low, own, mask, buf, cols, extra, sems):
+def band_kernel(pattern, weights, reg, high, low, own, turned_high, turned_low, mask, buf, cols, extra, sems):
     def copy(t):
         return pltpu.make_async_copy(weights.at[t], buf.at[t], sems.at[t])
 
@@ -147,13 +151,14 @@
     lax.fori_loop(0, T // 2, step, 0)
     tail.wait()
     own[...] += jnp.sum(cols[:T], axis=1) + extra[...]
+    turn(high, low, turned_high, turned_low)
 
 
 def band_pieces(pattern, weights, reg):
     pattern, weights, reg = in_hbm(pattern), in_hbm(weights), in_hbm(reg)
     return call(
         band_kernel,
-        (shape(*BAND, dtype=BF16), shape(*BAND, dtype=BF16), shape(T, N)),
+        (shape(*BAND, dtype=BF16), shape(*BAND, dtype=BF16), shape(T, N), TURNED, TURNED),
         [HBM, HBM, HBM],
         [
             pltpu.SMEM((T, T), jnp.int32),
@@ -238,26 +243,23 @@
 ONE_WAY = 2 * 3 * 40 * R * N * N
 
 
-def choose(flag, first, second):
-    return jnp.where(jnp.broadcast_to(flag[0:1, :], (R, N)) > 0, first, second)
-
-
-def hand_out(flag, vec, high, low, one, two, sent, pieces):
-    for t in range(T):
-        put_pieces(pieces, t, vec[t])
-    to_next(pieces, high, low, sent)
-    for t in range(T):
-        one[t] = choose(flag, sent[t], vec[t])
-        two[t] = choose(flag, vec[t], sent[t])
-
-
-BLOCKS = shape(T, R, N)
-SENT = pltpu.VMEM((T, R, N), F32)
-TURNED = shape((T // 2) * (T // 2 + 1) * N, 2 * N, dtype=BF16)
-
-
 def on_parity(parity):
     return pl.when(lax.axis_index("tm") % 2 == parity)
+
+
+def hand_out(vec, high, low, one, two, pieces):
+    for t in range(T):
+        put_pieces(pieces, t, vec[t])
+
+    @on_parity(0)
+    def _():
+        to_next(pieces, high, low, one)
+        two[...] = vec[...]
+
+    @on_parity(1)
+    def _():
+        to_next(pieces, high, low, two)
+        one[...] = vec[...]
 
 
 def first_kernel(rhs, own, inflow, high, low, diag, vec, two, pieces):
@@ -288,7 +290,7 @@
     for t in range(T):
         put_pieces(pieces, t, vecs[-1][t])
     if more:
-        one, *turned = more
+        (one,) = more
 
         @on_parity(0)
         def _():
@@ -298,7 +300,6 @@
         def _():
             one[...] = vecs[0][...]
 
-        turn(high, low, *turned)
     within(pieces, high, low, out)
     for i, vec in enumerate(vecs):
         h, l = moments(vec, image)
@@ -307,7 +308,7 @@
 
 
 def local(vecs, image, high, low):
-    more = (BLOCKS, TURNED, TURNED) if len(vecs) == 1 else ()
+    more = (BLOCKS,) if len(vecs) == 1 else ()
     return call(
         functools.partial(local_kernel, len(vecs)),
         (BLOCKS, shape(len(vecs), 2, R, N)) + more,
@@ -317,22 +318,27 @@
     )(*vecs, image, high, low)
 
 
-def add_received(flag, got_one, got_two, partial, turned_high, turned_low, image, pieces):
-    for t in range(T):
-        put_pieces(pieces, t, choose(flag, got_one[t], got_two[t]))
-        image[t] = partial[t] + choose(flag, got_two[t], got_one[t])
+def add_received(got_one, got_two, partial, turned_high, turned_low, image, pieces):
+    for parity, ahead, arrived in ((0, got_one, got_two), (1, got_two, got_one)):
+
+        @on_parity(parity)
+        def _():
+            for t in range(T):
+                put_pieces(pieces, t, ahead[t])
+                image[t] = partial[t] + arrived[t]
+
     from_next(pieces, turned_high, turned_low, image)
 
 
-def step_kernel(flag, got_one, got_two, partial, diag, high, low, turned_high, turned_low, image, vec, one, two, sent, pieces):
-    add_received(flag, got_one, got_two, partial, turned_high, turned_low, image, pieces)
+def step_kernel(got_one, got_two, partial, diag, high, low, turned_high, turned_low, image, vec, one, two, pieces):
+    add_received(got_one, got_two, partial, turned_high, turned_low, image, pieces)
     for t in range(T):
         vec[t] = image[t] / diag[t : t + 1, :]
-    hand_out(flag, vec, high, low, one, two, sent, pieces)
+    hand_out(vec, high, low, one, two, pieces)
 
 
 def next_step(*args):
-    return call(step_kernel, (BLOCKS,) * 4, [VMEM] * 9, [SENT, PIECES], flops=2 * ONE_WAY)(*args)
+    return call(step_kernel, (BLOCKS,) * 4, [VMEM] * 8, [PIECES], flops=2 * ONE_WAY)(*args)
 
 
 PAIRS = 5
@@ -350,9 +356,9 @@
 
 
 def gram_kernel(
-    flag, got_one, got_two, partial, turned_high, turned_low, v0, v1, v2, m0, m1, m2, image, out, pieces
+    got_one, got_two, partial, turned_high, turned_low, v0, v1, v2, m0, m1, m2, image, out, pieces
 ):
-    add_received(flag, got_one, got_two, partial, turned_high, turned_low, image, pieces)
+    add_received(got_one, got_two, partial, turned_high, turned_low, image, pieces)
     last = [moments(v, image) for v in (v0, v1, v2)]
     every = [(m[i, 0], m[i, 1]) for m in (m0, m1, m2) for i in range(m.shape[0])] + last + last[-1:]
     for q in range(PAIRS):
@@ -362,7 +368,7 @@
 
 
 def gram(*args):
-    return call(gram_kernel, (BLOCKS, shape(1, PAIRS * N)), [VMEM] * 12, [PIECES], flops=ONE_WAY)(*args)
+    return call(gram_kernel, (BLOCKS, shape(1, PAIRS * N)), [VMEM] * 11, [PIECES], flops=ONE_WAY)(*args)
 
 
 def solve(matrix, right):
@@ -420,8 +426,8 @@
 
 def all_parts(value):
     count = lax.axis_size("tm")
-    half, quarter = count // 2, count // 8
-    turns = [*range(half + quarter, count), *range(half - quarter, half + quarter), *range(half - quarter)]
+    last = [count // 2 - 1, count // 2]
+    turns = sorted(range(count), key=lambda i: (i in last, 2 * (i // 8) + 3 * (i % 4), i))
     spread = lax.all_to_all(
         jnp.broadcast_to(value[None], (count,) + value.shape), "tm", 0, 0, axis_index_groups=[turns]
     )
@@ -438,23 +444,21 @@
 
 
 def shards(weights, pattern, shift_reg, rhs):
-    flag = jnp.broadcast_to((1 - lax.axis_index("tm") % 2).astype(F32), (8, N))
-    flag, pattern = lax.optimization_barrier((flag, pattern))
     inflow = shift(ahead_sums(pattern, weights), 1)
-    high, low, own = band_pieces(pattern, weights, shift_reg)
+    high, low, own, *turned = band_pieces(pattern, weights, shift_reg)
     diag, vec, two = first(rhs, own, inflow, high, low)
     got_two = swap_across(two)
-    partial, part, one, *turned = local([vec], rhs, high, low)
+    partial, part, one = local([vec], rhs, high, low)
     got = swap_within(one), got_two
     vecs, images, found = [vec], [rhs], [part]
     for step in range(2):
-        image, vec, one, two = next_step(flag, *got, partial, diag, high, low, *turned)
+        image, vec, one, two = next_step(*got, partial, diag, high, low, *turned)
         got = swap_within(one), swap_across(two)
         images.append(image)
         vecs.append(vec)
         partial, part = local(vecs, image, high, low)
         found.append(part)
-    image, part = gram(flag, *got, partial, *turned, *vecs, *found)
+    image, part = gram(*got, partial, *turned, *vecs, *found)
     return result(all_parts(part), vecs, images + [image])
 
 

time: 67.4 us -> 69.9 us (1.037)
  waiting for transfers between devices: 26 us -> 27.1 us
  Pallas kernels: 13.1 us -> 14.1 us
  blocking collectives: 16.4 us -> 17.3 us
    ppermute x3, waiting for transfers between devices: 4.07 us -> 5.85 us  [swap_within(): lax.ppermute(value, 'tm', [(i, i ^ 1) for i in range(lax.axis_size('tm'))])]
    all_to_all x1, blocking collectives: 16.4 us -> 17.3 us  [all_parts(): lax.all_to_all(jnp.broadcast_to(value[None], (count,) + value.shape), 'tm...]
    ppermute x1, waiting for transfers between devices: 6.09 us -> 5.38 us  [shift(): lax.ppermute(value, 'tm', [(i, (i + steps) % count) for i in range(count)])]
    pallas_call x1, Pallas kernels: 2.85 us -> 3.56 us  [band_pieces(): call(band_kernel, (shape(*BAND, dtype=BF16), shape(*BAND, dtype=BF16), sh...]
  transfers between devices with their start and end apart: 7 -> 7, of which waited for: 7 -> 7; matrix products, arithmetic and copies ran while one was open for 0% -> 0% of each run, Pallas kernels for 10% -> 11%
where the time goes in v12:
time: 69.9 us; the launch traced here: 69.7 us
  waiting for transfers between devices  27.1 us (39%)
  blocking collectives  17.3 us (25%)
  Pallas kernels  14.1 us (20%)
  starting transfers between devices  10.3 us (15%)
  between operations  0.74 us (1%)
    all_to_all x1, blocking collectives, all_parts(): lax.all_to_all(jnp.broadcast_to(value[None], (count,) + value.shape), 'tm...  17.3 us
    ppermute x3, waiting for transfers between devices, swap_across(): lax.ppermute(value, 'tm', [(i, (i + (1 if i % 2 else -1)) % count) for i...  15.9 us
    ppermute x3, starting transfers between devices, swap_across(): lax.ppermute(value, 'tm', [(i, (i + (1 if i % 2 else -1)) % count) for i...  8.04 us
    ppermute x3, waiting for transfers between devices, swap_within(): lax.ppermute(value, 'tm', [(i, i ^ 1) for i in range(lax.axis_size('tm'))])  5.85 us
    ppermute x1, waiting for transfers between devices, shift(): lax.ppermute(value, 'tm', [(i, (i + steps) % count) for i in range(count)])  5.38 us
    pallas_call x3, Pallas kernels, local(): call(functools.partial(local_kernel, len(vecs)), (BLOCKS, shape(len(vecs)...  4.07 us
    pallas_call x1, Pallas kernels, band_pieces(): call(band_kernel, (shape(*BAND, dtype=BF16), shape(*BAND, dtype=BF16), sh...  3.56 us
    pallas_call x2, Pallas kernels, next_step(): call(step_kernel, (BLOCKS,) * 4, [VMEM] * 8, [PIECES], flops=2 * ONE_WAY)  2.43 us
  transfers between devices with their start and end apart: 7, of which 7 were waited for; matrix products, arithmetic and copies ran while one was open for 0% of the time, Pallas kernels for 11%

profile of v12, /device:TPU:4, one launch (start us, length us, event | category | flops | bytes accessed | tf_op | source)
XLA Modules:
  0.0 69.7 jit_solution(8546205236990979019)
XLA Ops:
  0.6 1.8 %shard_map.60 = f32[8,128]{1,0:T(8,128)S(1)} custom-call(s32[8,8]{1,0:T(8,128)} %pattern.3, f32[8,8,128,128]{3,2,1,0:T(8,128)} %weights.3), custom_call_target="tpu_custom_call" | custom-call | flops 4194304 | bytes 4194304 | tf_op jit(solution)/shard_map/pallas_call | solution.py:102
  2.5 1.7 %collective-permute-start = (f32[8,128]{1,0:T(8,128)S(1)}, f32[8,128]{1,0:T(8,128)S(1)}, u32[]{:S(2)}, u32[]{:S(2)}) collective-permute-start(f32[8,128]{1,0:T(8,128)S(1)} %shard_map.60), channel_id=1, source_target_pairs={{0,1},{1,2},{2,3},{3,4},{4,5},{5,6},{6,7},{7,8},{8,9},{9,10},{10,1... | collective-permute-start | bytes 12296 | tf_op jit(solution)/shard_map/ppermute | solution.py:424
  4.1 3.6 %shard_map.59 = (bf16[4,256,1152]{2,1,0:T(8,128)(2,1)S(1)}, bf16[4,256,1152]{2,1,0:T(8,128)(2,1)S(1)}, f32[8,128]{1,0:T(8,128)S(1)}, bf16[2560,256]{1,0:T(8,128)(2,1)S(1)}, bf16[2560,256]{1,0:T(8,128)(2,1)S(1)}) custom-call(s32[8,8]{1,0:T(8,128)} %pattern.3, f32[8,8,128,128]{3,2,1,0:T(8,128)} %weights.3, f32[8,128]{1,0:T(8,128)} %reg.1), custom_call_target="tpu_custom_call" | custom-call | flops 2147483648 | bytes 8388608 | tf_op jit(solution)/shard_map/pallas_call | solution.py:159
  7.7 5.4 %collective-permute-done.inflow = f32[8,128]{1,0:T(8,128)S(1)} collective-permute-done((f32[8,128]{1,0:T(8,128)S(1)}, f32[8,128]{1,0:T(8,128)S(1)}, u32[]{:S(2)}, u32[]{:S(2)}) %collective-permute-start) | collective-permute-done | bytes 4128 | tf_op jit(solution)/shard_map/ppermute | solution.py:424
  13.1 2.6 %collective-permute-start.2 = (f32[8,64,128]{2,1,0:T(8,128)S(1)}, f32[8,64,128]{2,1,0:T(8,128)S(1)}, u32[]{:S(2)}, u32[]{:S(2)}) collective-permute-start(f32[8,64,128]{2,1,0:T(8,128)S(1)} %get-tuple-element.32), channel_id=1, source_target_pairs={{0,63},{1,2},{2,1},{3,4},{4,3},{5,6},{6,5},{7,8},{8,7},{9,10},{10,... | collective-permute-start | bytes 786440 | tf_op jit(solution)/shard_map/ppermute | solution.py:443
  15.8 1.7 %shard_map.62 = (f32[8,64,128]{2,1,0:T(8,128)S(1)}, f32[1,2,64,128]{3,2,1,0:T(8,128)S(1)}, f32[8,64,128]{2,1,0:T(8,128)S(1)}) custom-call(f32[8,64,128]{2,1,0:T(8,128)S(1)} %get-tuple-element.30.refs_0_.v0, f32[8,64,128]{2,1,0:T(8,128)S(1)} %copy-done, bf16[4,256,1152]{2,1,0:T(8,128)(2,1)S(1)} %get-tuple-element.28.high.refs_2_.refs_3_.refs_4_, ...), custom_call_target="tpu_custom_call" | custom-call | flops 503316480 | tf_op jit(solution)/shard_map/pallas_call | solution.py:312
  17.5 0.1 collective-permute-start.1
  17.6 7.0 %collective-permute-done.2.got_two = f32[8,64,128]{2,1,0:T(8,128)S(1)} collective-permute-done((f32[8,64,128]{2,1,0:T(8,128)S(1)}, f32[8,64,128]{2,1,0:T(8,128)S(1)}, u32[]{:S(2)}, u32[]{:S(2)}) %collective-permute-start.2) | collective-permute-done | bytes 262176 | tf_op jit(solution)/shard_map/ppermute | solution.py:443
  24.6 0.7 %collective-permute-done.1.got_one = f32[8,64,128]{2,1,0:T(8,128)S(1)} collective-permute-done((f32[8,64,128]{2,1,0:T(8,128)S(1)}, f32[8,64,128]{2,1,0:T(8,128)S(1)}, u32[]{:S(2)}, u32[]{:S(2)}) %collective-permute-start.1) | collective-permute-done | bytes 262176 | tf_op jit(solution)/shard_map/ppermute | solution.py:438
  25.3 1.2 %shard_map.63 = (f32[8,64,128]{2,1,0:T(8,128)S(1)}, f32[8,64,128]{2,1,0:T(8,128)S(1)}, f32[8,64,128]{2,1,0:T(8,128)S(1)}, f32[8,64,128]{2,1,0:T(8,128)S(1)}) custom-call(f32[8,64,128]{2,1,0:T(8,128)S(1)} %collective-permute-done.1.got_one, f32[8,64,128]{2,1,0:T(8,128)S(1)} %collective-permute-done.2.got_two, f32[8,64,128]{2,1,0:T(8,128)S(1)} %get-tuple-element.33.partial, ...), custom_call_target="tpu_custom_call" | custom-call | flops 503316480 | tf_op jit(solution)/shard_map/pallas_call | solution.py:341
  26.6 0.4 collective-permute-start.3
  27.0 2.5 %collective-permute-start.4 = (f32[8,64,128]{2,1,0:T(8,128)S(1)}, f32[8,64,128]{2,1,0:T(8,128)S(1)}, u32[]{:S(2)}, u32[]{:S(2)}) collective-permute-start(f32[8,64,128]{2,1,0:T(8,128)S(1)} %get-tuple-element.38), channel_id=1, source_target_pairs={{0,63},{1,2},{2,1},{3,4},{4,3},{5,6},{6,5},{7,8},{8,7},{9,10},{10,... | collective-permute-start | bytes 786440 | tf_op jit(solution)/shard_map/ppermute | solution.py:443
  29.5 1.2 %shard_map.64 = (f32[8,64,128]{2,1,0:T(8,128)S(1)}, f32[2,2,64,128]{3,2,1,0:T(8,128)S(1)}) custom-call(f32[8,64,128]{2,1,0:T(8,128)S(1)} %get-tuple-element.30.refs_0_.v0, f32[8,64,128]{2,1,0:T(8,128)S(1)} %get-tuple-element.39.refs_1_.v1, f32[8,64,128]{2,1,0:T(8,128)S(1)} %get-tuple-element.40.refs_2_.y1, ...), custom_call_target="tpu_custom_call" | custom-call | flops 503316480 | tf_op jit(solution)/shard_map/pallas_call | solution.py:312
  30.6 2.9 %collective-permute-done.3.got_one = f32[8,64,128]{2,1,0:T(8,128)S(1)} collective-permute-done((f32[8,64,128]{2,1,0:T(8,128)S(1)}, f32[8,64,128]{2,1,0:T(8,128)S(1)}, u32[]{:S(2)}, u32[]{:S(2)}) %collective-permute-start.3) | collective-permute-done | bytes 262176 | tf_op jit(solution)/shard_map/ppermute | solution.py:438
  33.5 4.5 %collective-permute-done.4.got_two = f32[8,64,128]{2,1,0:T(8,128)S(1)} collective-permute-done((f32[8,64,128]{2,1,0:T(8,128)S(1)}, f32[8,64,128]{2,1,0:T(8,128)S(1)}, u32[]{:S(2)}, u32[]{:S(2)}) %collective-permute-start.4) | collective-permute-done | bytes 262176 | tf_op jit(solution)/shard_map/ppermute | solution.py:443
  38.1 1.2 %shard_map.65 = (f32[8,64,128]{2,1,0:T(8,128)S(1)}, f32[8,64,128]{2,1,0:T(8,128)S(1)}, f32[8,64,128]{2,1,0:T(8,128)S(1)}, f32[8,64,128]{2,1,0:T(8,128)S(1)}) custom-call(f32[8,64,128]{2,1,0:T(8,128)S(1)} %collective-permute-done.3.got_one, f32[8,64,128]{2,1,0:T(8,128)S(1)} %collective-permute-done.4.got_two, f32[8,64,128]{2,1,0:T(8,128)S(1)} %get-tuple-element.41.partial, ...), custom_call_target="tpu_custom_call" | custom-call | flops 503316480 | tf_op jit(solution)/shard_map/pallas_call | solution.py:341
  39.3 0.1 collective-permute-start.5
  39.4 2.9 %collective-permute-start.6 = (f32[8,64,128]{2,1,0:T(8,128)S(1)}, f32[8,64,128]{2,1,0:T(8,128)S(1)}, u32[]{:S(2)}, u32[]{:S(2)}) collective-permute-start(f32[8,64,128]{2,1,0:T(8,128)S(1)} %get-tuple-element.43), channel_id=1, source_target_pairs={{0,63},{1,2},{2,1},{3,4},{4,3},{5,6},{6,5},{7,8},{8,7},{9,10},{10,... | collective-permute-start | bytes 786440 | tf_op jit(solution)/shard_map/ppermute | solution.py:443
  42.3 1.2 %shard_map.66 = (f32[8,64,128]{2,1,0:T(8,128)S(1)}, f32[3,2,64,128]{3,2,1,0:T(8,128)S(1)}) custom-call(f32[8,64,128]{2,1,0:T(8,128)S(1)} %get-tuple-element.30.refs_0_.v0, f32[8,64,128]{2,1,0:T(8,128)S(1)} %get-tuple-element.39.refs_1_.v1, f32[8,64,128]{2,1,0:T(8,128)S(1)} %get-tuple-element.44.refs_2_.v2, f32[8,64,128]{2,1,0:T(8,128)S(1)} %get-tuple-element.45.refs_3_.y2, ...), custom_call_target="tpu_custom_call" | custom-call | flops 503316480 | tf_op jit(solution)/shard_map/pallas_call | solution.py:312
  43.5 2.2 %collective-permute-done.5.got_one = f32[8,64,128]{2,1,0:T(8,128)S(1)} collective-permute-done((f32[8,64,128]{2,1,0:T(8,128)S(1)}, f32[8,64,128]{2,1,0:T(8,128)S(1)}, u32[]{:S(2)}, u32[]{:S(2)}) %collective-permute-start.5) | collective-permute-done | bytes 262176 | tf_op jit(solution)/shard_map/ppermute | solution.py:438
  45.7 4.3 %collective-permute-done.6.got_two = f32[8,64,128]{2,1,0:T(8,128)S(1)} collective-permute-done((f32[8,64,128]{2,1,0:T(8,128)S(1)}, f32[8,64,128]{2,1,0:T(8,128)S(1)}, u32[]{:S(2)}, u32[]{:S(2)}) %collective-permute-start.6) | collective-permute-done | bytes 262176 | tf_op jit(solution)/shard_map/ppermute | solution.py:443
  50.1 0.9 %shard_map.67 = (f32[8,64,128]{2,1,0:T(8,128)S(1)}, f32[1,640]{1,0:T(1,128)S(1)}) custom-call(f32[8,64,128]{2,1,0:T(8,128)S(1)} %collective-permute-done.5.got_one, f32[8,64,128]{2,1,0:T(8,128)S(1)} %collective-permute-done.6.got_two, f32[8,64,128]{2,1,0:T(8,128)S(1)} %get-tuple-element.46.partial, bf16[2560,256]{1,0:T(8,128)(2,1)S(1)} %get-tuple-element.35.turned_high, ...), custom_call_target="tpu_custom_call" | custom-call | flops 251658240 | tf_op jit(solution)/shard_map/pallas_call | solution.py:371
  51.1 17.3 %all_to_all.5 = f32[64,1,640]{2,1,0:T(1,128)S(1)} all-to-all(f32[64,1,640]{2,1,0:T(1,128)S(1)} %broadcast_in_dim.9), channel_id=1, replica_groups={{0,4,8,12,1,5,16,20,9,13,2,6,24,28,17,21,10,14,36,3,7,25,29,18,22,40,44..., dimensions={0} | all-to-all | bytes 327680 | tf_op jit(solution)/shard_map/all_to_all | solution.py:431
  68.4 1.3 %shard_map.68 = (f32[8,64,128]{2,1,0:T(8,128)}, f32[8,64,128]{2,1,0:T(8,128)}) custom-call(f32[64,640]{1,0:T(8,128)S(1)} %bitcast.3, f32[8,64,128]{2,1,0:T(8,128)S(1)} %get-tuple-element.30.refs_0_.v0, f32[8,64,128]{2,1,0:T(8,128)S(1)} %get-tuple-element.39.refs_1_.v1, f32[8,64,128]{2,1,0:T(8,128)S(1)} %get-tuple-element.44.refs_2_.v2, ...), custom_call_target="tpu_custom_call" | custom-call | tf_op jit(solution)/shard_map/pallas_call | solution.py:419
  (6 shorter events, 0.2 us)
Async XLA Ops:
  2.5 10.6 %copy-start = (f32[8,64,128]{2,1,0:T(8,128)S(1)}, f32[8,64,128]{2,1,0:T(8,128)}, u32[]{:S(2)}) copy-start(f32[8,64,128]{2,1,0:T(8,128)} %y0.1) | copy-start | bytes 786436
  2.5 10.6 %collective-permute-start = (f32[8,128]{1,0:T(8,128)S(1)}, f32[8,128]{1,0:T(8,128)S(1)}, u32[]{:S(2)}, u32[]{:S(2)}) collective-permute-start(f32[8,128]{1,0:T(8,128)S(1)} %shard_map.60), channel_id=1, source_target_pairs={{0,1},{1,2},{2,3},{3,4},{4,5},{5,6},{6,7},{7,8},{8,9},{9,10},{10,1... | collective-permute-start | bytes 12296 | tf_op jit(solution)/shard_map/ppermute | solution.py:424
  13.1 11.5 %collective-permute-start.2 = (f32[8,64,128]{2,1,0:T(8,128)S(1)}, f32[8,64,128]{2,1,0:T(8,128)S(1)}, u32[]{:S(2)}, u32[]{:S(2)}) collective-permute-start(f32[8,64,128]{2,1,0:T(8,128)S(1)} %get-tuple-element.32), channel_id=1, source_target_pairs={{0,63},{1,2},{2,1},{3,4},{4,3},{5,6},{6,5},{7,8},{8,7},{9,10},{10,... | collective-permute-start | bytes 786440 | tf_op jit(solution)/shard_map/ppermute | solution.py:443
  17.5 7.9 %collective-permute-start.1 = (f32[8,64,128]{2,1,0:T(8,128)S(1)}, f32[8,64,128]{2,1,0:T(8,128)S(1)}, u32[]{:S(2)}, u32[]{:S(2)}) collective-permute-start(f32[8,64,128]{2,1,0:T(8,128)S(1)} %get-tuple-element.31), channel_id=1, source_target_pairs={{0,1},{1,0},{2,3},{3,2},{4,5},{5,4},{6,7},{7,6},{8,9},{9,8},{10,11... | collective-permute-start | bytes 786440 | tf_op jit(solution)/shard_map/ppermute | solution.py:438
  26.6 6.9 %collective-permute-start.3 = (f32[8,64,128]{2,1,0:T(8,128)S(1)}, f32[8,64,128]{2,1,0:T(8,128)S(1)}, u32[]{:S(2)}, u32[]{:S(2)}) collective-permute-start(f32[8,64,128]{2,1,0:T(8,128)S(1)} %get-tuple-element.37), channel_id=1, source_target_pairs={{0,1},{1,0},{2,3},{3,2},{4,5},{5,4},{6,7},{7,6},{8,9},{9,8},{10,11... | collective-permute-start | bytes 786440 | tf_op jit(solution)/shard_map/ppermute | solution.py:438
  27.0 11.1 %collective-permute-start.4 = (f32[8,64,128]{2,1,0:T(8,128)S(1)}, f32[8,64,128]{2,1,0:T(8,128)S(1)}, u32[]{:S(2)}, u32[]{:S(2)}) collective-permute-start(f32[8,64,128]{2,1,0:T(8,128)S(1)} %get-tuple-element.38), channel_id=1, source_target_pairs={{0,63},{1,2},{2,1},{3,4},{4,3},{5,6},{6,5},{7,8},{8,7},{9,10},{10,... | collective-permute-start | bytes 786440 | tf_op jit(solution)/shard_map/ppermute | solution.py:443
  39.3 6.5 %collective-permute-start.5 = (f32[8,64,128]{2,1,0:T(8,128)S(1)}, f32[8,64,128]{2,1,0:T(8,128)S(1)}, u32[]{:S(2)}, u32[]{:S(2)}) collective-permute-start(f32[8,64,128]{2,1,0:T(8,128)S(1)} %get-tuple-element.42), channel_id=1, source_target_pairs={{0,1},{1,0},{2,3},{3,2},{4,5},{5,4},{6,7},{7,6},{8,9},{9,8},{10,11... | collective-permute-start | bytes 786440 | tf_op jit(solution)/shard_map/ppermute | solution.py:438
  39.4 10.7 %collective-permute-start.6 = (f32[8,64,128]{2,1,0:T(8,128)S(1)}, f32[8,64,128]{2,1,0:T(8,128)S(1)}, u32[]{:S(2)}, u32[]{:S(2)}) collective-permute-start(f32[8,64,128]{2,1,0:T(8,128)S(1)} %get-tuple-element.43), channel_id=1, source_target_pairs={{0,63},{1,2},{2,1},{3,4},{4,3},{5,6},{6,5},{7,8},{8,7},{9,10},{10,... | collective-permute-start | bytes 786440 | tf_op jit(solution)/shard_map/ppermute | solution.py:443

commit v13 on v11

--- a/solution.py
+++ b/solution.py
@@ -421,9 +421,10 @@
 def all_parts(value):
     count = lax.axis_size("tm")
     half, eighth = count // 2, count // 8
-    last = [half - 1, half]
-    near = [i for i in range(half - eighth, half + eighth) if i not in last]
-    turns = [*range(half + eighth, count), *near, *last, *range(half - eighth)]
+    edges = [i for i in range(half - eighth, count) if i % eighth in (0, eighth - 1)]
+    edges.sort(key=lambda i: (i in (half - 1, half), i))
+    inner = [i for i in range(half - eighth, count) if i not in edges]
+    turns = [*inner, *edges, *range(half - eighth)]
     spread = lax.all_to_all(
         jnp.broadcast_to(value[None], (count,) + value.shape), "tm", 0, 0, axis_index_groups=[turns]
     )

time: 67.2 us -> 67.8 us (level)
  blocking collectives: 16.2 us -> 16.9 us
where the time goes in v13:
time: 67.8 us; the launch traced here: 67.7 us
  waiting for transfers between devices  26 us (38%)
  blocking collectives  16.9 us (25%)
  Pallas kernels  13.1 us (19%)
  starting transfers between devices  10.9 us (16%)
  between operations  0.76 us (1%)
    all_to_all x1, blocking collectives, all_parts(): lax.all_to_all(jnp.broadcast_to(value[None], (count,) + value.shape), 'tm...  16.9 us
    ppermute x3, waiting for transfers between devices, swap_across(): lax.ppermute(value, 'tm', [(i, (i + (1 if i % 2 else -1)) % count) for i...  15.8 us
    ppermute x3, starting transfers between devices, swap_across(): lax.ppermute(value, 'tm', [(i, (i + (1 if i % 2 else -1)) % count) for i...  8.66 us
    ppermute x1, waiting for transfers between devices, shift(): lax.ppermute(value, 'tm', [(i, (i + steps) % count) for i in range(count)])  6.09 us
    pallas_call x3, Pallas kernels, local(): call(functools.partial(local_kernel, len(vecs)), (BLOCKS, shape(len(vecs)...  4.17 us
    ppermute x3, waiting for transfers between devices, swap_within(): lax.ppermute(value, 'tm', [(i, i ^ 1) for i in range(lax.axis_size('tm'))])  4.07 us
    pallas_call x1, Pallas kernels, band_pieces(): call(band_kernel, (shape(*BAND, dtype=BF16), shape(*BAND, dtype=BF16), sh...  2.85 us
    pallas_call x2, Pallas kernels, next_step(): call(step_kernel, (BLOCKS,) * 4, [VMEM] * 9, [SENT, PIECES], flops=2 * ON...  2.02 us
  transfers between devices with their start and end apart: 7, of which 7 were waited for; matrix products, arithmetic and copies ran while one was open for 0% of the time, Pallas kernels for 10%

profile of v13, /device:TPU:4, one launch (start us, length us, event | category | flops | bytes accessed | tf_op | source)
XLA Modules:
  0.0 67.7 jit_solution(18383412578694847479)
XLA Ops:
  0.7 1.8 %shard_map.60 = f32[8,128]{1,0:T(8,128)S(1)} custom-call(s32[8,8]{1,0:T(8,128)} %pattern.1, f32[8,8,128,128]{3,2,1,0:T(8,128)} %weights.3), custom_call_target="tpu_custom_call" | custom-call | flops 4194304 | bytes 4194304 | tf_op jit(solution)/shard_map/pallas_call | solution.py:98
  2.5 1.7 %collective-permute-start = (f32[8,128]{1,0:T(8,128)S(1)}, f32[8,128]{1,0:T(8,128)S(1)}, u32[]{:S(2)}, u32[]{:S(2)}) collective-permute-start(f32[8,128]{1,0:T(8,128)S(1)} %shard_map.60), channel_id=1, source_target_pairs={{0,1},{1,2},{2,3},{3,4},{4,5},{5,6},{6,7},{7,8},{8,9},{9,10},{10,1... | collective-permute-start | bytes 12296 | tf_op jit(solution)/shard_map/ppermute | solution.py:418
  4.2 2.8 %shard_map.59 = (bf16[4,256,1152]{2,1,0:T(8,128)(2,1)S(1)}, bf16[4,256,1152]{2,1,0:T(8,128)(2,1)S(1)}, f32[8,128]{1,0:T(8,128)S(1)}) custom-call(s32[8,8]{1,0:T(8,128)} %pattern.1, f32[8,8,128,128]{3,2,1,0:T(8,128)} %weights.3, f32[8,128]{1,0:T(8,128)} %reg.1), custom_call_target="tpu_custom_call" | custom-call | flops 2147483648 | bytes 8388608 | tf_op jit(solution)/shard_map/pallas_call | solution.py:154
  7.0 6.1 %collective-permute-done.inflow = f32[8,128]{1,0:T(8,128)S(1)} collective-permute-done((f32[8,128]{1,0:T(8,128)S(1)}, f32[8,128]{1,0:T(8,128)S(1)}, u32[]{:S(2)}, u32[]{:S(2)}) %collective-permute-start) | collective-permute-done | bytes 4128 | tf_op jit(solution)/shard_map/ppermute | solution.py:418
  13.2 2.6 %collective-permute-start.2 = (f32[8,64,128]{2,1,0:T(8,128)S(1)}, f32[8,64,128]{2,1,0:T(8,128)S(1)}, u32[]{:S(2)}, u32[]{:S(2)}) collective-permute-start(f32[8,64,128]{2,1,0:T(8,128)S(1)} %get-tuple-element.36), channel_id=1, source_target_pairs={{0,63},{1,2},{2,1},{3,4},{4,3},{5,6},{6,5},{7,8},{8,7},{9,10},{10,... | collective-permute-start | bytes 786440 | tf_op jit(solution)/shard_map/ppermute | solution.py:440
  15.8 1.8 %shard_map.62 = (f32[8,64,128]{2,1,0:T(8,128)S(1)}, f32[1,2,64,128]{3,2,1,0:T(8,128)S(1)}, f32[8,64,128]{2,1,0:T(8,128)S(1)}, bf16[2560,256]{1,0:T(8,128)(2,1)S(1)}, bf16[2560,256]{1,0:T(8,128)(2,1)S(1)}) custom-call(f32[8,64,128]{2,1,0:T(8,128)S(1)} %get-tuple-element.34.refs_0_.v0, f32[8,64,128]{2,1,0:T(8,128)S(1)} %copy-done, ...), custom_call_target="tpu_custom_call" | custom-call | flops 503316480 | tf_op jit(solution)/shard_map/pallas_call | solution.py:311
  17.6 0.1 collective-permute-start.1
  17.7 7.0 %collective-permute-done.2.got_two = f32[8,64,128]{2,1,0:T(8,128)S(1)} collective-permute-done((f32[8,64,128]{2,1,0:T(8,128)S(1)}, f32[8,64,128]{2,1,0:T(8,128)S(1)}, u32[]{:S(2)}, u32[]{:S(2)}) %collective-permute-start.2) | collective-permute-done | bytes 262176 | tf_op jit(solution)/shard_map/ppermute | solution.py:440
  24.7 1.0 %shard_map.63 = (f32[8,64,128]{2,1,0:T(8,128)S(1)}, f32[8,64,128]{2,1,0:T(8,128)S(1)}, f32[8,64,128]{2,1,0:T(8,128)S(1)}, f32[8,64,128]{2,1,0:T(8,128)S(1)}) custom-call(f32[8,128]{1,0:T(8,128)S(1)} %broadcast_in_dim.11.flag, f32[8,64,128]{2,1,0:T(8,128)S(1)} %collective-permute-done.1.got_one, f32[8,64,128]{2,1,0:T(8,128)S(1)} %collective-permute-done.2.got_two, ...), custom_call_target="tpu_custom_call" | custom-call | flops 503316480 | tf_op jit(solution)/shard_map/pallas_call | solution.py:335
  25.7 0.4 collective-permute-start.3
  26.1 3.0 %collective-permute-start.4 = (f32[8,64,128]{2,1,0:T(8,128)S(1)}, f32[8,64,128]{2,1,0:T(8,128)S(1)}, u32[]{:S(2)}, u32[]{:S(2)}) collective-permute-start(f32[8,64,128]{2,1,0:T(8,128)S(1)} %get-tuple-element.42), channel_id=1, source_target_pairs={{0,63},{1,2},{2,1},{3,4},{4,3},{5,6},{6,5},{7,8},{8,7},{9,10},{10,... | collective-permute-start | bytes 786440 | tf_op jit(solution)/shard_map/ppermute | solution.py:440
  29.1 1.2 %shard_map.64 = (f32[8,64,128]{2,1,0:T(8,128)S(1)}, f32[2,2,64,128]{3,2,1,0:T(8,128)S(1)}) custom-call(f32[8,64,128]{2,1,0:T(8,128)S(1)} %get-tuple-element.34.refs_0_.v0, f32[8,64,128]{2,1,0:T(8,128)S(1)} %get-tuple-element.43.refs_1_.v1, f32[8,64,128]{2,1,0:T(8,128)S(1)} %get-tuple-element.44.refs_2_.y1, ...), custom_call_target="tpu_custom_call" | custom-call | flops 503316480 | tf_op jit(solution)/shard_map/pallas_call | solution.py:311
  30.3 1.9 %collective-permute-done.3.got_one = f32[8,64,128]{2,1,0:T(8,128)S(1)} collective-permute-done((f32[8,64,128]{2,1,0:T(8,128)S(1)}, f32[8,64,128]{2,1,0:T(8,128)S(1)}, u32[]{:S(2)}, u32[]{:S(2)}) %collective-permute-start.3) | collective-permute-done | bytes 262176 | tf_op jit(solution)/shard_map/ppermute | solution.py:435
  32.2 4.5 %collective-permute-done.4.got_two = f32[8,64,128]{2,1,0:T(8,128)S(1)} collective-permute-done((f32[8,64,128]{2,1,0:T(8,128)S(1)}, f32[8,64,128]{2,1,0:T(8,128)S(1)}, u32[]{:S(2)}, u32[]{:S(2)}) %collective-permute-start.4) | collective-permute-done | bytes 262176 | tf_op jit(solution)/shard_map/ppermute | solution.py:440
  36.7 1.0 %shard_map.65 = (f32[8,64,128]{2,1,0:T(8,128)S(1)}, f32[8,64,128]{2,1,0:T(8,128)S(1)}, f32[8,64,128]{2,1,0:T(8,128)S(1)}, f32[8,64,128]{2,1,0:T(8,128)S(1)}) custom-call(f32[8,128]{1,0:T(8,128)S(1)} %broadcast_in_dim.11.flag, f32[8,64,128]{2,1,0:T(8,128)S(1)} %collective-permute-done.3.got_one, f32[8,64,128]{2,1,0:T(8,128)S(1)} %collective-permute-done.4.got_two, ...), custom_call_target="tpu_custom_call" | custom-call | flops 503316480 | tf_op jit(solution)/shard_map/pallas_call | solution.py:335
  37.7 0.1 collective-permute-start.5
  37.8 3.1 %collective-permute-start.6 = (f32[8,64,128]{2,1,0:T(8,128)S(1)}, f32[8,64,128]{2,1,0:T(8,128)S(1)}, u32[]{:S(2)}, u32[]{:S(2)}) collective-permute-start(f32[8,64,128]{2,1,0:T(8,128)S(1)} %get-tuple-element.47), channel_id=1, source_target_pairs={{0,63},{1,2},{2,1},{3,4},{4,3},{5,6},{6,5},{7,8},{8,7},{9,10},{10,... | collective-permute-start | bytes 786440 | tf_op jit(solution)/shard_map/ppermute | solution.py:440
  40.9 1.2 %shard_map.66 = (f32[8,64,128]{2,1,0:T(8,128)S(1)}, f32[3,2,64,128]{3,2,1,0:T(8,128)S(1)}) custom-call(f32[8,64,128]{2,1,0:T(8,128)S(1)} %get-tuple-element.34.refs_0_.v0, f32[8,64,128]{2,1,0:T(8,128)S(1)} %get-tuple-element.43.refs_1_.v1, f32[8,64,128]{2,1,0:T(8,128)S(1)} %get-tuple-element.48.refs_2_.v2, f32[8,64,128]{2,1,0:T(8,128)S(1)} %get-tuple-element.49.refs_3_.y2, ...), custom_call_target="tpu_custom_call" | custom-call | flops 503316480 | tf_op jit(solution)/shard_map/pallas_call | solution.py:311
  42.1 2.1 %collective-permute-done.5.got_one = f32[8,64,128]{2,1,0:T(8,128)S(1)} collective-permute-done((f32[8,64,128]{2,1,0:T(8,128)S(1)}, f32[8,64,128]{2,1,0:T(8,128)S(1)}, u32[]{:S(2)}, u32[]{:S(2)}) %collective-permute-start.5) | collective-permute-done | bytes 262176 | tf_op jit(solution)/shard_map/ppermute | solution.py:435
  44.2 4.3 %collective-permute-done.6.got_two = f32[8,64,128]{2,1,0:T(8,128)S(1)} collective-permute-done((f32[8,64,128]{2,1,0:T(8,128)S(1)}, f32[8,64,128]{2,1,0:T(8,128)S(1)}, u32[]{:S(2)}, u32[]{:S(2)}) %collective-permute-start.6) | collective-permute-done | bytes 262176 | tf_op jit(solution)/shard_map/ppermute | solution.py:440
  48.5 0.9 %shard_map.67 = (f32[8,64,128]{2,1,0:T(8,128)S(1)}, f32[1,640]{1,0:T(1,128)S(1)}) custom-call(f32[8,128]{1,0:T(8,128)S(1)} %broadcast_in_dim.11.flag, f32[8,64,128]{2,1,0:T(8,128)S(1)} %collective-permute-done.5.got_one, f32[8,64,128]{2,1,0:T(8,128)S(1)} %collective-permute-done.6.got_two, f32[8,64,128]{2,1,0:T(8,128)S(1)} %get-tuple-element.50.partial, ...), custom_call_target="tpu_custom_call" | custom-call | flops 251658240 | tf_op jit(solution)/shard_map/pallas_call | solution.py:365
  49.4 0.1 broadcast_in_dim.13
  49.5 16.9 %all_to_all.5 = f32[64,1,640]{2,1,0:T(1,128)S(1)} all-to-all(f32[64,1,640]{2,1,0:T(1,128)S(1)} %broadcast_in_dim.13), channel_id=1, replica_groups={{25,26,27,28,29,30,33,34,35,36,37,38,41,42,43,44,45,46,49,50,51,52,53,5..., dimensions={0} | all-to-all | bytes 327680 | tf_op jit(solution)/shard_map/all_to_all | solution.py:428
  66.4 1.3 %shard_map.68 = (f32[8,64,128]{2,1,0:T(8,128)}, f32[8,64,128]{2,1,0:T(8,128)}) custom-call(f32[64,640]{1,0:T(8,128)S(1)} %bitcast.3, f32[8,64,128]{2,1,0:T(8,128)S(1)} %get-tuple-element.34.refs_0_.v0, f32[8,64,128]{2,1,0:T(8,128)S(1)} %get-tuple-element.43.refs_1_.v1, f32[8,64,128]{2,1,0:T(8,128)S(1)} %get-tuple-element.48.refs_2_.v2, ...), custom_call_target="tpu_custom_call" | custom-call | tf_op jit(solution)/shard_map/pallas_call | solution.py:413
  (7 shorter events, 0.2 us)
Async XLA Ops:
  2.5 10.6 %copy-start = (f32[8,64,128]{2,1,0:T(8,128)S(1)}, f32[8,64,128]{2,1,0:T(8,128)}, u32[]{:S(2)}) copy-start(f32[8,64,128]{2,1,0:T(8,128)} %y0.1) | copy-start | bytes 786436
  2.5 10.6 %collective-permute-start = (f32[8,128]{1,0:T(8,128)S(1)}, f32[8,128]{1,0:T(8,128)S(1)}, u32[]{:S(2)}, u32[]{:S(2)}) collective-permute-start(f32[8,128]{1,0:T(8,128)S(1)} %shard_map.60), channel_id=1, source_target_pairs={{0,1},{1,2},{2,3},{3,4},{4,5},{5,6},{6,7},{7,8},{8,9},{9,10},{10,1... | collective-permute-start | bytes 12296 | tf_op jit(solution)/shard_map/ppermute | solution.py:418
  13.2 11.5 %collective-permute-start.2 = (f32[8,64,128]{2,1,0:T(8,128)S(1)}, f32[8,64,128]{2,1,0:T(8,128)S(1)}, u32[]{:S(2)}, u32[]{:S(2)}) collective-permute-start(f32[8,64,128]{2,1,0:T(8,128)S(1)} %get-tuple-element.36), channel_id=1, source_target_pairs={{0,63},{1,2},{2,1},{3,4},{4,3},{5,6},{6,5},{7,8},{8,7},{9,10},{10,... | collective-permute-start | bytes 786440 | tf_op jit(solution)/shard_map/ppermute | solution.py:440
  17.6 7.2 %collective-permute-start.1 = (f32[8,64,128]{2,1,0:T(8,128)S(1)}, f32[8,64,128]{2,1,0:T(8,128)S(1)}, u32[]{:S(2)}, u32[]{:S(2)}) collective-permute-start(f32[8,64,128]{2,1,0:T(8,128)S(1)} %get-tuple-element.35), channel_id=1, source_target_pairs={{0,1},{1,0},{2,3},{3,2},{4,5},{5,4},{6,7},{7,6},{8,9},{9,8},{10,11... | collective-permute-start | bytes 786440 | tf_op jit(solution)/shard_map/ppermute | solution.py:435
  25.7 6.5 %collective-permute-start.3 = (f32[8,64,128]{2,1,0:T(8,128)S(1)}, f32[8,64,128]{2,1,0:T(8,128)S(1)}, u32[]{:S(2)}, u32[]{:S(2)}) collective-permute-start(f32[8,64,128]{2,1,0:T(8,128)S(1)} %get-tuple-element.41), channel_id=1, source_target_pairs={{0,1},{1,0},{2,3},{3,2},{4,5},{5,4},{6,7},{7,6},{8,9},{9,8},{10,11... | collective-permute-start | bytes 786440 | tf_op jit(solution)/shard_map/ppermute | solution.py:435
  26.1 10.6 %collective-permute-start.4 = (f32[8,64,128]{2,1,0:T(8,128)S(1)}, f32[8,64,128]{2,1,0:T(8,128)S(1)}, u32[]{:S(2)}, u32[]{:S(2)}) collective-permute-start(f32[8,64,128]{2,1,0:T(8,128)S(1)} %get-tuple-element.42), channel_id=1, source_target_pairs={{0,63},{1,2},{2,1},{3,4},{4,3},{5,6},{6,5},{7,8},{8,7},{9,10},{10,... | collective-permute-start | bytes 786440 | tf_op jit(solution)/shard_map/ppermute | solution.py:440
  37.7 6.5 %collective-permute-start.5 = (f32[8,64,128]{2,1,0:T(8,128)S(1)}, f32[8,64,128]{2,1,0:T(8,128)S(1)}, u32[]{:S(2)}, u32[]{:S(2)}) collective-permute-start(f32[8,64,128]{2,1,0:T(8,128)S(1)} %get-tuple-element.46), channel_id=1, source_target_pairs={{0,1},{1,0},{2,3},{3,2},{4,5},{5,4},{6,7},{7,6},{8,9},{9,8},{10,11... | collective-permute-start | bytes 786440 | tf_op jit(solution)/shard_map/ppermute | solution.py:435
  37.8 10.7 %collective-permute-start.6 = (f32[8,64,128]{2,1,0:T(8,128)S(1)}, f32[8,64,128]{2,1,0:T(8,128)S(1)}, u32[]{:S(2)}, u32[]{:S(2)}) collective-permute-start(f32[8,64,128]{2,1,0:T(8,128)S(1)} %get-tuple-element.47), channel_id=1, source_target_pairs={{0,63},{1,2},{2,1},{3,4},{4,3},{5,6},{6,5},{7,8},{8,7},{9,10},{10,... | collective-permute-start | bytes 786440 | tf_op jit(solution)/shard_map/ppermute | solution.py:440

commit v14 on v11

--- a/solution.py
+++ b/solution.py
@@ -178,15 +178,15 @@
     return (both[:R] + mult(pieces[0:R, cols], low)) + both[R:]
 
 
-def to_next(pieces, high, low, out):
+def to_next(pieces, high, low, put):
     for b in range(T // 2):
         total = None
         for a in range(b, T // 2):
             at = slice((7 + 2 * b - 2 * a) * N, (9 + 2 * b - 2 * a) * N)
             term = product(pieces, slice(a * 2 * N, (a + 1) * 2 * N), high[a, :, at], low[a, :, at], dot)
             total = term if total is None else total + term
-        out[2 * b] = total[:, :N]
-        out[2 * b + 1] = total[:, N:]
+        put(2 * b, total[:, :N])
+        put(2 * b + 1, total[:, N:])
 
 
 def within(pieces, high, low, out):
@@ -218,12 +218,19 @@
             out[turned_rows(a), :] = piece[a, :, (7 - 2 * a) * N :].T
 
 
-def from_next(pieces, high, low, out):
+def from_next(pieces, high, low, put):
     for a in range(T // 2):
         rows = turned_rows(a)
         term = product(pieces, slice(0, (2 * a + 2) * N), high[rows, :], low[rows, :], dot)
-        out[2 * a] += term[:, :N]
-        out[2 * a + 1] += term[:, N:]
+        put(2 * a, term[:, :N])
+        put(2 * a + 1, term[:, N:])
+
+
+def store(out):
+    def put(t, value):
+        out[t] = value
+
+    return put
 
 
 def moments(first, second):
@@ -242,17 +249,7 @@
     return jnp.where(jnp.broadcast_to(flag[0:1, :], (R, N)) > 0, first, second)
 
 
-def hand_out(flag, vec, high, low, one, two, sent, pieces):
-    for t in range(T):
-        put_pieces(pieces, t, vec[t])
-    to_next(pieces, high, low, sent)
-    for t in range(T):
-        one[t] = choose(flag, sent[t], vec[t])
-        two[t] = choose(flag, vec[t], sent[t])
-
-
 BLOCKS = shape(T, R, N)
-SENT = pltpu.VMEM((T, R, N), F32)
 TURNED = shape((T // 2) * (T // 2 + 1) * N, 2 * N, dtype=BF16)
 
 
@@ -276,7 +273,7 @@
             value = rhs[t] / diag[t : t + 1, :]
             vec[t] = value
             put_pieces(pieces, t, value)
-        to_next(pieces, high, low, two)
+        to_next(pieces, high, low, store(two))
 
 
 def first(*args):
@@ -292,7 +289,7 @@
 
         @on_parity(0)
         def _():
-            to_next(pieces, high, low, one)
+            to_next(pieces, high, low, store(one))
 
         @on_parity(1)
         def _():
@@ -317,22 +314,35 @@
     )(*vecs, image, high, low)
 
 
-def add_received(flag, got_one, got_two, partial, turned_high, turned_low, image, pieces):
+def add_received(flag, got_one, got_two, partial, turned_high, turned_low, pieces, put):
     for t in range(T):
         put_pieces(pieces, t, choose(flag, got_one[t], got_two[t]))
-        image[t] = partial[t] + choose(flag, got_two[t], got_one[t])
-    from_next(pieces, turned_high, turned_low, image)
-
-
-def step_kernel(flag, got_one, got_two, partial, diag, high, low, turned_high, turned_low, image, vec, one, two, sent, pieces):
-    add_received(flag, got_one, got_two, partial, turned_high, turned_low, image, pieces)
-    for t in range(T):
-        vec[t] = image[t] / diag[t : t + 1, :]
-    hand_out(flag, vec, high, low, one, two, sent, pieces)
+
+    def add(t, term):
+        put(t, (partial[t] + choose(flag, got_two[t], got_one[t])) + term)
+
+    from_next(pieces, turned_high, turned_low, add)
+
+
+def step_kernel(
+    flag, got_one, got_two, partial, diag, high, low, turned_high, turned_low, image, vec, one, two, pieces, made
+):
+    def take(t, value):
+        image[t] = value
+        value = value / diag[t : t + 1, :]
+        vec[t] = value
+        put_pieces(made, t, value)
+
+    def give(t, value):
+        one[t] = choose(flag, value, vec[t])
+        two[t] = choose(flag, vec[t], value)
+
+    add_received(flag, got_one, got_two, partial, turned_high, turned_low, pieces, take)
+    to_next(made, high, low, give)
 
 
 def next_step(*args):
-    return call(step_kernel, (BLOCKS,) * 4, [VMEM] * 9, [SENT, PIECES], flops=2 * ONE_WAY)(*args)
+    return call(step_kernel, (BLOCKS,) * 4, [VMEM] * 9, [PIECES, PIECES], flops=2 * ONE_WAY)(*args)
 
 
 PAIRS = 5
@@ -352,7 +362,7 @@
 def gram_kernel(
     flag, got_one, got_two, partial, turned_high, turned_low, v0, v1, v2, m0, m1, m2, image, out, pieces
 ):
-    add_received(flag, got_one, got_two, partial, turned_high, turned_low, image, pieces)
+    add_received(flag, got_one, got_two, partial, turned_high, turned_low, pieces, store(image))
     last = [moments(v, image) for v in (v0, v1, v2)]
     every = [(m[i, 0], m[i, 1]) for m in (m0, m1, m2) for i in range(m.shape[0])] + last + last[-1:]
     for q in range(PAIRS):

time: 67.2 us -> 67.2 us (level)
  no operation moved by 1% of the time
where the time goes in v14:
time: 67.2 us; the launch traced here: 67 us
  waiting for transfers between devices  26 us (39%)
  blocking collectives  16.2 us (24%)
  Pallas kernels  13.1 us (19%)
  starting transfers between devices  10.9 us (16%)
  between operations  0.76 us (1%)
    all_to_all x1, blocking collectives, all_parts(): lax.all_to_all(jnp.broadcast_to(value[None], (count,) + value.shape), 'tm...  16.2 us
    ppermute x3, waiting for transfers between devices, swap_across(): lax.ppermute(value, 'tm', [(i, (i + (1 if i % 2 else -1)) % count) for i...  15.8 us
    ppermute x3, starting transfers between devices, swap_across(): lax.ppermute(value, 'tm', [(i, (i + (1 if i % 2 else -1)) % count) for i...  8.65 us
    ppermute x1, waiting for transfers between devices, shift(): lax.ppermute(value, 'tm', [(i, (i + steps) % count) for i in range(count)])  6.09 us
    pallas_call x3, Pallas kernels, local(): call(functools.partial(local_kernel, len(vecs)), (BLOCKS, shape(len(vecs)...  4.17 us
    ppermute x3, waiting for transfers between devices, swap_within(): lax.ppermute(value, 'tm', [(i, i ^ 1) for i in range(lax.axis_size('tm'))])  4.09 us
    pallas_call x1, Pallas kernels, band_pieces(): call(band_kernel, (shape(*BAND, dtype=BF16), shape(*BAND, dtype=BF16), sh...  2.85 us
    pallas_call x2, Pallas kernels, next_step(): call(step_kernel, (BLOCKS,) * 4, [VMEM] * 9, [PIECES, PIECES], flops=2 *...  2 us
  transfers between devices with their start and end apart: 7, of which 7 were waited for; matrix products, arithmetic and copies ran while one was open for 0% of the time, Pallas kernels for 10%

profile of v14, /device:TPU:4, one launch (start us, length us, event | category | flops | bytes accessed | tf_op | source)
XLA Modules:
  0.0 67.0 jit_solution(3372932192803661464)
XLA Ops:
  0.7 1.8 %shard_map.60 = f32[8,128]{1,0:T(8,128)S(1)} custom-call(s32[8,8]{1,0:T(8,128)} %pattern.1, f32[8,8,128,128]{3,2,1,0:T(8,128)} %weights.3), custom_call_target="tpu_custom_call" | custom-call | flops 4194304 | bytes 4194304 | tf_op jit(solution)/shard_map/pallas_call | solution.py:98
  2.5 1.7 %collective-permute-start = (f32[8,128]{1,0:T(8,128)S(1)}, f32[8,128]{1,0:T(8,128)S(1)}, u32[]{:S(2)}, u32[]{:S(2)}) collective-permute-start(f32[8,128]{1,0:T(8,128)S(1)} %shard_map.60), channel_id=1, source_target_pairs={{0,1},{1,2},{2,3},{3,4},{4,5},{5,6},{6,7},{7,8},{8,9},{9,10},{10,1... | collective-permute-start | bytes 12296 | tf_op jit(solution)/shard_map/ppermute | solution.py:428
  4.2 2.8 %shard_map.59 = (bf16[4,256,1152]{2,1,0:T(8,128)(2,1)S(1)}, bf16[4,256,1152]{2,1,0:T(8,128)(2,1)S(1)}, f32[8,128]{1,0:T(8,128)S(1)}) custom-call(s32[8,8]{1,0:T(8,128)} %pattern.1, f32[8,8,128,128]{3,2,1,0:T(8,128)} %weights.3, f32[8,128]{1,0:T(8,128)} %reg.1), custom_call_target="tpu_custom_call" | custom-call | flops 2147483648 | bytes 8388608 | tf_op jit(solution)/shard_map/pallas_call | solution.py:154
  7.0 6.1 %collective-permute-done.inflow = f32[8,128]{1,0:T(8,128)S(1)} collective-permute-done((f32[8,128]{1,0:T(8,128)S(1)}, f32[8,128]{1,0:T(8,128)S(1)}, u32[]{:S(2)}, u32[]{:S(2)}) %collective-permute-start) | collective-permute-done | bytes 4128 | tf_op jit(solution)/shard_map/ppermute | solution.py:428
  13.2 2.6 %collective-permute-start.2 = (f32[8,64,128]{2,1,0:T(8,128)S(1)}, f32[8,64,128]{2,1,0:T(8,128)S(1)}, u32[]{:S(2)}, u32[]{:S(2)}) collective-permute-start(f32[8,64,128]{2,1,0:T(8,128)S(1)} %get-tuple-element.36), channel_id=1, source_target_pairs={{0,63},{1,2},{2,1},{3,4},{4,3},{5,6},{6,5},{7,8},{8,7},{9,10},{10,... | collective-permute-start | bytes 786440 | tf_op jit(solution)/shard_map/ppermute | solution.py:449
  15.8 1.8 %shard_map.62 = (f32[8,64,128]{2,1,0:T(8,128)S(1)}, f32[1,2,64,128]{3,2,1,0:T(8,128)S(1)}, f32[8,64,128]{2,1,0:T(8,128)S(1)}, bf16[2560,256]{1,0:T(8,128)(2,1)S(1)}, bf16[2560,256]{1,0:T(8,128)(2,1)S(1)}) custom-call(f32[8,64,128]{2,1,0:T(8,128)S(1)} %get-tuple-element.34.refs_0_.v0, f32[8,64,128]{2,1,0:T(8,128)S(1)} %copy-done, ...), custom_call_target="tpu_custom_call" | custom-call | flops 503316480 | tf_op jit(solution)/shard_map/pallas_call | solution.py:308
  17.6 0.1 collective-permute-start.1
  17.7 7.0 %collective-permute-done.2.got_two = f32[8,64,128]{2,1,0:T(8,128)S(1)} collective-permute-done((f32[8,64,128]{2,1,0:T(8,128)S(1)}, f32[8,64,128]{2,1,0:T(8,128)S(1)}, u32[]{:S(2)}, u32[]{:S(2)}) %collective-permute-start.2) | collective-permute-done | bytes 262176 | tf_op jit(solution)/shard_map/ppermute | solution.py:449
  24.7 1.0 %shard_map.63 = (f32[8,64,128]{2,1,0:T(8,128)S(1)}, f32[8,64,128]{2,1,0:T(8,128)S(1)}, f32[8,64,128]{2,1,0:T(8,128)S(1)}, f32[8,64,128]{2,1,0:T(8,128)S(1)}) custom-call(f32[8,128]{1,0:T(8,128)S(1)} %broadcast_in_dim.11.flag, f32[8,64,128]{2,1,0:T(8,128)S(1)} %collective-permute-done.1.got_one, f32[8,64,128]{2,1,0:T(8,128)S(1)} %collective-permute-done.2.got_two, ...), custom_call_target="tpu_custom_call" | custom-call | flops 503316480 | tf_op jit(solution)/shard_map/pallas_call | solution.py:345
  25.7 0.4 collective-permute-start.3
  26.1 3.0 %collective-permute-start.4 = (f32[8,64,128]{2,1,0:T(8,128)S(1)}, f32[8,64,128]{2,1,0:T(8,128)S(1)}, u32[]{:S(2)}, u32[]{:S(2)}) collective-permute-start(f32[8,64,128]{2,1,0:T(8,128)S(1)} %get-tuple-element.42), channel_id=1, source_target_pairs={{0,63},{1,2},{2,1},{3,4},{4,3},{5,6},{6,5},{7,8},{8,7},{9,10},{10,... | collective-permute-start | bytes 786440 | tf_op jit(solution)/shard_map/ppermute | solution.py:449
  29.1 1.2 %shard_map.64 = (f32[8,64,128]{2,1,0:T(8,128)S(1)}, f32[2,2,64,128]{3,2,1,0:T(8,128)S(1)}) custom-call(f32[8,64,128]{2,1,0:T(8,128)S(1)} %get-tuple-element.34.refs_0_.v0, f32[8,64,128]{2,1,0:T(8,128)S(1)} %get-tuple-element.43.refs_1_.v1, f32[8,64,128]{2,1,0:T(8,128)S(1)} %get-tuple-element.44.refs_2_.y1, ...), custom_call_target="tpu_custom_call" | custom-call | flops 503316480 | tf_op jit(solution)/shard_map/pallas_call | solution.py:308
  30.3 1.9 %collective-permute-done.3.got_one = f32[8,64,128]{2,1,0:T(8,128)S(1)} collective-permute-done((f32[8,64,128]{2,1,0:T(8,128)S(1)}, f32[8,64,128]{2,1,0:T(8,128)S(1)}, u32[]{:S(2)}, u32[]{:S(2)}) %collective-permute-start.3) | collective-permute-done | bytes 262176 | tf_op jit(solution)/shard_map/ppermute | solution.py:444
  32.2 4.5 %collective-permute-done.4.got_two = f32[8,64,128]{2,1,0:T(8,128)S(1)} collective-permute-done((f32[8,64,128]{2,1,0:T(8,128)S(1)}, f32[8,64,128]{2,1,0:T(8,128)S(1)}, u32[]{:S(2)}, u32[]{:S(2)}) %collective-permute-start.4) | collective-permute-done | bytes 262176 | tf_op jit(solution)/shard_map/ppermute | solution.py:449
  36.7 1.0 %shard_map.65 = (f32[8,64,128]{2,1,0:T(8,128)S(1)}, f32[8,64,128]{2,1,0:T(8,128)S(1)}, f32[8,64,128]{2,1,0:T(8,128)S(1)}, f32[8,64,128]{2,1,0:T(8,128)S(1)}) custom-call(f32[8,128]{1,0:T(8,128)S(1)} %broadcast_in_dim.11.flag, f32[8,64,128]{2,1,0:T(8,128)S(1)} %collective-permute-done.3.got_one, f32[8,64,128]{2,1,0:T(8,128)S(1)} %collective-permute-done.4.got_two, ...), custom_call_target="tpu_custom_call" | custom-call | flops 503316480 | tf_op jit(solution)/shard_map/pallas_call | solution.py:345
  37.7 0.1 collective-permute-start.5
  37.8 3.0 %collective-permute-start.6 = (f32[8,64,128]{2,1,0:T(8,128)S(1)}, f32[8,64,128]{2,1,0:T(8,128)S(1)}, u32[]{:S(2)}, u32[]{:S(2)}) collective-permute-start(f32[8,64,128]{2,1,0:T(8,128)S(1)} %get-tuple-element.47), channel_id=1, source_target_pairs={{0,63},{1,2},{2,1},{3,4},{4,3},{5,6},{6,5},{7,8},{8,7},{9,10},{10,... | collective-permute-start | bytes 786440 | tf_op jit(solution)/shard_map/ppermute | solution.py:449
  40.9 1.2 %shard_map.66 = (f32[8,64,128]{2,1,0:T(8,128)S(1)}, f32[3,2,64,128]{3,2,1,0:T(8,128)S(1)}) custom-call(f32[8,64,128]{2,1,0:T(8,128)S(1)} %get-tuple-element.34.refs_0_.v0, f32[8,64,128]{2,1,0:T(8,128)S(1)} %get-tuple-element.43.refs_1_.v1, f32[8,64,128]{2,1,0:T(8,128)S(1)} %get-tuple-element.48.refs_2_.v2, f32[8,64,128]{2,1,0:T(8,128)S(1)} %get-tuple-element.49.refs_3_.y2, ...), custom_call_target="tpu_custom_call" | custom-call | flops 503316480 | tf_op jit(solution)/shard_map/pallas_call | solution.py:308
  42.1 2.1 %collective-permute-done.5.got_one = f32[8,64,128]{2,1,0:T(8,128)S(1)} collective-permute-done((f32[8,64,128]{2,1,0:T(8,128)S(1)}, f32[8,64,128]{2,1,0:T(8,128)S(1)}, u32[]{:S(2)}, u32[]{:S(2)}) %collective-permute-start.5) | collective-permute-done | bytes 262176 | tf_op jit(solution)/shard_map/ppermute | solution.py:444
  44.2 4.3 %collective-permute-done.6.got_two = f32[8,64,128]{2,1,0:T(8,128)S(1)} collective-permute-done((f32[8,64,128]{2,1,0:T(8,128)S(1)}, f32[8,64,128]{2,1,0:T(8,128)S(1)}, u32[]{:S(2)}, u32[]{:S(2)}) %collective-permute-start.6) | collective-permute-done | bytes 262176 | tf_op jit(solution)/shard_map/ppermute | solution.py:449
  48.5 0.9 %shard_map.67 = (f32[8,64,128]{2,1,0:T(8,128)S(1)}, f32[1,640]{1,0:T(1,128)S(1)}) custom-call(f32[8,128]{1,0:T(8,128)S(1)} %broadcast_in_dim.11.flag, f32[8,64,128]{2,1,0:T(8,128)S(1)} %collective-permute-done.5.got_one, f32[8,64,128]{2,1,0:T(8,128)S(1)} %collective-permute-done.6.got_two, f32[8,64,128]{2,1,0:T(8,128)S(1)} %get-tuple-element.50.partial, ...), custom_call_target="tpu_custom_call" | custom-call | flops 251658240 | tf_op jit(solution)/shard_map/pallas_call | solution.py:375
  49.4 0.1 broadcast_in_dim.13
  49.5 16.2 %all_to_all.5 = f32[64,1,640]{2,1,0:T(1,128)S(1)} all-to-all(f32[64,1,640]{2,1,0:T(1,128)S(1)} %broadcast_in_dim.13), channel_id=1, replica_groups={{40,41,42,43,44,45,46,47,48,49,50,51,52,53,54,55,56,57,58,59,60,61,62,6..., dimensions={0} | all-to-all | bytes 327680 | tf_op jit(solution)/shard_map/all_to_all | solution.py:437
  65.7 1.3 %shard_map.68 = (f32[8,64,128]{2,1,0:T(8,128)}, f32[8,64,128]{2,1,0:T(8,128)}) custom-call(f32[64,640]{1,0:T(8,128)S(1)} %bitcast.3, f32[8,64,128]{2,1,0:T(8,128)S(1)} %get-tuple-element.34.refs_0_.v0, f32[8,64,128]{2,1,0:T(8,128)S(1)} %get-tuple-element.43.refs_1_.v1, f32[8,64,128]{2,1,0:T(8,128)S(1)} %get-tuple-element.48.refs_2_.v2, ...), custom_call_target="tpu_custom_call" | custom-call | tf_op jit(solution)/shard_map/pallas_call | solution.py:423
  (7 shorter events, 0.2 us)
Async XLA Ops:
  2.5 10.6 %copy-start = (f32[8,64,128]{2,1,0:T(8,128)S(1)}, f32[8,64,128]{2,1,0:T(8,128)}, u32[]{:S(2)}) copy-start(f32[8,64,128]{2,1,0:T(8,128)} %y0.1) | copy-start | bytes 786436
  2.5 10.6 %collective-permute-start = (f32[8,128]{1,0:T(8,128)S(1)}, f32[8,128]{1,0:T(8,128)S(1)}, u32[]{:S(2)}, u32[]{:S(2)}) collective-permute-start(f32[8,128]{1,0:T(8,128)S(1)} %shard_map.60), channel_id=1, source_target_pairs={{0,1},{1,2},{2,3},{3,4},{4,5},{5,6},{6,7},{7,8},{8,9},{9,10},{10,1... | collective-permute-start | bytes 12296 | tf_op jit(solution)/shard_map/ppermute | solution.py:428
  13.2 11.5 %collective-permute-start.2 = (f32[8,64,128]{2,1,0:T(8,128)S(1)}, f32[8,64,128]{2,1,0:T(8,128)S(1)}, u32[]{:S(2)}, u32[]{:S(2)}) collective-permute-start(f32[8,64,128]{2,1,0:T(8,128)S(1)} %get-tuple-element.36), channel_id=1, source_target_pairs={{0,63},{1,2},{2,1},{3,4},{4,3},{5,6},{6,5},{7,8},{8,7},{9,10},{10,... | collective-permute-start | bytes 786440 | tf_op jit(solution)/shard_map/ppermute | solution.py:449
  17.6 7.2 %collective-permute-start.1 = (f32[8,64,128]{2,1,0:T(8,128)S(1)}, f32[8,64,128]{2,1,0:T(8,128)S(1)}, u32[]{:S(2)}, u32[]{:S(2)}) collective-permute-start(f32[8,64,128]{2,1,0:T(8,128)S(1)} %get-tuple-element.35), channel_id=1, source_target_pairs={{0,1},{1,0},{2,3},{3,2},{4,5},{5,4},{6,7},{7,6},{8,9},{9,8},{10,11... | collective-permute-start | bytes 786440 | tf_op jit(solution)/shard_map/ppermute | solution.py:444
  25.7 6.5 %collective-permute-start.3 = (f32[8,64,128]{2,1,0:T(8,128)S(1)}, f32[8,64,128]{2,1,0:T(8,128)S(1)}, u32[]{:S(2)}, u32[]{:S(2)}) collective-permute-start(f32[8,64,128]{2,1,0:T(8,128)S(1)} %get-tuple-element.41), channel_id=1, source_target_pairs={{0,1},{1,0},{2,3},{3,2},{4,5},{5,4},{6,7},{7,6},{8,9},{9,8},{10,11... | collective-permute-start | bytes 786440 | tf_op jit(solution)/shard_map/ppermute | solution.py:444
  26.1 10.6 %collective-permute-start.4 = (f32[8,64,128]{2,1,0:T(8,128)S(1)}, f32[8,64,128]{2,1,0:T(8,128)S(1)}, u32[]{:S(2)}, u32[]{:S(2)}) collective-permute-start(f32[8,64,128]{2,1,0:T(8,128)S(1)} %get-tuple-element.42), channel_id=1, source_target_pairs={{0,63},{1,2},{2,1},{3,4},{4,3},{5,6},{6,5},{7,8},{8,7},{9,10},{10,... | collective-permute-start | bytes 786440 | tf_op jit(solution)/shard_map/ppermute | solution.py:449
  37.7 6.5 %collective-permute-start.5 = (f32[8,64,128]{2,1,0:T(8,128)S(1)}, f32[8,64,128]{2,1,0:T(8,128)S(1)}, u32[]{:S(2)}, u32[]{:S(2)}) collective-permute-start(f32[8,64,128]{2,1,0:T(8,128)S(1)} %get-tuple-element.46), channel_id=1, source_target_pairs={{0,1},{1,0},{2,3},{3,2},{4,5},{5,4},{6,7},{7,6},{8,9},{9,8},{10,11... | collective-permute-start | bytes 786440 | tf_op jit(solution)/shard_map/ppermute | solution.py:444
  37.8 10.7 %collective-permute-start.6 = (f32[8,64,128]{2,1,0:T(8,128)S(1)}, f32[8,64,128]{2,1,0:T(8,128)S(1)}, u32[]{:S(2)}, u32[]{:S(2)}) collective-permute-start(f32[8,64,128]{2,1,0:T(8,128)S(1)} %get-tuple-element.47), channel_id=1, source_target_pairs={{0,63},{1,2},{2,1},{3,4},{4,3},{5,6},{6,5},{7,8},{8,7},{9,10},{10,... | collective-permute-start | bytes 786440 | tf_op jit(solution)/shard_map/ppermute | solution.py:449

commit v15 on v14

--- a/solution.py
+++ b/solution.py
@@ -433,7 +433,8 @@
     half, eighth = count // 2, count // 8
     last = [half - 1, half]
     near = [i for i in range(half - eighth, half + eighth) if i not in last]
-    turns = [*range(half + eighth, count), *near, *last, *range(half - eighth)]
+    early = sorted(range(half - eighth), key=lambda i: (2 * (i // eighth) + 3 * (i % 4), i))
+    turns = [*range(half + eighth, count), *near, *last, *early]
     spread = lax.all_to_all(
         jnp.broadcast_to(value[None], (count,) + value.shape), "tm", 0, 0, axis_index_groups=[turns]
     )

time: 67.2 us -> 67.3 us (level)
  no operation moved by 1% of the time
where the time goes in v15:
time: 67.3 us; the launch traced here: 67.1 us
  waiting for transfers between devices  26 us (39%)
  blocking collectives  16.3 us (24%)
  Pallas kernels  13.1 us (19%)
  starting transfers between devices  10.9 us (16%)
  between operations  0.76 us (1%)
    all_to_all x1, blocking collectives, all_parts(): lax.all_to_all(jnp.broadcast_to(value[None], (count,) + value.shape), 'tm...  16.3 us
    ppermute x3, waiting for transfers between devices, swap_across(): lax.ppermute(value, 'tm', [(i, (i + (1 if i % 2 else -1)) % count) for i...  15.8 us
    ppermute x3, starting transfers between devices, swap_across(): lax.ppermute(value, 'tm', [(i, (i + (1 if i % 2 else -1)) % count) for i...  8.65 us
    ppermute x1, waiting for transfers between devices, shift(): lax.ppermute(value, 'tm', [(i, (i + steps) % count) for i in range(count)])  6.09 us
    pallas_call x3, Pallas kernels, local(): call(functools.partial(local_kernel, len(vecs)), (BLOCKS, shape(len(vecs)...  4.17 us
    ppermute x3, waiting for transfers between devices, swap_within(): lax.ppermute(value, 'tm', [(i, i ^ 1) for i in range(lax.axis_size('tm'))])  4.09 us
    pallas_call x1, Pallas kernels, band_pieces(): call(band_kernel, (shape(*BAND, dtype=BF16), shape(*BAND, dtype=BF16), sh...  2.85 us
    pallas_call x2, Pallas kernels, next_step(): call(step_kernel, (BLOCKS,) * 4, [VMEM] * 9, [PIECES, PIECES], flops=2 *...  2 us
  transfers between devices with their start and end apart: 7, of which 7 were waited for; matrix products, arithmetic and copies ran while one was open for 0% of the time, Pallas kernels for 10%

profile of v15, /device:TPU:4, one launch (start us, length us, event | category | flops | bytes accessed | tf_op | source)
XLA Modules:
  0.0 67.1 jit_solution(3913558893531099045)
XLA Ops:
  0.7 1.8 %shard_map.60 = f32[8,128]{1,0:T(8,128)S(1)} custom-call(s32[8,8]{1,0:T(8,128)} %pattern.1, f32[8,8,128,128]{3,2,1,0:T(8,128)} %weights.3), custom_call_target="tpu_custom_call" | custom-call | flops 4194304 | bytes 4194304 | tf_op jit(solution)/shard_map/pallas_call | solution.py:98
  2.5 1.7 %collective-permute-start = (f32[8,128]{1,0:T(8,128)S(1)}, f32[8,128]{1,0:T(8,128)S(1)}, u32[]{:S(2)}, u32[]{:S(2)}) collective-permute-start(f32[8,128]{1,0:T(8,128)S(1)} %shard_map.60), channel_id=1, source_target_pairs={{0,1},{1,2},{2,3},{3,4},{4,5},{5,6},{6,7},{7,8},{8,9},{9,10},{10,1... | collective-permute-start | bytes 12296 | tf_op jit(solution)/shard_map/ppermute | solution.py:428
  4.2 2.8 %shard_map.59 = (bf16[4,256,1152]{2,1,0:T(8,128)(2,1)S(1)}, bf16[4,256,1152]{2,1,0:T(8,128)(2,1)S(1)}, f32[8,128]{1,0:T(8,128)S(1)}) custom-call(s32[8,8]{1,0:T(8,128)} %pattern.1, f32[8,8,128,128]{3,2,1,0:T(8,128)} %weights.3, f32[8,128]{1,0:T(8,128)} %reg.1), custom_call_target="tpu_custom_call" | custom-call | flops 2147483648 | bytes 8388608 | tf_op jit(solution)/shard_map/pallas_call | solution.py:154
  7.0 6.1 %collective-permute-done.inflow = f32[8,128]{1,0:T(8,128)S(1)} collective-permute-done((f32[8,128]{1,0:T(8,128)S(1)}, f32[8,128]{1,0:T(8,128)S(1)}, u32[]{:S(2)}, u32[]{:S(2)}) %collective-permute-start) | collective-permute-done | bytes 4128 | tf_op jit(solution)/shard_map/ppermute | solution.py:428
  13.2 2.6 %collective-permute-start.2 = (f32[8,64,128]{2,1,0:T(8,128)S(1)}, f32[8,64,128]{2,1,0:T(8,128)S(1)}, u32[]{:S(2)}, u32[]{:S(2)}) collective-permute-start(f32[8,64,128]{2,1,0:T(8,128)S(1)} %get-tuple-element.36), channel_id=1, source_target_pairs={{0,63},{1,2},{2,1},{3,4},{4,3},{5,6},{6,5},{7,8},{8,7},{9,10},{10,... | collective-permute-start | bytes 786440 | tf_op jit(solution)/shard_map/ppermute | solution.py:450
  15.8 1.8 %shard_map.62 = (f32[8,64,128]{2,1,0:T(8,128)S(1)}, f32[1,2,64,128]{3,2,1,0:T(8,128)S(1)}, f32[8,64,128]{2,1,0:T(8,128)S(1)}, bf16[2560,256]{1,0:T(8,128)(2,1)S(1)}, bf16[2560,256]{1,0:T(8,128)(2,1)S(1)}) custom-call(f32[8,64,128]{2,1,0:T(8,128)S(1)} %get-tuple-element.34.refs_0_.v0, f32[8,64,128]{2,1,0:T(8,128)S(1)} %copy-done, ...), custom_call_target="tpu_custom_call" | custom-call | flops 503316480 | tf_op jit(solution)/shard_map/pallas_call | solution.py:308
  17.6 0.1 collective-permute-start.1
  17.7 7.0 %collective-permute-done.2.got_two = f32[8,64,128]{2,1,0:T(8,128)S(1)} collective-permute-done((f32[8,64,128]{2,1,0:T(8,128)S(1)}, f32[8,64,128]{2,1,0:T(8,128)S(1)}, u32[]{:S(2)}, u32[]{:S(2)}) %collective-permute-start.2) | collective-permute-done | bytes 262176 | tf_op jit(solution)/shard_map/ppermute | solution.py:450
  24.7 1.0 %shard_map.63 = (f32[8,64,128]{2,1,0:T(8,128)S(1)}, f32[8,64,128]{2,1,0:T(8,128)S(1)}, f32[8,64,128]{2,1,0:T(8,128)S(1)}, f32[8,64,128]{2,1,0:T(8,128)S(1)}) custom-call(f32[8,128]{1,0:T(8,128)S(1)} %broadcast_in_dim.11.flag, f32[8,64,128]{2,1,0:T(8,128)S(1)} %collective-permute-done.1.got_one, f32[8,64,128]{2,1,0:T(8,128)S(1)} %collective-permute-done.2.got_two, ...), custom_call_target="tpu_custom_call" | custom-call | flops 503316480 | tf_op jit(solution)/shard_map/pallas_call | solution.py:345
  25.7 0.4 collective-permute-start.3
  26.1 3.0 %collective-permute-start.4 = (f32[8,64,128]{2,1,0:T(8,128)S(1)}, f32[8,64,128]{2,1,0:T(8,128)S(1)}, u32[]{:S(2)}, u32[]{:S(2)}) collective-permute-start(f32[8,64,128]{2,1,0:T(8,128)S(1)} %get-tuple-element.42), channel_id=1, source_target_pairs={{0,63},{1,2},{2,1},{3,4},{4,3},{5,6},{6,5},{7,8},{8,7},{9,10},{10,... | collective-permute-start | bytes 786440 | tf_op jit(solution)/shard_map/ppermute | solution.py:450
  29.1 1.2 %shard_map.64 = (f32[8,64,128]{2,1,0:T(8,128)S(1)}, f32[2,2,64,128]{3,2,1,0:T(8,128)S(1)}) custom-call(f32[8,64,128]{2,1,0:T(8,128)S(1)} %get-tuple-element.34.refs_0_.v0, f32[8,64,128]{2,1,0:T(8,128)S(1)} %get-tuple-element.43.refs_1_.v1, f32[8,64,128]{2,1,0:T(8,128)S(1)} %get-tuple-element.44.refs_2_.y1, ...), custom_call_target="tpu_custom_call" | custom-call | flops 503316480 | tf_op jit(solution)/shard_map/pallas_call | solution.py:308
  30.3 1.9 %collective-permute-done.3.got_one = f32[8,64,128]{2,1,0:T(8,128)S(1)} collective-permute-done((f32[8,64,128]{2,1,0:T(8,128)S(1)}, f32[8,64,128]{2,1,0:T(8,128)S(1)}, u32[]{:S(2)}, u32[]{:S(2)}) %collective-permute-start.3) | collective-permute-done | bytes 262176 | tf_op jit(solution)/shard_map/ppermute | solution.py:445
  32.2 4.5 %collective-permute-done.4.got_two = f32[8,64,128]{2,1,0:T(8,128)S(1)} collective-permute-done((f32[8,64,128]{2,1,0:T(8,128)S(1)}, f32[8,64,128]{2,1,0:T(8,128)S(1)}, u32[]{:S(2)}, u32[]{:S(2)}) %collective-permute-start.4) | collective-permute-done | bytes 262176 | tf_op jit(solution)/shard_map/ppermute | solution.py:450
  36.7 1.0 %shard_map.65 = (f32[8,64,128]{2,1,0:T(8,128)S(1)}, f32[8,64,128]{2,1,0:T(8,128)S(1)}, f32[8,64,128]{2,1,0:T(8,128)S(1)}, f32[8,64,128]{2,1,0:T(8,128)S(1)}) custom-call(f32[8,128]{1,0:T(8,128)S(1)} %broadcast_in_dim.11.flag, f32[8,64,128]{2,1,0:T(8,128)S(1)} %collective-permute-done.3.got_one, f32[8,64,128]{2,1,0:T(8,128)S(1)} %collective-permute-done.4.got_two, ...), custom_call_target="tpu_custom_call" | custom-call | flops 503316480 | tf_op jit(solution)/shard_map/pallas_call | solution.py:345
  37.7 0.1 collective-permute-start.5
  37.8 3.0 %collective-permute-start.6 = (f32[8,64,128]{2,1,0:T(8,128)S(1)}, f32[8,64,128]{2,1,0:T(8,128)S(1)}, u32[]{:S(2)}, u32[]{:S(2)}) collective-permute-start(f32[8,64,128]{2,1,0:T(8,128)S(1)} %get-tuple-element.47), channel_id=1, source_target_pairs={{0,63},{1,2},{2,1},{3,4},{4,3},{5,6},{6,5},{7,8},{8,7},{9,10},{10,... | collective-permute-start | bytes 786440 | tf_op jit(solution)/shard_map/ppermute | solution.py:450
  40.9 1.2 %shard_map.66 = (f32[8,64,128]{2,1,0:T(8,128)S(1)}, f32[3,2,64,128]{3,2,1,0:T(8,128)S(1)}) custom-call(f32[8,64,128]{2,1,0:T(8,128)S(1)} %get-tuple-element.34.refs_0_.v0, f32[8,64,128]{2,1,0:T(8,128)S(1)} %get-tuple-element.43.refs_1_.v1, f32[8,64,128]{2,1,0:T(8,128)S(1)} %get-tuple-element.48.refs_2_.v2, f32[8,64,128]{2,1,0:T(8,128)S(1)} %get-tuple-element.49.refs_3_.y2, ...), custom_call_target="tpu_custom_call" | custom-call | flops 503316480 | tf_op jit(solution)/shard_map/pallas_call | solution.py:308
  42.1 2.1 %collective-permute-done.5.got_one = f32[8,64,128]{2,1,0:T(8,128)S(1)} collective-permute-done((f32[8,64,128]{2,1,0:T(8,128)S(1)}, f32[8,64,128]{2,1,0:T(8,128)S(1)}, u32[]{:S(2)}, u32[]{:S(2)}) %collective-permute-start.5) | collective-permute-done | bytes 262176 | tf_op jit(solution)/shard_map/ppermute | solution.py:445
  44.2 4.3 %collective-permute-done.6.got_two = f32[8,64,128]{2,1,0:T(8,128)S(1)} collective-permute-done((f32[8,64,128]{2,1,0:T(8,128)S(1)}, f32[8,64,128]{2,1,0:T(8,128)S(1)}, u32[]{:S(2)}, u32[]{:S(2)}) %collective-permute-start.6) | collective-permute-done | bytes 262176 | tf_op jit(solution)/shard_map/ppermute | solution.py:450
  48.5 0.9 %shard_map.67 = (f32[8,64,128]{2,1,0:T(8,128)S(1)}, f32[1,640]{1,0:T(1,128)S(1)}) custom-call(f32[8,128]{1,0:T(8,128)S(1)} %broadcast_in_dim.11.flag, f32[8,64,128]{2,1,0:T(8,128)S(1)} %collective-permute-done.5.got_one, f32[8,64,128]{2,1,0:T(8,128)S(1)} %collective-permute-done.6.got_two, f32[8,64,128]{2,1,0:T(8,128)S(1)} %get-tuple-element.50.partial, ...), custom_call_target="tpu_custom_call" | custom-call | flops 251658240 | tf_op jit(solution)/shard_map/pallas_call | solution.py:375
  49.4 0.1 broadcast_in_dim.13
  49.5 16.3 %all_to_all.5 = f32[64,1,640]{2,1,0:T(1,128)S(1)} all-to-all(f32[64,1,640]{2,1,0:T(1,128)S(1)} %broadcast_in_dim.13), channel_id=1, replica_groups={{40,41,42,43,44,45,46,47,48,49,50,51,52,53,54,55,56,57,58,59,60,61,62,6..., dimensions={0} | all-to-all | bytes 327680 | tf_op jit(solution)/shard_map/all_to_all | solution.py:438
  65.8 1.3 %shard_map.68 = (f32[8,64,128]{2,1,0:T(8,128)}, f32[8,64,128]{2,1,0:T(8,128)}) custom-call(f32[64,640]{1,0:T(8,128)S(1)} %bitcast.3, f32[8,64,128]{2,1,0:T(8,128)S(1)} %get-tuple-element.34.refs_0_.v0, f32[8,64,128]{2,1,0:T(8,128)S(1)} %get-tuple-element.43.refs_1_.v1, f32[8,64,128]{2,1,0:T(8,128)S(1)} %get-tuple-element.48.refs_2_.v2, ...), custom_call_target="tpu_custom_call" | custom-call | tf_op jit(solution)/shard_map/pallas_call | solution.py:423
  (7 shorter events, 0.2 us)
Async XLA Ops:
  2.5 10.6 %copy-start = (f32[8,64,128]{2,1,0:T(8,128)S(1)}, f32[8,64,128]{2,1,0:T(8,128)}, u32[]{:S(2)}) copy-start(f32[8,64,128]{2,1,0:T(8,128)} %y0.1) | copy-start | bytes 786436
  2.5 10.6 %collective-permute-start = (f32[8,128]{1,0:T(8,128)S(1)}, f32[8,128]{1,0:T(8,128)S(1)}, u32[]{:S(2)}, u32[]{:S(2)}) collective-permute-start(f32[8,128]{1,0:T(8,128)S(1)} %shard_map.60), channel_id=1, source_target_pairs={{0,1},{1,2},{2,3},{3,4},{4,5},{5,6},{6,7},{7,8},{8,9},{9,10},{10,1... | collective-permute-start | bytes 12296 | tf_op jit(solution)/shard_map/ppermute | solution.py:428
  13.2 11.5 %collective-permute-start.2 = (f32[8,64,128]{2,1,0:T(8,128)S(1)}, f32[8,64,128]{2,1,0:T(8,128)S(1)}, u32[]{:S(2)}, u32[]{:S(2)}) collective-permute-start(f32[8,64,128]{2,1,0:T(8,128)S(1)} %get-tuple-element.36), channel_id=1, source_target_pairs={{0,63},{1,2},{2,1},{3,4},{4,3},{5,6},{6,5},{7,8},{8,7},{9,10},{10,... | collective-permute-start | bytes 786440 | tf_op jit(solution)/shard_map/ppermute | solution.py:450
  17.6 7.2 %collective-permute-start.1 = (f32[8,64,128]{2,1,0:T(8,128)S(1)}, f32[8,64,128]{2,1,0:T(8,128)S(1)}, u32[]{:S(2)}, u32[]{:S(2)}) collective-permute-start(f32[8,64,128]{2,1,0:T(8,128)S(1)} %get-tuple-element.35), channel_id=1, source_target_pairs={{0,1},{1,0},{2,3},{3,2},{4,5},{5,4},{6,7},{7,6},{8,9},{9,8},{10,11... | collective-permute-start | bytes 786440 | tf_op jit(solution)/shard_map/ppermute | solution.py:445
  25.7 6.5 %collective-permute-start.3 = (f32[8,64,128]{2,1,0:T(8,128)S(1)}, f32[8,64,128]{2,1,0:T(8,128)S(1)}, u32[]{:S(2)}, u32[]{:S(2)}) collective-permute-start(f32[8,64,128]{2,1,0:T(8,128)S(1)} %get-tuple-element.41), channel_id=1, source_target_pairs={{0,1},{1,0},{2,3},{3,2},{4,5},{5,4},{6,7},{7,6},{8,9},{9,8},{10,11... | collective-permute-start | bytes 786440 | tf_op jit(solution)/shard_map/ppermute | solution.py:445
  26.1 10.6 %collective-permute-start.4 = (f32[8,64,128]{2,1,0:T(8,128)S(1)}, f32[8,64,128]{2,1,0:T(8,128)S(1)}, u32[]{:S(2)}, u32[]{:S(2)}) collective-permute-start(f32[8,64,128]{2,1,0:T(8,128)S(1)} %get-tuple-element.42), channel_id=1, source_target_pairs={{0,63},{1,2},{2,1},{3,4},{4,3},{5,6},{6,5},{7,8},{8,7},{9,10},{10,... | collective-permute-start | bytes 786440 | tf_op jit(solution)/shard_map/ppermute | solution.py:450
  37.7 6.5 %collective-permute-start.5 = (f32[8,64,128]{2,1,0:T(8,128)S(1)}, f32[8,64,128]{2,1,0:T(8,128)S(1)}, u32[]{:S(2)}, u32[]{:S(2)}) collective-permute-start(f32[8,64,128]{2,1,0:T(8,128)S(1)} %get-tuple-element.46), channel_id=1, source_target_pairs={{0,1},{1,0},{2,3},{3,2},{4,5},{5,4},{6,7},{7,6},{8,9},{9,8},{10,11... | collective-permute-start | bytes 786440 | tf_op jit(solution)/shard_map/ppermute | solution.py:445
  37.8 10.7 %collective-permute-start.6 = (f32[8,64,128]{2,1,0:T(8,128)S(1)}, f32[8,64,128]{2,1,0:T(8,128)S(1)}, u32[]{:S(2)}, u32[]{:S(2)}) collective-permute-start(f32[8,64,128]{2,1,0:T(8,128)S(1)} %get-tuple-element.47), channel_id=1, source_target_pairs={{0,63},{1,2},{2,1},{3,4},{4,3},{5,6},{6,5},{7,8},{8,7},{9,10},{10,... | collective-permute-start | bytes 786440 | tf_op jit(solution)/shard_map/ppermute | solution.py:450

commit v16 on v14

--- a/solution.py
+++ b/solution.py
@@ -71,7 +71,7 @@
     return p, ((ah * bh - p) + ah * bl + al * bh) + al * bl
 
 
-def ahead_kernel(pattern, weights, ahead, mask, buf, cols, sems):
+def ahead_kernel(pattern, weights, ahead, buf, mask, cols, sems):
     head = pltpu.make_async_copy(pattern, mask, sems.at[T])
     head.start()
     copies = []
@@ -97,11 +97,10 @@
     pattern, weights = in_hbm(pattern), in_hbm(weights)
     return call(
         ahead_kernel,
-        shape(T, N),
+        (shape(T, N), shape(T, T, N, N)),
         [HBM, HBM],
         [
             pltpu.SMEM((T, T), jnp.int32),
-            pltpu.VMEM((T, T, N, N), F32),
             pltpu.VMEM((T, T, 8, N), F32),
             pltpu.SemaphoreType.DMA((T + 1,)),
         ],
@@ -110,14 +109,15 @@
     )(pattern, weights)
 
 
-def band_kernel(pattern, weights, reg, high, low, own, mask, buf, cols, extra, sems):
+def band_kernel(pattern, weights, kept, reg, high, low, own, mask, buf, cols, extra, sems):
     def copy(t):
-        return pltpu.make_async_copy(weights.at[t], buf.at[t], sems.at[t])
+        some = slice(0, T - 1 - t)
+        return pltpu.make_async_copy(weights.at[t, some], buf.at[t, some], sems.at[t])
 
     head = pltpu.make_async_copy(pattern, mask, sems.at[T])
     tail = pltpu.make_async_copy(reg, extra, sems.at[T + 1])
     head.start()
-    for t in range(T):
+    for t in range(T - 1):
         copy(t).start()
     tail.start()
     cols[...] = jnp.zeros_like(cols)
@@ -128,33 +128,31 @@
             piece[a, 0:N, T * N : (T + 1) * N] = zero
     head.wait()
 
-    def step(a, carry):
+    for a in range(T // 2):
         for half in range(2):
             t = 2 * a + half
-            copy(t).wait()
+            if t < T - 1:
+                copy(t).wait()
             rows = jnp.zeros((N, N), F32)
             for k in range(T):
-                m = buf[t, k] * mask[t, k].astype(F32)
+                m = (kept if k >= T - 1 - t else buf)[t, k] * mask[t, k].astype(F32)
                 rows = rows + m
                 cols[t + k + 1] += jnp.sum(m.reshape(N // 8, 8, N), axis=0)
                 h = m.astype(BF16)
                 place = slice((k + half) * N, (k + half + 1) * N)
                 high[a, half * N : (half + 1) * N, place] = h
                 low[a, half * N : (half + 1) * N, place] = (m - h.astype(F32)).astype(BF16)
-            own[pl.ds(t, 1), :] = jnp.sum(rows.T, axis=0, keepdims=True)
-        return carry
-
-    lax.fori_loop(0, T // 2, step, 0)
+            own[t : t + 1, :] = jnp.sum(rows.T, axis=0, keepdims=True)
     tail.wait()
     own[...] += jnp.sum(cols[:T], axis=1) + extra[...]
 
 
-def band_pieces(pattern, weights, reg):
+def band_pieces(pattern, weights, kept, reg):
     pattern, weights, reg = in_hbm(pattern), in_hbm(weights), in_hbm(reg)
     return call(
         band_kernel,
         (shape(*BAND, dtype=BF16), shape(*BAND, dtype=BF16), shape(T, N)),
-        [HBM, HBM, HBM],
+        [HBM, HBM, VMEM, HBM],
         [
             pltpu.SMEM((T, T), jnp.int32),
             pltpu.VMEM((T, T, N, N), F32),
@@ -164,7 +162,7 @@
         ],
         flops=2048 * T * T * N * N,
         moved=8 * T * T * N * N,
-    )(pattern, weights, reg)
+    )(pattern, weights, kept, reg)
 
 
 def put_pieces(pieces, t, value):
@@ -452,8 +450,9 @@
 def shards(weights, pattern, shift_reg, rhs):
     flag = jnp.broadcast_to((1 - lax.axis_index("tm") % 2).astype(F32), (8, N))
     flag, pattern = lax.optimization_barrier((flag, pattern))
-    inflow = shift(ahead_sums(pattern, weights), 1)
-    high, low, own = band_pieces(pattern, weights, shift_reg)
+    ahead, kept = ahead_sums(pattern, weights)
+    inflow = shift(ahead, 1)
+    high, low, own = band_pieces(pattern, weights, kept, shift_reg)
     diag, vec, two = first(rhs, own, inflow, high, low)
     got_two = swap_across(two)
     partial, part, one, *turned = local([vec], rhs, high, low)

time: 67.2 us -> 67.2 us (level)
  transfers between devices with their start and end apart: 7 -> 7, of which waited for: 7 -> 6; matrix products, arithmetic and copies ran while one was open for 0% -> 0% of each run, Pallas kernels for 10% -> 10%
where the time goes in v16:
time: 67.2 us; the launch traced here: 67 us
  waiting for transfers between devices  25.8 us (38%)
  blocking collectives  16.3 us (24%)
  Pallas kernels  13 us (19%)
  starting transfers between devices  11 us (16%)
  between operations  0.75 us (1%)
    all_to_all x1, blocking collectives, all_parts(): lax.all_to_all(jnp.broadcast_to(value[None], (count,) + value.shape), 'tm...  16.3 us
    ppermute x3, waiting for transfers between devices, swap_across(): lax.ppermute(value, 'tm', [(i, (i + (1 if i % 2 else -1)) % count) for i...  15.8 us
    ppermute x3, starting transfers between devices, swap_across(): lax.ppermute(value, 'tm', [(i, (i + (1 if i % 2 else -1)) % count) for i...  8.83 us
    ppermute x1, waiting for transfers between devices, shift(): lax.ppermute(value, 'tm', [(i, (i + steps) % count) for i in range(count)])  6.2 us
    pallas_call x3, Pallas kernels, local(): call(functools.partial(local_kernel, len(vecs)), (BLOCKS, shape(len(vecs)...  4.15 us
    ppermute x3, waiting for transfers between devices, swap_within(): lax.ppermute(value, 'tm', [(i, i ^ 1) for i in range(lax.axis_size('tm'))])  3.86 us
    pallas_call x1, Pallas kernels, band_pieces(): call(band_kernel, (shape(*BAND, dtype=BF16), shape(*BAND, dtype=BF16), sh...  2.74 us
    pallas_call x2, Pallas kernels, next_step(): call(step_kernel, (BLOCKS,) * 4, [VMEM] * 9, [PIECES, PIECES], flops=2 *...  2.04 us
  transfers between devices with their start and end apart: 7, of which 6 were waited for; matrix products, arithmetic and copies ran while one was open for 0% of the time, Pallas kernels for 10%

profile of v16, /device:TPU:4, one launch (start us, length us, event | category | flops | bytes accessed | tf_op | source)
XLA Modules:
  0.0 67.0 jit_solution(10245592901989168108)
XLA Ops:
  0.7 1.8 %shard_map.59 = (f32[8,128]{1,0:T(8,128)S(1)}, f32[8,8,128,128]{3,2,1,0:T(8,128)S(1)}) custom-call(s32[8,8]{1,0:T(8,128)} %pattern.1, f32[8,8,128,128]{3,2,1,0:T(8,128)} %weights.3), custom_call_target="tpu_custom_call" | custom-call | flops 4194304 | bytes 4194304 | tf_op jit(solution)/shard_map/pallas_call | solution.py:98
  2.5 1.7 %collective-permute-start = (f32[8,128]{1,0:T(8,128)S(1)}, f32[8,128]{1,0:T(8,128)S(1)}, u32[]{:S(2)}, u32[]{:S(2)}) collective-permute-start(f32[8,128]{1,0:T(8,128)S(1)} %get-tuple-element.35), channel_id=1, source_target_pairs={{0,1},{1,2},{2,3},{3,4},{4,5},{5,6},{6,7},{7,8},{8,9},{9,10},{10,1... | collective-permute-start | bytes 12296 | tf_op jit(solution)/shard_map/ppermute | solution.py:426
  4.1 2.7 %shard_map.60 = (bf16[4,256,1152]{2,1,0:T(8,128)(2,1)S(1)}, bf16[4,256,1152]{2,1,0:T(8,128)(2,1)S(1)}, f32[8,128]{1,0:T(8,128)S(1)}) custom-call(s32[8,8]{1,0:T(8,128)} %pattern.1, f32[8,8,128,128]{3,2,1,0:T(8,128)} %weights.3, f32[8,8,128,128]{3,2,1,0:T(8,128)S(1)} %get-tuple-element.33.kept, f32[8,128]{1,0:T(8,128)} %reg.1), custom_call_target="tpu_custom_call" | custom-call | flops 2147483648 | bytes 8388608 | tf_op jit(solution)/shard_map/pallas_call | solution.py:152
  6.9 6.2 %collective-permute-done.inflow = f32[8,128]{1,0:T(8,128)S(1)} collective-permute-done((f32[8,128]{1,0:T(8,128)S(1)}, f32[8,128]{1,0:T(8,128)S(1)}, u32[]{:S(2)}, u32[]{:S(2)}) %collective-permute-start) | collective-permute-done | bytes 4128 | tf_op jit(solution)/shard_map/ppermute | solution.py:426
  13.2 2.6 %collective-permute-start.2 = (f32[8,64,128]{2,1,0:T(8,128)S(1)}, f32[8,64,128]{2,1,0:T(8,128)S(1)}, u32[]{:S(2)}, u32[]{:S(2)}) collective-permute-start(f32[8,64,128]{2,1,0:T(8,128)S(1)} %get-tuple-element.40), channel_id=1, source_target_pairs={{0,63},{1,2},{2,1},{3,4},{4,3},{5,6},{6,5},{7,8},{8,7},{9,10},{10,... | collective-permute-start | bytes 786440 | tf_op jit(solution)/shard_map/ppermute | solution.py:447
  15.8 1.7 %shard_map.62 = (f32[8,64,128]{2,1,0:T(8,128)S(1)}, f32[1,2,64,128]{3,2,1,0:T(8,128)S(1)}, f32[8,64,128]{2,1,0:T(8,128)S(1)}, bf16[2560,256]{1,0:T(8,128)(2,1)S(1)}, bf16[2560,256]{1,0:T(8,128)(2,1)S(1)}) custom-call(f32[8,64,128]{2,1,0:T(8,128)S(1)} %get-tuple-element.38.refs_0_.v0, f32[8,64,128]{2,1,0:T(8,128)S(1)} %copy-done, ...), custom_call_target="tpu_custom_call" | custom-call | flops 503316480 | tf_op jit(solution)/shard_map/pallas_call | solution.py:306
  17.5 0.1 collective-permute-start.1
  17.6 7.0 %collective-permute-done.2.got_two = f32[8,64,128]{2,1,0:T(8,128)S(1)} collective-permute-done((f32[8,64,128]{2,1,0:T(8,128)S(1)}, f32[8,64,128]{2,1,0:T(8,128)S(1)}, u32[]{:S(2)}, u32[]{:S(2)}) %collective-permute-start.2) | collective-permute-done | bytes 262176 | tf_op jit(solution)/shard_map/ppermute | solution.py:447
  24.6 1.0 %shard_map.63 = (f32[8,64,128]{2,1,0:T(8,128)S(1)}, f32[8,64,128]{2,1,0:T(8,128)S(1)}, f32[8,64,128]{2,1,0:T(8,128)S(1)}, f32[8,64,128]{2,1,0:T(8,128)S(1)}) custom-call(f32[8,128]{1,0:T(8,128)S(1)} %broadcast_in_dim.11.flag, f32[8,64,128]{2,1,0:T(8,128)S(1)} %collective-permute-done.1.got_one, f32[8,64,128]{2,1,0:T(8,128)S(1)} %collective-permute-done.2.got_two, ...), custom_call_target="tpu_custom_call" | custom-call | flops 503316480 | tf_op jit(solution)/shard_map/pallas_call | solution.py:343
  25.7 0.3 collective-permute-start.3
  26.0 3.1 %collective-permute-start.4 = (f32[8,64,128]{2,1,0:T(8,128)S(1)}, f32[8,64,128]{2,1,0:T(8,128)S(1)}, u32[]{:S(2)}, u32[]{:S(2)}) collective-permute-start(f32[8,64,128]{2,1,0:T(8,128)S(1)} %get-tuple-element.46), channel_id=1, source_target_pairs={{0,63},{1,2},{2,1},{3,4},{4,3},{5,6},{6,5},{7,8},{8,7},{9,10},{10,... | collective-permute-start | bytes 786440 | tf_op jit(solution)/shard_map/ppermute | solution.py:447
  29.1 1.2 %shard_map.64 = (f32[8,64,128]{2,1,0:T(8,128)S(1)}, f32[2,2,64,128]{3,2,1,0:T(8,128)S(1)}) custom-call(f32[8,64,128]{2,1,0:T(8,128)S(1)} %get-tuple-element.38.refs_0_.v0, f32[8,64,128]{2,1,0:T(8,128)S(1)} %get-tuple-element.47.refs_1_.v1, f32[8,64,128]{2,1,0:T(8,128)S(1)} %get-tuple-element.48.refs_2_.y1, ...), custom_call_target="tpu_custom_call" | custom-call | flops 503316480 | tf_op jit(solution)/shard_map/pallas_call | solution.py:306
  30.2 1.9 %collective-permute-done.3.got_one = f32[8,64,128]{2,1,0:T(8,128)S(1)} collective-permute-done((f32[8,64,128]{2,1,0:T(8,128)S(1)}, f32[8,64,128]{2,1,0:T(8,128)S(1)}, u32[]{:S(2)}, u32[]{:S(2)}) %collective-permute-start.3) | collective-permute-done | bytes 262176 | tf_op jit(solution)/shard_map/ppermute | solution.py:442
  32.1 4.5 %collective-permute-done.4.got_two = f32[8,64,128]{2,1,0:T(8,128)S(1)} collective-permute-done((f32[8,64,128]{2,1,0:T(8,128)S(1)}, f32[8,64,128]{2,1,0:T(8,128)S(1)}, u32[]{:S(2)}, u32[]{:S(2)}) %collective-permute-start.4) | collective-permute-done | bytes 262176 | tf_op jit(solution)/shard_map/ppermute | solution.py:447
  36.6 1.0 %shard_map.65 = (f32[8,64,128]{2,1,0:T(8,128)S(1)}, f32[8,64,128]{2,1,0:T(8,128)S(1)}, f32[8,64,128]{2,1,0:T(8,128)S(1)}, f32[8,64,128]{2,1,0:T(8,128)S(1)}) custom-call(f32[8,128]{1,0:T(8,128)S(1)} %broadcast_in_dim.11.flag, f32[8,64,128]{2,1,0:T(8,128)S(1)} %collective-permute-done.3.got_one, f32[8,64,128]{2,1,0:T(8,128)S(1)} %collective-permute-done.4.got_two, ...), custom_call_target="tpu_custom_call" | custom-call | flops 503316480 | tf_op jit(solution)/shard_map/pallas_call | solution.py:343
  37.6 0.1 collective-permute-start.5
  37.7 3.1 %collective-permute-start.6 = (f32[8,64,128]{2,1,0:T(8,128)S(1)}, f32[8,64,128]{2,1,0:T(8,128)S(1)}, u32[]{:S(2)}, u32[]{:S(2)}) collective-permute-start(f32[8,64,128]{2,1,0:T(8,128)S(1)} %get-tuple-element.51), channel_id=1, source_target_pairs={{0,63},{1,2},{2,1},{3,4},{4,3},{5,6},{6,5},{7,8},{8,7},{9,10},{10,... | collective-permute-start | bytes 786440 | tf_op jit(solution)/shard_map/ppermute | solution.py:447
  40.9 1.2 %shard_map.66 = (f32[8,64,128]{2,1,0:T(8,128)S(1)}, f32[3,2,64,128]{3,2,1,0:T(8,128)S(1)}) custom-call(f32[8,64,128]{2,1,0:T(8,128)S(1)} %get-tuple-element.38.refs_0_.v0, f32[8,64,128]{2,1,0:T(8,128)S(1)} %get-tuple-element.47.refs_1_.v1, f32[8,64,128]{2,1,0:T(8,128)S(1)} %get-tuple-element.52.refs_2_.v2, f32[8,64,128]{2,1,0:T(8,128)S(1)} %get-tuple-element.53.refs_3_.y2, ...), custom_call_target="tpu_custom_call" | custom-call | flops 503316480 | tf_op jit(solution)/shard_map/pallas_call | solution.py:306
  42.1 2.0 %collective-permute-done.5.got_one = f32[8,64,128]{2,1,0:T(8,128)S(1)} collective-permute-done((f32[8,64,128]{2,1,0:T(8,128)S(1)}, f32[8,64,128]{2,1,0:T(8,128)S(1)}, u32[]{:S(2)}, u32[]{:S(2)}) %collective-permute-start.5) | collective-permute-done | bytes 262176 | tf_op jit(solution)/shard_map/ppermute | solution.py:442
  44.1 4.3 %collective-permute-done.6.got_two = f32[8,64,128]{2,1,0:T(8,128)S(1)} collective-permute-done((f32[8,64,128]{2,1,0:T(8,128)S(1)}, f32[8,64,128]{2,1,0:T(8,128)S(1)}, u32[]{:S(2)}, u32[]{:S(2)}) %collective-permute-start.6) | collective-permute-done | bytes 262176 | tf_op jit(solution)/shard_map/ppermute | solution.py:447
  48.4 0.9 %shard_map.67 = (f32[8,64,128]{2,1,0:T(8,128)S(1)}, f32[1,640]{1,0:T(1,128)S(1)}) custom-call(f32[8,128]{1,0:T(8,128)S(1)} %broadcast_in_dim.11.flag, f32[8,64,128]{2,1,0:T(8,128)S(1)} %collective-permute-done.5.got_one, f32[8,64,128]{2,1,0:T(8,128)S(1)} %collective-permute-done.6.got_two, f32[8,64,128]{2,1,0:T(8,128)S(1)} %get-tuple-element.54.partial, ...), custom_call_target="tpu_custom_call" | custom-call | flops 251658240 | tf_op jit(solution)/shard_map/pallas_call | solution.py:373
  49.3 0.1 broadcast_in_dim.13
  49.4 16.3 %all_to_all.5 = f32[64,1,640]{2,1,0:T(1,128)S(1)} all-to-all(f32[64,1,640]{2,1,0:T(1,128)S(1)} %broadcast_in_dim.13), channel_id=1, replica_groups={{40,41,42,43,44,45,46,47,48,49,50,51,52,53,54,55,56,57,58,59,60,61,62,6..., dimensions={0} | all-to-all | bytes 327680 | tf_op jit(solution)/shard_map/all_to_all | solution.py:435
  65.7 1.3 %shard_map.68 = (f32[8,64,128]{2,1,0:T(8,128)}, f32[8,64,128]{2,1,0:T(8,128)}) custom-call(f32[64,640]{1,0:T(8,128)S(1)} %bitcast.3, f32[8,64,128]{2,1,0:T(8,128)S(1)} %get-tuple-element.38.refs_0_.v0, f32[8,64,128]{2,1,0:T(8,128)S(1)} %get-tuple-element.47.refs_1_.v1, f32[8,64,128]{2,1,0:T(8,128)S(1)} %get-tuple-element.52.refs_2_.v2, ...), custom_call_target="tpu_custom_call" | custom-call | tf_op jit(solution)/shard_map/pallas_call | solution.py:421
  (7 shorter events, 0.1 us)
Async XLA Ops:
  2.5 10.6 %collective-permute-start = (f32[8,128]{1,0:T(8,128)S(1)}, f32[8,128]{1,0:T(8,128)S(1)}, u32[]{:S(2)}, u32[]{:S(2)}) collective-permute-start(f32[8,128]{1,0:T(8,128)S(1)} %get-tuple-element.35), channel_id=1, source_target_pairs={{0,1},{1,2},{2,3},{3,4},{4,5},{5,6},{6,7},{7,8},{8,9},{9,10},{10,1... | collective-permute-start | bytes 12296 | tf_op jit(solution)/shard_map/ppermute | solution.py:426
  4.1 9.0 %copy-start = (f32[8,64,128]{2,1,0:T(8,128)S(1)}, f32[8,64,128]{2,1,0:T(8,128)}, u32[]{:S(2)}) copy-start(f32[8,64,128]{2,1,0:T(8,128)} %y0.1) | copy-start | bytes 786436
  13.2 11.5 %collective-permute-start.2 = (f32[8,64,128]{2,1,0:T(8,128)S(1)}, f32[8,64,128]{2,1,0:T(8,128)S(1)}, u32[]{:S(2)}, u32[]{:S(2)}) collective-permute-start(f32[8,64,128]{2,1,0:T(8,128)S(1)} %get-tuple-element.40), channel_id=1, source_target_pairs={{0,63},{1,2},{2,1},{3,4},{4,3},{5,6},{6,5},{7,8},{8,7},{9,10},{10,... | collective-permute-start | bytes 786440 | tf_op jit(solution)/shard_map/ppermute | solution.py:447
  17.5 7.1 %collective-permute-start.1 = (f32[8,64,128]{2,1,0:T(8,128)S(1)}, f32[8,64,128]{2,1,0:T(8,128)S(1)}, u32[]{:S(2)}, u32[]{:S(2)}) collective-permute-start(f32[8,64,128]{2,1,0:T(8,128)S(1)} %get-tuple-element.39), channel_id=1, source_target_pairs={{0,1},{1,0},{2,3},{3,2},{4,5},{5,4},{6,7},{7,6},{8,9},{9,8},{10,11... | collective-permute-start | bytes 786440 | tf_op jit(solution)/shard_map/ppermute | solution.py:442
  25.7 6.5 %collective-permute-start.3 = (f32[8,64,128]{2,1,0:T(8,128)S(1)}, f32[8,64,128]{2,1,0:T(8,128)S(1)}, u32[]{:S(2)}, u32[]{:S(2)}) collective-permute-start(f32[8,64,128]{2,1,0:T(8,128)S(1)} %get-tuple-element.45), channel_id=1, source_target_pairs={{0,1},{1,0},{2,3},{3,2},{4,5},{5,4},{6,7},{7,6},{8,9},{9,8},{10,11... | collective-permute-start | bytes 786440 | tf_op jit(solution)/shard_map/ppermute | solution.py:442
  26.0 10.6 %collective-permute-start.4 = (f32[8,64,128]{2,1,0:T(8,128)S(1)}, f32[8,64,128]{2,1,0:T(8,128)S(1)}, u32[]{:S(2)}, u32[]{:S(2)}) collective-permute-start(f32[8,64,128]{2,1,0:T(8,128)S(1)} %get-tuple-element.46), channel_id=1, source_target_pairs={{0,63},{1,2},{2,1},{3,4},{4,3},{5,6},{6,5},{7,8},{8,7},{9,10},{10,... | collective-permute-start | bytes 786440 | tf_op jit(solution)/shard_map/ppermute | solution.py:447
  37.6 6.5 %collective-permute-start.5 = (f32[8,64,128]{2,1,0:T(8,128)S(1)}, f32[8,64,128]{2,1,0:T(8,128)S(1)}, u32[]{:S(2)}, u32[]{:S(2)}) collective-permute-start(f32[8,64,128]{2,1,0:T(8,128)S(1)} %get-tuple-element.50), channel_id=1, source_target_pairs={{0,1},{1,0},{2,3},{3,2},{4,5},{5,4},{6,7},{7,6},{8,9},{9,8},{10,11... | collective-permute-start | bytes 786440 | tf_op jit(solution)/shard_map/ppermute | solution.py:442
  37.7 10.7 %collective-permute-start.6 = (f32[8,64,128]{2,1,0:T(8,128)S(1)}, f32[8,64,128]{2,1,0:T(8,128)S(1)}, u32[]{:S(2)}, u32[]{:S(2)}) collective-permute-start(f32[8,64,128]{2,1,0:T(8,128)S(1)} %get-tuple-element.51), channel_id=1, source_target_pairs={{0,63},{1,2},{2,1},{3,4},{4,3},{5,6},{6,5},{7,8},{8,7},{9,10},{10,... | collective-permute-start | bytes 786440 | tf_op jit(solution)/shard_map/ppermute | solution.py:447

commit v17 on v14

--- a/solution.py
+++ b/solution.py
@@ -402,8 +402,8 @@
     matrix = [[minus(row[j], row[j + 1]) for j in range(3)] for row in full]
     right = [row[1] for row in full]
     near = [[m[0] + m[1] for m in row] for row in matrix]
-    coef = [jnp.zeros_like(g00[0])] * 3
-    for _ in range(3):
+    coef = solve(near, [value[0] + value[1] for value in right])
+    for _ in range(2):
         left = []
         for row, value in zip(matrix, right):
             for m, c in zip(row, coef):

time: 67.2 us -> 67.2 us (level)
  no operation moved by 1% of the time
where the time goes in v17:
time: 67.2 us; the launch traced here: 67 us
  waiting for transfers between devices  26 us (39%)
  blocking collectives  16.2 us (24%)
  Pallas kernels  13.1 us (19%)
  starting transfers between devices  10.9 us (16%)
  between operations  0.76 us (1%)
    all_to_all x1, blocking collectives, all_parts(): lax.all_to_all(jnp.broadcast_to(value[None], (count,) + value.shape), 'tm...  16.2 us
    ppermute x3, waiting for transfers between devices, swap_across(): lax.ppermute(value, 'tm', [(i, (i + (1 if i % 2 else -1)) % count) for i...  15.8 us
    ppermute x3, starting transfers between devices, swap_across(): lax.ppermute(value, 'tm', [(i, (i + (1 if i % 2 else -1)) % count) for i...  8.65 us
    ppermute x1, waiting for transfers between devices, shift(): lax.ppermute(value, 'tm', [(i, (i + steps) % count) for i in range(count)])  6.09 us
    pallas_call x3, Pallas kernels, local(): call(functools.partial(local_kernel, len(vecs)), (BLOCKS, shape(len(vecs)...  4.17 us
    ppermute x3, waiting for transfers between devices, swap_within(): lax.ppermute(value, 'tm', [(i, i ^ 1) for i in range(lax.axis_size('tm'))])  4.09 us
    pallas_call x1, Pallas kernels, band_pieces(): call(band_kernel, (shape(*BAND, dtype=BF16), shape(*BAND, dtype=BF16), sh...  2.85 us
    pallas_call x2, Pallas kernels, next_step(): call(step_kernel, (BLOCKS,) * 4, [VMEM] * 9, [PIECES, PIECES], flops=2 *...  2 us
  transfers between devices with their start and end apart: 7, of which 7 were waited for; matrix products, arithmetic and copies ran while one was open for 0% of the time, Pallas kernels for 10%

profile of v17, /device:TPU:4, one launch (start us, length us, event | category | flops | bytes accessed | tf_op | source)
XLA Modules:
  0.0 67.0 jit_solution(11160762610014392829)
XLA Ops:
  0.7 1.8 %shard_map.60 = f32[8,128]{1,0:T(8,128)S(1)} custom-call(s32[8,8]{1,0:T(8,128)} %pattern.1, f32[8,8,128,128]{3,2,1,0:T(8,128)} %weights.3), custom_call_target="tpu_custom_call" | custom-call | flops 4194304 | bytes 4194304 | tf_op jit(solution)/shard_map/pallas_call | solution.py:98
  2.5 1.7 %collective-permute-start = (f32[8,128]{1,0:T(8,128)S(1)}, f32[8,128]{1,0:T(8,128)S(1)}, u32[]{:S(2)}, u32[]{:S(2)}) collective-permute-start(f32[8,128]{1,0:T(8,128)S(1)} %shard_map.60), channel_id=1, source_target_pairs={{0,1},{1,2},{2,3},{3,4},{4,5},{5,6},{6,7},{7,8},{8,9},{9,10},{10,1... | collective-permute-start | bytes 12296 | tf_op jit(solution)/shard_map/ppermute | solution.py:428
  4.2 2.8 %shard_map.59 = (bf16[4,256,1152]{2,1,0:T(8,128)(2,1)S(1)}, bf16[4,256,1152]{2,1,0:T(8,128)(2,1)S(1)}, f32[8,128]{1,0:T(8,128)S(1)}) custom-call(s32[8,8]{1,0:T(8,128)} %pattern.1, f32[8,8,128,128]{3,2,1,0:T(8,128)} %weights.3, f32[8,128]{1,0:T(8,128)} %reg.1), custom_call_target="tpu_custom_call" | custom-call | flops 2147483648 | bytes 8388608 | tf_op jit(solution)/shard_map/pallas_call | solution.py:154
  7.0 6.1 %collective-permute-done.inflow = f32[8,128]{1,0:T(8,128)S(1)} collective-permute-done((f32[8,128]{1,0:T(8,128)S(1)}, f32[8,128]{1,0:T(8,128)S(1)}, u32[]{:S(2)}, u32[]{:S(2)}) %collective-permute-start) | collective-permute-done | bytes 4128 | tf_op jit(solution)/shard_map/ppermute | solution.py:428
  13.2 2.6 %collective-permute-start.2 = (f32[8,64,128]{2,1,0:T(8,128)S(1)}, f32[8,64,128]{2,1,0:T(8,128)S(1)}, u32[]{:S(2)}, u32[]{:S(2)}) collective-permute-start(f32[8,64,128]{2,1,0:T(8,128)S(1)} %get-tuple-element.36), channel_id=1, source_target_pairs={{0,63},{1,2},{2,1},{3,4},{4,3},{5,6},{6,5},{7,8},{8,7},{9,10},{10,... | collective-permute-start | bytes 786440 | tf_op jit(solution)/shard_map/ppermute | solution.py:449
  15.8 1.8 %shard_map.62 = (f32[8,64,128]{2,1,0:T(8,128)S(1)}, f32[1,2,64,128]{3,2,1,0:T(8,128)S(1)}, f32[8,64,128]{2,1,0:T(8,128)S(1)}, bf16[2560,256]{1,0:T(8,128)(2,1)S(1)}, bf16[2560,256]{1,0:T(8,128)(2,1)S(1)}) custom-call(f32[8,64,128]{2,1,0:T(8,128)S(1)} %get-tuple-element.34.refs_0_.v0, f32[8,64,128]{2,1,0:T(8,128)S(1)} %copy-done, ...), custom_call_target="tpu_custom_call" | custom-call | flops 503316480 | tf_op jit(solution)/shard_map/pallas_call | solution.py:308
  17.6 0.1 collective-permute-start.1
  17.7 7.0 %collective-permute-done.2.got_two = f32[8,64,128]{2,1,0:T(8,128)S(1)} collective-permute-done((f32[8,64,128]{2,1,0:T(8,128)S(1)}, f32[8,64,128]{2,1,0:T(8,128)S(1)}, u32[]{:S(2)}, u32[]{:S(2)}) %collective-permute-start.2) | collective-permute-done | bytes 262176 | tf_op jit(solution)/shard_map/ppermute | solution.py:449
  24.7 1.0 %shard_map.63 = (f32[8,64,128]{2,1,0:T(8,128)S(1)}, f32[8,64,128]{2,1,0:T(8,128)S(1)}, f32[8,64,128]{2,1,0:T(8,128)S(1)}, f32[8,64,128]{2,1,0:T(8,128)S(1)}) custom-call(f32[8,128]{1,0:T(8,128)S(1)} %broadcast_in_dim.11.flag, f32[8,64,128]{2,1,0:T(8,128)S(1)} %collective-permute-done.1.got_one, f32[8,64,128]{2,1,0:T(8,128)S(1)} %collective-permute-done.2.got_two, ...), custom_call_target="tpu_custom_call" | custom-call | flops 503316480 | tf_op jit(solution)/shard_map/pallas_call | solution.py:345
  25.7 0.4 collective-permute-start.3
  26.1 3.0 %collective-permute-start.4 = (f32[8,64,128]{2,1,0:T(8,128)S(1)}, f32[8,64,128]{2,1,0:T(8,128)S(1)}, u32[]{:S(2)}, u32[]{:S(2)}) collective-permute-start(f32[8,64,128]{2,1,0:T(8,128)S(1)} %get-tuple-element.42), channel_id=1, source_target_pairs={{0,63},{1,2},{2,1},{3,4},{4,3},{5,6},{6,5},{7,8},{8,7},{9,10},{10,... | collective-permute-start | bytes 786440 | tf_op jit(solution)/shard_map/ppermute | solution.py:449
  29.1 1.2 %shard_map.64 = (f32[8,64,128]{2,1,0:T(8,128)S(1)}, f32[2,2,64,128]{3,2,1,0:T(8,128)S(1)}) custom-call(f32[8,64,128]{2,1,0:T(8,128)S(1)} %get-tuple-element.34.refs_0_.v0, f32[8,64,128]{2,1,0:T(8,128)S(1)} %get-tuple-element.43.refs_1_.v1, f32[8,64,128]{2,1,0:T(8,128)S(1)} %get-tuple-element.44.refs_2_.y1, ...), custom_call_target="tpu_custom_call" | custom-call | flops 503316480 | tf_op jit(solution)/shard_map/pallas_call | solution.py:308
  30.3 1.9 %collective-permute-done.3.got_one = f32[8,64,128]{2,1,0:T(8,128)S(1)} collective-permute-done((f32[8,64,128]{2,1,0:T(8,128)S(1)}, f32[8,64,128]{2,1,0:T(8,128)S(1)}, u32[]{:S(2)}, u32[]{:S(2)}) %collective-permute-start.3) | collective-permute-done | bytes 262176 | tf_op jit(solution)/shard_map/ppermute | solution.py:444
  32.2 4.5 %collective-permute-done.4.got_two = f32[8,64,128]{2,1,0:T(8,128)S(1)} collective-permute-done((f32[8,64,128]{2,1,0:T(8,128)S(1)}, f32[8,64,128]{2,1,0:T(8,128)S(1)}, u32[]{:S(2)}, u32[]{:S(2)}) %collective-permute-start.4) | collective-permute-done | bytes 262176 | tf_op jit(solution)/shard_map/ppermute | solution.py:449
  36.7 1.0 %shard_map.65 = (f32[8,64,128]{2,1,0:T(8,128)S(1)}, f32[8,64,128]{2,1,0:T(8,128)S(1)}, f32[8,64,128]{2,1,0:T(8,128)S(1)}, f32[8,64,128]{2,1,0:T(8,128)S(1)}) custom-call(f32[8,128]{1,0:T(8,128)S(1)} %broadcast_in_dim.11.flag, f32[8,64,128]{2,1,0:T(8,128)S(1)} %collective-permute-done.3.got_one, f32[8,64,128]{2,1,0:T(8,128)S(1)} %collective-permute-done.4.got_two, ...), custom_call_target="tpu_custom_call" | custom-call | flops 503316480 | tf_op jit(solution)/shard_map/pallas_call | solution.py:345
  37.7 0.1 collective-permute-start.5
  37.8 3.0 %collective-permute-start.6 = (f32[8,64,128]{2,1,0:T(8,128)S(1)}, f32[8,64,128]{2,1,0:T(8,128)S(1)}, u32[]{:S(2)}, u32[]{:S(2)}) collective-permute-start(f32[8,64,128]{2,1,0:T(8,128)S(1)} %get-tuple-element.47), channel_id=1, source_target_pairs={{0,63},{1,2},{2,1},{3,4},{4,3},{5,6},{6,5},{7,8},{8,7},{9,10},{10,... | collective-permute-start | bytes 786440 | tf_op jit(solution)/shard_map/ppermute | solution.py:449
  40.9 1.2 %shard_map.66 = (f32[8,64,128]{2,1,0:T(8,128)S(1)}, f32[3,2,64,128]{3,2,1,0:T(8,128)S(1)}) custom-call(f32[8,64,128]{2,1,0:T(8,128)S(1)} %get-tuple-element.34.refs_0_.v0, f32[8,64,128]{2,1,0:T(8,128)S(1)} %get-tuple-element.43.refs_1_.v1, f32[8,64,128]{2,1,0:T(8,128)S(1)} %get-tuple-element.48.refs_2_.v2, f32[8,64,128]{2,1,0:T(8,128)S(1)} %get-tuple-element.49.refs_3_.y2, ...), custom_call_target="tpu_custom_call" | custom-call | flops 503316480 | tf_op jit(solution)/shard_map/pallas_call | solution.py:308
  42.1 2.1 %collective-permute-done.5.got_one = f32[8,64,128]{2,1,0:T(8,128)S(1)} collective-permute-done((f32[8,64,128]{2,1,0:T(8,128)S(1)}, f32[8,64,128]{2,1,0:T(8,128)S(1)}, u32[]{:S(2)}, u32[]{:S(2)}) %collective-permute-start.5) | collective-permute-done | bytes 262176 | tf_op jit(solution)/shard_map/ppermute | solution.py:444
  44.2 4.3 %collective-permute-done.6.got_two = f32[8,64,128]{2,1,0:T(8,128)S(1)} collective-permute-done((f32[8,64,128]{2,1,0:T(8,128)S(1)}, f32[8,64,128]{2,1,0:T(8,128)S(1)}, u32[]{:S(2)}, u32[]{:S(2)}) %collective-permute-start.6) | collective-permute-done | bytes 262176 | tf_op jit(solution)/shard_map/ppermute | solution.py:449
  48.5 0.9 %shard_map.67 = (f32[8,64,128]{2,1,0:T(8,128)S(1)}, f32[1,640]{1,0:T(1,128)S(1)}) custom-call(f32[8,128]{1,0:T(8,128)S(1)} %broadcast_in_dim.11.flag, f32[8,64,128]{2,1,0:T(8,128)S(1)} %collective-permute-done.5.got_one, f32[8,64,128]{2,1,0:T(8,128)S(1)} %collective-permute-done.6.got_two, f32[8,64,128]{2,1,0:T(8,128)S(1)} %get-tuple-element.50.partial, ...), custom_call_target="tpu_custom_call" | custom-call | flops 251658240 | tf_op jit(solution)/shard_map/pallas_call | solution.py:375
  49.4 0.1 broadcast_in_dim.13
  49.5 16.2 %all_to_all.5 = f32[64,1,640]{2,1,0:T(1,128)S(1)} all-to-all(f32[64,1,640]{2,1,0:T(1,128)S(1)} %broadcast_in_dim.13), channel_id=1, replica_groups={{40,41,42,43,44,45,46,47,48,49,50,51,52,53,54,55,56,57,58,59,60,61,62,6..., dimensions={0} | all-to-all | bytes 327680 | tf_op jit(solution)/shard_map/all_to_all | solution.py:437
  65.7 1.3 %shard_map.68 = (f32[8,64,128]{2,1,0:T(8,128)}, f32[8,64,128]{2,1,0:T(8,128)}) custom-call(f32[64,640]{1,0:T(8,128)S(1)} %bitcast.3, f32[8,64,128]{2,1,0:T(8,128)S(1)} %get-tuple-element.34.refs_0_.v0, f32[8,64,128]{2,1,0:T(8,128)S(1)} %get-tuple-element.43.refs_1_.v1, f32[8,64,128]{2,1,0:T(8,128)S(1)} %get-tuple-element.48.refs_2_.v2, ...), custom_call_target="tpu_custom_call" | custom-call | tf_op jit(solution)/shard_map/pallas_call | solution.py:423
  (7 shorter events, 0.2 us)
Async XLA Ops:
  2.5 10.6 %copy-start = (f32[8,64,128]{2,1,0:T(8,128)S(1)}, f32[8,64,128]{2,1,0:T(8,128)}, u32[]{:S(2)}) copy-start(f32[8,64,128]{2,1,0:T(8,128)} %y0.1) | copy-start | bytes 786436
  2.5 10.6 %collective-permute-start = (f32[8,128]{1,0:T(8,128)S(1)}, f32[8,128]{1,0:T(8,128)S(1)}, u32[]{:S(2)}, u32[]{:S(2)}) collective-permute-start(f32[8,128]{1,0:T(8,128)S(1)} %shard_map.60), channel_id=1, source_target_pairs={{0,1},{1,2},{2,3},{3,4},{4,5},{5,6},{6,7},{7,8},{8,9},{9,10},{10,1... | collective-permute-start | bytes 12296 | tf_op jit(solution)/shard_map/ppermute | solution.py:428
  13.2 11.5 %collective-permute-start.2 = (f32[8,64,128]{2,1,0:T(8,128)S(1)}, f32[8,64,128]{2,1,0:T(8,128)S(1)}, u32[]{:S(2)}, u32[]{:S(2)}) collective-permute-start(f32[8,64,128]{2,1,0:T(8,128)S(1)} %get-tuple-element.36), channel_id=1, source_target_pairs={{0,63},{1,2},{2,1},{3,4},{4,3},{5,6},{6,5},{7,8},{8,7},{9,10},{10,... | collective-permute-start | bytes 786440 | tf_op jit(solution)/shard_map/ppermute | solution.py:449
  17.6 7.2 %collective-permute-start.1 = (f32[8,64,128]{2,1,0:T(8,128)S(1)}, f32[8,64,128]{2,1,0:T(8,128)S(1)}, u32[]{:S(2)}, u32[]{:S(2)}) collective-permute-start(f32[8,64,128]{2,1,0:T(8,128)S(1)} %get-tuple-element.35), channel_id=1, source_target_pairs={{0,1},{1,0},{2,3},{3,2},{4,5},{5,4},{6,7},{7,6},{8,9},{9,8},{10,11... | collective-permute-start | bytes 786440 | tf_op jit(solution)/shard_map/ppermute | solution.py:444
  25.7 6.5 %collective-permute-start.3 = (f32[8,64,128]{2,1,0:T(8,128)S(1)}, f32[8,64,128]{2,1,0:T(8,128)S(1)}, u32[]{:S(2)}, u32[]{:S(2)}) collective-permute-start(f32[8,64,128]{2,1,0:T(8,128)S(1)} %get-tuple-element.41), channel_id=1, source_target_pairs={{0,1},{1,0},{2,3},{3,2},{4,5},{5,4},{6,7},{7,6},{8,9},{9,8},{10,11... | collective-permute-start | bytes 786440 | tf_op jit(solution)/shard_map/ppermute | solution.py:444
  26.1 10.6 %collective-permute-start.4 = (f32[8,64,128]{2,1,0:T(8,128)S(1)}, f32[8,64,128]{2,1,0:T(8,128)S(1)}, u32[]{:S(2)}, u32[]{:S(2)}) collective-permute-start(f32[8,64,128]{2,1,0:T(8,128)S(1)} %get-tuple-element.42), channel_id=1, source_target_pairs={{0,63},{1,2},{2,1},{3,4},{4,3},{5,6},{6,5},{7,8},{8,7},{9,10},{10,... | collective-permute-start | bytes 786440 | tf_op jit(solution)/shard_map/ppermute | solution.py:449
  37.7 6.5 %collective-permute-start.5 = (f32[8,64,128]{2,1,0:T(8,128)S(1)}, f32[8,64,128]{2,1,0:T(8,128)S(1)}, u32[]{:S(2)}, u32[]{:S(2)}) collective-permute-start(f32[8,64,128]{2,1,0:T(8,128)S(1)} %get-tuple-element.46), channel_id=1, source_target_pairs={{0,1},{1,0},{2,3},{3,2},{4,5},{5,4},{6,7},{7,6},{8,9},{9,8},{10,11... | collective-permute-start | bytes 786440 | tf_op jit(solution)/shard_map/ppermute | solution.py:444
  37.8 10.7 %collective-permute-start.6 = (f32[8,64,128]{2,1,0:T(8,128)S(1)}, f32[8,64,128]{2,1,0:T(8,128)S(1)}, u32[]{:S(2)}, u32[]{:S(2)}) collective-permute-start(f32[8,64,128]{2,1,0:T(8,128)S(1)} %get-tuple-element.47), channel_id=1, source_target_pairs={{0,63},{1,2},{2,1},{3,4},{4,3},{5,6},{6,5},{7,8},{8,7},{9,10},{10,... | collective-permute-start | bytes 786440 | tf_op jit(solution)/shard_map/ppermute | solution.py:449
